TPU v7x, 32 devices: a whole 2x2x4 slice. The times are simulated.
32 devices in a mesh: grp: 4 (over y, x), sub: 8 (over z, core).
Axes of the slice: x: 2, y: 2, z: 4, core: 2. Of those that a mesh axis runs over, the one named last changes fastest.
Arguments:
- right_side: float32 [64, 16384], P(None, ('grp', 'sub')), may hold values from -6 to 6
- order: int32 [16384], P(('grp', 'sub')), may hold values from 0 to 16383, as said below
- leaf_split: int32 [32], P(('grp', 'sub')), may hold values from 128 to 384
- leaf_inverse: float32 [16384, 512], P(('grp', 'sub')), may hold values from -2 to 2
- basis_left: float32 [6, 16384, 128], P(None, ('grp', 'sub')), may hold values from -0.5 to 0.5
- basis_right: float32 [6, 16384, 128], P(None, ('grp', 'sub')), may hold values from -1.5 to 1.5
- coupling: float32 [32, 6, 256, 256], P(('grp', 'sub')), may hold values from -0.5 to 0.5, as said below
Outputs:
- solution: float32 [64, 16384], P(None, ('grp', 'sub'))
Inputs may be any that keep to these rules, and one draw needn't show every extreme that they name: order[i] lies in the same block of 512 positions as i, and each block's entries are a permutation of that block's indices. coupling[d, k] is the same for all device blocks d with the same d // 2^(5 - k).
All inputs are finite; a program needn't handle non-finite values.
Results may differ from a plain program's by a relative error of at most 0.0001.
Values sent between devices are 32-bit elements; how exact they have to be, the bound alone decides.
No kernel may reach another device: no remote copies, remote signals or barrier semaphores. Data moves between devices by JAX's collectives and lax.ppermute only.
A program may use at most 64 MiB of HBM per device.

v0:
```python
import jax
import jax.numpy as jnp
from jax import lax
from jax.sharding import PartitionSpec as P


def partner(value, axis, distance):
    return lax.ppermute(value, axis, [(i, i ^ 1 << distance) for i in range(lax.axis_size(axis))])


def reduce_summand(summand, bit_count):
    for bit_number in range(bit_count):
        summand = summand + partner(summand, ("grp", "sub"), bit_number)
    return summand


def solve_columns(current, is_left, leaf_masked, basis_left, basis_right, coupling):
    highest_level = lax.Precision.HIGHEST
    contract = (((1,), (1,)), ((), ()))
    current = jnp.dot(
        current, leaf_masked, precision=highest_level, preferred_element_type=jnp.float32
    )
    levels_all = basis_left.shape[0]
    top_level = levels_all - 1
    rank_width = basis_left.shape[2]
    left_row_slice = jnp.where(is_left[None, :], current, 0.0)
    right_row_slice = jnp.where(is_left[None, :], 0.0, current)
    weights = jnp.concatenate(
        [
            jnp.dot(
                left_row_slice,
                basis_right[top_level],
                precision=highest_level,
                preferred_element_type=jnp.float32,
            ),
            jnp.dot(
                right_row_slice,
                basis_right[top_level],
                precision=highest_level,
                preferred_element_type=jnp.float32,
            ),
        ],
        axis=1,
    )
    coupled_system = jnp.dot(
        weights, coupling[0, top_level], precision=highest_level, preferred_element_type=jnp.float32
    )
    upper_update = lax.dot_general(
        coupled_system[:, :rank_width],
        basis_left[top_level],
        contract,
        precision=highest_level,
        preferred_element_type=jnp.float32,
    )
    lower_update = lax.dot_general(
        coupled_system[:, rank_width:],
        basis_left[top_level],
        contract,
        precision=highest_level,
        preferred_element_type=jnp.float32,
    )
    current = current - jnp.where(is_left[None, :], upper_update, lower_update)
    device_id = lax.axis_index(("grp", "sub"))
    for tree_level in range(top_level - 1, -1, -1):
        bit_count = top_level - tree_level
        on_right = jnp.right_shift(device_id, bit_count - 1) & 1
        partial_value = jnp.dot(
            current,
            basis_right[tree_level],
            precision=highest_level,
            preferred_element_type=jnp.float32,
        )
        zeros_part = jnp.zeros_like(partial_value)
        summand = jnp.where(
            on_right == 0,
            jnp.concatenate([partial_value, zeros_part], axis=1),
            jnp.concatenate([zeros_part, partial_value], axis=1),
        )
        summand = reduce_summand(summand, bit_count)
        coupled_system = jnp.dot(
            summand,
            coupling[0, tree_level],
            precision=highest_level,
            preferred_element_type=jnp.float32,
        )
        chosen = jnp.where(
            on_right == 0, coupled_system[:, :rank_width], coupled_system[:, rank_width:]
        )
        current = current - lax.dot_general(
            chosen,
            basis_left[tree_level],
            contract,
            precision=highest_level,
            preferred_element_type=jnp.float32,
        )
    return current


def per_device(right_side, order, leaf_split, leaf_inverse, basis_left, basis_right, coupling):
    row_count = right_side.shape[1]
    local_order = order % row_count
    gathered = jnp.take(right_side, local_order, axis=1)
    positions = lax.iota(jnp.int32, row_count)
    is_left = positions < leaf_split[0]
    block_mask = is_left[:, None] == is_left[None, :]
    leaf_masked = jnp.where(block_mask, leaf_inverse, 0.0)
    return solve_columns(gathered, is_left, leaf_masked, basis_left, basis_right, coupling)


def solution(mesh):
    in_specs = (
        P(None, ("grp", "sub")),
        P(("grp", "sub")),
        P(("grp", "sub")),
        P(("grp", "sub"), None),
        P(None, ("grp", "sub"), None),
        P(None, ("grp", "sub"), None),
        P(("grp", "sub"), None, None, None),
    )
    out_specs = P(None, ("grp", "sub"))
    return jax.shard_map(
        per_device, mesh=mesh, in_specs=in_specs, out_specs=out_specs, check_vma=False
    )
```

profile of v0, /device:TPU:0, one launch (start us, length us, event | category | flops | bytes accessed | tf_op | source)
XLA Modules:
  0.0 73.3 jit_solution(17686523979821772136)
XLA Ops:
  0.0 0.0 copy-start.1
  0.8 0.7 compare_and_fusion
  1.5 1.0 %copy.8 = f32[64,512]{0,1:T(8,128)S(1)} copy(f32[64,512]{1,0:T(8,128)} %param.7) | data formatting | bytes 262144 | tf_op args[0]
  2.5 1.0 %gather_fusion = f32[512,64]{1,0:T(8,128)S(1)} fusion(f32[64,512]{0,1:T(8,128)S(1)} %copy.8, s32[1024]{0:T(1024)S(1)} %pad_clamp_fusion), kind=kCustom, calls=%fused_computation | custom fusion | bytes 264192 | tf_op jit(solution)/shard_map/jit(_take)/gather | solution.py:102
  3.6 0.0 copy-start
  3.6 2.2 %fusion.1 = f32[64,512]{1,0:T(8,128)S(1)} fusion(f32[512,512]{1,0:T(8,128)} %param.10, pred[512]{0:T(512)(128)(4,1)S(1)} %get-tuple-element.7, f32[512,64]{1,0:T(8,128)S(1)} %gather_fusion, pred[512]{0:T(512)(128)(4,1)S(1)} %get-tuple-element.5), kind=kOutput, calls=%fused_computation.8 | convolution fusion | flops 201883648 | bytes 1311744 | tf_op jit(solution)/shard_map/dot_general | solution.py:20
  5.8 0.0 copy-done.1
  5.8 0.3 fusion.39
  6.1 0.3 fusion.37
  6.4 1.2 %fusion.35 = f32[64,256]{1,0:T(8,128)S(1)} fusion(f32[1,6,256,256]{3,2,1,0:T(8,128)} %param.13, f32[64,128]{1,0:T(8,128)S(1)} %fusion.37, f32[64,128]{1,0:T(8,128)S(1)} %fusion.39), kind=kOutput, calls=%fused_computation.42 | convolution fusion | flops 50348032 | bytes 393216 | tf_op jit(solution)/shard_map/dot_general | solution.py:45
  7.6 0.0 copy-done
  7.6 0.4 fusion.33
  8.0 0.4 fusion
  8.4 0.3 fusion.30
  8.7 0.5 collective-permute-start
  9.2 0.9 %collective-permute-done = f32[64,256]{1,0:T(8,128)S(1)} collective-permute-done((f32[64,256]{1,0:T(8,128)S(1)}, f32[64,256]{1,0:T(8,128)S(1)}, u32[]{:S(2)}, u32[]{:S(2)}) %collective-permute-start) | collective-permute-done | bytes 65568 | tf_op jit(solution)/shard_map/ppermute | solution.py:8
  10.1 1.2 %fusion.28 = f32[64,256]{1,0:T(8,128)S(1)} fusion(f32[1,6,256,256]{3,2,1,0:T(8,128)} %param.13, f32[64,256]{1,0:T(8,128)S(1)} %collective-permute-done, f32[64,128]{1,0:T(8,128)S(1)} %fusion.30, pred[]{:T(512)S(6)} %eq.38), kind=kOutput, calls=%fused_computation.35 | convolution fusion | flops 50364416 | bytes 425985 | tf_op jit(solution)/shard_map/dot_general | solution.py:80
  11.3 0.4 convolution_subtract_fusion.4
  11.7 0.3 fusion.25
  12.0 0.4 collective-permute-start.1
  12.4 0.9 %collective-permute-done.1 = f32[64,256]{1,0:T(8,128)S(1)} collective-permute-done((f32[64,256]{1,0:T(8,128)S(1)}, f32[64,256]{1,0:T(8,128)S(1)}, u32[]{:S(2)}, u32[]{:S(2)}) %collective-permute-start.1) | collective-permute-done | bytes 65568 | tf_op jit(solution)/shard_map/ppermute | solution.py:8
  13.3 3.0 %collective-permute-start.2 = (f32[64,256]{1,0:T(8,128)S(1)}, f32[64,256]{1,0:T(8,128)S(1)}, u32[]{:S(2)}, u32[]{:S(2)}) collective-permute-start(f32[64,256]{1,0:T(8,128)S(1)} %fusion.90), channel_id=1, source_target_pairs={{0,2},{1,3},{2,0},{3,1},{4,6},{5,7},{6,4},{7,5},{8,10},{9,11},{10,... | collective-permute-start | bytes 196616 | tf_op jit(solution)/shard_map/ppermute | solution.py:8
  16.3 2.4 %collective-permute-done.2 = f32[64,256]{1,0:T(8,128)S(1)} collective-permute-done((f32[64,256]{1,0:T(8,128)S(1)}, f32[64,256]{1,0:T(8,128)S(1)}, u32[]{:S(2)}, u32[]{:S(2)}) %collective-permute-start.2) | collective-permute-done | bytes 65568 | tf_op jit(solution)/shard_map/ppermute | solution.py:8
  18.7 1.2 %fusion.23 = f32[64,256]{1,0:T(8,128)S(1)} fusion(f32[1,6,256,256]{3,2,1,0:T(8,128)} %param.13, f32[64,256]{1,0:T(8,128)S(1)} %fusion.90, f32[64,256]{1,0:T(8,128)S(1)} %collective-permute-done.2), kind=kOutput, calls=%fused_computation.30 | convolution fusion | flops 50348032 | bytes 458752 | tf_op jit(solution)/shard_map/dot_general | solution.py:80
  19.9 0.4 convolution_subtract_fusion.3
  20.3 0.3 fusion.20
  20.6 0.1 collective-permute-start.3
  20.7 1.2 %collective-permute-done.3 = f32[64,256]{1,0:T(8,128)S(1)} collective-permute-done((f32[64,256]{1,0:T(8,128)S(1)}, f32[64,256]{1,0:T(8,128)S(1)}, u32[]{:S(2)}, u32[]{:S(2)}) %collective-permute-start.3) | collective-permute-done | bytes 65568 | tf_op jit(solution)/shard_map/ppermute | solution.py:8
  22.0 1.9 %collective-permute-start.4 = (f32[64,256]{1,0:T(8,128)S(1)}, f32[64,256]{1,0:T(8,128)S(1)}, u32[]{:S(2)}, u32[]{:S(2)}) collective-permute-start(f32[64,256]{1,0:T(8,128)S(1)} %fusion.91), channel_id=1, source_target_pairs={{0,2},{1,3},{2,0},{3,1},{4,6},{5,7},{6,4},{7,5},{8,10},{9,11},{10,... | collective-permute-start | bytes 196616 | tf_op jit(solution)/shard_map/ppermute | solution.py:8
  23.9 2.4 %collective-permute-done.4 = f32[64,256]{1,0:T(8,128)S(1)} collective-permute-done((f32[64,256]{1,0:T(8,128)S(1)}, f32[64,256]{1,0:T(8,128)S(1)}, u32[]{:S(2)}, u32[]{:S(2)}) %collective-permute-start.4) | collective-permute-done | bytes 65568 | tf_op jit(solution)/shard_map/ppermute | solution.py:8
  26.3 2.9 %collective-permute-start.5 = (f32[64,256]{1,0:T(8,128)S(1)}, f32[64,256]{1,0:T(8,128)S(1)}, u32[]{:S(2)}, u32[]{:S(2)}) collective-permute-start(f32[64,256]{1,0:T(8,128)S(1)} %add.87), channel_id=1, source_target_pairs={{0,4},{1,5},{2,6},{3,7},{4,0},{5,1},{6,2},{7,3},{8,12},{9,13},{10,... | collective-permute-start | bytes 196616 | tf_op jit(solution)/shard_map/ppermute | solution.py:8
  29.2 2.3 %collective-permute-done.5 = f32[64,256]{1,0:T(8,128)S(1)} collective-permute-done((f32[64,256]{1,0:T(8,128)S(1)}, f32[64,256]{1,0:T(8,128)S(1)}, u32[]{:S(2)}, u32[]{:S(2)}) %collective-permute-start.5) | collective-permute-done | bytes 65568 | tf_op jit(solution)/shard_map/ppermute | solution.py:8
  31.6 1.2 %fusion.18 = f32[64,256]{1,0:T(8,128)S(1)} fusion(f32[1,6,256,256]{3,2,1,0:T(8,128)} %param.13, f32[64,256]{1,0:T(8,128)S(1)} %add.87, f32[64,256]{1,0:T(8,128)S(1)} %collective-permute-done.5), kind=kOutput, calls=%fused_computation.25 | convolution fusion | flops 50348032 | bytes 458752 | tf_op jit(solution)/shard_map/dot_general | solution.py:80
  32.8 0.4 convolution_subtract_fusion.2
  33.1 0.3 fusion.15
  33.4 0.1 collective-permute-start.6
  33.5 1.2 %collective-permute-done.6 = f32[64,256]{1,0:T(8,128)S(1)} collective-permute-done((f32[64,256]{1,0:T(8,128)S(1)}, f32[64,256]{1,0:T(8,128)S(1)}, u32[]{:S(2)}, u32[]{:S(2)}) %collective-permute-start.6) | collective-permute-done | bytes 65568 | tf_op jit(solution)/shard_map/ppermute | solution.py:8
  34.8 1.9 %collective-permute-start.7 = (f32[64,256]{1,0:T(8,128)S(1)}, f32[64,256]{1,0:T(8,128)S(1)}, u32[]{:S(2)}, u32[]{:S(2)}) collective-permute-start(f32[64,256]{1,0:T(8,128)S(1)} %fusion.92), channel_id=1, source_target_pairs={{0,2},{1,3},{2,0},{3,1},{4,6},{5,7},{6,4},{7,5},{8,10},{9,11},{10,... | collective-permute-start | bytes 196616 | tf_op jit(solution)/shard_map/ppermute | solution.py:8
  36.7 2.4 %collective-permute-done.7 = f32[64,256]{1,0:T(8,128)S(1)} collective-permute-done((f32[64,256]{1,0:T(8,128)S(1)}, f32[64,256]{1,0:T(8,128)S(1)}, u32[]{:S(2)}, u32[]{:S(2)}) %collective-permute-start.7) | collective-permute-done | bytes 65568 | tf_op jit(solution)/shard_map/ppermute | solution.py:8
  39.1 3.2 %collective-permute-start.8 = (f32[64,256]{1,0:T(8,128)S(1)}, f32[64,256]{1,0:T(8,128)S(1)}, u32[]{:S(2)}, u32[]{:S(2)}) collective-permute-start(f32[64,256]{1,0:T(8,128)S(1)} %add.90), channel_id=1, source_target_pairs={{0,4},{1,5},{2,6},{3,7},{4,0},{5,1},{6,2},{7,3},{8,12},{9,13},{10,... | collective-permute-start | bytes 196616 | tf_op jit(solution)/shard_map/ppermute | solution.py:8
  42.4 2.6 %collective-permute-done.8 = f32[64,256]{1,0:T(8,128)S(1)} collective-permute-done((f32[64,256]{1,0:T(8,128)S(1)}, f32[64,256]{1,0:T(8,128)S(1)}, u32[]{:S(2)}, u32[]{:S(2)}) %collective-permute-start.8) | collective-permute-done | bytes 65568 | tf_op jit(solution)/shard_map/ppermute | solution.py:8
  45.0 1.6 %collective-permute-start.9 = (f32[64,256]{1,0:T(8,128)S(1)}, f32[64,256]{1,0:T(8,128)S(1)}, u32[]{:S(2)}, u32[]{:S(2)}) collective-permute-start(f32[64,256]{1,0:T(8,128)S(1)} %add.91), channel_id=1, source_target_pairs={{0,8},{1,9},{2,10},{3,11},{4,12},{5,13},{6,14},{7,15},{8,0},{9,1},... | collective-permute-start | bytes 196616 | tf_op jit(solution)/shard_map/ppermute | solution.py:8
  46.5 2.8 %collective-permute-done.9 = f32[64,256]{1,0:T(8,128)S(1)} collective-permute-done((f32[64,256]{1,0:T(8,128)S(1)}, f32[64,256]{1,0:T(8,128)S(1)}, u32[]{:S(2)}, u32[]{:S(2)}) %collective-permute-start.9) | collective-permute-done | bytes 65568 | tf_op jit(solution)/shard_map/ppermute | solution.py:8
  49.3 1.2 %fusion.13 = f32[64,256]{1,0:T(8,128)S(1)} fusion(f32[1,6,256,256]{3,2,1,0:T(8,128)} %param.13, f32[64,256]{1,0:T(8,128)S(1)} %add.91, f32[64,256]{1,0:T(8,128)S(1)} %collective-permute-done.9), kind=kOutput, calls=%fused_computation.20 | convolution fusion | flops 50348032 | bytes 458752 | tf_op jit(solution)/shard_map/dot_general | solution.py:80
  50.5 0.4 convolution_subtract_fusion.1
  50.9 0.3 fusion.10
  51.2 0.1 collective-permute-start.10
  51.3 1.2 %collective-permute-done.10 = f32[64,256]{1,0:T(8,128)S(1)} collective-permute-done((f32[64,256]{1,0:T(8,128)S(1)}, f32[64,256]{1,0:T(8,128)S(1)}, u32[]{:S(2)}, u32[]{:S(2)}) %collective-permute-start.10) | collective-permute-done | bytes 65568 | tf_op jit(solution)/shard_map/ppermute | solution.py:8
  52.5 1.6 %collective-permute-start.11 = (f32[64,256]{1,0:T(8,128)S(1)}, f32[64,256]{1,0:T(8,128)S(1)}, u32[]{:S(2)}, u32[]{:S(2)}) collective-permute-start(f32[64,256]{1,0:T(8,128)S(1)} %fusion.93), channel_id=1, source_target_pairs={{0,2},{1,3},{2,0},{3,1},{4,6},{5,7},{6,4},{7,5},{8,10},{9,11},{10,... | collective-permute-start | bytes 196616 | tf_op jit(solution)/shard_map/ppermute | solution.py:8
  54.1 2.8 %collective-permute-done.11 = f32[64,256]{1,0:T(8,128)S(1)} collective-permute-done((f32[64,256]{1,0:T(8,128)S(1)}, f32[64,256]{1,0:T(8,128)S(1)}, u32[]{:S(2)}, u32[]{:S(2)}) %collective-permute-start.11) | collective-permute-done | bytes 65568 | tf_op jit(solution)/shard_map/ppermute | solution.py:8
  56.9 2.9 %collective-permute-start.12 = (f32[64,256]{1,0:T(8,128)S(1)}, f32[64,256]{1,0:T(8,128)S(1)}, u32[]{:S(2)}, u32[]{:S(2)}) collective-permute-start(f32[64,256]{1,0:T(8,128)S(1)} %add.94), channel_id=1, source_target_pairs={{0,4},{1,5},{2,6},{3,7},{4,0},{5,1},{6,2},{7,3},{8,12},{9,13},{10,... | collective-permute-start | bytes 196616 | tf_op jit(solution)/shard_map/ppermute | solution.py:8
  59.8 2.6 %collective-permute-done.12 = f32[64,256]{1,0:T(8,128)S(1)} collective-permute-done((f32[64,256]{1,0:T(8,128)S(1)}, f32[64,256]{1,0:T(8,128)S(1)}, u32[]{:S(2)}, u32[]{:S(2)}) %collective-permute-start.12) | collective-permute-done | bytes 65568 | tf_op jit(solution)/shard_map/ppermute | solution.py:8
  62.4 1.6 %collective-permute-start.13 = (f32[64,256]{1,0:T(8,128)S(1)}, f32[64,256]{1,0:T(8,128)S(1)}, u32[]{:S(2)}, u32[]{:S(2)}) collective-permute-start(f32[64,256]{1,0:T(8,128)S(1)} %add.95), channel_id=1, source_target_pairs={{0,8},{1,9},{2,10},{3,11},{4,12},{5,13},{6,14},{7,15},{8,0},{9,1},... | collective-permute-start | bytes 196616 | tf_op jit(solution)/shard_map/ppermute | solution.py:8
  64.0 2.8 %collective-permute-done.13 = f32[64,256]{1,0:T(8,128)S(1)} collective-permute-done((f32[64,256]{1,0:T(8,128)S(1)}, f32[64,256]{1,0:T(8,128)S(1)}, u32[]{:S(2)}, u32[]{:S(2)}) %collective-permute-start.13) | collective-permute-done | bytes 65568 | tf_op jit(solution)/shard_map/ppermute | solution.py:8
  66.8 1.6 %collective-permute-start.14 = (f32[64,256]{1,0:T(8,128)S(1)}, f32[64,256]{1,0:T(8,128)S(1)}, u32[]{:S(2)}, u32[]{:S(2)}) collective-permute-start(f32[64,256]{1,0:T(8,128)S(1)} %add.96), channel_id=1, source_target_pairs={{0,16},{1,17},{2,18},{3,19},{4,20},{5,21},{6,22},{7,23},{8,24},{9,... | collective-permute-start | bytes 196616 | tf_op jit(solution)/shard_map/ppermute | solution.py:8
  68.4 2.7 %collective-permute-done.14 = f32[64,256]{1,0:T(8,128)S(1)} collective-permute-done((f32[64,256]{1,0:T(8,128)S(1)}, f32[64,256]{1,0:T(8,128)S(1)}, u32[]{:S(2)}, u32[]{:S(2)}) %collective-permute-start.14) | collective-permute-done | bytes 65568 | tf_op jit(solution)/shard_map/ppermute | solution.py:8
  71.1 1.2 %fusion.8 = f32[64,256]{1,0:T(8,128)S(1)} fusion(f32[1,6,256,256]{3,2,1,0:T(8,128)} %param.13, f32[64,256]{1,0:T(8,128)S(1)} %add.96, f32[64,256]{1,0:T(8,128)S(1)} %collective-permute-done.14), kind=kOutput, calls=%fused_computation.15 | convolution fusion | flops 50348032 | bytes 458752 | tf_op jit(solution)/shard_map/dot_general | solution.py:80
  72.3 1.0 %convolution_subtract_fusion = f32[64,512]{1,0:T(8,128)} fusion(f32[64,512]{1,0:T(8,128)S(1)} %convolution_subtract_fusion.1, f32[6,512,128]{2,1,0:T(8,128)S(1)} %copy-done, f32[64,256]{1,0:T(8,128)S(1)} %fusion.8, pred[]{:T(512)S(6)} %eq.42), kind=kOutput, calls=%fused_computation.1 | convolution fusion | flops 50372608 | bytes 589825 | tf_op jit(solution)/shard_map/dot_general | solution.py:89
  (16 shorter events, 0.1 us)
Async XLA Ops:
  0.0 5.8 %copy-start.1 = (f32[6,512,128]{2,1,0:T(8,128)S(1)}, f32[6,512,128]{2,1,0:T(8,128)}, u32[]{:S(2)}) copy-start(f32[6,512,128]{2,1,0:T(8,128)} %param.12) | copy-start | bytes 4718596
  3.6 4.0 %copy-start = (f32[6,512,128]{2,1,0:T(8,128)S(1)}, f32[6,512,128]{2,1,0:T(8,128)}, u32[]{:S(2)}) copy-start(f32[6,512,128]{2,1,0:T(8,128)} %param.11) | copy-start | bytes 4718596
  8.7 1.4 %collective-permute-start = (f32[64,256]{1,0:T(8,128)S(1)}, f32[64,256]{1,0:T(8,128)S(1)}, u32[]{:S(2)}, u32[]{:S(2)}) collective-permute-start(f32[64,256]{1,0:T(8,128)S(1)} %pad_select_fusion.4), channel_id=1, source_target_pairs={{0,1},{1,0},{2,3},{3,2},{4,5},{5,4},{6,7},{7,6},{8,9},{9,8},{10,11... | collective-permute-start | bytes 196616 | tf_op jit(solution)/shard_map/ppermute | solution.py:8
  12.0 1.3 %collective-permute-start.1 = (f32[64,256]{1,0:T(8,128)S(1)}, f32[64,256]{1,0:T(8,128)S(1)}, u32[]{:S(2)}, u32[]{:S(2)}) collective-permute-start(f32[64,256]{1,0:T(8,128)S(1)} %pad_select_fusion.3), channel_id=1, source_target_pairs={{0,1},{1,0},{2,3},{3,2},{4,5},{5,4},{6,7},{7,6},{8,9},{9,8},{10,11... | collective-permute-start | bytes 196616 | tf_op jit(solution)/shard_map/ppermute | solution.py:8
  13.3 5.4 %collective-permute-start.2 = (f32[64,256]{1,0:T(8,128)S(1)}, f32[64,256]{1,0:T(8,128)S(1)}, u32[]{:S(2)}, u32[]{:S(2)}) collective-permute-start(f32[64,256]{1,0:T(8,128)S(1)} %fusion.90), channel_id=1, source_target_pairs={{0,2},{1,3},{2,0},{3,1},{4,6},{5,7},{6,4},{7,5},{8,10},{9,11},{10,... | collective-permute-start | bytes 196616 | tf_op jit(solution)/shard_map/ppermute | solution.py:8
  20.6 1.3 %collective-permute-start.3 = (f32[64,256]{1,0:T(8,128)S(1)}, f32[64,256]{1,0:T(8,128)S(1)}, u32[]{:S(2)}, u32[]{:S(2)}) collective-permute-start(f32[64,256]{1,0:T(8,128)S(1)} %pad_select_fusion.2), channel_id=1, source_target_pairs={{0,1},{1,0},{2,3},{3,2},{4,5},{5,4},{6,7},{7,6},{8,9},{9,8},{10,11... | collective-permute-start | bytes 196616 | tf_op jit(solution)/shard_map/ppermute | solution.py:8
  22.0 4.3 %collective-permute-start.4 = (f32[64,256]{1,0:T(8,128)S(1)}, f32[64,256]{1,0:T(8,128)S(1)}, u32[]{:S(2)}, u32[]{:S(2)}) collective-permute-start(f32[64,256]{1,0:T(8,128)S(1)} %fusion.91), channel_id=1, source_target_pairs={{0,2},{1,3},{2,0},{3,1},{4,6},{5,7},{6,4},{7,5},{8,10},{9,11},{10,... | collective-permute-start | bytes 196616 | tf_op jit(solution)/shard_map/ppermute | solution.py:8
  26.3 5.3 %collective-permute-start.5 = (f32[64,256]{1,0:T(8,128)S(1)}, f32[64,256]{1,0:T(8,128)S(1)}, u32[]{:S(2)}, u32[]{:S(2)}) collective-permute-start(f32[64,256]{1,0:T(8,128)S(1)} %add.87), channel_id=1, source_target_pairs={{0,4},{1,5},{2,6},{3,7},{4,0},{5,1},{6,2},{7,3},{8,12},{9,13},{10,... | collective-permute-start | bytes 196616 | tf_op jit(solution)/shard_map/ppermute | solution.py:8
  33.4 1.3 %collective-permute-start.6 = (f32[64,256]{1,0:T(8,128)S(1)}, f32[64,256]{1,0:T(8,128)S(1)}, u32[]{:S(2)}, u32[]{:S(2)}) collective-permute-start(f32[64,256]{1,0:T(8,128)S(1)} %pad_select_fusion.1), channel_id=1, source_target_pairs={{0,1},{1,0},{2,3},{3,2},{4,5},{5,4},{6,7},{7,6},{8,9},{9,8},{10,11... | collective-permute-start | bytes 196616 | tf_op jit(solution)/shard_map/ppermute | solution.py:8
  34.8 4.3 %collective-permute-start.7 = (f32[64,256]{1,0:T(8,128)S(1)}, f32[64,256]{1,0:T(8,128)S(1)}, u32[]{:S(2)}, u32[]{:S(2)}) collective-permute-start(f32[64,256]{1,0:T(8,128)S(1)} %fusion.92), channel_id=1, source_target_pairs={{0,2},{1,3},{2,0},{3,1},{4,6},{5,7},{6,4},{7,5},{8,10},{9,11},{10,... | collective-permute-start | bytes 196616 | tf_op jit(solution)/shard_map/ppermute | solution.py:8
  39.1 5.8 %collective-permute-start.8 = (f32[64,256]{1,0:T(8,128)S(1)}, f32[64,256]{1,0:T(8,128)S(1)}, u32[]{:S(2)}, u32[]{:S(2)}) collective-permute-start(f32[64,256]{1,0:T(8,128)S(1)} %add.90), channel_id=1, source_target_pairs={{0,4},{1,5},{2,6},{3,7},{4,0},{5,1},{6,2},{7,3},{8,12},{9,13},{10,... | collective-permute-start | bytes 196616 | tf_op jit(solution)/shard_map/ppermute | solution.py:8
  45.0 4.3 %collective-permute-start.9 = (f32[64,256]{1,0:T(8,128)S(1)}, f32[64,256]{1,0:T(8,128)S(1)}, u32[]{:S(2)}, u32[]{:S(2)}) collective-permute-start(f32[64,256]{1,0:T(8,128)S(1)} %add.91), channel_id=1, source_target_pairs={{0,8},{1,9},{2,10},{3,11},{4,12},{5,13},{6,14},{7,15},{8,0},{9,1},... | collective-permute-start | bytes 196616 | tf_op jit(solution)/shard_map/ppermute | solution.py:8
  51.2 1.3 %collective-permute-start.10 = (f32[64,256]{1,0:T(8,128)S(1)}, f32[64,256]{1,0:T(8,128)S(1)}, u32[]{:S(2)}, u32[]{:S(2)}) collective-permute-start(f32[64,256]{1,0:T(8,128)S(1)} %pad_select_fusion), channel_id=1, source_target_pairs={{0,1},{1,0},{2,3},{3,2},{4,5},{5,4},{6,7},{7,6},{8,9},{9,8},{10,11... | collective-permute-start | bytes 196616 | tf_op jit(solution)/shard_map/ppermute | solution.py:8
  52.5 4.3 %collective-permute-start.11 = (f32[64,256]{1,0:T(8,128)S(1)}, f32[64,256]{1,0:T(8,128)S(1)}, u32[]{:S(2)}, u32[]{:S(2)}) collective-permute-start(f32[64,256]{1,0:T(8,128)S(1)} %fusion.93), channel_id=1, source_target_pairs={{0,2},{1,3},{2,0},{3,1},{4,6},{5,7},{6,4},{7,5},{8,10},{9,11},{10,... | collective-permute-start | bytes 196616 | tf_op jit(solution)/shard_map/ppermute | solution.py:8
  56.9 5.5 %collective-permute-start.12 = (f32[64,256]{1,0:T(8,128)S(1)}, f32[64,256]{1,0:T(8,128)S(1)}, u32[]{:S(2)}, u32[]{:S(2)}) collective-permute-start(f32[64,256]{1,0:T(8,128)S(1)} %add.94), channel_id=1, source_target_pairs={{0,4},{1,5},{2,6},{3,7},{4,0},{5,1},{6,2},{7,3},{8,12},{9,13},{10,... | collective-permute-start | bytes 196616 | tf_op jit(solution)/shard_map/ppermute | solution.py:8
  62.4 4.3 %collective-permute-start.13 = (f32[64,256]{1,0:T(8,128)S(1)}, f32[64,256]{1,0:T(8,128)S(1)}, u32[]{:S(2)}, u32[]{:S(2)}) collective-permute-start(f32[64,256]{1,0:T(8,128)S(1)} %add.95), channel_id=1, source_target_pairs={{0,8},{1,9},{2,10},{3,11},{4,12},{5,13},{6,14},{7,15},{8,0},{9,1},... | collective-permute-start | bytes 196616 | tf_op jit(solution)/shard_map/ppermute | solution.py:8
  66.8 4.3 %collective-permute-start.14 = (f32[64,256]{1,0:T(8,128)S(1)}, f32[64,256]{1,0:T(8,128)S(1)}, u32[]{:S(2)}, u32[]{:S(2)}) collective-permute-start(f32[64,256]{1,0:T(8,128)S(1)} %add.96), channel_id=1, source_target_pairs={{0,16},{1,17},{2,18},{3,19},{4,20},{5,21},{6,22},{7,23},{8,24},{9,... | collective-permute-start | bytes 196616 | tf_op jit(solution)/shard_map/ppermute | solution.py:8
where the time goes:
time: 73.7 us; the launch traced here: 73.3 us
  waiting for transfers between devices  31.4 us (43%)
  starting transfers between devices  23.3 us (32%)
  matrix products  14.7 us (20%)
  local copies, waits for them, and re-layouts  2.07 us (3%)
  between operations  1.05 us (1%)
  other arithmetic  0.84 us (1%)
    ppermute x15, waiting for transfers between devices, partner(): lax.ppermute(value, axis, [(i, i ^ 1 << distance) for i in range(lax.axis...  31.4 us
    ppermute x15, starting transfers between devices, partner(): lax.ppermute(value, axis, [(i, i ^ 1 << distance) for i in range(lax.axis...  23.3 us
    dot_general x5, matrix products, solve_columns(): jnp.dot(summand, coupling[0, tree_level], precision=highest_level, prefer...  5.96 us
    dot_general x5, matrix products, solve_columns(): lax.dot_general(chosen, basis_left[tree_level], contract, precision=highe...  2.6 us
    dot_general x1, matrix products, solve_columns(): jnp.dot(current, leaf_masked, precision=highest_level, preferred_element_...  2.2 us
  transfers between devices with their start and end apart: 15, of which 15 were waited for; matrix products, arithmetic and copies ran while one was open for 0% of the time, Pallas kernels for 0%

commit v1 on v0

v1 whole, which is shorter than its diff:
```python
import jax
import jax.numpy as jnp
from jax import lax
from jax.sharding import PartitionSpec as P

AXES = ("grp", "sub")
HIGH = lax.Precision.HIGHEST


def dot(a, b):
    return jnp.dot(a, b, precision=HIGH, preferred_element_type=jnp.float32)


def dot_nt(a, b):
    return lax.dot_general(
        a, b, (((1,), (1,)), ((), ())), precision=HIGH, preferred_element_type=jnp.float32
    )


def dot_tn(a, b):
    return lax.dot_general(
        a, b, (((0,), (0,)), ((), ())), precision=HIGH, preferred_element_type=jnp.float32
    )


def odd_partner(value, bit):
    return lax.ppermute(value, AXES, [(i, i ^ 1 << bit) for i in range(1, lax.axis_size(AXES), 2)])


def to_odd(value):
    return lax.ppermute(value, AXES, [(i, i + 1) for i in range(0, lax.axis_size(AXES), 2)])


def to_even(value):
    return lax.ppermute(value, AXES, [(i, i - 1) for i in range(1, lax.axis_size(AXES), 2)])


def per_device(right_side, order, leaf_split, leaf_inverse, basis_left, basis_right, coupling):
    row_count = right_side.shape[1]
    rank = basis_left.shape[2]
    top = basis_left.shape[0] - 1
    device_id = lax.axis_index(AXES)
    right_cols = jnp.concatenate([basis_right[k] for k in range(top)], axis=1)
    gram = {k: dot_tn(basis_left[k], right_cols[:, : k * rank]) for k in range(1, top)}
    gram_even = {k: to_odd(gram[k]) for k in range(1, top)}

    gathered = jnp.take(right_side, order % row_count, axis=1)
    is_left = lax.iota(jnp.int32, row_count) < leaf_split[0]
    leaf = jnp.where(is_left[:, None] == is_left[None, :], leaf_inverse, 0.0)
    current = dot(gathered, leaf)
    rows = current.shape[0]
    halves = jnp.concatenate(
        [jnp.where(is_left[None, :], current, 0.0), jnp.where(is_left[None, :], 0.0, current)], axis=0
    )
    w = dot(halves, basis_right[top])
    w = jnp.concatenate([w[:rows], w[rows:]], axis=1)
    z = dot(w, coupling[0, top])
    both = dot_nt(jnp.concatenate([z[:, :rank], z[:, rank:]], axis=0), basis_left[top])
    current = current - jnp.where(is_left[None, :], both[:rows], both[rows:])

    sums = dot(current, right_cols)
    left_sums, right_sums = to_odd(sums), sums
    left_gram, right_gram = gram_even, gram
    chosen = []
    for bit in range(top):
        k = top - 1 - bit
        own = slice(k * rank, (k + 1) * rank)
        z = dot(jnp.concatenate([left_sums[:, own], right_sums[:, own]], axis=1), coupling[0, k])
        if bit == 0:
            chosen.append((z[:, rank:], z[:, :rank]))
        else:
            side = jnp.where(on_right, z[:, rank:], z[:, :rank])
            chosen.append((side, side))
        if k == 0:
            break
        gram_pair = jnp.concatenate([left_gram[k], right_gram[k]], axis=0)
        sums = left_sums[:, : k * rank] + right_sums[:, : k * rank] - dot(z, gram_pair)
        gram = {j: left_gram[j] + right_gram[j] for j in range(1, k)}
        on_right = (device_id >> (bit + 1)) & 1 == 1
        got_sums = odd_partner(sums, bit + 1)
        left_sums = jnp.where(on_right, got_sums, sums)
        right_sums = jnp.where(on_right, sums, got_sums)
        got = {j: odd_partner(gram[j], bit + 1) for j in range(1, k)}
        left_gram = {j: jnp.where(on_right, got[j], gram[j]) for j in range(1, k)}
        right_gram = {j: jnp.where(on_right, gram[j], got[j]) for j in range(1, k)}
    is_odd = device_id & 1 == 1
    z_all = jnp.concatenate(
        [jnp.where(is_odd, mine, to_even(other)) for mine, other in chosen], axis=1
    )
    left_cols = jnp.concatenate([basis_left[top - 1 - bit] for bit in range(top)], axis=1)
    return current - dot_nt(z_all, left_cols)


def solution(mesh):
    in_specs = (
        P(None, AXES),
        P(AXES),
        P(AXES),
        P(AXES, None),
        P(None, AXES, None),
        P(None, AXES, None),
        P(AXES, None, None, None),
    )
    return jax.shard_map(
        per_device, mesh=mesh, in_specs=in_specs, out_specs=P(None, AXES), check_vma=False
    )
```

time: 73.7 us -> 83.9 us (1.14)
  waiting for transfers between devices: 31.4 us -> 35.2 us
  other arithmetic: 0.84 us -> 4.36 us
  local copies, waits for them, and re-layouts: 2.07 us -> 4.11 us
    ppermute x15 -> x20, waiting for transfers between devices: 31.4 us -> 35.2 us  [the longest x5 34.4 us: to_even(): lax.ppermute(value, AXES, [(i, i - 1) for i in range(1, lax.axis_size(AXE...]
    add x10 -> x6, other arithmetic: 0.09 us -> 3.43 us  [per_device(): gram = {j: left_gram[j] + right_gram[j] for j in range(1, k)}]
    unnamed x5 -> x15, local copies, waits for them, and re-layouts: 1.04 us -> 2.16 us
    ppermute x15 -> x20, starting transfers between devices: 23.3 us -> 24 us  [the longest x5 10.3 us: to_odd(): lax.ppermute(value, AXES, [(i, i + 1) for i in range(0, lax.axis_size(AXE...]
    dot_general x21 -> x19, matrix products: 14.7 us -> 14 us  [the longest x13 8.19 us: dot(): return jnp.dot(a, b, precision=HIGH, preferred_element_type=jnp.float32)]
  transfers between devices with their start and end apart: 15 -> 20, of which waited for: 15 -> 6; matrix products, arithmetic and copies ran while one was open for 0% -> 13% of each run, Pallas kernels for 0% -> 0%
where the time goes in v1:
time: 83.9 us; the launch traced here: 83 us
  waiting for transfers between devices  35.2 us (42%)
  starting transfers between devices  24 us (29%)
  matrix products  14 us (17%)
  other arithmetic  4.36 us (5%)
  local copies, waits for them, and re-layouts  4.11 us (5%)
  between operations  1.33 us (2%)
    ppermute x5, waiting for transfers between devices, to_even(): lax.ppermute(value, AXES, [(i, i - 1) for i in range(1, lax.axis_size(AXE...  34.4 us
    ppermute x5, starting transfers between devices, to_odd(): lax.ppermute(value, AXES, [(i, i + 1) for i in range(0, lax.axis_size(AXE...  10.3 us
    dot_general x13, matrix products, dot(): return jnp.dot(a, b, precision=HIGH, preferred_element_type=jnp.float32)  8.19 us
    ppermute x10, starting transfers between devices, odd_partner(): lax.ppermute(value, AXES, [(i, i ^ 1 << bit) for i in range(1, lax.axis_s...  7.28 us
    ppermute x5, starting transfers between devices, to_even(): lax.ppermute(value, AXES, [(i, i - 1) for i in range(1, lax.axis_size(AXE...  6.46 us
    add x6, other arithmetic, per_device(): gram = {j: left_gram[j] + right_gram[j] for j in range(1, k)}  3.43 us
    dot_general x4, matrix products, dot_tn(): lax.dot_general(a, b, (((0,), (0,)), ((), ())), precision=HIGH, preferred...  3.4 us
    dot_general x2, matrix products, dot_nt(): lax.dot_general(a, b, (((1,), (1,)), ((), ())), precision=HIGH, preferred...  2.43 us
  transfers between devices with their start and end apart: 20, of which 6 were waited for; matrix products, arithmetic and copies ran while one was open for 13% of the time, Pallas kernels for 0%

profile of v1, /device:TPU:0, one launch (start us, length us, event | category | flops | bytes accessed | tf_op | source)
XLA Modules:
  0.0 83.0 jit_solution(7651276900996292883)
XLA Ops:
  0.7 0.7 compare_and_fusion
  1.4 1.0 %copy.8 = f32[64,512]{0,1:T(8,128)S(1)} copy(f32[64,512]{1,0:T(8,128)} %param.7) | data formatting | bytes 262144 | tf_op args[0]
  2.4 1.0 %constant_dynamic-update-slice_fusion.3 = f32[512,640]{1,0:T(8,128)S(1)} fusion(f32[6,512,128]{2,1,0:T(8,128)} %param.12), kind=kLoop, calls=%fused_computation.152 | loop fusion | bytes 524288
  3.4 0.0 copy-start
  3.4 1.0 %gather_fusion = f32[512,64]{1,0:T(8,128)S(1)} fusion(f32[64,512]{0,1:T(8,128)S(1)} %copy.8, s32[1024]{0:T(1024)S(1)} %pad_clamp_fusion), kind=kCustom, calls=%fused_computation | custom fusion | bytes 264192 | tf_op jit(solution)/shard_map/jit(_take)/gather | solution.py:47
  4.4 2.1 %broadcast_select_fusion.3 = (f32[64,512]{1,0:T(8,128)S(1)}, f32[64,512]{1,0:T(8,128)S(1)}, f32[64,512]{1,0:T(8,128)S(1)}) fusion(pred[512]{0:T(512)(128)(4,1)S(1)} %get-tuple-element.32, f32[512,512]{1,0:T(8,128)} %param.10, f32[512,64]{1,0:T(8,128)S(1)} %gather_fusion, pred[512]{0:T(512)(128)(4,1)S(1)} %get-tuple-element.5), kind=kOutput, calls=%fused_computation.126 | convolution fusion | flops 201949184 | bytes 1573888 | tf_op jit(solution)/shard_map/dot_general | solution.py:11
  6.5 0.0 copy-start.1
  6.6 0.4 fusion.29
  7.0 1.3 %fusion.54 = f32[64,256]{1,0:T(8,128)S(1)} fusion(f32[1,6,256,256]{3,2,1,0:T(8,128)} %param.13, f32[64,128]{1,0:T(8,128)S(1)} %get-tuple-element.30, f32[64,128]{1,0:T(8,128)S(1)} %get-tuple-element.29), kind=kOutput, calls=%fused_computation.65 | convolution fusion | flops 50348032 | bytes 393216 | tf_op jit(solution)/shard_map/dot_general | solution.py:11
  8.4 0.4 fusion.52
  8.8 0.9 %fusion.131 = f32[64,640]{1,0:T(8,128)S(1)} fusion(f32[64,512]{1,0:T(8,128)S(1)} %fusion.71, f32[512,640]{1,0:T(8,128)S(1)} %bitcast_dynamic-update-slice_fusion.5), kind=kOutput, calls=%fused_computation.182 | convolution fusion | flops 251658240 | bytes 1605632 | tf_op jit(solution)/shard_map/dot_general | solution.py:11
  9.7 3.0 %collective-permute-start = (f32[64,640]{1,0:T(8,128)S(1)}, f32[64,640]{1,0:T(8,128)}, u32[]{:S(2)}, u32[]{:S(2)}) collective-permute-start(f32[64,640]{1,0:T(8,128)S(1)} %fusion.131), channel_id=1, source_target_pairs={{0,1},{2,3},{4,5},{6,7},{8,9},{10,11},{12,13},{14,15},{16,17},{18,... | collective-permute-start | bytes 491528 | tf_op jit(solution)/shard_map/ppermute | solution.py:31
  12.7 0.1 slice_bitcast_fusion.3
  12.8 1.5 %convolution_bitcast_fusion = f32[128,512]{1,0:T(8,128)} fusion(f32[512,128]{1,0:T(8,128)S(1)} %get-tuple-element.10, f32[512,128]{1,0:T(8,128)S(1)} %get-tuple-element.8, f32[512,128]{1,0:T(8,128)S(1)} %get-tuple-element.9, f32[512,128]{1,0:T(8,128)S(1)} %get-tuple-element.7, f32[6,512,128]{2,1,0:T(8,128)S(1)} %copy-done.1), kind=kOutput, calls=%fused_computation.1 | convolution fusion | flops 403439616 | bytes 1572864 | tf_op jit(solution)/shard_map/dot_general | solution.py:21
  14.3 2.0 %collective-permute-start.2 = (f32[128,512]{1,0:T(8,128)}, f32[128,512]{1,0:T(8,128)}, u32[]{:S(2)}, u32[]{:S(2)}) collective-permute-start(f32[128,512]{1,0:T(8,128)} %convolution_bitcast_fusion), channel_id=1, source_target_pairs={{0,1},{2,3},{4,5},{6,7},{8,9},{10,11},{12,13},{14,15},{16,17},{18,... | collective-permute-start | bytes 786440 | tf_op jit(solution)/shard_map/ppermute | solution.py:31
  16.3 0.7 convolution_bitcast_fusion.1
  17.0 2.0 %collective-permute-start.5 = (f32[128,384]{1,0:T(8,128)S(1)}, f32[128,384]{1,0:T(8,128)}, u32[]{:S(2)}, u32[]{:S(2)}) collective-permute-start(f32[128,384]{1,0:T(8,128)S(1)} %convolution_bitcast_fusion.1), channel_id=1, source_target_pairs={{0,1},{2,3},{4,5},{6,7},{8,9},{10,11},{12,13},{14,15},{16,17},{18,... | collective-permute-start | bytes 589832 | tf_op jit(solution)/shard_map/ppermute | solution.py:31
  19.0 0.6 convolution_bitcast_fusion.2
  19.6 2.0 %collective-permute-start.9 = (f32[128,256]{1,0:T(8,128)S(1)}, f32[128,256]{1,0:T(8,128)}, u32[]{:S(2)}, u32[]{:S(2)}) collective-permute-start(f32[128,256]{1,0:T(8,128)S(1)} %convolution_bitcast_fusion.2), channel_id=1, source_target_pairs={{0,1},{2,3},{4,5},{6,7},{8,9},{10,11},{12,13},{14,15},{16,17},{18,... | collective-permute-start | bytes 393224 | tf_op jit(solution)/shard_map/ppermute | solution.py:31
  21.6 0.6 fusion.39
  22.2 1.3 %collective-permute-start.14 = (f32[128,128]{1,0:T(8,128)S(1)}, f32[128,128]{1,0:T(8,128)S(1)}, u32[]{:S(2)}, u32[]{:S(2)}) collective-permute-start(f32[128,128]{1,0:T(8,128)S(1)} %fusion.39), channel_id=1, source_target_pairs={{0,1},{2,3},{4,5},{6,7},{8,9},{10,11},{12,13},{14,15},{16,17},{18,... | collective-permute-start | bytes 196616 | tf_op jit(solution)/shard_map/ppermute | solution.py:31
  23.5 0.0 copy-start.2
  23.6 0.8 collective-permute-done.14
  24.3 0.6 add.55
  25.0 1.3 %collective-permute-start.15 = (f32[128,128]{1,0:T(8,128)}, f32[128,128]{1,0:T(8,128)}, u32[]{:S(2)}, u32[]{:S(2)}) collective-permute-start(f32[128,128]{1,0:T(8,128)} %add.55), channel_id=1, source_target_pairs={{1,3},{3,1},{5,7},{7,5},{9,11},{11,9},{13,15},{15,13},{17,19},{19,... | collective-permute-start | bytes 196616 | tf_op jit(solution)/shard_map/ppermute | solution.py:27
  26.3 0.0 collective-permute-done.9
  26.3 0.9 %add.52 = f32[128,256]{1,0:T(8,128)S(1)} add(f32[128,256]{1,0:T(8,128)} %collective-permute-done.9, f32[128,256]{1,0:T(8,128)S(1)} %convolution_bitcast_fusion.2) | non-fusion elementwise | flops 32768 | bytes 393216 | tf_op jit(solution)/shard_map/add | solution.py:78
  27.2 0.7 collective-permute-start.10
  27.9 0.9 %select_add_fusion.2 = f32[128,128]{1,0:T(8,128)S(1)} fusion(f32[128,128]{1,0:T(8,128)} %add.55, f32[128,128]{1,0:T(8,128)} %collective-permute-done.15, pred[]{:T(512)S(6)} %eq.34), kind=kLoop, calls=%fused_computation.124 | loop fusion | flops 49152 | bytes 196609 | tf_op jit(solution)/shard_map/add | solution.py:78
  28.8 0.7 collective-permute-start.16
  29.5 0.8 slice.218
  30.3 0.2 fusion.50
  30.5 1.3 %collective-permute-start.1 = (f32[64,128]{1,0:T(8,128)S(1)}, f32[64,128]{1,0:T(8,128)S(1)}, u32[]{:S(2)}, u32[]{:S(2)}) collective-permute-start(f32[64,128]{1,0:T(8,128)S(1)} %slice.221), channel_id=1, source_target_pairs={{1,0},{3,2},{5,4},{7,6},{9,8},{11,10},{13,12},{15,14},{17,16},{19,... | collective-permute-start | bytes 98312 | tf_op jit(solution)/shard_map/ppermute | solution.py:35
  31.9 0.7 collective-permute-start.17
  32.5 0.0 collective-permute-done.5
  32.5 0.9 %add.50 = f32[128,384]{1,0:T(8,128)S(1)} add(f32[128,384]{1,0:T(8,128)} %collective-permute-done.5, f32[128,384]{1,0:T(8,128)S(1)} %convolution_bitcast_fusion.1) | non-fusion elementwise | flops 49152 | bytes 589824 | tf_op jit(solution)/shard_map/add | solution.py:78
  33.5 0.7 collective-permute-start.6
  34.2 6.4 %collective-permute-done.1 = f32[64,128]{1,0:T(8,128)S(1)} collective-permute-done((f32[64,128]{1,0:T(8,128)S(1)}, f32[64,128]{1,0:T(8,128)S(1)}, u32[]{:S(2)}, u32[]{:S(2)}) %collective-permute-start.1) | collective-permute-done | bytes 32800 | tf_op jit(solution)/shard_map/ppermute | solution.py:35
  40.6 0.0 collective-permute-done.2
  40.6 1.5 %fusion.70 = f32[64,512]{1,0:T(8,128)S(1)} fusion(f32[64,640]{1,0:T(8,128)S(1)} %fusion.131, f32[64,640]{1,0:T(8,128)} %collective-permute-done, f32[64,256]{1,0:T(8,128)S(1)} %fusion.50, f32[128,512]{1,0:T(8,128)} %convolution_bitcast_fusion, f32[128,512]{1,0:T(8,128)} %collective-permute-done.2), kind=kOutput, calls=%fused_computation.86 | convolution fusion | flops 100859904 | bytes 983040 | tf_op jit(solution)/shard_map/dot_general | solution.py:11
  42.1 0.7 collective-permute-start.3
  42.8 0.7 collective-permute-start.11
  43.5 0.0 collective-permute-done.17
  43.5 0.0 collective-permute-done.3
  43.6 0.2 fusion.47
  43.9 1.3 %collective-permute-start.4 = (f32[64,128]{1,0:T(8,128)S(1)}, f32[64,128]{1,0:T(8,128)S(1)}, u32[]{:S(2)}, u32[]{:S(2)}) collective-permute-start(f32[64,128]{1,0:T(8,128)S(1)} %slice_select_fusion.4), channel_id=1, source_target_pairs={{1,0},{3,2},{5,4},{7,6},{9,8},{11,10},{13,12},{15,14},{17,16},{19,... | collective-permute-start | bytes 98312 | tf_op jit(solution)/shard_map/ppermute | solution.py:35
  45.2 0.0 collective-permute-done.11
  45.2 0.3 fusion.78
  45.6 0.7 collective-permute-start.7
  46.3 11.0 %collective-permute-done.4 = f32[64,128]{1,0:T(8,128)S(1)} collective-permute-done((f32[64,128]{1,0:T(8,128)S(1)}, f32[64,128]{1,0:T(8,128)S(1)}, u32[]{:S(2)}, u32[]{:S(2)}) %collective-permute-start.4) | collective-permute-done | bytes 32800 | tf_op jit(solution)/shard_map/ppermute | solution.py:35
  57.3 0.2 fusion.44
  57.6 1.3 %collective-permute-start.8 = (f32[64,128]{1,0:T(8,128)S(1)}, f32[64,128]{1,0:T(8,128)S(1)}, u32[]{:S(2)}, u32[]{:S(2)}) collective-permute-start(f32[64,128]{1,0:T(8,128)S(1)} %slice_select_fusion.3), channel_id=1, source_target_pairs={{1,0},{3,2},{5,4},{7,6},{9,8},{11,10},{13,12},{15,14},{17,16},{19,... | collective-permute-start | bytes 98312 | tf_op jit(solution)/shard_map/ppermute | solution.py:35
  58.9 0.2 fusion.79
  59.1 0.7 collective-permute-start.12
  59.8 9.1 %collective-permute-done.8 = f32[64,128]{1,0:T(8,128)S(1)} collective-permute-done((f32[64,128]{1,0:T(8,128)S(1)}, f32[64,128]{1,0:T(8,128)S(1)}, u32[]{:S(2)}, u32[]{:S(2)}) %collective-permute-start.8) | collective-permute-done | bytes 32800 | tf_op jit(solution)/shard_map/ppermute | solution.py:35
  69.0 0.2 fusion.41
  69.3 0.2 fusion.101
  69.5 0.7 collective-permute-start.18
  70.2 1.3 %collective-permute-start.13 = (f32[64,128]{1,0:T(8,128)S(1)}, f32[64,128]{1,0:T(8,128)S(1)}, u32[]{:S(2)}, u32[]{:S(2)}) collective-permute-start(f32[64,128]{1,0:T(8,128)S(1)} %slice_select_fusion.2), channel_id=1, source_target_pairs={{1,0},{3,2},{5,4},{7,6},{9,8},{11,10},{13,12},{15,14},{17,16},{19,... | collective-permute-start | bytes 98312 | tf_op jit(solution)/shard_map/ppermute | solution.py:35
  71.5 0.2 fusion.37
  71.8 1.3 %collective-permute-start.19 = (f32[64,128]{1,0:T(8,128)S(1)}, f32[64,128]{1,0:T(8,128)S(1)}, u32[]{:S(2)}, u32[]{:S(2)}) collective-permute-start(f32[64,128]{1,0:T(8,128)S(1)} %slice_select_fusion.1), channel_id=1, source_target_pairs={{1,0},{3,2},{5,4},{7,6},{9,8},{11,10},{13,12},{15,14},{17,16},{19,... | collective-permute-start | bytes 98312 | tf_op jit(solution)/shard_map/ppermute | solution.py:35
  73.1 6.1 %collective-permute-done.13 = f32[64,128]{1,0:T(8,128)S(1)} collective-permute-done((f32[64,128]{1,0:T(8,128)S(1)}, f32[64,128]{1,0:T(8,128)S(1)}, u32[]{:S(2)}, u32[]{:S(2)}) %collective-permute-start.13) | collective-permute-done | bytes 32800 | tf_op jit(solution)/shard_map/ppermute | solution.py:35
  79.2 1.8 %collective-permute-done.19 = f32[64,128]{1,0:T(8,128)S(1)} collective-permute-done((f32[64,128]{1,0:T(8,128)S(1)}, f32[64,128]{1,0:T(8,128)S(1)}, u32[]{:S(2)}, u32[]{:S(2)}) %collective-permute-start.19) | collective-permute-done | bytes 32800 | tf_op jit(solution)/shard_map/ppermute | solution.py:35
  81.0 2.1 %convolution_subtract_fusion = f32[64,512]{1,0:T(8,128)} fusion(f32[64,512]{1,0:T(8,128)S(1)} %fusion.71, f32[64,640]{1,0:T(8,128)S(1)} %select_dynamic-update-slice_fusion, f32[512,640]{1,0:T(8,128)S(1)} %bitcast_dynamic-update-slice_fusion), kind=kOutput, calls=%fused_computation.4 | convolution fusion | flops 251691008 | bytes 1736704 | tf_op jit(solution)/shard_map/dot_general | solution.py:15
  (50 shorter events, 0.5 us)
Async XLA Ops:
  3.4 3.2 %copy-start = (f32[6,512,128]{2,1,0:T(8,128)S(1)}, f32[6,512,128]{2,1,0:T(8,128)}, u32[]{:S(2)}) copy-start(f32[6,512,128]{2,1,0:T(8,128)} %param.12) | copy-start | bytes 4718596
  6.5 1.8 %copy-start.1 = (f32[6,512,128]{2,1,0:T(8,128)S(1)}, f32[6,512,128]{2,1,0:T(8,128)}, u32[]{:S(2)}) copy-start(f32[6,512,128]{2,1,0:T(8,128)} %param.11) | copy-start | bytes 4718596
  9.7 19.8 %collective-permute-start = (f32[64,640]{1,0:T(8,128)S(1)}, f32[64,640]{1,0:T(8,128)}, u32[]{:S(2)}, u32[]{:S(2)}) collective-permute-start(f32[64,640]{1,0:T(8,128)S(1)} %fusion.131), channel_id=1, source_target_pairs={{0,1},{2,3},{4,5},{6,7},{8,9},{10,11},{12,13},{14,15},{16,17},{18,... | collective-permute-start | bytes 491528 | tf_op jit(solution)/shard_map/ppermute | solution.py:31
  14.3 26.3 %collective-permute-start.2 = (f32[128,512]{1,0:T(8,128)}, f32[128,512]{1,0:T(8,128)}, u32[]{:S(2)}, u32[]{:S(2)}) collective-permute-start(f32[128,512]{1,0:T(8,128)} %convolution_bitcast_fusion), channel_id=1, source_target_pairs={{0,1},{2,3},{4,5},{6,7},{8,9},{10,11},{12,13},{14,15},{16,17},{18,... | collective-permute-start | bytes 786440 | tf_op jit(solution)/shard_map/ppermute | solution.py:31
  17.0 15.5 %collective-permute-start.5 = (f32[128,384]{1,0:T(8,128)S(1)}, f32[128,384]{1,0:T(8,128)}, u32[]{:S(2)}, u32[]{:S(2)}) collective-permute-start(f32[128,384]{1,0:T(8,128)S(1)} %convolution_bitcast_fusion.1), channel_id=1, source_target_pairs={{0,1},{2,3},{4,5},{6,7},{8,9},{10,11},{12,13},{14,15},{16,17},{18,... | collective-permute-start | bytes 589832 | tf_op jit(solution)/shard_map/ppermute | solution.py:31
  19.6 6.7 %collective-permute-start.9 = (f32[128,256]{1,0:T(8,128)S(1)}, f32[128,256]{1,0:T(8,128)}, u32[]{:S(2)}, u32[]{:S(2)}) collective-permute-start(f32[128,256]{1,0:T(8,128)S(1)} %convolution_bitcast_fusion.2), channel_id=1, source_target_pairs={{0,1},{2,3},{4,5},{6,7},{8,9},{10,11},{12,13},{14,15},{16,17},{18,... | collective-permute-start | bytes 393224 | tf_op jit(solution)/shard_map/ppermute | solution.py:31
  22.2 2.2 %collective-permute-start.14 = (f32[128,128]{1,0:T(8,128)S(1)}, f32[128,128]{1,0:T(8,128)S(1)}, u32[]{:S(2)}, u32[]{:S(2)}) collective-permute-start(f32[128,128]{1,0:T(8,128)S(1)} %fusion.39), channel_id=1, source_target_pairs={{0,1},{2,3},{4,5},{6,7},{8,9},{10,11},{12,13},{14,15},{16,17},{18,... | collective-permute-start | bytes 196616 | tf_op jit(solution)/shard_map/ppermute | solution.py:31
  23.5 6.8 %copy-start.2 = (f32[1,6,256,256]{3,2,1,0:T(8,128)S(1)}, f32[1,6,256,256]{3,2,1,0:T(8,128)}, u32[]{:S(2)}) copy-start(f32[1,6,256,256]{3,2,1,0:T(8,128)} %param.13) | copy-start | bytes 4718596
  25.0 2.9 %collective-permute-start.15 = (f32[128,128]{1,0:T(8,128)}, f32[128,128]{1,0:T(8,128)}, u32[]{:S(2)}, u32[]{:S(2)}) collective-permute-start(f32[128,128]{1,0:T(8,128)} %add.55), channel_id=1, source_target_pairs={{1,3},{3,1},{5,7},{7,5},{9,11},{11,9},{13,15},{15,13},{17,19},{19,... | collective-permute-start | bytes 196616 | tf_op jit(solution)/shard_map/ppermute | solution.py:27
  27.2 15.5 %collective-permute-start.10 = (f32[128,256]{1,0:T(8,128)S(1)}, f32[128,256]{1,0:T(8,128)S(1)}, u32[]{:S(2)}, u32[]{:S(2)}) collective-permute-start(f32[128,256]{1,0:T(8,128)S(1)} %add.52), channel_id=1, source_target_pairs={{1,3},{3,1},{5,7},{7,5},{9,11},{11,9},{13,15},{15,13},{17,19},{19,... | collective-permute-start | bytes 393224 | tf_op jit(solution)/shard_map/ppermute | solution.py:27
  28.8 3.0 %collective-permute-start.16 = (f32[128,128]{1,0:T(8,128)S(1)}, f32[128,128]{1,0:T(8,128)S(1)}, u32[]{:S(2)}, u32[]{:S(2)}) collective-permute-start(f32[128,128]{1,0:T(8,128)S(1)} %select_add_fusion.2), channel_id=1, source_target_pairs={{1,5},{3,7},{5,1},{7,3},{9,13},{11,15},{13,9},{15,11},{17,21},{19,... | collective-permute-start | bytes 196616 | tf_op jit(solution)/shard_map/ppermute | solution.py:27
  30.5 10.1 %collective-permute-start.1 = (f32[64,128]{1,0:T(8,128)S(1)}, f32[64,128]{1,0:T(8,128)S(1)}, u32[]{:S(2)}, u32[]{:S(2)}) collective-permute-start(f32[64,128]{1,0:T(8,128)S(1)} %slice.221), channel_id=1, source_target_pairs={{1,0},{3,2},{5,4},{7,6},{9,8},{11,10},{13,12},{15,14},{17,16},{19,... | collective-permute-start | bytes 98312 | tf_op jit(solution)/shard_map/ppermute | solution.py:35
  31.9 11.6 %collective-permute-start.17 = (f32[128,128]{1,0:T(8,128)S(1)}, f32[128,128]{1,0:T(8,128)S(1)}, u32[]{:S(2)}, u32[]{:S(2)}) collective-permute-start(f32[128,128]{1,0:T(8,128)S(1)} %select_add_fusion.1), channel_id=1, source_target_pairs={{1,9},{3,11},{5,13},{7,15},{9,1},{11,3},{13,5},{15,7},{17,25},{19,... | collective-permute-start | bytes 196616 | tf_op jit(solution)/shard_map/ppermute | solution.py:27
  33.5 11.7 %collective-permute-start.6 = (f32[128,384]{1,0:T(8,128)S(1)}, f32[128,384]{1,0:T(8,128)S(1)}, u32[]{:S(2)}, u32[]{:S(2)}) collective-permute-start(f32[128,384]{1,0:T(8,128)S(1)} %add.50), channel_id=1, source_target_pairs={{1,3},{3,1},{5,7},{7,5},{9,11},{11,9},{13,15},{15,13},{17,19},{19,... | collective-permute-start | bytes 589832 | tf_op jit(solution)/shard_map/ppermute | solution.py:27
  42.1 1.4 %collective-permute-start.3 = (f32[64,512]{1,0:T(8,128)S(1)}, f32[64,512]{1,0:T(8,128)S(1)}, u32[]{:S(2)}, u32[]{:S(2)}) collective-permute-start(f32[64,512]{1,0:T(8,128)S(1)} %fusion.70), channel_id=1, source_target_pairs={{1,3},{3,1},{5,7},{7,5},{9,11},{11,9},{13,15},{15,13},{17,19},{19,... | collective-permute-start | bytes 393224 | tf_op jit(solution)/shard_map/ppermute | solution.py:27
  42.8 2.4 %collective-permute-start.11 = (f32[128,256]{1,0:T(8,128)S(1)}, f32[128,256]{1,0:T(8,128)S(1)}, u32[]{:S(2)}, u32[]{:S(2)}) collective-permute-start(f32[128,256]{1,0:T(8,128)S(1)} %select_add_fusion), channel_id=1, source_target_pairs={{1,5},{3,7},{5,1},{7,3},{9,13},{11,15},{13,9},{15,11},{17,21},{19,... | collective-permute-start | bytes 393224 | tf_op jit(solution)/shard_map/ppermute | solution.py:27
  43.9 13.4 %collective-permute-start.4 = (f32[64,128]{1,0:T(8,128)S(1)}, f32[64,128]{1,0:T(8,128)S(1)}, u32[]{:S(2)}, u32[]{:S(2)}) collective-permute-start(f32[64,128]{1,0:T(8,128)S(1)} %slice_select_fusion.4), channel_id=1, source_target_pairs={{1,0},{3,2},{5,4},{7,6},{9,8},{11,10},{13,12},{15,14},{17,16},{19,... | collective-permute-start | bytes 98312 | tf_op jit(solution)/shard_map/ppermute | solution.py:35
  45.6 11.6 %collective-permute-start.7 = (f32[64,384]{1,0:T(8,128)S(1)}, f32[64,384]{1,0:T(8,128)S(1)}, u32[]{:S(2)}, u32[]{:S(2)}) collective-permute-start(f32[64,384]{1,0:T(8,128)S(1)} %fusion.78), channel_id=1, source_target_pairs={{1,5},{3,7},{5,1},{7,3},{9,13},{11,15},{13,9},{15,11},{17,21},{19,... | collective-permute-start | bytes 294920 | tf_op jit(solution)/shard_map/ppermute | solution.py:27
  57.6 11.4 %collective-permute-start.8 = (f32[64,128]{1,0:T(8,128)S(1)}, f32[64,128]{1,0:T(8,128)S(1)}, u32[]{:S(2)}, u32[]{:S(2)}) collective-permute-start(f32[64,128]{1,0:T(8,128)S(1)} %slice_select_fusion.3), channel_id=1, source_target_pairs={{1,0},{3,2},{5,4},{7,6},{9,8},{11,10},{13,12},{15,14},{17,16},{19,... | collective-permute-start | bytes 98312 | tf_op jit(solution)/shard_map/ppermute | solution.py:35
  59.1 9.8 %collective-permute-start.12 = (f32[64,256]{1,0:T(8,128)S(1)}, f32[64,256]{1,0:T(8,128)S(1)}, u32[]{:S(2)}, u32[]{:S(2)}) collective-permute-start(f32[64,256]{1,0:T(8,128)S(1)} %fusion.79), channel_id=1, source_target_pairs={{1,9},{3,11},{5,13},{7,15},{9,1},{11,3},{13,5},{15,7},{17,25},{19,... | collective-permute-start | bytes 196616 | tf_op jit(solution)/shard_map/ppermute | solution.py:27
  69.5 2.0 %collective-permute-start.18 = (f32[64,128]{1,0:T(8,128)S(1)}, f32[64,128]{1,0:T(8,128)S(1)}, u32[]{:S(2)}, u32[]{:S(2)}) collective-permute-start(f32[64,128]{1,0:T(8,128)S(1)} %fusion.101), channel_id=1, source_target_pairs={{1,17},{3,19},{5,21},{7,23},{9,25},{11,27},{13,29},{15,31},{17,1},... | collective-permute-start | bytes 98312 | tf_op jit(solution)/shard_map/ppermute | solution.py:27
  70.2 9.0 %collective-permute-start.13 = (f32[64,128]{1,0:T(8,128)S(1)}, f32[64,128]{1,0:T(8,128)S(1)}, u32[]{:S(2)}, u32[]{:S(2)}) collective-permute-start(f32[64,128]{1,0:T(8,128)S(1)} %slice_select_fusion.2), channel_id=1, source_target_pairs={{1,0},{3,2},{5,4},{7,6},{9,8},{11,10},{13,12},{15,14},{17,16},{19,... | collective-permute-start | bytes 98312 | tf_op jit(solution)/shard_map/ppermute | solution.py:35
  71.8 9.2 %collective-permute-start.19 = (f32[64,128]{1,0:T(8,128)S(1)}, f32[64,128]{1,0:T(8,128)S(1)}, u32[]{:S(2)}, u32[]{:S(2)}) collective-permute-start(f32[64,128]{1,0:T(8,128)S(1)} %slice_select_fusion.1), channel_id=1, source_target_pairs={{1,0},{3,2},{5,4},{7,6},{9,8},{11,10},{13,12},{15,14},{17,16},{19,... | collective-permute-start | bytes 98312 | tf_op jit(solution)/shard_map/ppermute | solution.py:35

commit v2 on v1

v2 whole, which is shorter than its diff:
```python
import jax
import jax.numpy as jnp
from jax import lax
from jax.sharding import PartitionSpec as P

AXES = ("grp", "sub")
HIGH = lax.Precision.HIGH


def dot(a, b):
    return jnp.dot(a, b, precision=HIGH, preferred_element_type=jnp.float32)


def dot_nt(a, b):
    return lax.dot_general(
        a, b, (((1,), (1,)), ((), ())), precision=HIGH, preferred_element_type=jnp.float32
    )


def dot_tn(a, b):
    return lax.dot_general(
        a, b, (((0,), (0,)), ((), ())), precision=HIGH, preferred_element_type=jnp.float32
    )


def exchange(value, mask):
    return lax.ppermute(value, AXES, [(i, i ^ mask) for i in range(lax.axis_size(AXES))])


def split(value, half):
    n = value.shape[0] // 2
    return jnp.where(half, value[n:], value[:n]), jnp.where(half, value[:n], value[n:])


def join(mine, other, half):
    return jnp.where(
        half, jnp.concatenate([other, mine], axis=0), jnp.concatenate([mine, other], axis=0)
    )


def ordered(own, got, on_right):
    return jnp.where(on_right, got, own), jnp.where(on_right, own, got)


def per_device(right_side, order, leaf_split, leaf_inverse, basis_left, basis_right, coupling):
    row_count = right_side.shape[1]
    rank = basis_left.shape[2]
    top = basis_left.shape[0] - 1
    device_id = lax.axis_index(AXES)
    parity = device_id & 1
    for bit in range(1, top):
        parity = parity ^ ((device_id >> bit) & 1)
    half = parity == 1
    right_cols = jnp.concatenate([basis_right[k] for k in range(top)], axis=1)
    gram = {k: dot_tn(basis_left[k], right_cols[:, : k * rank]) for k in range(1, top)}
    on_right = device_id & 1 == 1
    lower = jnp.concatenate([gram[k] for k in range(top - 2, 0, -1)], axis=1)
    low_keep, low_send = split(lower, half)
    low_width = lower.shape[1]
    n = rank // 2
    first = jnp.concatenate([low_send, gram[top - 1][:n], gram[top - 1][n:]], axis=1)
    got = exchange(first, 1)
    low = low_keep + got[:, :low_width]
    w = (top - 1) * rank
    got_top = jnp.concatenate([got[:, low_width : low_width + w], got[:, low_width + w :]], axis=0)
    gram_pair = jnp.concatenate(ordered(gram[top - 1], got_top, on_right), axis=0)
    pairs = {top - 1: gram_pair}
    for k in range(top - 2, 0, -1):
        bit = top - 1 - k
        right = (device_id >> bit) & 1 == 1
        got_low = exchange(low, 1 << bit | 1)
        w = k * rank
        mine = jnp.concatenate([low[:, :w], got_low[:, :w]], axis=0)
        other = exchange(mine, 1)
        own_full = join(mine[:n], other[:n], half)
        got_full = join(mine[n:], other[n:], half)
        pairs[k] = jnp.concatenate(ordered(own_full, got_full, right), axis=0)
        low = low[:, w:] + got_low[:, w:]

    gathered = jnp.take(right_side, order % row_count, axis=1)
    is_left = lax.iota(jnp.int32, row_count) < leaf_split[0]
    leaf = jnp.where(is_left[:, None] == is_left[None, :], leaf_inverse, 0.0)
    current = dot(gathered, leaf)
    rows = current.shape[0]
    halves = jnp.concatenate(
        [jnp.where(is_left[None, :], current, 0.0), jnp.where(is_left[None, :], 0.0, current)], axis=0
    )
    w = dot(halves, basis_right[top])
    w = jnp.concatenate([w[:rows], w[rows:]], axis=1)
    z = dot(w, coupling[0, top])
    both = dot_nt(jnp.concatenate([z[:, :rank], z[:, rank:]], axis=0), basis_left[top])
    current = current - jnp.where(is_left[None, :], both[:rows], both[rows:])

    sums, send = split(dot(current, right_cols), half)
    got_sums = exchange(send, 1)
    chosen = []
    for bit in range(top):
        k = top - 1 - bit
        own = slice(k * rank, (k + 1) * rank)
        right = (device_id >> bit) & 1 == 1
        if bit > 0:
            got_sums = exchange(sums, 1 << bit | 1)
        left_sums, right_sums = ordered(sums, got_sums, right)
        z = dot(jnp.concatenate([left_sums[:, own], right_sums[:, own]], axis=1), coupling[0, k])
        side = jnp.where(right, z[:, rank:], z[:, :rank])
        chosen.append((side, jnp.where(right, z[:, :rank], z[:, rank:]) if bit == 0 else side))
        if k > 0:
            sums = sums[:, : k * rank] + got_sums[:, : k * rank] - dot(z, pairs[k])
    mine = jnp.concatenate([a for a, _ in chosen], axis=1)
    other = exchange(jnp.concatenate([b for _, b in chosen], axis=1), 1)
    z_all = join(mine, other, half)
    left_cols = jnp.concatenate([basis_left[top - 1 - bit] for bit in range(top)], axis=1)
    return current - dot_nt(z_all, left_cols)


def solution(mesh):
    in_specs = (
        P(None, AXES),
        P(AXES),
        P(AXES),
        P(AXES, None),
        P(None, AXES, None),
        P(None, AXES, None),
        P(AXES, None, None, None),
    )
    return jax.shard_map(
        per_device, mesh=mesh, in_specs=in_specs, out_specs=P(None, AXES), check_vma=False
    )
```

time: 83.9 us -> 81.8 us (0.975)
  starting transfers between devices: 24 us -> 11.6 us
  local copies, waits for them, and re-layouts: 4.11 us -> 16.2 us
  waiting for transfers between devices: 35.2 us -> 32.2 us
  matrix products: 14 us -> 15.3 us
    ppermute x20 -> x13, starting transfers between devices: 24 us -> 11.6 us  [exchange(): lax.ppermute(value, AXES, [(i, i ^ mask) for i in range(lax.axis_size(AXE...]
    unnamed x15 -> x36, local copies, waits for them, and re-layouts: 2.16 us -> 7.35 us
    select_n x11, other arithmetic: 0.16 us -> 3.43 us  [the longest x9 2.6 us: ordered(): return (jnp.where(on_right, got, own), jnp.where(on_right, own, got))]
    add x6 -> x3, other arithmetic: 3.43 us -> 0.22 us  [the longest x1 0.17 us: per_device(): low = low_keep + got[:, :low_width]]
    dot_general x4, matrix products: 3.4 us -> 6.56 us  [dot_tn(): lax.dot_general(a, b, (((0,), (0,)), ((), ())), precision=HIGH, preferred...]
    ppermute x20 -> x13, waiting for transfers between devices: 35.2 us -> 32.2 us  [exchange(): lax.ppermute(value, AXES, [(i, i ^ mask) for i in range(lax.axis_size(AXE...]
    slice x9 -> x8, local copies, waits for them, and re-layouts: 0.8 us -> 3.73 us  [the longest x1 1.7 us: per_device(): got[:, low_width:low_width + w]]
    squeeze x1, local copies, waits for them, and re-layouts: 0.07 us -> 1.38 us  [per_device(): right_cols = jnp.concatenate([basis_right[k] for k in range(top)], axis=1)]
  transfers between devices with their start and end apart: 20 -> 13, of which waited for: 6 -> 9; matrix products, arithmetic and copies ran while one was open for 13% -> 15% of each run, Pallas kernels for 0% -> 0%
where the time goes in v2:
time: 81.8 us; the launch traced here: 81.2 us
  waiting for transfers between devices  32.2 us (39%)
  local copies, waits for them, and re-layouts  16.2 us (20%)
  matrix products  15.3 us (19%)
  starting transfers between devices  11.6 us (14%)
  other arithmetic  4.74 us (6%)
  between operations  1.2 us (1%)
    ppermute x13, waiting for transfers between devices, exchange(): lax.ppermute(value, AXES, [(i, i ^ mask) for i in range(lax.axis_size(AXE...  32.2 us
    ppermute x13, starting transfers between devices, exchange(): lax.ppermute(value, AXES, [(i, i ^ mask) for i in range(lax.axis_size(AXE...  11.6 us
    unnamed x36, local copies, waits for them, and re-layouts  7.35 us
    dot_general x13, matrix products, dot(): return jnp.dot(a, b, precision=HIGH, preferred_element_type=jnp.float32)  7.07 us
    dot_general x4, matrix products, dot_tn(): lax.dot_general(a, b, (((0,), (0,)), ((), ())), precision=HIGH, preferred...  6.56 us
    select_n x9, other arithmetic, ordered(): return (jnp.where(on_right, got, own), jnp.where(on_right, own, got))  2.6 us
    slice x1, local copies, waits for them, and re-layouts, per_device(): got[:, low_width:low_width + w]  1.7 us
    dot_general x2, matrix products, dot_nt(): lax.dot_general(a, b, (((1,), (1,)), ((), ())), precision=HIGH, preferred...  1.67 us
  transfers between devices with their start and end apart: 13, of which 9 were waited for; matrix products, arithmetic and copies ran while one was open for 15% of the time, Pallas kernels for 0%

profile of v2, /device:TPU:0, one launch (start us, length us, event | category | flops | bytes accessed | tf_op | source)
XLA Modules:
  0.0 81.2 jit_solution(12501069182972763082)
XLA Ops:
  0.0 1.4 %slice_bitcast_fusion.3 = (f32[512,128]{1,0:T(8,128)S(1)}, f32[512,128]{1,0:T(8,128)S(1)}, f32[512,128]{1,0:T(8,128)S(1)}, f32[512,128]{1,0:T(8,128)S(1)}) fusion(f32[6,512,128]{2,1,0:T(8,128)} %param.12), kind=kLoop, calls=%fused_computation.82 | loop fusion | bytes 2097152 | tf_op jit(solution)/shard_map/squeeze | solution.py:54
  1.4 0.3 copy-done
  1.7 1.3 %fusion.46 = f32[128,128]{0,1:T(8,128)S(1)} fusion(f32[6,512,128]{2,1,0:T(8,128)} %param.11, f32[6,512,128]{2,1,0:T(8,128)S(1)} %copy-done), kind=kOutput, calls=%fused_computation.59 | convolution fusion | flops 50331648 | bytes 589824 | tf_op jit(solution)/shard_map/dot_general | solution.py:21
  3.1 1.5 %convolution_bitcast_fusion.2 = f32[128,256]{0,1:T(8,128)S(1)} fusion(f32[512,128]{1,0:T(8,128)S(1)} %get-tuple-element.9, f32[512,128]{1,0:T(8,128)S(1)} %get-tuple-element.7, f32[6,512,128]{2,1,0:T(8,128)} %param.11), kind=kOutput, calls=%fused_computation.3 | convolution fusion | flops 100794368 | bytes 917504 | tf_op jit(solution)/shard_map/dot_general | solution.py:21
  4.6 1.7 %convolution_bitcast_fusion.1 = f32[128,384]{0,1:T(8,128)S(1)} fusion(f32[512,128]{1,0:T(8,128)S(1)} %get-tuple-element.8, f32[512,128]{1,0:T(8,128)S(1)} %get-tuple-element.9, f32[512,128]{1,0:T(8,128)S(1)} %get-tuple-element.7, f32[6,512,128]{2,1,0:T(8,128)} %param.11), kind=kOutput, calls=%fused_computation.2 | convolution fusion | flops 151388160 | bytes 1245184 | tf_op jit(solution)/shard_map/dot_general | solution.py:21
  6.4 1.9 %convolution_bitcast_fusion = f32[128,512]{0,1:T(8,128)S(1)} fusion(f32[512,128]{1,0:T(8,128)S(1)} %get-tuple-element.10, f32[512,128]{1,0:T(8,128)S(1)} %get-tuple-element.8, f32[512,128]{1,0:T(8,128)S(1)} %get-tuple-element.9, f32[512,128]{1,0:T(8,128)S(1)} %get-tuple-element.7, f32[6,512,128]{2,1,0:T(8,128)} %param.11), kind=kOutput, calls=%fused_computation.1 | convolution fusion | flops 202113024 | bytes 1572864 | tf_op jit(solution)/shard_map/dot_general | solution.py:21
  8.3 0.1 fusion.136
  8.5 0.2 slice_select_fusion
  8.8 1.1 %copy.12 = f32[64,1792]{1,0:T(8,128)} copy(f32[64,1792]{0,1:T(8,128)S(1)} %pad_maximum_fusion) | data formatting | bytes 917504 | tf_op jit(solution)/shard_map/concatenate | solution.py:61
  9.8 0.5 collective-permute-start.1
  10.3 0.8 constant_dynamic-update-slice_fusion.3
  11.8 0.1 copy.10
  11.9 1.6 %gather_fusion = f32[512,64]{1,0:T(8,128)} fusion(f32[64,512]{0,1:T(8,128)S(1)} %copy.10, s32[1024]{0:T(1024)S(1)} %pad_clamp_fusion), kind=kCustom, calls=%fused_computation | custom fusion | bytes 264192 | tf_op jit(solution)/shard_map/jit(_take)/gather | solution.py:80
  13.5 2.0 %broadcast_select_fusion.5 = (f32[64,512]{1,0:T(8,128)S(1)}, f32[64,512]{1,0:T(8,128)S(1)}, f32[64,512]{1,0:T(8,128)S(1)}) fusion(pred[512]{0:T(512)(128)(4,1)S(1)} %get-tuple-element.61, f32[512,512]{1,0:T(8,128)} %param.10, f32[512,64]{1,0:T(8,128)} %gather_fusion, pred[512]{0:T(512)(128)(4,1)S(1)} %get-tuple-element.5), kind=kOutput, calls=%fused_computation.130 | convolution fusion | flops 101285888 | bytes 1573888 | tf_op jit(solution)/shard_map/dot_general | solution.py:11
  15.6 0.3 fusion.29
  15.8 1.3 %fusion.54 = f32[64,256]{1,0:T(8,128)S(1)} fusion(f32[1,6,256,256]{3,2,1,0:T(8,128)} %param.13, f32[64,128]{1,0:T(8,128)S(1)} %get-tuple-element.47, f32[64,128]{1,0:T(8,128)S(1)} %get-tuple-element.46), kind=kOutput, calls=%fused_computation.70 | convolution fusion | flops 25182208 | bytes 393216 | tf_op jit(solution)/shard_map/dot_general | solution.py:11
  17.3 0.3 fusion.52
  17.6 0.5 fusion.142
  18.2 0.7 slice_select_fusion.3
  19.0 1.4 %collective-permute-done = f32[32,640]{1,0:T(8,128)} collective-permute-done((f32[32,640]{1,0:T(8,128)}, f32[32,640]{1,0:T(8,128)}, u32[]{:S(2)}, u32[]{:S(2)}) %collective-permute-start) | collective-permute-done | bytes 81952 | tf_op jit(solution)/shard_map/ppermute | solution.py:27
  20.4 0.7 slice_select_fusion.15
  21.2 0.2 fusion.50
  21.4 0.6 copy-done.7
  22.0 0.6 constant_dynamic-update-slice_fusion.8
  22.6 1.7 %fusion.135 = (f32[64,512]{1,0:T(8,128)}, f32[64,512]{1,0:T(8,128)}) fusion(f32[64,1792]{1,0:T(8,128)} %collective-permute-done.1), kind=kLoop, calls=%fused_computation.211 | loop fusion | bytes 524288 | tf_op jit(solution)/shard_map/slice | solution.py:65
  24.3 1.7 %copy.17 = f32[64,512]{0,1:T(8,128)} copy(f32[64,512]{1,0:T(8,128)} %get-tuple-element.17) | data formatting | bytes 262144
  26.1 1.6 %slice.340 = f32[64,768]{1,0:T(8,128)} slice(f32[64,1792]{1,0:T(8,128)} %collective-permute-done.1), slice={[0:64], [0:768]} | slice | bytes 393216 | tf_op jit(solution)/shard_map/slice | solution.py:63
  27.7 1.8 %copy.19 = f32[64,768]{0,1:T(8,128)} copy(f32[64,768]{1,0:T(8,128)} %slice.340) | data formatting | bytes 393216
  29.5 1.7 %copy.18 = f32[64,512]{0,1:T(8,128)} copy(f32[64,512]{1,0:T(8,128)} %get-tuple-element.18) | data formatting | bytes 262144
  31.2 1.2 %broadcast_select_fusion.1 = (f32[128,512]{0,1:T(8,128)S(1)}, f32[128,512]{0,1:T(8,128)S(1)}) fusion(f32[128,512]{0,1:T(8,128)S(1)} %convolution_bitcast_fusion, pred[]{:T(512)S(6)} %eq.45, f32[64,512]{0,1:T(8,128)} %copy.18, f32[64,512]{0,1:T(8,128)} %copy.17), kind=kLoop, calls=%fused_computation.111 | loop fusion | flops 196608 | bytes 1048577 | tf_op jit(solution)/shard_map/jit(_where)/select_n | solution.py:42
  32.5 1.3 %fusion.83 = f32[32,512]{1,0:T(8,128)S(1)} fusion(f32[32,640]{1,0:T(8,128)} %collective-permute-done, f32[32,640]{1,0:T(8,128)} %get-tuple-element.31, f32[32,256]{1,0:T(8,128)} %copy-done.7, f32[128,512]{0,1:T(8,128)S(1)} %get-tuple-element.14, f32[128,512]{0,1:T(8,128)S(1)} %get-tuple-element.13), kind=kOutput, calls=%fused_computation.120 | convolution fusion | flops 25329664 | bytes 753664 | tf_op jit(solution)/shard_map/dot_general | solution.py:11
  33.8 2.8 %collective-permute-start.2 = (f32[32,512]{1,0:T(8,128)S(1)}, f32[32,512]{1,0:T(8,128)S(1)}, u32[]{:S(2)}, u32[]{:S(2)}) collective-permute-start(f32[32,512]{1,0:T(8,128)S(1)} %fusion.83), channel_id=1, source_target_pairs={{0,3},{1,2},{2,1},{3,0},{4,7},{5,6},{6,5},{7,4},{8,11},{9,10},{10,... | collective-permute-start | bytes 196616 | tf_op jit(solution)/shard_map/ppermute | solution.py:27
  36.5 0.2 select_add_fusion
  36.8 2.2 %collective-permute-done.2 = f32[32,512]{1,0:T(8,128)S(1)} collective-permute-done((f32[32,512]{1,0:T(8,128)S(1)}, f32[32,512]{1,0:T(8,128)S(1)}, u32[]{:S(2)}, u32[]{:S(2)}) %collective-permute-start.2) | collective-permute-done | bytes 65568 | tf_op jit(solution)/shard_map/ppermute | solution.py:27
  38.9 0.2 fusion.43
  39.2 8.7 %collective-permute-done.3 = f32[64,768]{0,1:T(8,128)S(1)} collective-permute-done((f32[64,768]{0,1:T(8,128)S(1)}, f32[64,768]{0,1:T(8,128)S(1)}, u32[]{:S(2)}, u32[]{:S(2)}) %collective-permute-start.3) | collective-permute-done | bytes 196640 | tf_op jit(solution)/shard_map/ppermute | solution.py:27
  47.9 2.4 %collective-permute-start.6 = (f32[64,384]{0,1:T(8,128)S(1)}, f32[64,384]{0,1:T(8,128)S(1)}, u32[]{:S(2)}, u32[]{:S(2)}) collective-permute-start(f32[64,384]{0,1:T(8,128)S(1)} %get-tuple-element.19), channel_id=1, source_target_pairs={{0,5},{1,4},{2,7},{3,6},{4,1},{5,0},{6,3},{7,2},{8,13},{9,12},{10,... | collective-permute-start | bytes 294920 | tf_op jit(solution)/shard_map/ppermute | solution.py:27
  50.3 0.1 pad_maximum_fusion.3
  50.5 0.4 collective-permute-start.4
  50.9 9.1 %collective-permute-done.6 = f32[64,384]{0,1:T(8,128)S(1)} collective-permute-done((f32[64,384]{0,1:T(8,128)S(1)}, f32[64,384]{0,1:T(8,128)S(1)}, u32[]{:S(2)}, u32[]{:S(2)}) %collective-permute-start.6) | collective-permute-done | bytes 98336 | tf_op jit(solution)/shard_map/ppermute | solution.py:27
  60.0 1.3 %collective-permute-start.9 = (f32[64,128]{0,1:T(8,128)S(1)}, f32[64,128]{0,1:T(8,128)S(1)}, u32[]{:S(2)}, u32[]{:S(2)}) collective-permute-start(f32[64,128]{0,1:T(8,128)S(1)} %slice_add_fusion.1), channel_id=1, source_target_pairs={{0,9},{1,8},{2,11},{3,10},{4,13},{5,12},{6,15},{7,14},{8,1},{9,0},... | collective-permute-start | bytes 98312 | tf_op jit(solution)/shard_map/ppermute | solution.py:27
  61.4 0.4 collective-permute-start.7
  61.8 2.3 %collective-permute-done.9 = f32[64,128]{0,1:T(8,128)S(1)} collective-permute-done((f32[64,128]{0,1:T(8,128)S(1)}, f32[64,128]{0,1:T(8,128)S(1)}, u32[]{:S(2)}, u32[]{:S(2)}) %collective-permute-start.9) | collective-permute-done | bytes 32800 | tf_op jit(solution)/shard_map/ppermute | solution.py:27
  64.2 0.2 collective-permute-start.10
  64.4 0.1 fusion.137
  64.5 0.3 broadcast_select_fusion.3
  64.8 0.3 fusion.90
  65.1 0.2 collective-permute-start.5
  65.3 0.2 collective-permute-done.10
  65.6 0.1 broadcast_select_fusion.9
  65.8 0.2 broadcast_select_fusion.7
  66.0 4.6 %collective-permute-done.5 = f32[32,384]{1,0:T(8,128)S(1)} collective-permute-done((f32[32,384]{1,0:T(8,128)S(1)}, f32[32,384]{1,0:T(8,128)S(1)}, u32[]{:S(2)}, u32[]{:S(2)}) %collective-permute-start.5) | collective-permute-done | bytes 49184 | tf_op jit(solution)/shard_map/ppermute | solution.py:27
  70.7 0.2 fusion.41
  70.9 0.3 fusion.91
  71.2 1.4 %collective-permute-start.8 = (f32[32,256]{1,0:T(8,128)S(1)}, f32[32,256]{1,0:T(8,128)S(1)}, u32[]{:S(2)}, u32[]{:S(2)}) collective-permute-start(f32[32,256]{1,0:T(8,128)S(1)} %fusion.91), channel_id=1, source_target_pairs={{0,9},{1,8},{2,11},{3,10},{4,13},{5,12},{6,15},{7,14},{8,1},{9,0},... | collective-permute-start | bytes 98312 | tf_op jit(solution)/shard_map/ppermute | solution.py:27
  72.6 2.0 %collective-permute-done.8 = f32[32,256]{1,0:T(8,128)S(1)} collective-permute-done((f32[32,256]{1,0:T(8,128)S(1)}, f32[32,256]{1,0:T(8,128)S(1)}, u32[]{:S(2)}, u32[]{:S(2)}) %collective-permute-start.8) | collective-permute-done | bytes 32800 | tf_op jit(solution)/shard_map/ppermute | solution.py:27
  74.6 0.2 fusion.39
  74.8 0.2 fusion.107
  75.0 1.5 %collective-permute-start.11 = (f32[32,128]{1,0:T(8,128)S(1)}, f32[32,128]{1,0:T(8,128)S(1)}, u32[]{:S(2)}, u32[]{:S(2)}) collective-permute-start(f32[32,128]{1,0:T(8,128)S(1)} %fusion.107), channel_id=1, source_target_pairs={{0,17},{1,16},{2,19},{3,18},{4,21},{5,20},{6,23},{7,22},{8,25},{9,... | collective-permute-start | bytes 49160 | tf_op jit(solution)/shard_map/ppermute | solution.py:27
  76.5 1.8 %collective-permute-done.11 = f32[32,128]{1,0:T(8,128)S(1)} collective-permute-done((f32[32,128]{1,0:T(8,128)S(1)}, f32[32,128]{1,0:T(8,128)S(1)}, u32[]{:S(2)}, u32[]{:S(2)}) %collective-permute-start.11) | collective-permute-done | bytes 16416 | tf_op jit(solution)/shard_map/ppermute | solution.py:27
  78.2 0.2 fusion.37
  78.4 0.3 collective-permute-start.12
  78.8 1.0 %bitcast_dynamic-update-slice_fusion = f32[512,640]{1,0:T(8,128)S(1)} fusion(f32[512,640]{1,0:T(8,128)S(1)} %bitcast_dynamic-update-slice_fusion.2, f32[6,512,128]{2,1,0:T(8,128)} %param.11), kind=kLoop, calls=%fused_computation.47 | loop fusion | bytes 524288 | tf_op jit(solution)/shard_map/concatenate | solution.py:112
  79.8 1.4 %convolution_subtract_fusion = f32[64,512]{1,0:T(8,128)} fusion(f32[64,512]{1,0:T(8,128)S(1)} %copy-done.6, f32[512,640]{1,0:T(8,128)S(1)} %bitcast_dynamic-update-slice_fusion, f32[32,640]{1,0:T(8,128)S(1)} %get-tuple-element.49, f32[32,640]{1,0:T(8,128)S(1)} %collective-permute-done.12, pred[]{:T(512)S(6)} %eq.42), kind=kOutput, calls=%fused_computation.4 | convolution fusion | flops 125984768 | bytes 1736705 | tf_op jit(solution)/shard_map/dot_general | solution.py:15
  (59 shorter events, 1.0 us)
Async XLA Ops:
  0.0 1.7 %copy-start = (f32[6,512,128]{2,1,0:T(8,128)S(1)}, f32[6,512,128]{2,1,0:T(8,128)}, u32[]{:S(2)}) copy-start(f32[6,512,128]{2,1,0:T(8,128)} %param.12) | copy-start | bytes 4718596
  8.7 3.1 %copy-start.11 = (s32[512]{0:T(512)S(1)}, s32[512]{0:T(512)}, u32[]{:S(2)}) copy-start(s32[512]{0:T(512)} %param.8) | copy-start | bytes 6148
  8.7 3.0 %copy-start.8 = (f32[64,512]{1,0:T(8,128)S(1)}, f32[64,512]{1,0:T(8,128)}, u32[]{:S(2)}) copy-start(f32[64,512]{1,0:T(8,128)} %param.7) | copy-start | bytes 393220
  9.8 12.8 %collective-permute-start.1 = (f32[64,1792]{1,0:T(8,128)}, f32[64,1792]{1,0:T(8,128)}, u32[]{:S(2)}, u32[]{:S(2)}) collective-permute-start(f32[64,1792]{1,0:T(8,128)} %copy.12), channel_id=1, source_target_pairs={{0,1},{1,0},{2,3},{3,2},{4,5},{5,4},{6,7},{7,6},{8,9},{9,8},{10,11... | collective-permute-start | bytes 1376264 | tf_op jit(solution)/shard_map/ppermute | solution.py:27
  13.5 3.6 %copy-start.2 = (f32[512,640]{1,0:T(8,128)S(1)}, f32[512,640]{1,0:T(8,128)}, u32[]{:S(2)}) copy-start(f32[512,640]{1,0:T(8,128)} %constant_dynamic-update-slice_fusion.3) | copy-start | bytes 3932164
  15.5 1.7 %copy-start.1 = (f32[6,512,128]{2,1,0:T(8,128)S(1)}, f32[6,512,128]{2,1,0:T(8,128)}, u32[]{:S(2)}) copy-start(f32[6,512,128]{2,1,0:T(8,128)} %param.11) | copy-start | bytes 4718596
  17.6 1.4 %copy-start.5 = (f32[64,512]{1,0:T(8,128)}, f32[64,512]{1,0:T(8,128)S(1)}, u32[]{:S(2)}) copy-start(f32[64,512]{1,0:T(8,128)S(1)} %fusion.75) | copy-start | bytes 393220
  18.1 3.0 %copy-start.3 = (f32[1,6,256,256]{3,2,1,0:T(8,128)S(1)}, f32[1,6,256,256]{3,2,1,0:T(8,128)}, u32[]{:S(2)}) copy-start(f32[1,6,256,256]{3,2,1,0:T(8,128)} %param.13) | copy-start | bytes 4718596
  18.8 1.6 %collective-permute-start = (f32[32,640]{1,0:T(8,128)}, f32[32,640]{1,0:T(8,128)}, u32[]{:S(2)}, u32[]{:S(2)}) collective-permute-start(f32[32,640]{1,0:T(8,128)} %get-tuple-element.30), channel_id=1, source_target_pairs={{0,1},{1,0},{2,3},{3,2},{4,5},{5,4},{6,7},{7,6},{8,9},{9,8},{10,11... | collective-permute-start | bytes 245768 | tf_op jit(solution)/shard_map/ppermute | solution.py:27
  21.4 0.6 copy-start.7
  31.2 5.3 %copy-start.4 = (f32[64,768]{0,1:T(8,128)S(1)}, f32[64,768]{0,1:T(8,128)}, u32[]{:S(2)}) copy-start(f32[64,768]{0,1:T(8,128)} %copy.19) | copy-start | bytes 589828
  32.5 6.7 %copy-start.9 = (f32[32,640]{1,0:T(8,128)S(1)}, f32[32,640]{1,0:T(8,128)}, u32[]{:S(2)}) copy-start(f32[32,640]{1,0:T(8,128)} %get-tuple-element.57) | copy-start | bytes 245764
  32.5 6.7 %copy-start.10 = (f32[32,640]{1,0:T(8,128)S(1)}, f32[32,640]{1,0:T(8,128)}, u32[]{:S(2)}) copy-start(f32[32,640]{1,0:T(8,128)} %get-tuple-element.56) | copy-start | bytes 245764
  33.8 5.2 %collective-permute-start.2 = (f32[32,512]{1,0:T(8,128)S(1)}, f32[32,512]{1,0:T(8,128)S(1)}, u32[]{:S(2)}, u32[]{:S(2)}) collective-permute-start(f32[32,512]{1,0:T(8,128)S(1)} %fusion.83), channel_id=1, source_target_pairs={{0,3},{1,2},{2,1},{3,0},{4,7},{5,6},{6,5},{7,4},{8,11},{9,10},{10,... | collective-permute-start | bytes 196616 | tf_op jit(solution)/shard_map/ppermute | solution.py:27
  36.7 11.1 %collective-permute-start.3 = (f32[64,768]{0,1:T(8,128)S(1)}, f32[64,768]{0,1:T(8,128)S(1)}, u32[]{:S(2)}, u32[]{:S(2)}) collective-permute-start(f32[64,768]{0,1:T(8,128)S(1)} %select_add_fusion), channel_id=1, source_target_pairs={{0,3},{1,2},{2,1},{3,0},{4,7},{5,6},{6,5},{7,4},{8,11},{9,10},{10,... | collective-permute-start | bytes 589832 | tf_op jit(solution)/shard_map/ppermute | solution.py:27
  47.9 12.0 %collective-permute-start.6 = (f32[64,384]{0,1:T(8,128)S(1)}, f32[64,384]{0,1:T(8,128)S(1)}, u32[]{:S(2)}, u32[]{:S(2)}) collective-permute-start(f32[64,384]{0,1:T(8,128)S(1)} %get-tuple-element.19), channel_id=1, source_target_pairs={{0,5},{1,4},{2,7},{3,6},{4,1},{5,0},{6,3},{7,2},{8,13},{9,12},{10,... | collective-permute-start | bytes 294920 | tf_op jit(solution)/shard_map/ppermute | solution.py:27
  50.5 13.9 %collective-permute-start.4 = (f32[128,384]{0,1:T(8,128)S(1)}, f32[128,384]{0,1:T(8,128)S(1)}, u32[]{:S(2)}, u32[]{:S(2)}) collective-permute-start(f32[128,384]{0,1:T(8,128)S(1)} %pad_maximum_fusion.3), channel_id=1, source_target_pairs={{0,1},{1,0},{2,3},{3,2},{4,5},{5,4},{6,7},{7,6},{8,9},{9,8},{10,11... | collective-permute-start | bytes 589832 | tf_op jit(solution)/shard_map/ppermute | solution.py:27
  60.0 4.1 %collective-permute-start.9 = (f32[64,128]{0,1:T(8,128)S(1)}, f32[64,128]{0,1:T(8,128)S(1)}, u32[]{:S(2)}, u32[]{:S(2)}) collective-permute-start(f32[64,128]{0,1:T(8,128)S(1)} %slice_add_fusion.1), channel_id=1, source_target_pairs={{0,9},{1,8},{2,11},{3,10},{4,13},{5,12},{6,15},{7,14},{8,1},{9,0},... | collective-permute-start | bytes 98312 | tf_op jit(solution)/shard_map/ppermute | solution.py:27
  61.4 4.3 %collective-permute-start.7 = (f32[128,256]{0,1:T(8,128)S(1)}, f32[128,256]{0,1:T(8,128)S(1)}, u32[]{:S(2)}, u32[]{:S(2)}) collective-permute-start(f32[128,256]{0,1:T(8,128)S(1)} %pad_maximum_fusion.4), channel_id=1, source_target_pairs={{0,1},{1,0},{2,3},{3,2},{4,5},{5,4},{6,7},{7,6},{8,9},{9,8},{10,11... | collective-permute-start | bytes 393224 | tf_op jit(solution)/shard_map/ppermute | solution.py:27
  64.2 1.3 %collective-permute-start.10 = (f32[128,128]{0,1:T(8,128)S(1)}, f32[128,128]{0,1:T(8,128)S(1)}, u32[]{:S(2)}, u32[]{:S(2)}) collective-permute-start(f32[128,128]{0,1:T(8,128)S(1)} %pad_maximum_fusion.5), channel_id=1, source_target_pairs={{0,1},{1,0},{2,3},{3,2},{4,5},{5,4},{6,7},{7,6},{8,9},{9,8},{10,11... | collective-permute-start | bytes 196616 | tf_op jit(solution)/shard_map/ppermute | solution.py:27
  65.1 5.6 %collective-permute-start.5 = (f32[32,384]{1,0:T(8,128)S(1)}, f32[32,384]{1,0:T(8,128)S(1)}, u32[]{:S(2)}, u32[]{:S(2)}) collective-permute-start(f32[32,384]{1,0:T(8,128)S(1)} %fusion.90), channel_id=1, source_target_pairs={{0,5},{1,4},{2,7},{3,6},{4,1},{5,0},{6,3},{7,2},{8,13},{9,12},{10,... | collective-permute-start | bytes 147464 | tf_op jit(solution)/shard_map/ppermute | solution.py:27
  65.8 14.0 %copy-start.6 = (f32[64,512]{1,0:T(8,128)S(1)}, f32[64,512]{1,0:T(8,128)}, u32[]{:S(2)}) copy-start(f32[64,512]{1,0:T(8,128)} %copy-done.5) | copy-start | bytes 393220
  71.2 3.4 %collective-permute-start.8 = (f32[32,256]{1,0:T(8,128)S(1)}, f32[32,256]{1,0:T(8,128)S(1)}, u32[]{:S(2)}, u32[]{:S(2)}) collective-permute-start(f32[32,256]{1,0:T(8,128)S(1)} %fusion.91), channel_id=1, source_target_pairs={{0,9},{1,8},{2,11},{3,10},{4,13},{5,12},{6,15},{7,14},{8,1},{9,0},... | collective-permute-start | bytes 98312 | tf_op jit(solution)/shard_map/ppermute | solution.py:27
  75.0 3.2 %collective-permute-start.11 = (f32[32,128]{1,0:T(8,128)S(1)}, f32[32,128]{1,0:T(8,128)S(1)}, u32[]{:S(2)}, u32[]{:S(2)}) collective-permute-start(f32[32,128]{1,0:T(8,128)S(1)} %fusion.107), channel_id=1, source_target_pairs={{0,17},{1,16},{2,19},{3,18},{4,21},{5,20},{6,23},{7,22},{8,25},{9,... | collective-permute-start | bytes 49160 | tf_op jit(solution)/shard_map/ppermute | solution.py:27
  78.4 1.3 %collective-permute-start.12 = (f32[32,640]{1,0:T(8,128)S(1)}, f32[32,640]{1,0:T(8,128)S(1)}, u32[]{:S(2)}, u32[]{:S(2)}) collective-permute-start(f32[32,640]{1,0:T(8,128)S(1)} %get-tuple-element.48), channel_id=1, source_target_pairs={{0,1},{1,0},{2,3},{3,2},{4,5},{5,4},{6,7},{7,6},{8,9},{9,8},{10,11... | collective-permute-start | bytes 245768 | tf_op jit(solution)/shard_map/ppermute | solution.py:27

commit v3 on v2

v3 whole, which is shorter than its diff:
```python
import functools

import jax
import jax.numpy as jnp
from jax import lax
from jax.experimental import pallas as pl
from jax.experimental.pallas import tpu as pltpu
from jax.sharding import PartitionSpec as P

AXES = ("grp", "sub")
F32, BF16 = jnp.float32, jnp.bfloat16
NN = (((1,), (0,)), ((), ()))
NT = (((1,), (1,)), ((), ()))
TN = (((0,), (0,)), ((), ()))
ANY = pl.BlockSpec(memory_space=pl.ANY)
VMEM = pl.BlockSpec(memory_space=pltpu.VMEM)
SMEM = pl.BlockSpec(memory_space=pltpu.SMEM)
LIMIT = 40 * 1024 * 1024


def parts(x):
    high = x.astype(BF16)
    return high, (x - high.astype(F32)).astype(BF16)


def product(a, b, dims):
    return lax.dot_general(a, b, dims, preferred_element_type=F32)


def dot(a, b, dims=NN):
    ah, al = parts(a)
    bh, bl = parts(b)
    if dims[0][0] == (0,):
        return product(ah, bh, dims) + (product(al, bh, dims) + product(ah, bl, dims))
    rows = a.shape[0]
    both = product(jnp.concatenate([ah, al], axis=0), bh, dims)
    return both[:rows] + (both[rows:] + product(ah, bl, dims))


def parity_of(device_id, bits):
    parity = device_id & 1
    for bit in range(1, bits):
        parity = parity ^ ((device_id >> bit) & 1)
    return parity


def gram_kernel(top, left, right, low_keep, first, gram_top, left_v, right_v, sems):
    rank = left.shape[2]
    n = rank // 2
    copies = []
    for j in range(top - 1):
        cols = slice(j * rank, (j + 1) * rank)
        copies.append(pltpu.make_async_copy(right.at[j], right_v.at[:, cols], sems.at[0, j]))
        copies.append(pltpu.make_async_copy(left.at[j + 1], left_v.at[:, cols], sems.at[1, j]))
    for copy in copies:
        copy.start()
    for copy in copies:
        copy.wait()
    half = parity_of(lax.axis_index(AXES), top) == 1
    at = 0
    for k in range(top - 1, 0, -1):
        value = dot(left_v[:, (k - 1) * rank : k * rank], right_v[:, : k * rank], TN)
        w = k * rank
        if k == top - 1:
            gram_top[...] = value
            base = first.shape[1] - 2 * w
            first[:, base : base + w] = value[:n]
            first[:, base + w :] = value[n:]
        else:
            low_keep[:, at : at + w] = jnp.where(half, value[n:], value[:n])
            first[:, at : at + w] = jnp.where(half, value[:n], value[n:])
            at += w


def local_kernel(
    top, order, split, rhs, leaf, left, right, coupling, current_out, keep, send,
    rhs_v, leaf_v, left_v, right_top, right_v, coupling_v, sems,
):
    rank = left.shape[2]
    count, size = rhs_v.shape
    device_id = lax.axis_index(AXES)
    c_rhs = pltpu.make_async_copy(rhs, rhs_v, sems.at[0])
    c_leaf = pltpu.make_async_copy(leaf, leaf_v, sems.at[1])
    c_rtop = pltpu.make_async_copy(right.at[top], right_top, sems.at[2])
    c_coup = pltpu.make_async_copy(coupling.at[0, top], coupling_v, sems.at[3])
    c_left = pltpu.make_async_copy(left.at[top], left_v, sems.at[4])
    c_right = [
        pltpu.make_async_copy(right.at[j], right_v.at[:, j * rank : (j + 1) * rank], sems.at[5 + j])
        for j in range(top)
    ]
    for copy in [c_rhs, c_leaf, c_rtop, c_coup, c_left] + c_right:
        copy.start()
    local = order[...] - device_id * size
    pick = (lax.broadcasted_iota(jnp.int32, (size, size), 0) == local).astype(F32).astype(BF16)
    c_rhs.wait()
    high, low = parts(rhs_v[...])
    moved = product(jnp.concatenate([high, low], axis=0), pick, NN).astype(BF16)
    is_left = lax.broadcasted_iota(jnp.int32, (1, size), 1) < split[0]
    left_rows = lax.broadcasted_iota(jnp.int32, (size, 1), 0) < split[0]
    c_leaf.wait()
    lh, ll = parts(jnp.where(left_rows == is_left, leaf_v[...], 0.0))
    both = product(moved, lh, NN)
    current = both[:count] + (both[count:] + product(moved[:count], ll, NN))
    c_rtop.wait()
    halves = jnp.concatenate(
        [jnp.where(is_left, current, 0.0), jnp.where(is_left, 0.0, current)], axis=0
    )
    w = dot(halves, right_top[...])
    c_coup.wait()
    z = dot(jnp.concatenate([w[:count], w[count:]], axis=1), coupling_v[...])
    c_left.wait()
    update = dot(jnp.concatenate([z[:, :rank], z[:, rank:]], axis=0), left_v[...], NT)
    current = current - jnp.where(is_left, update[:count], update[count:])
    current_out[...] = current
    for copy in c_right:
        copy.wait()
    sums = dot(current, right_v[...])
    half = parity_of(device_id, top) == 1
    n = count // 2
    keep[...] = jnp.where(half, sums[n:], sums[:n])
    send[...] = jnp.where(half, sums[:n], sums[n:])


def pair_kernel_top(gram_top, low_keep, first, coupling, d_out, low_out, pair):
    rank, w = gram_top.shape
    n = rank // 2
    right = lax.axis_index(AXES) & 1
    low_w = low_keep.shape[1]
    low_out[...] = low_keep[...] + first[:, :low_w]
    own, got = pl.multiple_of(right * rank, rank), pl.multiple_of((1 - right) * rank, rank)
    pair[pl.ds(own, rank), :] = gram_top[...]
    pair[pl.ds(got, n), :] = first[:, low_w : low_w + w]
    pair[pl.ds(got + n, n), :] = first[:, low_w + w :]
    d_out[...] = dot(coupling[...], pair[...])


def pair_kernel(top, bit, mine, other, coupling, d_out, pair):
    n, rank = mine.shape[0] // 2, mine.shape[0]
    device_id = lax.axis_index(AXES)
    half = parity_of(device_id, top)
    right = (device_id >> bit) & 1
    for child, rows in ((right, slice(0, n)), (1 - right, slice(n, 2 * n))):
        pair[pl.ds(pl.multiple_of(child * rank + half * n, n), n), :] = mine[rows, :]
        pair[pl.ds(pl.multiple_of(child * rank + (1 - half) * n, n), n), :] = other[rows, :]
    d_out[...] = dot(coupling[...], pair[...])


def last_kernel(top, current, mine, other, left, out, left_v, z_v, sems):
    rank = left.shape[2]
    copies = [
        pltpu.make_async_copy(left.at[j], left_v.at[:, j * rank : (j + 1) * rank], sems.at[j])
        for j in range(top)
    ]
    for copy in copies:
        copy.start()
    half = parity_of(lax.axis_index(AXES), top)
    n = mine.shape[0]
    z_v[pl.ds(pl.multiple_of(half * n, n), n), :] = mine[...]
    z_v[pl.ds(pl.multiple_of((1 - half) * n, n), n), :] = other[...]
    for copy in copies:
        copy.wait()
    out[...] = current[...] - dot(z_v[...], left_v[...], NT)


def call(kernel, outs, in_specs, out_specs, scratch, *args):
    return pl.pallas_call(
        kernel,
        out_shape=outs,
        in_specs=in_specs,
        out_specs=out_specs,
        scratch_shapes=scratch,
        compiler_params=pltpu.CompilerParams(vmem_limit_bytes=LIMIT),
    )(*args)


def shape(*dims):
    return jax.ShapeDtypeStruct(dims, F32)


def xdot(a, b):
    return jnp.dot(a, b, precision=lax.Precision.HIGH, preferred_element_type=F32)


def exchange(value, mask):
    return lax.ppermute(value, AXES, [(i, i ^ mask) for i in range(lax.axis_size(AXES))])


def ordered(own, got, on_right):
    return jnp.where(on_right, got, own), jnp.where(on_right, own, got)


def per_device(right_side, order, leaf_split, leaf_inverse, basis_left, basis_right, coupling):
    count, size = right_side.shape
    rank = basis_left.shape[2]
    top = basis_left.shape[0] - 1
    n = rank // 2
    device_id = lax.axis_index(AXES)
    low_w = rank * (top - 1) * (top - 2) // 2
    top_w = (top - 1) * rank
    dma = pltpu.SemaphoreType.DMA
    low_keep, first, gram_top = call(
        functools.partial(gram_kernel, top),
        [shape(n, low_w), shape(n, low_w + 2 * top_w), shape(rank, top_w)],
        [ANY, ANY],
        [VMEM] * 3,
        [pltpu.VMEM((size, top_w), F32), pltpu.VMEM((size, top_w), F32), dma((2, top - 1))],
        basis_left,
        basis_right,
    )
    got_first = exchange(first, 1)
    current, keep, send = call(
        functools.partial(local_kernel, top),
        [shape(count, size), shape(count // 2, top * rank), shape(count // 2, top * rank)],
        [VMEM, SMEM, ANY, ANY, ANY, ANY, ANY],
        [VMEM] * 3,
        [
            pltpu.VMEM((count, size), F32),
            pltpu.VMEM((size, size), F32),
            pltpu.VMEM((size, rank), F32),
            pltpu.VMEM((size, rank), F32),
            pltpu.VMEM((size, top * rank), F32),
            pltpu.VMEM((2 * rank, 2 * rank), F32),
            dma((5 + top,)),
        ],
        order.reshape(1, size),
        leaf_split,
        right_side,
        leaf_inverse,
        basis_left,
        basis_right,
        coupling,
    )
    got_sums = exchange(send, 1)
    factors = {}
    factors[top - 1], low = call(
        pair_kernel_top,
        [shape(2 * rank, top_w), shape(n, low_w)],
        [VMEM] * 4,
        [VMEM] * 2,
        [pltpu.VMEM((2 * rank, top_w), F32)],
        gram_top,
        low_keep,
        got_first,
        coupling[0, top - 1],
    )
    for k in range(top - 2, 0, -1):
        bit = top - 1 - k
        got_low = exchange(low, 1 << bit | 1)
        w = k * rank
        mine = jnp.concatenate([low[:, :w], got_low[:, :w]], axis=0)
        other = exchange(mine, 1)
        factors[k] = call(
            functools.partial(pair_kernel, top, bit),
            shape(2 * rank, w),
            [VMEM] * 3,
            VMEM,
            [pltpu.VMEM((2 * rank, w), F32)],
            mine,
            other,
            coupling[0, k],
        )
        low = low[:, w:] + got_low[:, w:]

    sums = keep
    chosen = []
    for bit in range(top):
        k = top - 1 - bit
        own = slice(k * rank, (k + 1) * rank)
        right = (device_id >> bit) & 1 == 1
        if bit > 0:
            got_sums = exchange(sums, 1 << bit | 1)
        left_sums, right_sums = ordered(sums[:, own], got_sums[:, own], right)
        w = jnp.concatenate([left_sums, right_sums], axis=1)
        z = xdot(w, coupling[0, k])
        side = jnp.where(right, z[:, rank:], z[:, :rank])
        chosen.append((side, jnp.where(right, z[:, :rank], z[:, rank:]) if bit == 0 else side))
        if k > 0:
            sums = sums[:, : k * rank] + got_sums[:, : k * rank] - xdot(w, factors[k])
    mine = jnp.concatenate([a for a, _ in chosen[::-1]], axis=1)
    other = exchange(jnp.concatenate([b for _, b in chosen[::-1]], axis=1), 1)
    return call(
        functools.partial(last_kernel, top),
        shape(count, size),
        [VMEM, VMEM, VMEM, ANY],
        VMEM,
        [pltpu.VMEM((size, top * rank), F32), pltpu.VMEM((count, top * rank), F32), dma((top,))],
        current,
        mine,
        other,
        basis_left,
    )


def solution(mesh):
    in_specs = (
        P(None, AXES),
        P(AXES),
        P(AXES),
        P(AXES, None),
        P(None, AXES, None),
        P(None, AXES, None),
        P(AXES, None, None, None),
    )
    return jax.shard_map(
        per_device, mesh=mesh, in_specs=in_specs, out_specs=P(None, AXES), check_vma=False
    )
```

time: 81.8 us -> 59.6 us (0.73)
  matrix products: 15.3 us -> 2.71 us
  Pallas kernels: 0 us -> 9.33 us
  waiting for transfers between devices: 32.2 us -> 22.9 us
  local copies, waits for them, and re-layouts: 16.2 us -> 10.8 us
  other arithmetic: 4.74 us -> 0.86 us
    dot_general x19 -> x9, matrix products: 15.3 us -> 2.71 us  [xdot(): jnp.dot(a, b, precision=lax.Precision.HIGH, preferred_element_type=F32)]
    pallas_call x0 -> x7, Pallas kernels: none -> 9.33 us  [call(): pl.pallas_call(kernel, out_shape=outs, in_specs=in_specs, out_specs=out_s...]
    ppermute x13, waiting for transfers between devices: 32.2 us -> 22.9 us  [exchange(): lax.ppermute(value, AXES, [(i, i ^ mask) for i in range(lax.axis_size(AXE...]
    slice x8 -> x0, local copies, waits for them, and re-layouts: 3.72 us -> none  [the longest x1 1.7 us: per_device(): got[:, low_width:low_width + w]]
    unnamed x36 -> x35, local copies, waits for them, and re-layouts: 7.35 us -> 9.89 us
    concatenate x3 -> x0, local copies, waits for them, and re-layouts: 2.05 us -> none  [the longest x1 1.06 us: per_device(): jnp.concatenate([low_send, gram[top - 1][:n], gram[top - 1][n:]], axis=1)]
    select_n x9 -> x5, other arithmetic: 2.6 us -> 0.76 us  [ordered(): return (jnp.where(on_right, got, own), jnp.where(on_right, own, got))]
    gather x1 -> x0, local copies, waits for them, and re-layouts: 1.64 us -> none  [per_device(): gathered = jnp.take(right_side, order % row_count, axis=1)]
  transfers between devices with their start and end apart: 13 -> 13, of which waited for: 9 -> 9; matrix products, arithmetic and copies ran while one was open for 15% -> 5% of each run, Pallas kernels for 0% -> 5%
where the time goes in v3:
time: 59.6 us; the launch traced here: 59.1 us
  waiting for transfers between devices  22.9 us (38%)
  starting transfers between devices  11.6 us (19%)
  local copies, waits for them, and re-layouts  10.8 us (18%)
  Pallas kernels  9.33 us (16%)
  matrix products  2.71 us (5%)
  between operations  0.93 us (2%)
  other arithmetic  0.86 us (1%)
    ppermute x13, waiting for transfers between devices, exchange(): lax.ppermute(value, AXES, [(i, i ^ mask) for i in range(lax.axis_size(AXE...  22.9 us
    ppermute x13, starting transfers between devices, exchange(): lax.ppermute(value, AXES, [(i, i ^ mask) for i in range(lax.axis_size(AXE...  11.6 us
    unnamed x35, local copies, waits for them, and re-layouts  9.89 us
    pallas_call x7, Pallas kernels, call(): pl.pallas_call(kernel, out_shape=outs, in_specs=in_specs, out_specs=out_s...  9.33 us
    dot_general x9, matrix products, xdot(): jnp.dot(a, b, precision=lax.Precision.HIGH, preferred_element_type=F32)  2.71 us
  transfers between devices with their start and end apart: 13, of which 9 were waited for; matrix products, arithmetic and copies ran while one was open for 5% of the time, Pallas kernels for 5%

profile of v3, /device:TPU:0, one launch (start us, length us, event | category | flops | bytes accessed | tf_op | source)
XLA Modules:
  0.0 59.1 jit_solution(1393340384940293596)
XLA Ops:
  0.7 0.0 copy-start
  0.7 1.4 %copy-done = f32[6,512,128]{2,1,0:T(8,128)S(1)} copy-done((f32[6,512,128]{2,1,0:T(8,128)S(1)}, f32[6,512,128]{2,1,0:T(8,128)}, u32[]{:S(2)}) %copy-start) | copy-done | bytes 1572888
  2.1 1.4 %copy-done.2 = f32[1,6,256,256]{3,2,1,0:T(8,128)S(1)} copy-done((f32[1,6,256,256]{3,2,1,0:T(8,128)S(1)}, f32[1,6,256,256]{3,2,1,0:T(8,128)}, u32[]{:S(2)}) %copy-start.2) | copy-done | bytes 1572888
  3.5 1.4 %copy-done.4 = f32[6,512,128]{2,1,0:T(8,128)S(1)} copy-done((f32[6,512,128]{2,1,0:T(8,128)S(1)}, f32[6,512,128]{2,1,0:T(8,128)}, u32[]{:S(2)}) %copy-start.4) | copy-done | bytes 1572888
  4.9 1.2 %copy-done.6 = f32[512,512]{1,0:T(8,128)S(1)} copy-done((f32[512,512]{1,0:T(8,128)S(1)}, f32[512,512]{1,0:T(8,128)}, u32[]{:S(2)}) %copy-start.6) | copy-done | bytes 1048600
  6.1 0.9 %copy-done.14 = f32[64,512]{1,0:T(8,128)S(1)} copy-done((f32[64,512]{1,0:T(8,128)S(1)}, f32[64,512]{1,0:T(8,128)}, u32[]{:S(2)}) %copy-start.14) | copy-done | bytes 131096
  7.0 0.7 %copy-done.16 = s32[512]{0:T(512)S(1)} copy-done((s32[512]{0:T(512)S(1)}, s32[512]{0:T(512)}, u32[]{:S(2)}) %copy-start.16) | copy-done | bytes 2072
  7.7 3.3 %shard_map.73 = (f32[64,512]{1,0:T(8,128)S(1)}, f32[32,640]{1,0:T(8,128)S(1)}, f32[32,640]{1,0:T(8,128)}) custom-call(s32[1,512]{1,0:T(1,128)S(1)} %bitcast.20, s32[1]{0:T(128)S(6)} %copy.13.split, f32[64,512]{1,0:T(8,128)S(1)} %copy-done.14, f32[512,512]{1,0:T(8,128)S(1)} %copy-done.6, f32[6,512,128]{2,1,0:T(8,128)S(1)} %copy-done, ...), custom_call_target="tpu_custom_call" | custom-call | tf_op jit(solution)/shard_map/pallas_call | solution.py:166
  11.0 0.0 copy-start.15
  11.0 0.5 collective-permute-start
  11.5 0.0 copy-done.1
  11.5 0.0 copy-done.5
  11.5 2.2 %shard_map.74 = (f32[64,768]{1,0:T(8,128)S(1)}, f32[64,1792]{1,0:T(8,128)}, f32[128,512]{1,0:T(8,128)S(1)}) custom-call(f32[6,512,128]{2,1,0:T(8,128)S(1)} %copy-done.1, f32[6,512,128]{2,1,0:T(8,128)S(1)} %copy-done.5), custom_call_target="tpu_custom_call" | custom-call | tf_op jit(solution)/shard_map/pallas_call | solution.py:166
  13.7 0.0 copy-done.15
  13.7 0.0 copy-start.10
  13.7 0.0 copy-start.12
  13.7 0.0 copy-start.3
  13.7 0.1 collective-permute-start.1
  13.8 0.9 %slice_bitcast_fusion = (f32[256,256]{1,0:T(8,128)}, f32[256,256]{1,0:T(8,128)S(1)}, f32[256,256]{1,0:T(8,128)}, f32[256,256]{1,0:T(8,128)}) fusion(f32[1,6,256,256]{3,2,1,0:T(8,128)S(1)} %copy-done.2), kind=kLoop, calls=%fused_computation.3 | loop fusion | bytes 2097152 | tf_op jit(solution)/shard_map/squeeze | solution.py:260
  14.7 0.0 copy-done.10
  14.7 0.0 collective-permute-done
  14.7 0.7 %slice_select_fusion.11 = (f32[32,128]{1,0:T(8,128)S(1)}, f32[32,128]{1,0:T(8,128)S(1)}) fusion(f32[32,640]{1,0:T(8,128)} %collective-permute-done, f32[32,640]{1,0:T(8,128)} %copy-done.15, pred[]{:T(512)S(6)} %eq.16), kind=kLoop, calls=%fused_computation.56 | loop fusion | flops 8192 | bytes 65537 | tf_op jit(solution)/shard_map/jit(_where)/select_n | solution.py:189
  15.5 0.5 collective-permute-done.1.first
  15.9 0.9 %copy-done.9 = f32[256,256]{1,0:T(8,128)S(1)} copy-done((f32[256,256]{1,0:T(8,128)S(1)}, f32[256,256]{1,0:T(8,128)}, u32[]{:S(2)}) %copy-start.9) | copy-done | bytes 262168
  16.9 0.9 %copy-done.11 = f32[128,512]{1,0:T(8,128)S(1)} copy-done((f32[128,512]{1,0:T(8,128)S(1)}, f32[128,512]{1,0:T(8,128)}, u32[]{:S(2)}) %copy-start.11) | copy-done | bytes 262168
  17.8 0.9 %copy-done.13 = f32[64,768]{1,0:T(8,128)S(1)} copy-done((f32[64,768]{1,0:T(8,128)S(1)}, f32[64,768]{1,0:T(8,128)}, u32[]{:S(2)}) %copy-start.13) | copy-done | bytes 196632
  18.8 1.5 %shard_map.75 = (f32[256,512]{1,0:T(8,128)S(1)}, f32[64,768]{1,0:T(8,128)S(1)}) custom-call(f32[128,512]{1,0:T(8,128)S(1)} %copy-done.11, f32[64,768]{1,0:T(8,128)S(1)} %copy-done.13, f32[64,1792]{1,0:T(8,128)} %collective-permute-done.1.first, f32[256,256]{1,0:T(8,128)S(1)} %copy-done.9), custom_call_target="tpu_custom_call" | custom-call | tf_op jit(solution)/shard_map/pallas_call | solution.py:166
  20.3 0.0 copy-start.8
  20.3 1.2 %fusion.3 = f32[32,512]{1,0:T(8,128)S(1)} fusion(f32[32,640]{1,0:T(8,128)} %collective-permute-done, f32[32,640]{1,0:T(8,128)} %copy-done.15, f32[256,512]{1,0:T(8,128)S(1)} %get-tuple-element.19, f32[32,128]{1,0:T(8,128)S(1)} %get-tuple-element.29, f32[32,128]{1,0:T(8,128)S(1)} %get-tuple-element.28), kind=kOutput, calls=%fused_computation.11 | convolution fusion | flops 25206784 | bytes 753664 | tf_op jit(solution)/shard_map/dot_general | solution.py:181
  21.5 2.8 %collective-permute-start.2 = (f32[32,512]{1,0:T(8,128)S(1)}, f32[32,512]{1,0:T(8,128)S(1)}, u32[]{:S(2)}, u32[]{:S(2)}) collective-permute-start(f32[32,512]{1,0:T(8,128)S(1)} %fusion.3), channel_id=1, source_target_pairs={{0,3},{1,2},{2,1},{3,0},{4,7},{5,6},{6,5},{7,4},{8,11},{9,10},{10,... | collective-permute-start | bytes 196616 | tf_op jit(solution)/shard_map/ppermute | solution.py:185
  24.2 0.2 fusion.15
  24.5 0.1 collective-permute-start.3
  24.5 2.1 %collective-permute-done.2 = f32[32,512]{1,0:T(8,128)S(1)} collective-permute-done((f32[32,512]{1,0:T(8,128)S(1)}, f32[32,512]{1,0:T(8,128)S(1)}, u32[]{:S(2)}, u32[]{:S(2)}) %collective-permute-start.2) | collective-permute-done | bytes 65568 | tf_op jit(solution)/shard_map/ppermute | solution.py:185
  26.7 4.7 %collective-permute-done.3 = f32[64,768]{1,0:T(8,128)S(1)} collective-permute-done((f32[64,768]{1,0:T(8,128)S(1)}, f32[64,768]{1,0:T(8,128)S(1)}, u32[]{:S(2)}, u32[]{:S(2)}) %collective-permute-start.3) | collective-permute-done | bytes 196640 | tf_op jit(solution)/shard_map/ppermute | solution.py:185
  31.4 2.4 %collective-permute-start.6 = (f32[64,384]{1,0:T(8,128)S(1)}, f32[64,384]{1,0:T(8,128)S(1)}, u32[]{:S(2)}, u32[]{:S(2)}) collective-permute-start(f32[64,384]{1,0:T(8,128)S(1)} %get-tuple-element.25), channel_id=1, source_target_pairs={{0,5},{1,4},{2,7},{3,6},{4,1},{5,0},{6,3},{7,2},{8,13},{9,12},{10,... | collective-permute-start | bytes 294920 | tf_op jit(solution)/shard_map/ppermute | solution.py:185
  33.9 0.4 collective-permute-start.4
  34.3 5.0 %collective-permute-done.6 = f32[64,384]{1,0:T(8,128)S(1)} collective-permute-done((f32[64,384]{1,0:T(8,128)S(1)}, f32[64,384]{1,0:T(8,128)S(1)}, u32[]{:S(2)}, u32[]{:S(2)}) %collective-permute-start.6) | collective-permute-done | bytes 98336 | tf_op jit(solution)/shard_map/ppermute | solution.py:185
  39.3 1.2 %collective-permute-start.9 = (f32[64,128]{1,0:T(8,128)S(1)}, f32[64,128]{1,0:T(8,128)S(1)}, u32[]{:S(2)}, u32[]{:S(2)}) collective-permute-start(f32[64,128]{1,0:T(8,128)S(1)} %slice_add_fusion.3), channel_id=1, source_target_pairs={{0,9},{1,8},{2,11},{3,10},{4,13},{5,12},{6,15},{7,14},{8,1},{9,0},... | collective-permute-start | bytes 98312 | tf_op jit(solution)/shard_map/ppermute | solution.py:185
  40.5 0.4 collective-permute-start.7
  40.9 1.7 %collective-permute-done.9 = f32[64,128]{1,0:T(8,128)S(1)} collective-permute-done((f32[64,128]{1,0:T(8,128)S(1)}, f32[64,128]{1,0:T(8,128)S(1)}, u32[]{:S(2)}, u32[]{:S(2)}) %collective-permute-start.9) | collective-permute-done | bytes 32800 | tf_op jit(solution)/shard_map/ppermute | solution.py:185
  42.6 0.2 collective-permute-start.10
  42.8 0.0 collective-permute-done.4.other
  42.8 0.0 copy-done.8
  42.8 0.4 shard_map.76
  43.2 0.2 fusion.4
  43.4 0.6 %collective-permute-start.5 = (f32[32,384]{1,0:T(8,128)S(1)}, f32[32,384]{1,0:T(8,128)S(1)}, u32[]{:S(2)}, u32[]{:S(2)}) collective-permute-start(f32[32,384]{1,0:T(8,128)S(1)} %fusion.4), channel_id=1, source_target_pairs={{0,5},{1,4},{2,7},{3,6},{4,1},{5,0},{6,3},{7,2},{8,13},{9,12},{10,... | collective-permute-start | bytes 147464 | tf_op jit(solution)/shard_map/ppermute | solution.py:185
  44.0 0.2 fusion.13
  44.2 0.0 collective-permute-done.10.other
  44.2 0.3 shard_map.78
  44.5 0.0 collective-permute-done.7.other
  44.6 0.3 shard_map.77
  44.9 4.3 %collective-permute-done.5 = f32[32,384]{1,0:T(8,128)S(1)} collective-permute-done((f32[32,384]{1,0:T(8,128)S(1)}, f32[32,384]{1,0:T(8,128)S(1)}, u32[]{:S(2)}, u32[]{:S(2)}) %collective-permute-start.5) | collective-permute-done | bytes 49184 | tf_op jit(solution)/shard_map/ppermute | solution.py:185
  49.1 0.2 fusion.5
  49.3 1.3 %collective-permute-start.8 = (f32[32,256]{1,0:T(8,128)S(1)}, f32[32,256]{1,0:T(8,128)S(1)}, u32[]{:S(2)}, u32[]{:S(2)}) collective-permute-start(f32[32,256]{1,0:T(8,128)S(1)} %fusion.5), channel_id=1, source_target_pairs={{0,9},{1,8},{2,11},{3,10},{4,13},{5,12},{6,15},{7,14},{8,1},{9,0},... | collective-permute-start | bytes 98312 | tf_op jit(solution)/shard_map/ppermute | solution.py:185
  50.7 0.2 fusion.11
  50.9 1.9 %collective-permute-done.8 = f32[32,256]{1,0:T(8,128)S(1)} collective-permute-done((f32[32,256]{1,0:T(8,128)S(1)}, f32[32,256]{1,0:T(8,128)S(1)}, u32[]{:S(2)}, u32[]{:S(2)}) %collective-permute-start.8) | collective-permute-done | bytes 32800 | tf_op jit(solution)/shard_map/ppermute | solution.py:185
  52.8 0.2 fusion.17
  52.9 1.3 %collective-permute-start.11 = (f32[32,128]{1,0:T(8,128)S(1)}, f32[32,128]{1,0:T(8,128)S(1)}, u32[]{:S(2)}, u32[]{:S(2)}) collective-permute-start(f32[32,128]{1,0:T(8,128)S(1)} %fusion.17), channel_id=1, source_target_pairs={{0,17},{1,16},{2,19},{3,18},{4,21},{5,20},{6,23},{7,22},{8,25},{9,... | collective-permute-start | bytes 49160 | tf_op jit(solution)/shard_map/ppermute | solution.py:185
  54.3 0.2 fusion.9
  54.5 1.7 %collective-permute-done.11 = f32[32,128]{1,0:T(8,128)S(1)} collective-permute-done((f32[32,128]{1,0:T(8,128)S(1)}, f32[32,128]{1,0:T(8,128)S(1)}, u32[]{:S(2)}, u32[]{:S(2)}) %collective-permute-start.11) | collective-permute-done | bytes 16416 | tf_op jit(solution)/shard_map/ppermute | solution.py:185
  56.2 0.2 fusion
  56.4 0.2 collective-permute-start.12
  56.7 1.1 %collective-permute-done.12.other = f32[32,640]{1,0:T(8,128)S(1)} collective-permute-done((f32[32,640]{1,0:T(8,128)S(1)}, f32[32,640]{1,0:T(8,128)S(1)}, u32[]{:S(2)}, u32[]{:S(2)}) %collective-permute-start.12) | collective-permute-done | bytes 81952 | tf_op jit(solution)/shard_map/ppermute | solution.py:185
  57.8 1.4 %shard_map.79 = f32[64,512]{1,0:T(8,128)} custom-call(f32[64,512]{1,0:T(8,128)S(1)} %get-tuple-element.13.current, f32[32,640]{1,0:T(8,128)S(1)} %constant_dynamic-update-slice_fusion.mine, f32[32,640]{1,0:T(8,128)S(1)} %collective-permute-done.12.other, f32[6,512,128]{2,1,0:T(8,128)S(1)} %copy-done.1), custom_call_target="tpu_custom_call" | custom-call | tf_op jit(solution)/shard_map/pallas_call | solution.py:166
  (32 shorter events, 0.2 us)
Async XLA Ops:
  0.7 1.4 %copy-start = (f32[6,512,128]{2,1,0:T(8,128)S(1)}, f32[6,512,128]{2,1,0:T(8,128)}, u32[]{:S(2)}) copy-start(f32[6,512,128]{2,1,0:T(8,128)} %left.5) | copy-start | bytes 4718596
  2.1 1.4 %copy-start.2 = (f32[1,6,256,256]{3,2,1,0:T(8,128)S(1)}, f32[1,6,256,256]{3,2,1,0:T(8,128)}, u32[]{:S(2)}) copy-start(f32[1,6,256,256]{3,2,1,0:T(8,128)} %coupling.1) | copy-start | bytes 4718596
  3.5 1.4 %copy-start.4 = (f32[6,512,128]{2,1,0:T(8,128)S(1)}, f32[6,512,128]{2,1,0:T(8,128)}, u32[]{:S(2)}) copy-start(f32[6,512,128]{2,1,0:T(8,128)} %right.3) | copy-start | bytes 4718596
  4.9 1.2 %copy-start.6 = (f32[512,512]{1,0:T(8,128)S(1)}, f32[512,512]{1,0:T(8,128)}, u32[]{:S(2)}) copy-start(f32[512,512]{1,0:T(8,128)} %leaf.1) | copy-start | bytes 3145732
  6.1 0.9 %copy-start.14 = (f32[64,512]{1,0:T(8,128)S(1)}, f32[64,512]{1,0:T(8,128)}, u32[]{:S(2)}) copy-start(f32[64,512]{1,0:T(8,128)} %rhs.1) | copy-start | bytes 393220
  7.0 0.7 %copy-start.16 = (s32[512]{0:T(512)S(1)}, s32[512]{0:T(512)}, u32[]{:S(2)}) copy-start(s32[512]{0:T(512)} %param.8) | copy-start | bytes 6148
  7.7 3.8 %copy-start.1 = (f32[6,512,128]{2,1,0:T(8,128)S(1)}, f32[6,512,128]{2,1,0:T(8,128)}, u32[]{:S(2)}) copy-start(f32[6,512,128]{2,1,0:T(8,128)} %left.5) | copy-start | bytes 4718596
  7.7 3.8 %copy-start.5 = (f32[6,512,128]{2,1,0:T(8,128)S(1)}, f32[6,512,128]{2,1,0:T(8,128)}, u32[]{:S(2)}) copy-start(f32[6,512,128]{2,1,0:T(8,128)} %right.3) | copy-start | bytes 4718596
  11.0 2.7 %copy-start.15 = (f32[32,640]{1,0:T(8,128)}, f32[32,640]{1,0:T(8,128)S(1)}, u32[]{:S(2)}) copy-start(f32[32,640]{1,0:T(8,128)S(1)} %get-tuple-element.14) | copy-start | bytes 245764
  11.0 3.8 %collective-permute-start = (f32[32,640]{1,0:T(8,128)}, f32[32,640]{1,0:T(8,128)}, u32[]{:S(2)}, u32[]{:S(2)}) collective-permute-start(f32[32,640]{1,0:T(8,128)} %get-tuple-element.15), channel_id=1, source_target_pairs={{0,1},{1,0},{2,3},{3,2},{4,5},{5,4},{6,7},{7,6},{8,9},{9,8},{10,11... | collective-permute-start | bytes 245768 | tf_op jit(solution)/shard_map/ppermute | solution.py:185
  13.7 1.0 %copy-start.10 = (f32[128,512]{1,0:T(8,128)}, f32[128,512]{1,0:T(8,128)S(1)}, u32[]{:S(2)}) copy-start(f32[128,512]{1,0:T(8,128)S(1)} %get-tuple-element.16.gram_top) | copy-start | bytes 786436
  13.7 1.0 %copy-start.12 = (f32[64,768]{1,0:T(8,128)}, f32[64,768]{1,0:T(8,128)S(1)}, u32[]{:S(2)}) copy-start(f32[64,768]{1,0:T(8,128)S(1)} %get-tuple-element.17.low_keep) | copy-start | bytes 589828
  13.7 10.5 %copy-start.3 = (f32[1,6,256,256]{3,2,1,0:T(8,128)S(1)}, f32[1,6,256,256]{3,2,1,0:T(8,128)}, u32[]{:S(2)}) copy-start(f32[1,6,256,256]{3,2,1,0:T(8,128)} %coupling.1) | copy-start | bytes 4718596
  13.7 2.2 %collective-permute-start.1 = (f32[64,1792]{1,0:T(8,128)}, f32[64,1792]{1,0:T(8,128)}, u32[]{:S(2)}, u32[]{:S(2)}) collective-permute-start(f32[64,1792]{1,0:T(8,128)} %get-tuple-element.18), channel_id=1, source_target_pairs={{0,1},{1,0},{2,3},{3,2},{4,5},{5,4},{6,7},{7,6},{8,9},{9,8},{10,11... | collective-permute-start | bytes 1376264 | tf_op jit(solution)/shard_map/ppermute | solution.py:185
  15.9 1.0 %copy-start.9 = (f32[256,256]{1,0:T(8,128)S(1)}, f32[256,256]{1,0:T(8,128)}, u32[]{:S(2)}) copy-start(f32[256,256]{1,0:T(8,128)} %get-tuple-element.24.coupling) | copy-start | bytes 786436
  16.9 0.9 %copy-start.11 = (f32[128,512]{1,0:T(8,128)S(1)}, f32[128,512]{1,0:T(8,128)}, u32[]{:S(2)}) copy-start(f32[128,512]{1,0:T(8,128)} %copy-done.10) | copy-start | bytes 786436
  17.8 0.9 %copy-start.13 = (f32[64,768]{1,0:T(8,128)S(1)}, f32[64,768]{1,0:T(8,128)}, u32[]{:S(2)}) copy-start(f32[64,768]{1,0:T(8,128)} %copy-done.12) | copy-start | bytes 589828
  20.3 22.5 %copy-start.8 = (f32[256,256]{1,0:T(8,128)S(1)}, f32[256,256]{1,0:T(8,128)}, u32[]{:S(2)}) copy-start(f32[256,256]{1,0:T(8,128)} %get-tuple-element.23.coupling) | copy-start | bytes 786436
  21.5 5.2 %collective-permute-start.2 = (f32[32,512]{1,0:T(8,128)S(1)}, f32[32,512]{1,0:T(8,128)S(1)}, u32[]{:S(2)}, u32[]{:S(2)}) collective-permute-start(f32[32,512]{1,0:T(8,128)S(1)} %fusion.3), channel_id=1, source_target_pairs={{0,3},{1,2},{2,1},{3,0},{4,7},{5,6},{6,5},{7,4},{8,11},{9,10},{10,... | collective-permute-start | bytes 196616 | tf_op jit(solution)/shard_map/ppermute | solution.py:185
  24.5 6.9 %collective-permute-start.3 = (f32[64,768]{1,0:T(8,128)S(1)}, f32[64,768]{1,0:T(8,128)S(1)}, u32[]{:S(2)}, u32[]{:S(2)}) collective-permute-start(f32[64,768]{1,0:T(8,128)S(1)} %get-tuple-element.20), channel_id=1, source_target_pairs={{0,3},{1,2},{2,1},{3,0},{4,7},{5,6},{6,5},{7,4},{8,11},{9,10},{10,... | collective-permute-start | bytes 589832 | tf_op jit(solution)/shard_map/ppermute | solution.py:185
  31.4 12.8 %copy-start.7 = (f32[256,256]{1,0:T(8,128)S(1)}, f32[256,256]{1,0:T(8,128)}, u32[]{:S(2)}) copy-start(f32[256,256]{1,0:T(8,128)} %get-tuple-element.21.coupling) | copy-start | bytes 786436
  31.4 7.8 %collective-permute-start.6 = (f32[64,384]{1,0:T(8,128)S(1)}, f32[64,384]{1,0:T(8,128)S(1)}, u32[]{:S(2)}, u32[]{:S(2)}) collective-permute-start(f32[64,384]{1,0:T(8,128)S(1)} %get-tuple-element.25), channel_id=1, source_target_pairs={{0,5},{1,4},{2,7},{3,6},{4,1},{5,0},{6,3},{7,2},{8,13},{9,12},{10,... | collective-permute-start | bytes 294920 | tf_op jit(solution)/shard_map/ppermute | solution.py:185
  33.9 8.9 %collective-permute-start.4 = (f32[128,384]{1,0:T(8,128)S(1)}, f32[128,384]{1,0:T(8,128)S(1)}, u32[]{:S(2)}, u32[]{:S(2)}) collective-permute-start(f32[128,384]{1,0:T(8,128)S(1)} %pad_maximum_fusion.mine), channel_id=1, source_target_pairs={{0,1},{1,0},{2,3},{3,2},{4,5},{5,4},{6,7},{7,6},{8,9},{9,8},{10,11... | collective-permute-start | bytes 589832 | tf_op jit(solution)/shard_map/ppermute | solution.py:185
  39.3 3.3 %collective-permute-start.9 = (f32[64,128]{1,0:T(8,128)S(1)}, f32[64,128]{1,0:T(8,128)S(1)}, u32[]{:S(2)}, u32[]{:S(2)}) collective-permute-start(f32[64,128]{1,0:T(8,128)S(1)} %slice_add_fusion.3), channel_id=1, source_target_pairs={{0,9},{1,8},{2,11},{3,10},{4,13},{5,12},{6,15},{7,14},{8,1},{9,0},... | collective-permute-start | bytes 98312 | tf_op jit(solution)/shard_map/ppermute | solution.py:185
  40.5 4.0 %collective-permute-start.7 = (f32[128,256]{1,0:T(8,128)S(1)}, f32[128,256]{1,0:T(8,128)S(1)}, u32[]{:S(2)}, u32[]{:S(2)}) collective-permute-start(f32[128,256]{1,0:T(8,128)S(1)} %pad_maximum_fusion.1.mine), channel_id=1, source_target_pairs={{0,1},{1,0},{2,3},{3,2},{4,5},{5,4},{6,7},{7,6},{8,9},{9,8},{10,11... | collective-permute-start | bytes 393224 | tf_op jit(solution)/shard_map/ppermute | solution.py:185
  42.6 1.6 %collective-permute-start.10 = (f32[128,128]{1,0:T(8,128)S(1)}, f32[128,128]{1,0:T(8,128)S(1)}, u32[]{:S(2)}, u32[]{:S(2)}) collective-permute-start(f32[128,128]{1,0:T(8,128)S(1)} %pad_maximum_fusion.2.mine), channel_id=1, source_target_pairs={{0,1},{1,0},{2,3},{3,2},{4,5},{5,4},{6,7},{7,6},{8,9},{9,8},{10,11... | collective-permute-start | bytes 196616 | tf_op jit(solution)/shard_map/ppermute | solution.py:185
  43.4 5.7 %collective-permute-start.5 = (f32[32,384]{1,0:T(8,128)S(1)}, f32[32,384]{1,0:T(8,128)S(1)}, u32[]{:S(2)}, u32[]{:S(2)}) collective-permute-start(f32[32,384]{1,0:T(8,128)S(1)} %fusion.4), channel_id=1, source_target_pairs={{0,5},{1,4},{2,7},{3,6},{4,1},{5,0},{6,3},{7,2},{8,13},{9,12},{10,... | collective-permute-start | bytes 147464 | tf_op jit(solution)/shard_map/ppermute | solution.py:185
  49.3 3.4 %collective-permute-start.8 = (f32[32,256]{1,0:T(8,128)S(1)}, f32[32,256]{1,0:T(8,128)S(1)}, u32[]{:S(2)}, u32[]{:S(2)}) collective-permute-start(f32[32,256]{1,0:T(8,128)S(1)} %fusion.5), channel_id=1, source_target_pairs={{0,9},{1,8},{2,11},{3,10},{4,13},{5,12},{6,15},{7,14},{8,1},{9,0},... | collective-permute-start | bytes 98312 | tf_op jit(solution)/shard_map/ppermute | solution.py:185
  52.9 3.2 %collective-permute-start.11 = (f32[32,128]{1,0:T(8,128)S(1)}, f32[32,128]{1,0:T(8,128)S(1)}, u32[]{:S(2)}, u32[]{:S(2)}) collective-permute-start(f32[32,128]{1,0:T(8,128)S(1)} %fusion.17), channel_id=1, source_target_pairs={{0,17},{1,16},{2,19},{3,18},{4,21},{5,20},{6,23},{7,22},{8,25},{9,... | collective-permute-start | bytes 49160 | tf_op jit(solution)/shard_map/ppermute | solution.py:185
  56.4 1.3 %collective-permute-start.12 = (f32[32,640]{1,0:T(8,128)S(1)}, f32[32,640]{1,0:T(8,128)S(1)}, u32[]{:S(2)}, u32[]{:S(2)}) collective-permute-start(f32[32,640]{1,0:T(8,128)S(1)} %constant_dynamic-update-slice_fusion.5), channel_id=1, source_target_pairs={{0,1},{1,0},{2,3},{3,2},{4,5},{5,4},{6,7},{7,6},{8,9},{9,8},{10,11... | collective-permute-start | bytes 245768 | tf_op jit(solution)/shard_map/ppermute | solution.py:185

commit v4 on v3

v4 whole, which is shorter than its diff:
```python
import functools

import jax
import jax.numpy as jnp
from jax import lax
from jax.experimental import pallas as pl
from jax.experimental.pallas import tpu as pltpu
from jax.sharding import PartitionSpec as P

AXES = ("grp", "sub")
F32, BF16 = jnp.float32, jnp.bfloat16
NN = (((1,), (0,)), ((), ()))
NT = (((1,), (1,)), ((), ()))
TN = (((0,), (0,)), ((), ()))
HBM = pl.BlockSpec(memory_space=pltpu.HBM)
VMEM = pl.BlockSpec(memory_space=pltpu.VMEM)
SMEM = pl.BlockSpec(memory_space=pltpu.SMEM)
LIMIT = 24 * 1024 * 1024


def parts(x):
    high = x.astype(BF16)
    return high, (x - high.astype(F32)).astype(BF16)


def product(a, b, dims):
    return lax.dot_general(a, b, dims, preferred_element_type=F32)


def dot(a, b, dims=NN):
    ah, al = parts(a)
    bh, bl = parts(b)
    if dims[0][0] == (0,):
        return product(ah, bh, dims) + (product(al, bh, dims) + product(ah, bl, dims))
    rows = a.shape[0]
    both = product(jnp.concatenate([ah, al], axis=0), bh, dims)
    return both[:rows] + (both[rows:] + product(ah, bl, dims))


def parity_of(device_id, bits):
    parity = device_id & 1
    for bit in range(1, bits):
        parity = parity ^ ((device_id >> bit) & 1)
    return parity


def gram_kernel(
    top, left, right, coupling, rhs, leaf, low_keep, low_send, left_v, right_v, left_top, right_top,
    coupling_v, rhs_v, leaf_v, sems,
):
    rank = left.shape[2]
    n = rank // 2

    def cols(j):
        return slice(j * rank, (j + 1) * rank)

    used = []
    for j in range(top - 2):
        used.append(pltpu.make_async_copy(left.at[j + 1], left_v.at[:, cols(j + 1)], sems.at[0, j]))
        used.append(pltpu.make_async_copy(right.at[j], right_v.at[:, cols(j)], sems.at[1, j]))
    rest = [
        pltpu.make_async_copy(rhs, rhs_v, sems.at[2, 0]),
        pltpu.make_async_copy(leaf, leaf_v, sems.at[2, 1]),
        pltpu.make_async_copy(right.at[top], right_top, sems.at[2, 2]),
        pltpu.make_async_copy(coupling.at[0], coupling_v, sems.at[2, 3]),
        pltpu.make_async_copy(left.at[top], left_top, sems.at[2, 4]),
        pltpu.make_async_copy(left.at[0], left_v.at[:, cols(0)], sems.at[3, 0]),
        pltpu.make_async_copy(left.at[top - 1], left_v.at[:, cols(top - 1)], sems.at[3, 1]),
        pltpu.make_async_copy(right.at[top - 2], right_v.at[:, cols(top - 2)], sems.at[3, 2]),
        pltpu.make_async_copy(right.at[top - 1], right_v.at[:, cols(top - 1)], sems.at[3, 3]),
    ]
    for copy in used + rest:
        copy.start()
    for copy in used:
        copy.wait()
    half = parity_of(lax.axis_index(AXES), top) == 1
    at = 0
    for k in range(top - 2, 0, -1):
        w = k * rank
        value = dot(left_v[:, cols(k)], right_v[:, :w], TN)
        low_keep[:, at : at + w] = jnp.where(half, value[n:], value[:n])
        low_send[:, at : at + w] = jnp.where(half, value[:n], value[n:])
        at += w
    for copy in rest:
        copy.wait()


def leaf_kernel(top, order, split, rhs, leaf, left, right, current, gram_top):
    rank = left.shape[1] // top
    count, size = rhs.shape
    local = order[...] - lax.axis_index(AXES) * size
    pick = (lax.broadcasted_iota(jnp.int32, (size, size), 0) == local).astype(F32).astype(BF16)
    high, low = parts(rhs[...])
    moved = product(jnp.concatenate([high, low], axis=0), pick, NN).astype(BF16)
    is_left = lax.broadcasted_iota(jnp.int32, (1, size), 1) < split[0]
    left_rows = lax.broadcasted_iota(jnp.int32, (size, 1), 0) < split[0]
    lh, ll = parts(jnp.where(left_rows == is_left, leaf[...], 0.0))
    both = product(moved, lh, NN)
    current[...] = both[:count] + (both[count:] + product(moved[:count], ll, NN))
    w = (top - 1) * rank
    gram_top[...] = dot(left[:, w:], right[:, :w], TN)


def local_kernel(
    top, split, first, left_top, right_top, right, coupling, gram_top, current_out, keep, send
):
    rank = left_top.shape[1]
    count, size = first.shape
    current = first[...]
    is_left = lax.broadcasted_iota(jnp.int32, (1, size), 1) < split[0]
    halves = jnp.concatenate(
        [jnp.where(is_left, current, 0.0), jnp.where(is_left, 0.0, current)], axis=0
    )
    w = dot(halves, right_top[...])
    z = dot(jnp.concatenate([w[:count], w[count:]], axis=1), coupling[top])
    update = dot(jnp.concatenate([z[:, :rank], z[:, rank:]], axis=0), left_top[...], NT)
    current = current - jnp.where(is_left, update[:count], update[count:])
    current_out[...] = current
    sums = dot(current, right[...])
    half = parity_of(lax.axis_index(AXES), top) == 1
    n = count // 2
    keep[...] = jnp.where(half, sums[n:], sums[:n])
    send[:, : top * rank] = jnp.where(half, sums[:n], sums[n:])
    at = top * rank
    for row in range(0, rank, n):
        send[:, at : at + (top - 1) * rank] = gram_top[row : row + n, :]
        at += (top - 1) * rank


def top_kernel(top, keep, got, gram_top, coupling, sums, z_mine, z_other, pair):
    n, rank = keep.shape[0], gram_top.shape[0]
    w = (top - 1) * rank
    right = lax.axis_index(AXES) & 1
    own_at, got_at = right * rank, (1 - right) * rank
    pair[pl.ds(pl.multiple_of(own_at, rank), rank), :] = gram_top[...]
    at = top * rank
    for row in range(0, rank, n):
        pair[pl.ds(pl.multiple_of(got_at + row, n), n), :] = got[:, at : at + w]
        at += w
    mine, other = keep[:, w:], got[:, w : top * rank]
    is_right = right == 1
    both = jnp.concatenate(
        [jnp.where(is_right, other, mine), jnp.where(is_right, mine, other)], axis=1
    )
    z = dot(both, coupling[top - 1])
    sums[...] = keep[:, :w] + got[:, :w] - dot(z, pair[...])
    z_mine[...] = jnp.where(is_right, z[:, rank:], z[:, :rank])
    z_other[...] = jnp.where(is_right, z[:, :rank], z[:, rank:])


def pair_kernel(top, bit, mine, other, coupling, d_out, pair):
    n, rank = mine.shape[0] // 2, mine.shape[0]
    device_id = lax.axis_index(AXES)
    half = parity_of(device_id, top)
    right = (device_id >> bit) & 1
    for child, rows in ((right, slice(0, n)), (1 - right, slice(n, 2 * n))):
        pair[pl.ds(pl.multiple_of(child * rank + half * n, n), n), :] = mine[rows, :]
        pair[pl.ds(pl.multiple_of(child * rank + (1 - half) * n, n), n), :] = other[rows, :]
    d_out[...] = dot(coupling[top - 1 - bit], pair[...])


def joined(mine, other, top):
    half = parity_of(lax.axis_index(AXES), top) == 1
    return jnp.concatenate(
        [jnp.where(half, other, mine), jnp.where(half, mine, other)], axis=0
    )


def early_kernel(top, current, mine, other, left, coupling, out, factor):
    rank = left.shape[1] // top
    z = joined(mine[...], other[...], top)
    out[...] = current[...] - dot(z, left[:, rank:], NT)
    right = (lax.axis_index(AXES) >> (top - 1)) & 1 == 1
    side = jnp.where(right, coupling[0, :, rank:], coupling[0, :, :rank])
    factor[...] = dot(side, left[:, :rank], NT)


def last_kernel(top, current, mine, other, factor, out):
    out[...] = current[...] - dot(joined(mine[...], other[...], top), factor[...])


def call(kernel, outs, in_specs, out_specs, scratch, *args):
    return pl.pallas_call(
        kernel,
        out_shape=outs,
        in_specs=in_specs,
        out_specs=out_specs,
        scratch_shapes=scratch,
        compiler_params=pltpu.CompilerParams(vmem_limit_bytes=LIMIT),
    )(*args)


def shape(*dims):
    return jax.ShapeDtypeStruct(dims, F32)


def xdot(a, b):
    return jnp.dot(a, b, precision=lax.Precision.HIGH, preferred_element_type=F32)


def exchange(value, mask):
    return lax.ppermute(value, AXES, [(i, i ^ mask) for i in range(lax.axis_size(AXES))])


def level_sums(sums, got, k, rank, on_right):
    own, other = sums[:, k * rank :], got[:, k * rank :]
    both = jnp.concatenate(
        [jnp.where(on_right, other, own), jnp.where(on_right, own, other)], axis=1
    )
    return both, lambda z: jnp.where(on_right, z[:, rank:], z[:, :rank])


def per_device(right_side, order, leaf_split, leaf_inverse, basis_left, basis_right, coupling):
    count, size = right_side.shape
    rank = basis_left.shape[2]
    levels = basis_left.shape[0]
    top = levels - 1
    n = rank // 2
    device_id = lax.axis_index(AXES)
    low_w = rank * (top - 1) * (top - 2) // 2
    wide = top * rank
    rows = count // 2
    low_keep, low_send, left, right, left_top, right_top, coup, rhs, leaf = call(
        functools.partial(gram_kernel, top),
        [
            shape(n, low_w),
            shape(n, low_w),
            shape(size, wide),
            shape(size, wide),
            shape(size, rank),
            shape(size, rank),
            shape(levels, 2 * rank, 2 * rank),
            shape(count, size),
            shape(size, size),
        ],
        [HBM] * 5,
        [VMEM] * 9,
        [pltpu.SemaphoreType.DMA((4, max(5, top)))],
        *[
            pltpu.with_memory_space_constraint(x, pltpu.HBM)
            for x in (basis_left, basis_right, coupling, right_side, leaf_inverse)
        ],
    )
    got_low = exchange(low_send, 1)
    current, gram_top = call(
        functools.partial(leaf_kernel, top),
        [shape(count, size), shape(rank, wide - rank)],
        [VMEM, SMEM] + [VMEM] * 4,
        [VMEM] * 2,
        [],
        order.reshape(1, size),
        leaf_split,
        rhs,
        leaf,
        left,
        right,
    )
    low = low_keep + got_low
    current, low = lax.optimization_barrier((current, low))
    current, keep, send = call(
        functools.partial(local_kernel, top),
        [shape(count, size), shape(rows, wide), shape(rows, wide + rank // rows * (wide - rank))],
        [SMEM] + [VMEM] * 6,
        [VMEM] * 3,
        [],
        leaf_split,
        current,
        left_top,
        right_top,
        right,
        coup,
        gram_top,
    )
    got = exchange(send, 1)
    sums, z_mine, z_other = call(
        functools.partial(top_kernel, top),
        [shape(rows, wide - rank), shape(rows, rank), shape(rows, rank)],
        [VMEM] * 4,
        [VMEM] * 3,
        [pltpu.VMEM((2 * rank, wide - rank), F32)],
        keep,
        got,
        gram_top,
        coup,
    )
    z_mine, z_other = [z_mine], [z_other]
    for k in range(top - 2, 0, -1):
        bit = top - 1 - k
        w = k * rank
        got_low = exchange(low, 1 << bit | 1)
        got_sums = exchange(sums, 1 << bit | 1)
        mine = jnp.concatenate([low[:, :w], got_low[:, :w]], axis=0)
        other = exchange(mine, 1)
        factor = call(
            functools.partial(pair_kernel, top, bit),
            shape(2 * rank, w),
            [VMEM] * 3,
            VMEM,
            [pltpu.VMEM((2 * rank, w), F32)],
            mine,
            other,
            coup,
        )
        next_low = low[:, w:] + got_low[:, w:]
        both, side = level_sums(sums, got_sums, k, rank, (device_id >> bit) & 1 == 1)
        z = xdot(both, coup[k])
        z_mine.append(side(z))
        z_other.append(z_mine[-1])
        sums = sums[:, :w] + got_sums[:, :w] - xdot(both, factor)
        if k > 1:
            low, sums = lax.optimization_barrier((next_low, sums))
    got_sums = exchange(sums, 1 << (top - 1) | 1)
    mine = jnp.concatenate(z_mine[::-1], axis=1)
    other = exchange(jnp.concatenate(z_other[::-1], axis=1), 1)
    current, factor = call(
        functools.partial(early_kernel, top),
        [shape(count, size), shape(2 * rank, size)],
        [VMEM] * 5,
        [VMEM] * 2,
        [],
        current,
        mine,
        other,
        left,
        coup,
    )
    both, _ = level_sums(sums, got_sums, 0, rank, (device_id >> (top - 1)) & 1 == 1)
    return call(
        functools.partial(last_kernel, top),
        shape(count, size),
        [VMEM] * 4,
        VMEM,
        [],
        current,
        both,
        exchange(both, 1),
        factor,
    )


def solution(mesh):
    in_specs = (
        P(None, AXES),
        P(AXES),
        P(AXES),
        P(AXES, None),
        P(None, AXES, None),
        P(None, AXES, None),
        P(AXES, None, None, None),
    )
    return jax.shard_map(
        per_device, mesh=mesh, in_specs=in_specs, out_specs=P(None, AXES), check_vma=False
    )
```

time: 59.6 us -> 43.7 us (0.73)
  local copies, waits for them, and re-layouts: 10.8 us -> 0.02 us
  waiting for transfers between devices: 22.9 us -> 19.2 us
  Pallas kernels: 9.33 us -> 7.83 us
  matrix products: 2.71 us -> 1.96 us
  other arithmetic: 0.86 us -> 1.48 us
  starting transfers between devices: 11.6 us -> 12.2 us
    unnamed x35 -> x5, local copies, waits for them, and re-layouts: 9.89 us -> 0.01 us
    ppermute x13 -> x14, waiting for transfers between devices: 22.9 us -> 19.2 us  [exchange(): lax.ppermute(value, AXES, [(i, i ^ mask) for i in range(lax.axis_size(AXE...]
    pallas_call x7 -> x9, Pallas kernels: 9.33 us -> 7.83 us  [call(): pl.pallas_call(kernel, out_shape=outs, in_specs=in_specs, out_specs=out_s...]
    squeeze x1 -> x0, local copies, waits for them, and re-layouts: 0.89 us -> none  [per_device(): coupling[0, k]]
    dot_general x9 -> x6, matrix products: 2.71 us -> 1.96 us  [xdot(): jnp.dot(a, b, precision=lax.Precision.HIGH, preferred_element_type=F32)]
    slice x0 -> x1, other arithmetic: none -> 0.66 us  [per_device(): mine = jnp.concatenate([low[:, :w], got_low[:, :w]], axis=0)]
    ppermute x13 -> x14, starting transfers between devices: 11.6 us -> 12.2 us  [exchange(): lax.ppermute(value, AXES, [(i, i ^ mask) for i in range(lax.axis_size(AXE...]
  transfers between devices with their start and end apart: 13 -> 14, of which waited for: 9 -> 9; matrix products, arithmetic and copies ran while one was open for 5% -> 3% of each run, Pallas kernels for 5% -> 8%
where the time goes in v4:
time: 43.7 us; the launch traced here: 43.5 us
  waiting for transfers between devices  19.2 us (44%)
  starting transfers between devices  12.2 us (28%)
  Pallas kernels  7.83 us (18%)
  matrix products  1.96 us (4%)
  other arithmetic  1.48 us (3%)
  between operations  0.83 us (2%)
    ppermute x14, waiting for transfers between devices, exchange(): lax.ppermute(value, AXES, [(i, i ^ mask) for i in range(lax.axis_size(AXE...  19.2 us
    ppermute x14, starting transfers between devices, exchange(): lax.ppermute(value, AXES, [(i, i ^ mask) for i in range(lax.axis_size(AXE...  12.2 us
    pallas_call x9, Pallas kernels, call(): pl.pallas_call(kernel, out_shape=outs, in_specs=in_specs, out_specs=out_s...  7.83 us
    dot_general x6, matrix products, xdot(): jnp.dot(a, b, precision=lax.Precision.HIGH, preferred_element_type=F32)  1.96 us
  transfers between devices with their start and end apart: 14, of which 9 were waited for; matrix products, arithmetic and copies ran while one was open for 3% of the time, Pallas kernels for 8%

profile of v4, /device:TPU:0, one launch (start us, length us, event | category | flops | bytes accessed | tf_op | source)
XLA Modules:
  0.0 43.5 jit_solution(15349423363363220277)
XLA Ops:
  0.0 0.0 copy-start
  0.0 2.8 %shard_map.73 = (f32[64,768]{1,0:T(8,128)S(1)}, f32[64,768]{1,0:T(8,128)S(1)}, f32[512,640]{1,0:T(8,128)S(1)}, f32[512,640]{1,0:T(8,128)S(1)}, f32[512,128]{1,0:...) custom-call(f32[6,512,128]{2,1,0:T(8,128)} %left.1, ...), custom_call_target="tpu_custom_call" | custom-call | tf_op jit(solution)/shard_map/pallas_call | solution.py:183
  2.8 0.5 %collective-permute-start = (f32[64,768]{1,0:T(8,128)S(1)}, f32[64,768]{1,0:T(8,128)S(1)}, u32[]{:S(2)}, u32[]{:S(2)}) collective-permute-start(f32[64,768]{1,0:T(8,128)S(1)} %get-tuple-element.36), channel_id=1, source_target_pairs={{0,1},{1,0},{2,3},{3,2},{4,5},{5,4},{6,7},{7,6},{8,9},{9,8},{10,11... | collective-permute-start | bytes 589832 | tf_op jit(solution)/shard_map/ppermute | solution.py:202
  4.0 0.0 copy-done
  4.0 1.0 %shard_map.74 = (f32[64,512]{1,0:T(8,128)S(1)}, f32[128,512]{1,0:T(8,128)S(1)}) custom-call(s32[1,512]{1,0:T(1,128)S(1)} %bitcast.13, s32[1]{0:T(128)S(6)} %copy.9.split, f32[64,512]{1,0:T(8,128)S(1)} %get-tuple-element.30.rhs, f32[512,512]{1,0:T(8,128)S(1)} %get-tuple-element.31.leaf, f32[512,640]{1,0:T(8,128)S(1)} %get-tuple-element.32.left, ...), custom_call_target="tpu_custom_call" | custom-call | tf_op jit(solution)/shard_map/pallas_call | solution.py:183
  5.1 0.0 collective-permute-done
  5.1 2.8 %collective-permute-start.1 = (f32[64,768]{1,0:T(8,128)S(1)}, f32[64,768]{1,0:T(8,128)S(1)}, u32[]{:S(2)}, u32[]{:S(2)}) collective-permute-start(f32[64,768]{1,0:T(8,128)S(1)} %add.21), channel_id=1, source_target_pairs={{0,3},{1,2},{2,1},{3,0},{4,7},{5,6},{6,5},{7,4},{8,11},{9,10},{10,... | collective-permute-start | bytes 589832 | tf_op jit(solution)/shard_map/ppermute | solution.py:202
  7.8 1.0 %shard_map.75 = (f32[64,512]{1,0:T(8,128)S(1)}, f32[32,640]{1,0:T(8,128)S(1)}, f32[32,2688]{1,0:T(8,128)S(1)}) custom-call(s32[1]{0:T(128)S(6)} %copy.9.split, f32[64,512]{1,0:T(8,128)S(1)} %get-tuple-element.37.first, f32[512,128]{1,0:T(8,128)S(1)} %get-tuple-element.38.left_top, f32[512,128]{1,0:T(8,128)S(1)} %get-tuple-element.39.right_top, ...), custom_call_target="tpu_custom_call" | custom-call | tf_op jit(solution)/shard_map/pallas_call | solution.py:183
  8.8 0.1 collective-permute-start.2
  8.9 4.2 %collective-permute-done.1 = f32[64,768]{1,0:T(8,128)S(1)} collective-permute-done((f32[64,768]{1,0:T(8,128)S(1)}, f32[64,768]{1,0:T(8,128)S(1)}, u32[]{:S(2)}, u32[]{:S(2)}) %collective-permute-start.1) | collective-permute-done | bytes 196640 | tf_op jit(solution)/shard_map/ppermute | solution.py:202
  13.1 0.7 %fusion.21 = (f32[64,384]{1,0:T(8,128)S(1)}, f32[64,384]{1,0:T(8,128)}, f32[64,384]{1,0:T(8,128)S(1)}) fusion(f32[64,768]{1,0:T(8,128)S(1)} %add.21, f32[64,768]{1,0:T(8,128)S(1)} %collective-permute-done.1), kind=kLoop, calls=%fused_computation.48 | loop fusion | flops 24576 | bytes 688128 | tf_op jit(solution)/shard_map/slice | solution.py:292
  13.8 0.2 collective-permute-start.4
  14.0 0.0 collective-permute-done.2.got
  14.0 0.4 shard_map.76
  14.4 1.2 %collective-permute-start.3 = (f32[32,512]{1,0:T(8,128)S(1)}, f32[32,512]{1,0:T(8,128)}, u32[]{:S(2)}, u32[]{:S(2)}) collective-permute-start(f32[32,512]{1,0:T(8,128)S(1)} %get-tuple-element.46), channel_id=1, source_target_pairs={{0,3},{1,2},{2,1},{3,0},{4,7},{5,6},{6,5},{7,4},{8,11},{9,10},{10,... | collective-permute-start | bytes 196616 | tf_op jit(solution)/shard_map/ppermute | solution.py:202
  15.6 0.0 copy-start.1
  15.6 0.0 collective-permute-done.4.other
  15.6 0.4 shard_map.77
  16.0 2.3 %collective-permute-done.3 = f32[32,512]{1,0:T(8,128)} collective-permute-done((f32[32,512]{1,0:T(8,128)S(1)}, f32[32,512]{1,0:T(8,128)}, u32[]{:S(2)}, u32[]{:S(2)}) %collective-permute-start.3) | collective-permute-done | bytes 65568 | tf_op jit(solution)/shard_map/ppermute | solution.py:202
  18.4 0.7 %slice_select_fusion.8 = (f32[32,128]{1,0:T(8,128)S(1)}, f32[32,128]{1,0:T(8,128)S(1)}) fusion(f32[32,512]{1,0:T(8,128)} %collective-permute-done.3, f32[32,512]{1,0:T(8,128)S(1)} %get-tuple-element.46, pred[]{:T(512)S(6)} %eq.13), kind=kLoop, calls=%fused_computation.37 | loop fusion | flops 8192 | bytes 65537 | tf_op jit(solution)/shard_map/jit(_where)/select_n | solution.py:208
  19.1 1.0 %fusion.9 = f32[32,384]{1,0:T(8,128)S(1)} fusion(f32[32,512]{1,0:T(8,128)} %collective-permute-done.3, f32[32,512]{1,0:T(8,128)S(1)} %get-tuple-element.46, f32[256,384]{1,0:T(8,128)S(1)} %shard_map.77, f32[32,128]{1,0:T(8,128)S(1)} %get-tuple-element.59, f32[32,128]{1,0:T(8,128)S(1)} %get-tuple-element.58), kind=kOutput, calls=%fused_computation.16 | convolution fusion | flops 18907136 | bytes 573440 | tf_op jit(solution)/shard_map/dot_general | solution.py:198
  20.1 2.6 %collective-permute-start.6 = (f32[32,384]{1,0:T(8,128)S(1)}, f32[32,384]{1,0:T(8,128)S(1)}, u32[]{:S(2)}, u32[]{:S(2)}) collective-permute-start(f32[32,384]{1,0:T(8,128)S(1)} %fusion.9), channel_id=1, source_target_pairs={{0,5},{1,4},{2,7},{3,6},{4,1},{5,0},{6,3},{7,2},{8,13},{9,12},{10,... | collective-permute-start | bytes 147464 | tf_op jit(solution)/shard_map/ppermute | solution.py:202
  22.7 0.2 fusion
  22.9 0.0 copy-done.1
  22.9 0.1 collective-permute-start.5
  23.1 1.8 %collective-permute-done.6 = f32[32,384]{1,0:T(8,128)S(1)} collective-permute-done((f32[32,384]{1,0:T(8,128)S(1)}, f32[32,384]{1,0:T(8,128)S(1)}, u32[]{:S(2)}, u32[]{:S(2)}) %collective-permute-start.6) | collective-permute-done | bytes 49184 | tf_op jit(solution)/shard_map/ppermute | solution.py:202
  24.9 0.2 fusion.2
  25.1 5.5 %collective-permute-done.5 = f32[64,384]{1,0:T(8,128)S(1)} collective-permute-done((f32[64,384]{1,0:T(8,128)S(1)}, f32[64,384]{1,0:T(8,128)S(1)}, u32[]{:S(2)}, u32[]{:S(2)}) %collective-permute-start.5) | collective-permute-done | bytes 98336 | tf_op jit(solution)/shard_map/ppermute | solution.py:202
  30.6 0.4 %collective-permute-start.7 = (f32[128,256]{1,0:T(8,128)S(1)}, f32[128,256]{1,0:T(8,128)S(1)}, u32[]{:S(2)}, u32[]{:S(2)}) collective-permute-start(f32[128,256]{1,0:T(8,128)S(1)} %pad_maximum_fusion.1.mine), channel_id=1, source_target_pairs={{0,1},{1,0},{2,3},{3,2},{4,5},{5,4},{6,7},{7,6},{8,9},{9,8},{10,11... | collective-permute-start | bytes 393224 | tf_op jit(solution)/shard_map/ppermute | solution.py:202
  31.0 1.0 %collective-permute-done.7.other = f32[128,256]{1,0:T(8,128)S(1)} collective-permute-done((f32[128,256]{1,0:T(8,128)S(1)}, f32[128,256]{1,0:T(8,128)S(1)}, u32[]{:S(2)}, u32[]{:S(2)}) %collective-permute-start.7) | collective-permute-done | bytes 131104 | tf_op jit(solution)/shard_map/ppermute | solution.py:202
  32.0 0.3 shard_map.78
  32.3 0.2 fusion.10
  32.5 1.5 %collective-permute-start.10 = (f32[64,128]{1,0:T(8,128)S(1)}, f32[64,128]{1,0:T(8,128)S(1)}, u32[]{:S(2)}, u32[]{:S(2)}) collective-permute-start(f32[64,128]{1,0:T(8,128)S(1)} %slice_add_fusion.3), channel_id=1, source_target_pairs={{0,9},{1,8},{2,11},{3,10},{4,13},{5,12},{6,15},{7,14},{8,1},{9,0},... | collective-permute-start | bytes 98312 | tf_op jit(solution)/shard_map/ppermute | solution.py:202
  34.0 0.3 collective-permute-start.8
  34.3 1.6 %collective-permute-done.10 = f32[64,128]{1,0:T(8,128)S(1)} collective-permute-done((f32[64,128]{1,0:T(8,128)S(1)}, f32[64,128]{1,0:T(8,128)S(1)}, u32[]{:S(2)}, u32[]{:S(2)}) %collective-permute-start.10) | collective-permute-done | bytes 32800 | tf_op jit(solution)/shard_map/ppermute | solution.py:202
  35.9 0.3 collective-permute-start.11
  36.3 1.1 %collective-permute-done.8 = f32[32,256]{1,0:T(8,128)S(1)} collective-permute-done((f32[32,256]{1,0:T(8,128)S(1)}, f32[32,256]{1,0:T(8,128)S(1)}, u32[]{:S(2)}, u32[]{:S(2)}) %collective-permute-start.8) | collective-permute-done | bytes 32800 | tf_op jit(solution)/shard_map/ppermute | solution.py:202
  37.4 0.2 fusion.4
  37.6 0.0 collective-permute-done.11.other
  37.6 0.3 shard_map.80
  37.9 0.2 fusion.14
  38.1 1.4 %collective-permute-start.12 = (f32[32,128]{1,0:T(8,128)S(1)}, f32[32,128]{1,0:T(8,128)S(1)}, u32[]{:S(2)}, u32[]{:S(2)}) collective-permute-start(f32[32,128]{1,0:T(8,128)S(1)} %fusion.14), channel_id=1, source_target_pairs={{0,17},{1,16},{2,19},{3,18},{4,21},{5,20},{6,23},{7,22},{8,25},{9,... | collective-permute-start | bytes 49160 | tf_op jit(solution)/shard_map/ppermute | solution.py:202
  39.5 0.4 collective-permute-start.9
  39.9 1.4 %collective-permute-done.12 = f32[32,128]{1,0:T(8,128)S(1)} collective-permute-done((f32[32,128]{1,0:T(8,128)S(1)}, f32[32,128]{1,0:T(8,128)S(1)}, u32[]{:S(2)}, u32[]{:S(2)}) %collective-permute-start.12) | collective-permute-done | bytes 16416 | tf_op jit(solution)/shard_map/ppermute | solution.py:202
  41.3 0.2 collective-permute-start.13
  41.6 0.0 collective-permute-done.9.other
  41.6 0.7 %shard_map.79 = (f32[64,512]{1,0:T(8,128)S(1)}, f32[256,512]{1,0:T(8,128)S(1)}) custom-call(f32[64,512]{1,0:T(8,128)S(1)} %get-tuple-element.42.current, f32[32,512]{1,0:T(8,128)S(1)} %get-tuple-element.65.mine, f32[32,512]{1,0:T(8,128)S(1)} %collective-permute-done.9.other, f32[512,640]{1,0:T(8,128)S(1)} %get-tuple-element.32.left, ...), custom_call_target="tpu_custom_call" | custom-call | tf_op jit(solution)/shard_map/pallas_call | solution.py:183
  42.3 0.3 collective-permute-done.13.other
  42.6 0.9 %shard_map.81 = f32[64,512]{1,0:T(8,128)} custom-call(f32[64,512]{1,0:T(8,128)S(1)} %get-tuple-element.52.current, f32[32,256]{1,0:T(8,128)S(1)} %pad_maximum_fusion.8.mine, f32[32,256]{1,0:T(8,128)S(1)} %collective-permute-done.13.other, f32[256,512]{1,0:T(8,128)S(1)} %get-tuple-element.54.factor), custom_call_target="tpu_custom_call" | custom-call | tf_op jit(solution)/shard_map/pallas_call | solution.py:183
  (15 shorter events, 0.1 us)
Async XLA Ops:
  0.0 4.0 %copy-start = (s32[512]{0:T(512)S(1)}, s32[512]{0:T(512)}, u32[]{:S(2)}) copy-start(s32[512]{0:T(512)} %param.8) | copy-start | bytes 6148
  2.8 2.2 %collective-permute-start = (f32[64,768]{1,0:T(8,128)S(1)}, f32[64,768]{1,0:T(8,128)S(1)}, u32[]{:S(2)}, u32[]{:S(2)}) collective-permute-start(f32[64,768]{1,0:T(8,128)S(1)} %get-tuple-element.36), channel_id=1, source_target_pairs={{0,1},{1,0},{2,3},{3,2},{4,5},{5,4},{6,7},{7,6},{8,9},{9,8},{10,11... | collective-permute-start | bytes 589832 | tf_op jit(solution)/shard_map/ppermute | solution.py:202
  5.1 8.0 %collective-permute-start.1 = (f32[64,768]{1,0:T(8,128)S(1)}, f32[64,768]{1,0:T(8,128)S(1)}, u32[]{:S(2)}, u32[]{:S(2)}) collective-permute-start(f32[64,768]{1,0:T(8,128)S(1)} %add.21), channel_id=1, source_target_pairs={{0,3},{1,2},{2,1},{3,0},{4,7},{5,6},{6,5},{7,4},{8,11},{9,10},{10,... | collective-permute-start | bytes 589832 | tf_op jit(solution)/shard_map/ppermute | solution.py:202
  8.8 5.1 %collective-permute-start.2 = (f32[32,2688]{1,0:T(8,128)S(1)}, f32[32,2688]{1,0:T(8,128)S(1)}, u32[]{:S(2)}, u32[]{:S(2)}) collective-permute-start(f32[32,2688]{1,0:T(8,128)S(1)} %get-tuple-element.45), channel_id=1, source_target_pairs={{0,1},{1,0},{2,3},{3,2},{4,5},{5,4},{6,7},{7,6},{8,9},{9,8},{10,11... | collective-permute-start | bytes 1032200 | tf_op jit(solution)/shard_map/ppermute | solution.py:202
  13.8 1.8 %collective-permute-start.4 = (f32[128,384]{1,0:T(8,128)S(1)}, f32[128,384]{1,0:T(8,128)S(1)}, u32[]{:S(2)}, u32[]{:S(2)}) collective-permute-start(f32[128,384]{1,0:T(8,128)S(1)} %pad_maximum_fusion.mine), channel_id=1, source_target_pairs={{0,1},{1,0},{2,3},{3,2},{4,5},{5,4},{6,7},{7,6},{8,9},{9,8},{10,11... | collective-permute-start | bytes 589832 | tf_op jit(solution)/shard_map/ppermute | solution.py:202
  14.4 4.0 %collective-permute-start.3 = (f32[32,512]{1,0:T(8,128)S(1)}, f32[32,512]{1,0:T(8,128)}, u32[]{:S(2)}, u32[]{:S(2)}) collective-permute-start(f32[32,512]{1,0:T(8,128)S(1)} %get-tuple-element.46), channel_id=1, source_target_pairs={{0,3},{1,2},{2,1},{3,0},{4,7},{5,6},{6,5},{7,4},{8,11},{9,10},{10,... | collective-permute-start | bytes 196616 | tf_op jit(solution)/shard_map/ppermute | solution.py:202
  15.6 7.3 %copy-start.1 = (f32[64,384]{1,0:T(8,128)S(1)}, f32[64,384]{1,0:T(8,128)}, u32[]{:S(2)}) copy-start(f32[64,384]{1,0:T(8,128)} %get-tuple-element.47) | copy-start | bytes 294916
  20.1 4.8 %collective-permute-start.6 = (f32[32,384]{1,0:T(8,128)S(1)}, f32[32,384]{1,0:T(8,128)S(1)}, u32[]{:S(2)}, u32[]{:S(2)}) collective-permute-start(f32[32,384]{1,0:T(8,128)S(1)} %fusion.9), channel_id=1, source_target_pairs={{0,5},{1,4},{2,7},{3,6},{4,1},{5,0},{6,3},{7,2},{8,13},{9,12},{10,... | collective-permute-start | bytes 147464 | tf_op jit(solution)/shard_map/ppermute | solution.py:202
  22.9 7.6 %collective-permute-start.5 = (f32[64,384]{1,0:T(8,128)S(1)}, f32[64,384]{1,0:T(8,128)S(1)}, u32[]{:S(2)}, u32[]{:S(2)}) collective-permute-start(f32[64,384]{1,0:T(8,128)S(1)} %copy-done.1), channel_id=1, source_target_pairs={{0,5},{1,4},{2,7},{3,6},{4,1},{5,0},{6,3},{7,2},{8,13},{9,12},{10,... | collective-permute-start | bytes 294920 | tf_op jit(solution)/shard_map/ppermute | solution.py:202
  30.6 1.4 %collective-permute-start.7 = (f32[128,256]{1,0:T(8,128)S(1)}, f32[128,256]{1,0:T(8,128)S(1)}, u32[]{:S(2)}, u32[]{:S(2)}) collective-permute-start(f32[128,256]{1,0:T(8,128)S(1)} %pad_maximum_fusion.1.mine), channel_id=1, source_target_pairs={{0,1},{1,0},{2,3},{3,2},{4,5},{5,4},{6,7},{7,6},{8,9},{9,8},{10,11... | collective-permute-start | bytes 393224 | tf_op jit(solution)/shard_map/ppermute | solution.py:202
  32.5 3.4 %collective-permute-start.10 = (f32[64,128]{1,0:T(8,128)S(1)}, f32[64,128]{1,0:T(8,128)S(1)}, u32[]{:S(2)}, u32[]{:S(2)}) collective-permute-start(f32[64,128]{1,0:T(8,128)S(1)} %slice_add_fusion.3), channel_id=1, source_target_pairs={{0,9},{1,8},{2,11},{3,10},{4,13},{5,12},{6,15},{7,14},{8,1},{9,0},... | collective-permute-start | bytes 98312 | tf_op jit(solution)/shard_map/ppermute | solution.py:202
  34.0 3.3 %collective-permute-start.8 = (f32[32,256]{1,0:T(8,128)S(1)}, f32[32,256]{1,0:T(8,128)S(1)}, u32[]{:S(2)}, u32[]{:S(2)}) collective-permute-start(f32[32,256]{1,0:T(8,128)S(1)} %fusion.10), channel_id=1, source_target_pairs={{0,9},{1,8},{2,11},{3,10},{4,13},{5,12},{6,15},{7,14},{8,1},{9,0},... | collective-permute-start | bytes 98312 | tf_op jit(solution)/shard_map/ppermute | solution.py:202
  35.9 1.7 %collective-permute-start.11 = (f32[128,128]{1,0:T(8,128)S(1)}, f32[128,128]{1,0:T(8,128)S(1)}, u32[]{:S(2)}, u32[]{:S(2)}) collective-permute-start(f32[128,128]{1,0:T(8,128)S(1)} %constant_dynamic-update-slice_fusion.mine), channel_id=1, source_target_pairs={{0,1},{1,0},{2,3},{3,2},{4,5},{5,4},{6,7},{7,6},{8,9},{9,8},{10,11... | collective-permute-start | bytes 196616 | tf_op jit(solution)/shard_map/ppermute | solution.py:202
  38.1 3.2 %collective-permute-start.12 = (f32[32,128]{1,0:T(8,128)S(1)}, f32[32,128]{1,0:T(8,128)S(1)}, u32[]{:S(2)}, u32[]{:S(2)}) collective-permute-start(f32[32,128]{1,0:T(8,128)S(1)} %fusion.14), channel_id=1, source_target_pairs={{0,17},{1,16},{2,19},{3,18},{4,21},{5,20},{6,23},{7,22},{8,25},{9,... | collective-permute-start | bytes 49160 | tf_op jit(solution)/shard_map/ppermute | solution.py:202
  39.5 2.0 %collective-permute-start.9 = (f32[32,512]{1,0:T(8,128)S(1)}, f32[32,512]{1,0:T(8,128)S(1)}, u32[]{:S(2)}, u32[]{:S(2)}) collective-permute-start(f32[32,512]{1,0:T(8,128)S(1)} %get-tuple-element.64), channel_id=1, source_target_pairs={{0,1},{1,0},{2,3},{3,2},{4,5},{5,4},{6,7},{7,6},{8,9},{9,8},{10,11... | collective-permute-start | bytes 196616 | tf_op jit(solution)/shard_map/ppermute | solution.py:202
  41.3 1.3 %collective-permute-start.13 = (f32[32,256]{1,0:T(8,128)S(1)}, f32[32,256]{1,0:T(8,128)S(1)}, u32[]{:S(2)}, u32[]{:S(2)}) collective-permute-start(f32[32,256]{1,0:T(8,128)S(1)} %pad_maximum_fusion.8.mine), channel_id=1, source_target_pairs={{0,1},{1,0},{2,3},{3,2},{4,5},{5,4},{6,7},{7,6},{8,9},{9,8},{10,11... | collective-permute-start | bytes 98312 | tf_op jit(solution)/shard_map/ppermute | solution.py:202

commit v5 on v4

--- a/solution.py
+++ b/solution.py
@@ -12,6 +12,7 @@
 NN = (((1,), (0,)), ((), ()))
 NT = (((1,), (1,)), ((), ()))
 TN = (((0,), (0,)), ((), ()))
+ANY = pl.BlockSpec(memory_space=pl.ANY)
 HBM = pl.BlockSpec(memory_space=pltpu.HBM)
 VMEM = pl.BlockSpec(memory_space=pltpu.VMEM)
 SMEM = pl.BlockSpec(memory_space=pltpu.SMEM)
@@ -45,7 +46,7 @@
 
 
 def gram_kernel(
-    top, left, right, coupling, rhs, leaf, low_keep, low_send, left_v, right_v, left_top, right_top,
+    top, left, right, coupling, rhs, leaf, low_keep, send, gram_next, left_v, right_v, left_top, right_top,
     coupling_v, rhs_v, leaf_v, sems,
 ):
     rank = left.shape[2]
@@ -74,12 +75,17 @@
     for copy in used:
         copy.wait()
     half = parity_of(lax.axis_index(AXES), top) == 1
-    at = 0
     for k in range(top - 2, 0, -1):
         w = k * rank
         value = dot(left_v[:, cols(k)], right_v[:, :w], TN)
+        if k == top - 2:
+            gram_next[...] = value
+            send[:, :w] = value[:n]
+            send[:, w : 2 * w] = value[n:]
+            at, skip = 0, 2 * w
+            continue
         low_keep[:, at : at + w] = jnp.where(half, value[n:], value[:n])
-        low_send[:, at : at + w] = jnp.where(half, value[:n], value[n:])
+        send[:, skip + at : skip + at + w] = jnp.where(half, value[:n], value[n:])
         at += w
     for copy in rest:
         copy.wait()
@@ -102,7 +108,7 @@
 
 
 def local_kernel(
-    top, split, first, left_top, right_top, right, coupling, gram_top, current_out, keep, send
+    top, split, first, left_top, right_top, right, coupling, gram_top, _, current_out, keep, send
 ):
     rank = left_top.shape[1]
     count, size = first.shape
@@ -127,7 +133,7 @@
         at += (top - 1) * rank
 
 
-def top_kernel(top, keep, got, gram_top, coupling, sums, z_mine, z_other, pair):
+def top_kernel(top, keep, got, gram_top, coupling, sums, next_sums, z_mine, z_other, pair):
     n, rank = keep.shape[0], gram_top.shape[0]
     w = (top - 1) * rank
     right = lax.axis_index(AXES) & 1
@@ -143,20 +149,56 @@
         [jnp.where(is_right, other, mine), jnp.where(is_right, mine, other)], axis=1
     )
     z = dot(both, coupling[top - 1])
-    sums[...] = keep[:, :w] + got[:, :w] - dot(z, pair[...])
+    value = keep[:, :w] + got[:, :w] - dot(z, pair[...])
+    sums[...] = value[:, : w - rank]
+    next_sums[...] = value[:, w - rank :]
     z_mine[...] = jnp.where(is_right, z[:, rank:], z[:, :rank])
     z_other[...] = jnp.where(is_right, z[:, :rank], z[:, rank:])
 
 
-def pair_kernel(top, bit, mine, other, coupling, d_out, pair):
-    n, rank = mine.shape[0] // 2, mine.shape[0]
+def next_kernel(top, mine, got, sums, gram_next, got_gram, coupling, z_out, sums_out):
+    rank, w = gram_next.shape
+    n = rank // 2
+    right = (lax.axis_index(AXES) >> 1) & 1 == 1
+    both = jnp.concatenate(
+        [jnp.where(right, got[...], mine[...]), jnp.where(right, mine[...], got[...])], axis=1
+    )
+    k = top - 2
+    z = dot(both, jnp.where(right, coupling[k, :, rank:], coupling[k, :, :rank]))
+    gram = gram_next[...] + jnp.concatenate([got_gram[:, :w], got_gram[:, w : 2 * w]], axis=0)
+    z_out[...] = z
+    sums_out[...] = sums[...] - dot(z, gram)
+
+
+def merge_kernel(low, got, _, mine):
+    n, w = low.shape[0], mine.shape[1]
+    mine[:n, :] = low[:, :w]
+    mine[n:, :] = got[:, :w]
+
+
+def pair_kernel(top, bit, low, got, other, coupling, d_out, *rest):
+    (n, rank), w = (low.shape[0], 2 * low.shape[0]), d_out.shape[1]
+    pair = rest[-1]
     device_id = lax.axis_index(AXES)
     half = parity_of(device_id, top)
     right = (device_id >> bit) & 1
-    for child, rows in ((right, slice(0, n)), (1 - right, slice(n, 2 * n))):
-        pair[pl.ds(pl.multiple_of(child * rank + half * n, n), n), :] = mine[rows, :]
+    for child, value, rows in ((right, low, slice(0, n)), (1 - right, got, slice(n, 2 * n))):
+        pair[pl.ds(pl.multiple_of(child * rank + half * n, n), n), :] = value[:, :w]
         pair[pl.ds(pl.multiple_of(child * rank + (1 - half) * n, n), n), :] = other[rows, :]
     d_out[...] = dot(coupling[top - 1 - bit], pair[...])
+    if len(rest) > 1:
+        rest[0][...] = low[:, w:] + got[:, w:]
+
+
+def sums_kernel(bit, sums, got, factor, both, out):
+    w = out.shape[1]
+    on_right = (lax.axis_index(AXES) >> bit) & 1 == 1
+    own, other = sums[:, w:], got[:, w:]
+    pair = jnp.concatenate(
+        [jnp.where(on_right, other, own), jnp.where(on_right, own, other)], axis=1
+    )
+    both[...] = pair
+    out[...] = sums[:, :w] + got[:, :w] - dot(pair, factor[...])
 
 
 def joined(mine, other, top):
@@ -166,13 +208,21 @@
     )
 
 
-def early_kernel(top, current, mine, other, left, coupling, out, factor):
+def early_kernel(top, current, *refs):
+    left, coupling, out, factor = refs[-4:]
     rank = left.shape[1] // top
-    z = joined(mine[...], other[...], top)
-    out[...] = current[...] - dot(z, left[:, rank:], NT)
-    right = (lax.axis_index(AXES) >> (top - 1)) & 1 == 1
-    side = jnp.where(right, coupling[0, :, rank:], coupling[0, :, :rank])
-    factor[...] = dot(side, left[:, :rank], NT)
+    device_id = lax.axis_index(AXES)
+
+    def side(k):
+        right = (device_id >> (top - 1 - k)) & 1 == 1
+        return jnp.where(right, coupling[k, :, rank:], coupling[k, :, :rank])
+
+    z = []
+    for k in range(1, top):
+        pair = joined(refs[2 * k - 2][...], refs[2 * k - 1][...], top)
+        z.append(pair if k >= top - 2 else dot(pair, side(k)))
+    out[...] = current[...] - dot(jnp.concatenate(z, axis=1), left[:, rank:], NT)
+    factor[...] = dot(side(0), left[:, :rank], NT)
 
 
 def last_kernel(top, current, mine, other, factor, out):
@@ -186,6 +236,7 @@
         in_specs=in_specs,
         out_specs=out_specs,
         scratch_shapes=scratch,
+        cost_estimate=pl.CostEstimate(flops=1, bytes_accessed=1, transcendentals=0),
         compiler_params=pltpu.CompilerParams(vmem_limit_bytes=LIMIT),
     )(*args)
 
@@ -194,20 +245,8 @@
     return jax.ShapeDtypeStruct(dims, F32)
 
 
-def xdot(a, b):
-    return jnp.dot(a, b, precision=lax.Precision.HIGH, preferred_element_type=F32)
-
-
 def exchange(value, mask):
     return lax.ppermute(value, AXES, [(i, i ^ mask) for i in range(lax.axis_size(AXES))])
-
-
-def level_sums(sums, got, k, rank, on_right):
-    own, other = sums[:, k * rank :], got[:, k * rank :]
-    both = jnp.concatenate(
-        [jnp.where(on_right, other, own), jnp.where(on_right, own, other)], axis=1
-    )
-    return both, lambda z: jnp.where(on_right, z[:, rank:], z[:, :rank])
 
 
 def per_device(right_side, order, leaf_split, leaf_inverse, basis_left, basis_right, coupling):
@@ -217,14 +256,16 @@
     top = levels - 1
     n = rank // 2
     device_id = lax.axis_index(AXES)
-    low_w = rank * (top - 1) * (top - 2) // 2
+    low_w = rank * (top - 2) * (top - 3) // 2
+    next_w = (top - 2) * rank
     wide = top * rank
     rows = count // 2
-    low_keep, low_send, left, right, left_top, right_top, coup, rhs, leaf = call(
+    low_keep, send, gram_next, left, right, left_top, right_top, coup, rhs, leaf = call(
         functools.partial(gram_kernel, top),
         [
             shape(n, low_w),
-            shape(n, low_w),
+            shape(n, 2 * next_w + low_w),
+            shape(rank, next_w),
             shape(size, wide),
             shape(size, wide),
             shape(size, rank),
@@ -234,14 +275,14 @@
             shape(size, size),
         ],
         [HBM] * 5,
-        [VMEM] * 9,
+        [VMEM] * 10,
         [pltpu.SemaphoreType.DMA((4, max(5, top)))],
         *[
             pltpu.with_memory_space_constraint(x, pltpu.HBM)
             for x in (basis_left, basis_right, coupling, right_side, leaf_inverse)
         ],
     )
-    got_low = exchange(low_send, 1)
+    got_gram = exchange(send, 1)
     current, gram_top = call(
         functools.partial(leaf_kernel, top),
         [shape(count, size), shape(rank, wide - rank)],
@@ -255,12 +296,11 @@
         left,
         right,
     )
-    low = low_keep + got_low
-    current, low = lax.optimization_barrier((current, low))
+    low = low_keep + got_gram[:, 2 * next_w :]
     current, keep, send = call(
         functools.partial(local_kernel, top),
         [shape(count, size), shape(rows, wide), shape(rows, wide + rank // rows * (wide - rank))],
-        [SMEM] + [VMEM] * 6,
+        [SMEM] + [VMEM] * 6 + [ANY],
         [VMEM] * 3,
         [],
         leaf_split,
@@ -270,61 +310,93 @@
         right,
         coup,
         gram_top,
+        low,
     )
     got = exchange(send, 1)
-    sums, z_mine, z_other = call(
+    sums, next_sums, z_mine, z_other = call(
         functools.partial(top_kernel, top),
-        [shape(rows, wide - rank), shape(rows, rank), shape(rows, rank)],
+        [shape(rows, next_w), shape(rows, rank), shape(rows, rank), shape(rows, rank)],
         [VMEM] * 4,
-        [VMEM] * 3,
+        [VMEM] * 4,
         [pltpu.VMEM((2 * rank, wide - rank), F32)],
         keep,
         got,
         gram_top,
         coup,
     )
-    z_mine, z_other = [z_mine], [z_other]
-    for k in range(top - 2, 0, -1):
+    known = {top - 1: (z_mine, z_other)}
+    got_low = exchange(low, 3)
+    z, sums = call(
+        functools.partial(next_kernel, top),
+        [shape(rows, rank), shape(rows, next_w)],
+        [VMEM] * 6,
+        [VMEM] * 2,
+        [],
+        next_sums,
+        exchange(next_sums, 3),
+        sums,
+        gram_next,
+        got_gram,
+        coup,
+    )
+    known[top - 2] = (z, z)
+    sums = sums + exchange(sums, 3)
+    low = low + got_low
+    for k in range(top - 3, 0, -1):
         bit = top - 1 - k
         w = k * rank
+        got_sums = exchange(sums, 1 << bit | 1)
         got_low = exchange(low, 1 << bit | 1)
-        got_sums = exchange(sums, 1 << bit | 1)
-        mine = jnp.concatenate([low[:, :w], got_low[:, :w]], axis=0)
-        other = exchange(mine, 1)
-        factor = call(
+        mine = call(
+            merge_kernel, shape(rank, w), [VMEM, VMEM, ANY], VMEM, [], low, got_low, got_sums
+        )
+        outs = [shape(2 * rank, w), shape(n, low.shape[1] - w)][: 2 if k > 1 else 1]
+        factor, *low = call(
             functools.partial(pair_kernel, top, bit),
-            shape(2 * rank, w),
-            [VMEM] * 3,
-            VMEM,
+            outs,
+            [VMEM] * 4,
+            [VMEM] * len(outs),
             [pltpu.VMEM((2 * rank, w), F32)],
-            mine,
-            other,
+            low,
+            got_low,
+            exchange(mine, 1),
             coup,
         )
-        next_low = low[:, w:] + got_low[:, w:]
-        both, side = level_sums(sums, got_sums, k, rank, (device_id >> bit) & 1 == 1)
-        z = xdot(both, coup[k])
-        z_mine.append(side(z))
-        z_other.append(z_mine[-1])
-        sums = sums[:, :w] + got_sums[:, :w] - xdot(both, factor)
-        if k > 1:
-            low, sums = lax.optimization_barrier((next_low, sums))
+        low = low[0] if low else None
+        both, sums = call(
+            functools.partial(sums_kernel, bit),
+            [shape(rows, 2 * rank), shape(rows, w)],
+            [VMEM] * 3,
+            [VMEM] * 2,
+            [],
+            sums,
+            got_sums,
+            factor,
+        )
+        known[k] = (both, both)
     got_sums = exchange(sums, 1 << (top - 1) | 1)
-    mine = jnp.concatenate(z_mine[::-1], axis=1)
-    other = exchange(jnp.concatenate(z_other[::-1], axis=1), 1)
+    names = range(1, top)
+    others = exchange(jnp.concatenate([known[k][1] for k in names], axis=1), 1)
+    args, at = [], 0
+    for k in names:
+        mine = known[k][0]
+        args += [mine, others[:, at : at + mine.shape[1]]]
+        at += mine.shape[1]
     current, factor = call(
         functools.partial(early_kernel, top),
         [shape(count, size), shape(2 * rank, size)],
-        [VMEM] * 5,
+        [VMEM] * (3 + len(args)),
         [VMEM] * 2,
         [],
         current,
-        mine,
-        other,
+        *args,
         left,
         coup,
     )
-    both, _ = level_sums(sums, got_sums, 0, rank, (device_id >> (top - 1)) & 1 == 1)
+    on_right = (device_id >> (top - 1)) & 1 == 1
+    both = jnp.concatenate(
+        [jnp.where(on_right, got_sums, sums), jnp.where(on_right, sums, got_sums)], axis=1
+    )
     return call(
         functools.partial(last_kernel, top),
         shape(count, size),

time: 43.7 us -> 38.2 us (0.87)
  waiting for transfers between devices: 19.2 us -> 12.8 us
  starting transfers between devices: 12.2 us -> 16.2 us
  matrix products: 1.96 us -> 0 us
  other arithmetic: 1.48 us -> 0.05 us
    ppermute x14, waiting for transfers between devices: 19.2 us -> 12.8 us  [exchange(): lax.ppermute(value, AXES, [(i, i ^ mask) for i in range(lax.axis_size(AXE...]
    ppermute x14, starting transfers between devices: 12.2 us -> 16.2 us  [exchange(): lax.ppermute(value, AXES, [(i, i ^ mask) for i in range(lax.axis_size(AXE...]
    dot_general x6 -> x0, matrix products: 1.96 us -> none  [xdot(): jnp.dot(a, b, precision=lax.Precision.HIGH, preferred_element_type=F32)]
    select_n x6 -> x1, other arithmetic: 0.75 us -> 0.01 us  [per_device(): jnp.where(on_right, got_sums, sums)]
    slice x1 -> x0, other arithmetic: 0.66 us -> none  [per_device(): mine = jnp.concatenate([low[:, :w], got_low[:, :w]], axis=0)]
    pallas_call x9 -> x13, Pallas kernels: 7.83 us -> 8.15 us  [call(): pl.pallas_call(kernel, out_shape=outs, in_specs=in_specs, out_specs=out_s...]
  transfers between devices with their start and end apart: 14 -> 14, of which waited for: 9 -> 10; matrix products, arithmetic and copies ran while one was open for 3% -> 0% of each run, Pallas kernels for 8% -> 6%
where the time goes in v5:
time: 38.2 us; the launch traced here: 38 us
  starting transfers between devices  16.2 us (42%)
  waiting for transfers between devices  12.8 us (34%)
  Pallas kernels  8.15 us (21%)
  between operations  0.77 us (2%)
    ppermute x14, starting transfers between devices, exchange(): lax.ppermute(value, AXES, [(i, i ^ mask) for i in range(lax.axis_size(AXE...  16.2 us
    ppermute x14, waiting for transfers between devices, exchange(): lax.ppermute(value, AXES, [(i, i ^ mask) for i in range(lax.axis_size(AXE...  12.8 us
    pallas_call x13, Pallas kernels, call(): pl.pallas_call(kernel, out_shape=outs, in_specs=in_specs, out_specs=out_s...  8.15 us
  transfers between devices with their start and end apart: 14, of which 10 were waited for; matrix products, arithmetic and copies ran while one was open for 0% of the time, Pallas kernels for 6%

profile of v5, /device:TPU:0, one launch (start us, length us, event | category | flops | bytes accessed | tf_op | source)
XLA Modules:
  0.0 38.0 jit_solution(16204583919513850409)
XLA Ops:
  0.0 0.0 copy-start
  0.0 2.8 %shard_map.73 = (f32[64,384]{1,0:T(8,128)S(1)}, f32[64,1152]{1,0:T(8,128)S(1)}, f32[128,384]{1,0:T(8,128)S(1)}, f32[512,640]{1,0:T(8,128)S(1)}, f32[512,640]{1,0...) custom-call(f32[6,512,128]{2,1,0:T(8,128)} %left.1, ...), custom_call_target="tpu_custom_call" | custom-call | flops 1 | bytes 1 | tf_op jit(solution)/shard_map/pallas_call | solution.py:233
  2.8 0.5 %collective-permute-start = (f32[64,1152]{1,0:T(8,128)S(1)}, f32[64,1152]{1,0:T(8,128)S(1)}, u32[]{:S(2)}, u32[]{:S(2)}) collective-permute-start(f32[64,1152]{1,0:T(8,128)S(1)} %get-tuple-element.44), channel_id=1, source_target_pairs={{0,1},{1,0},{2,3},{3,2},{4,5},{5,4},{6,7},{7,6},{8,9},{9,8},{10,11... | collective-permute-start | bytes 884744 | tf_op jit(solution)/shard_map/ppermute | solution.py:249
  4.0 0.0 copy-done
  4.0 1.0 %shard_map.74 = (f32[64,512]{1,0:T(8,128)S(1)}, f32[128,512]{1,0:T(8,128)S(1)}) custom-call(s32[1,512]{1,0:T(1,128)S(1)} %bitcast.1, s32[1]{0:T(128)S(6)} %copy.8.split, f32[64,512]{1,0:T(8,128)S(1)} %get-tuple-element.34.rhs, f32[512,512]{1,0:T(8,128)S(1)} %get-tuple-element.35.leaf, f32[512,640]{1,0:T(8,128)S(1)} %get-tuple-element.36.left.refs_8_, ...), custom_call_target="tpu_custom_call" | custom-call | flops 1 | bytes 1 | tf_op jit(solution)/shard_map/pallas_call | solution.py:233
  5.1 0.0 collective-permute-done.got_gram
  5.1 1.0 %shard_map.75 = (f32[64,512]{1,0:T(8,128)S(1)}, f32[32,640]{1,0:T(8,128)S(1)}, f32[32,2688]{1,0:T(8,128)S(1)}) custom-call(s32[1]{0:T(128)S(6)} %copy.8.split, f32[64,512]{1,0:T(8,128)S(1)} %get-tuple-element.38.first, f32[512,128]{1,0:T(8,128)S(1)} %get-tuple-element.39.left_top, f32[512,128]{1,0:T(8,128)S(1)} %get-tuple-element.40.right_top, ...), custom_call_target="tpu_custom_call" | custom-call | flops 1 | bytes 1 | tf_op jit(solution)/shard_map/pallas_call | solution.py:233
  6.1 0.1 collective-permute-start.1
  6.2 2.7 %collective-permute-start.5 = (f32[64,384]{1,0:T(8,128)S(1)}, f32[64,384]{1,0:T(8,128)S(1)}, u32[]{:S(2)}, u32[]{:S(2)}) collective-permute-start(f32[64,384]{1,0:T(8,128)S(1)} %slice_add_fusion._), channel_id=1, source_target_pairs={{0,3},{1,2},{2,1},{3,0},{4,7},{5,6},{6,5},{7,4},{8,11},{9,10},{10,... | collective-permute-start | bytes 294920 | tf_op jit(solution)/shard_map/ppermute | solution.py:249
  8.9 0.0 collective-permute-done.1.got
  8.9 0.4 %shard_map.76 = (f32[32,384]{1,0:T(8,128)S(1)}, f32[32,128]{1,0:T(8,128)S(1)}, f32[32,128]{1,0:T(8,128)S(1)}, f32[32,128]{1,0:T(8,128)S(1)}) custom-call(f32[32,640]{1,0:T(8,128)S(1)} %get-tuple-element.46.keep, f32[32,2688]{1,0:T(8,128)S(1)} %collective-permute-done.1.got, f32[128,512]{1,0:T(8,128)S(1)} %get-tuple-element.42.gram_top, ...), custom_call_target="tpu_custom_call" | custom-call | flops 1 | bytes 1 | tf_op jit(solution)/shard_map/pallas_call | solution.py:233
  9.3 1.6 %collective-permute-start.2 = (f32[32,128]{1,0:T(8,128)S(1)}, f32[32,128]{1,0:T(8,128)S(1)}, u32[]{:S(2)}, u32[]{:S(2)}) collective-permute-start(f32[32,128]{1,0:T(8,128)S(1)} %get-tuple-element.48.mine), channel_id=1, source_target_pairs={{0,3},{1,2},{2,1},{3,0},{4,7},{5,6},{6,5},{7,4},{8,11},{9,10},{10,... | collective-permute-start | bytes 49160 | tf_op jit(solution)/shard_map/ppermute | solution.py:249
  10.9 1.1 %collective-permute-done.5 = f32[64,384]{1,0:T(8,128)S(1)} collective-permute-done((f32[64,384]{1,0:T(8,128)S(1)}, f32[64,384]{1,0:T(8,128)S(1)}, u32[]{:S(2)}, u32[]{:S(2)}) %collective-permute-start.5) | collective-permute-done | bytes 98336 | tf_op jit(solution)/shard_map/ppermute | solution.py:249
  12.0 0.5 %collective-permute-done.2.got = f32[32,128]{1,0:T(8,128)S(1)} collective-permute-done((f32[32,128]{1,0:T(8,128)S(1)}, f32[32,128]{1,0:T(8,128)S(1)}, u32[]{:S(2)}, u32[]{:S(2)}) %collective-permute-start.2) | collective-permute-done | bytes 16416 | tf_op jit(solution)/shard_map/ppermute | solution.py:249
  12.5 0.3 shard_map.77
  12.8 1.7 %collective-permute-start.3 = (f32[32,384]{1,0:T(8,128)S(1)}, f32[32,384]{1,0:T(8,128)S(1)}, u32[]{:S(2)}, u32[]{:S(2)}) collective-permute-start(f32[32,384]{1,0:T(8,128)S(1)} %get-tuple-element.51), channel_id=1, source_target_pairs={{0,3},{1,2},{2,1},{3,0},{4,7},{5,6},{6,5},{7,4},{8,11},{9,10},{10,... | collective-permute-start | bytes 147464 | tf_op jit(solution)/shard_map/ppermute | solution.py:249
  14.5 2.6 %collective-permute-start.6 = (f32[64,384]{1,0:T(8,128)S(1)}, f32[64,384]{1,0:T(8,128)S(1)}, u32[]{:S(2)}, u32[]{:S(2)}) collective-permute-start(f32[64,384]{1,0:T(8,128)S(1)} %add.14.low), channel_id=1, source_target_pairs={{0,5},{1,4},{2,7},{3,6},{4,1},{5,0},{6,3},{7,2},{8,13},{9,12},{10,... | collective-permute-start | bytes 294920 | tf_op jit(solution)/shard_map/ppermute | solution.py:249
  17.0 0.0 collective-permute-done.3
  17.0 2.6 %collective-permute-start.4 = (f32[32,384]{1,0:T(8,128)S(1)}, f32[32,384]{1,0:T(8,128)S(1)}, u32[]{:S(2)}, u32[]{:S(2)}) collective-permute-start(f32[32,384]{1,0:T(8,128)S(1)} %add.13.sums), channel_id=1, source_target_pairs={{0,5},{1,4},{2,7},{3,6},{4,1},{5,0},{6,3},{7,2},{8,13},{9,12},{10,... | collective-permute-start | bytes 147464 | tf_op jit(solution)/shard_map/ppermute | solution.py:249
  19.6 3.6 %collective-permute-done.6.got = f32[64,384]{1,0:T(8,128)S(1)} collective-permute-done((f32[64,384]{1,0:T(8,128)S(1)}, f32[64,384]{1,0:T(8,128)S(1)}, u32[]{:S(2)}, u32[]{:S(2)}) %collective-permute-start.6) | collective-permute-done | bytes 98336 | tf_op jit(solution)/shard_map/ppermute | solution.py:249
  23.2 1.1 %collective-permute-done.4._.got = f32[32,384]{1,0:T(8,128)S(1)} collective-permute-done((f32[32,384]{1,0:T(8,128)S(1)}, f32[32,384]{1,0:T(8,128)S(1)}, u32[]{:S(2)}, u32[]{:S(2)}) %collective-permute-start.4) | collective-permute-done | bytes 49184 | tf_op jit(solution)/shard_map/ppermute | solution.py:249
  24.3 0.3 collective-permute-start.7
  24.6 1.1 %collective-permute-done.7.other = f32[128,256]{1,0:T(8,128)S(1)} collective-permute-done((f32[128,256]{1,0:T(8,128)S(1)}, f32[128,256]{1,0:T(8,128)S(1)}, u32[]{:S(2)}, u32[]{:S(2)}) %collective-permute-start.7) | collective-permute-done | bytes 131104 | tf_op jit(solution)/shard_map/ppermute | solution.py:249
  25.7 0.3 shard_map.79
  26.0 0.2 shard_map.80
  26.1 1.4 %collective-permute-start.8 = (f32[32,256]{1,0:T(8,128)S(1)}, f32[32,256]{1,0:T(8,128)S(1)}, u32[]{:S(2)}, u32[]{:S(2)}) collective-permute-start(f32[32,256]{1,0:T(8,128)S(1)} %get-tuple-element.53.sums), channel_id=1, source_target_pairs={{0,9},{1,8},{2,11},{3,10},{4,13},{5,12},{6,15},{7,14},{8,1},{9,0},... | collective-permute-start | bytes 98312 | tf_op jit(solution)/shard_map/ppermute | solution.py:249
  27.6 0.4 collective-permute-start.9
  28.0 1.6 %collective-permute-done.8._.got = f32[32,256]{1,0:T(8,128)S(1)} collective-permute-done((f32[32,256]{1,0:T(8,128)S(1)}, f32[32,256]{1,0:T(8,128)S(1)}, u32[]{:S(2)}, u32[]{:S(2)}) %collective-permute-start.8) | collective-permute-done | bytes 32800 | tf_op jit(solution)/shard_map/ppermute | solution.py:249
  29.5 1.4 %collective-permute-done.9.got = f32[64,128]{1,0:T(8,128)S(1)} collective-permute-done((f32[64,128]{1,0:T(8,128)S(1)}, f32[64,128]{1,0:T(8,128)S(1)}, u32[]{:S(2)}, u32[]{:S(2)}) %collective-permute-start.9) | collective-permute-done | bytes 32800 | tf_op jit(solution)/shard_map/ppermute | solution.py:249
  30.9 0.2 collective-permute-start.10
  31.2 1.0 %collective-permute-done.10.other = f32[128,128]{1,0:T(8,128)S(1)} collective-permute-done((f32[128,128]{1,0:T(8,128)S(1)}, f32[128,128]{1,0:T(8,128)S(1)}, u32[]{:S(2)}, u32[]{:S(2)}) %collective-permute-start.10) | collective-permute-done | bytes 65568 | tf_op jit(solution)/shard_map/ppermute | solution.py:249
  32.2 0.3 shard_map.82.factor
  32.5 0.1 shard_map.83
  32.6 1.4 %collective-permute-start.12 = (f32[32,128]{1,0:T(8,128)S(1)}, f32[32,128]{1,0:T(8,128)S(1)}, u32[]{:S(2)}, u32[]{:S(2)}) collective-permute-start(f32[32,128]{1,0:T(8,128)S(1)} %get-tuple-element.61), channel_id=1, source_target_pairs={{0,17},{1,16},{2,19},{3,18},{4,21},{5,20},{6,23},{7,22},{8,25},{9,... | collective-permute-start | bytes 49160 | tf_op jit(solution)/shard_map/ppermute | solution.py:249
  34.1 0.3 collective-permute-start.11
  34.4 1.5 %collective-permute-done.12 = f32[32,128]{1,0:T(8,128)S(1)} collective-permute-done((f32[32,128]{1,0:T(8,128)S(1)}, f32[32,128]{1,0:T(8,128)S(1)}, u32[]{:S(2)}, u32[]{:S(2)}) %collective-permute-start.12) | collective-permute-done | bytes 16416 | tf_op jit(solution)/shard_map/ppermute | solution.py:249
  35.9 0.3 collective-permute-start.13
  36.2 0.0 collective-permute-done.11
  36.2 0.8 %shard_map.84 = (f32[64,512]{1,0:T(8,128)S(1)}, f32[256,512]{1,0:T(8,128)S(1)}) custom-call(f32[64,512]{1,0:T(8,128)S(1)} %get-tuple-element.45.current, f32[32,256]{1,0:T(8,128)S(1)} %get-tuple-element.55.refs_0_, f32[32,256]{1,0:T(8,128)S(1)} %get-tuple-element.66.refs_1_, f32[32,256]{1,0:T(8,128)S(1)} %get-tuple-element.56.refs_2_, ...), custom_call_target="tpu_custom_call" | custom-call | flops 1 | bytes 1 | tf_op jit(solution)/shard_map/pallas_call | solution.py:233
  37.0 0.1 collective-permute-done.13.other
  37.1 0.9 %shard_map.85 = f32[64,512]{1,0:T(8,128)} custom-call(f32[64,512]{1,0:T(8,128)S(1)} %get-tuple-element.60.current, f32[32,256]{1,0:T(8,128)S(1)} %pad_maximum_fusion.1.mine, f32[32,256]{1,0:T(8,128)S(1)} %collective-permute-done.13.other, f32[256,512]{1,0:T(8,128)S(1)} %get-tuple-element.62.factor), custom_call_target="tpu_custom_call" | custom-call | flops 1 | bytes 1 | tf_op jit(solution)/shard_map/pallas_call | solution.py:233
  (10 shorter events, 0.1 us)
Async XLA Ops:
  0.0 4.0 %copy-start = (s32[512]{0:T(512)S(1)}, s32[512]{0:T(512)}, u32[]{:S(2)}) copy-start(s32[512]{0:T(512)} %param.8) | copy-start | bytes 6148
  2.8 2.2 %collective-permute-start = (f32[64,1152]{1,0:T(8,128)S(1)}, f32[64,1152]{1,0:T(8,128)S(1)}, u32[]{:S(2)}, u32[]{:S(2)}) collective-permute-start(f32[64,1152]{1,0:T(8,128)S(1)} %get-tuple-element.44), channel_id=1, source_target_pairs={{0,1},{1,0},{2,3},{3,2},{4,5},{5,4},{6,7},{7,6},{8,9},{9,8},{10,11... | collective-permute-start | bytes 884744 | tf_op jit(solution)/shard_map/ppermute | solution.py:249
  6.1 2.8 %collective-permute-start.1 = (f32[32,2688]{1,0:T(8,128)S(1)}, f32[32,2688]{1,0:T(8,128)S(1)}, u32[]{:S(2)}, u32[]{:S(2)}) collective-permute-start(f32[32,2688]{1,0:T(8,128)S(1)} %get-tuple-element.47), channel_id=1, source_target_pairs={{0,1},{1,0},{2,3},{3,2},{4,5},{5,4},{6,7},{7,6},{8,9},{9,8},{10,11... | collective-permute-start | bytes 1032200 | tf_op jit(solution)/shard_map/ppermute | solution.py:249
  6.2 5.8 %collective-permute-start.5 = (f32[64,384]{1,0:T(8,128)S(1)}, f32[64,384]{1,0:T(8,128)S(1)}, u32[]{:S(2)}, u32[]{:S(2)}) collective-permute-start(f32[64,384]{1,0:T(8,128)S(1)} %slice_add_fusion._), channel_id=1, source_target_pairs={{0,3},{1,2},{2,1},{3,0},{4,7},{5,6},{6,5},{7,4},{8,11},{9,10},{10,... | collective-permute-start | bytes 294920 | tf_op jit(solution)/shard_map/ppermute | solution.py:249
  9.3 3.2 %collective-permute-start.2 = (f32[32,128]{1,0:T(8,128)S(1)}, f32[32,128]{1,0:T(8,128)S(1)}, u32[]{:S(2)}, u32[]{:S(2)}) collective-permute-start(f32[32,128]{1,0:T(8,128)S(1)} %get-tuple-element.48.mine), channel_id=1, source_target_pairs={{0,3},{1,2},{2,1},{3,0},{4,7},{5,6},{6,5},{7,4},{8,11},{9,10},{10,... | collective-permute-start | bytes 49160 | tf_op jit(solution)/shard_map/ppermute | solution.py:249
  12.8 4.2 %collective-permute-start.3 = (f32[32,384]{1,0:T(8,128)S(1)}, f32[32,384]{1,0:T(8,128)S(1)}, u32[]{:S(2)}, u32[]{:S(2)}) collective-permute-start(f32[32,384]{1,0:T(8,128)S(1)} %get-tuple-element.51), channel_id=1, source_target_pairs={{0,3},{1,2},{2,1},{3,0},{4,7},{5,6},{6,5},{7,4},{8,11},{9,10},{10,... | collective-permute-start | bytes 147464 | tf_op jit(solution)/shard_map/ppermute | solution.py:249
  14.5 8.7 %collective-permute-start.6 = (f32[64,384]{1,0:T(8,128)S(1)}, f32[64,384]{1,0:T(8,128)S(1)}, u32[]{:S(2)}, u32[]{:S(2)}) collective-permute-start(f32[64,384]{1,0:T(8,128)S(1)} %add.14.low), channel_id=1, source_target_pairs={{0,5},{1,4},{2,7},{3,6},{4,1},{5,0},{6,3},{7,2},{8,13},{9,12},{10,... | collective-permute-start | bytes 294920 | tf_op jit(solution)/shard_map/ppermute | solution.py:249
  17.0 7.2 %collective-permute-start.4 = (f32[32,384]{1,0:T(8,128)S(1)}, f32[32,384]{1,0:T(8,128)S(1)}, u32[]{:S(2)}, u32[]{:S(2)}) collective-permute-start(f32[32,384]{1,0:T(8,128)S(1)} %add.13.sums), channel_id=1, source_target_pairs={{0,5},{1,4},{2,7},{3,6},{4,1},{5,0},{6,3},{7,2},{8,13},{9,12},{10,... | collective-permute-start | bytes 147464 | tf_op jit(solution)/shard_map/ppermute | solution.py:249
  24.3 1.4 %collective-permute-start.7 = (f32[128,256]{1,0:T(8,128)S(1)}, f32[128,256]{1,0:T(8,128)S(1)}, u32[]{:S(2)}, u32[]{:S(2)}) collective-permute-start(f32[128,256]{1,0:T(8,128)S(1)} %shard_map.78), channel_id=1, source_target_pairs={{0,1},{1,0},{2,3},{3,2},{4,5},{5,4},{6,7},{7,6},{8,9},{9,8},{10,11... | collective-permute-start | bytes 393224 | tf_op jit(solution)/shard_map/ppermute | solution.py:249
  26.1 3.4 %collective-permute-start.8 = (f32[32,256]{1,0:T(8,128)S(1)}, f32[32,256]{1,0:T(8,128)S(1)}, u32[]{:S(2)}, u32[]{:S(2)}) collective-permute-start(f32[32,256]{1,0:T(8,128)S(1)} %get-tuple-element.53.sums), channel_id=1, source_target_pairs={{0,9},{1,8},{2,11},{3,10},{4,13},{5,12},{6,15},{7,14},{8,1},{9,0},... | collective-permute-start | bytes 98312 | tf_op jit(solution)/shard_map/ppermute | solution.py:249
  27.6 3.3 %collective-permute-start.9 = (f32[64,128]{1,0:T(8,128)S(1)}, f32[64,128]{1,0:T(8,128)S(1)}, u32[]{:S(2)}, u32[]{:S(2)}) collective-permute-start(f32[64,128]{1,0:T(8,128)S(1)} %get-tuple-element.54.low), channel_id=1, source_target_pairs={{0,9},{1,8},{2,11},{3,10},{4,13},{5,12},{6,15},{7,14},{8,1},{9,0},... | collective-permute-start | bytes 98312 | tf_op jit(solution)/shard_map/ppermute | solution.py:249
  30.9 1.3 %collective-permute-start.10 = (f32[128,128]{1,0:T(8,128)S(1)}, f32[128,128]{1,0:T(8,128)S(1)}, u32[]{:S(2)}, u32[]{:S(2)}) collective-permute-start(f32[128,128]{1,0:T(8,128)S(1)} %shard_map.81), channel_id=1, source_target_pairs={{0,1},{1,0},{2,3},{3,2},{4,5},{5,4},{6,7},{7,6},{8,9},{9,8},{10,11... | collective-permute-start | bytes 196616 | tf_op jit(solution)/shard_map/ppermute | solution.py:249
  32.6 3.2 %collective-permute-start.12 = (f32[32,128]{1,0:T(8,128)S(1)}, f32[32,128]{1,0:T(8,128)S(1)}, u32[]{:S(2)}, u32[]{:S(2)}) collective-permute-start(f32[32,128]{1,0:T(8,128)S(1)} %get-tuple-element.61), channel_id=1, source_target_pairs={{0,17},{1,16},{2,19},{3,18},{4,21},{5,20},{6,23},{7,22},{8,25},{9,... | collective-permute-start | bytes 49160 | tf_op jit(solution)/shard_map/ppermute | solution.py:249
  34.1 2.1 %collective-permute-start.11 = (f32[32,768]{1,0:T(8,128)S(1)}, f32[32,768]{1,0:T(8,128)S(1)}, u32[]{:S(2)}, u32[]{:S(2)}) collective-permute-start(f32[32,768]{1,0:T(8,128)S(1)} %pad_maximum_fusion), channel_id=1, source_target_pairs={{0,1},{1,0},{2,3},{3,2},{4,5},{5,4},{6,7},{7,6},{8,9},{9,8},{10,11... | collective-permute-start | bytes 294920 | tf_op jit(solution)/shard_map/ppermute | solution.py:249
  35.9 1.3 %collective-permute-start.13 = (f32[32,256]{1,0:T(8,128)S(1)}, f32[32,256]{1,0:T(8,128)S(1)}, u32[]{:S(2)}, u32[]{:S(2)}) collective-permute-start(f32[32,256]{1,0:T(8,128)S(1)} %pad_maximum_fusion.1.mine), channel_id=1, source_target_pairs={{0,1},{1,0},{2,3},{3,2},{4,5},{5,4},{6,7},{7,6},{8,9},{9,8},{10,11... | collective-permute-start | bytes 98312 | tf_op jit(solution)/shard_map/ppermute | solution.py:249

commit v6 on v5

v6 whole, which is shorter than its diff:
```python
import functools

import jax
import jax.numpy as jnp
from jax import lax
from jax.experimental import pallas as pl
from jax.experimental.pallas import tpu as pltpu
from jax.sharding import PartitionSpec as P

AXES = ("grp", "sub")
F32, BF16 = jnp.float32, jnp.bfloat16
NN = (((1,), (0,)), ((), ()))
NT = (((1,), (1,)), ((), ()))
TN = (((0,), (0,)), ((), ()))
ANY = pl.BlockSpec(memory_space=pl.ANY)
HBM = pl.BlockSpec(memory_space=pltpu.HBM)
VMEM = pl.BlockSpec(memory_space=pltpu.VMEM)
LIMIT = 24 * 1024 * 1024


def parts(x):
    high = x.astype(BF16)
    return high, (x - high.astype(F32)).astype(BF16)


def product(a, b, dims):
    return lax.dot_general(a, b, dims, preferred_element_type=F32)


def dot(a, b, dims=NN):
    if dims == TN:
        a, dims = a.T, NN
    ah, al = parts(a)
    bh, bl = parts(b)
    rows = a.shape[0]
    both = product(jnp.concatenate([ah, al], axis=0), bh, dims)
    return both[:rows] + (both[rows:] + product(ah, bl, dims))


def parity_of(device_id, bits):
    parity = device_id & 1
    for bit in range(1, bits):
        parity = parity ^ ((device_id >> bit) & 1)
    return parity


def low_kernel(
    top, left, right, rhs, leaf, order, keep, send, left_v, right_v, rhs_v, leaf_v, order_v, sems,
):
    rank = left.shape[2]
    n = rank // 2
    count = top - 3
    bases = []
    for j in range(count):
        cols = slice(j * rank, (j + 1) * rank)
        bases.append(pltpu.make_async_copy(left.at[j + 1], left_v.at[:, cols], sems.at[0, j]))
        bases.append(pltpu.make_async_copy(right.at[j], right_v.at[:, cols], sems.at[1, j]))
    rest = [
        pltpu.make_async_copy(order, order_v, sems.at[2, 1]),
        pltpu.make_async_copy(rhs, rhs_v, sems.at[2, 2]),
        pltpu.make_async_copy(leaf, leaf_v, sems.at[2, 3]),
    ]
    for copy in bases + rest:
        copy.start()
    for copy in bases:
        copy.wait()
    half = parity_of(lax.axis_index(AXES), top) == 1
    grams = dot(left_v[...], right_v[...], TN)
    at = 0
    for k in range(count, 0, -1):
        w = k * rank
        value = grams[w - rank : w, :w]
        keep[:, at : at + w] = jnp.where(half, value[n:], value[:n])
        send[:, at : at + w] = jnp.where(half, value[:n], value[n:])
        at += w
    for copy in rest:
        copy.wait()


def sides(split, size):
    border = split[...]
    return (
        lax.broadcasted_iota(jnp.int32, (1, size), 1) < border,
        lax.broadcasted_iota(jnp.int32, (size, 1), 0) < border,
    )


def leaf_kernel(
    top, order, split, rhs, leaf, right_low, left, right, coupling, current, gram_top, gram_next,
    left_v, right_v, left_top, right_top, coupling_v, sems,
):
    rank = left_top.shape[1]
    count, size = rhs.shape
    copies = [
        pltpu.make_async_copy(left.at[top - 2], left_v.at[:, rank : 2 * rank], sems.at[0]),
        pltpu.make_async_copy(left.at[top - 1], left_v.at[:, 2 * rank :], sems.at[1]),
        pltpu.make_async_copy(right.at[top - 3], right_v.at[:, :rank], sems.at[2]),
        pltpu.make_async_copy(right.at[top - 2], right_v.at[:, rank : 2 * rank], sems.at[3]),
        pltpu.make_async_copy(right.at[top], right_top, sems.at[4]),
        pltpu.make_async_copy(coupling.at[0], coupling_v, sems.at[5]),
        pltpu.make_async_copy(left.at[top], left_top, sems.at[6]),
        pltpu.make_async_copy(right.at[top - 1], right_v.at[:, 2 * rank :], sems.at[7]),
        pltpu.make_async_copy(left.at[0], left_v.at[:, :rank], sems.at[8]),
    ]
    for copy in copies:
        copy.start()
    local = order[...] - lax.axis_index(AXES) * size
    pick = (lax.broadcasted_iota(jnp.int32, (size, size), 0) == local).astype(F32).astype(BF16)
    high, low = parts(rhs[...])
    moved = product(jnp.concatenate([high, low], axis=0), pick, NN).astype(BF16)
    columns, rows = sides(split, size)
    lh, ll = parts(jnp.where(rows == columns, leaf[...], 0.0))
    both = product(moved, lh, NN)
    current[...] = both[:count] + (both[count:] + product(moved[:count], ll, NN))
    for copy in copies[:4]:
        copy.wait()
    low_w = right_low.shape[1]
    upper = left_v[:, rank:]
    value = dot(upper, right_low[...], TN)
    gram_next[:, :low_w] = value[:rank]
    gram_top[:, :low_w] = value[rank:]
    value = dot(upper, right_v[:, : 2 * rank], TN)
    gram_next[:, low_w:] = value[:rank, :rank]
    gram_top[:, low_w:] = value[rank:]
    for copy in copies[4:]:
        copy.wait()


def put_rows(out, at, value):
    rows, w = out.shape[0], value.shape[1]
    for row in range(0, value.shape[0], rows):
        out[:, at : at + w] = value[row : row + rows, :]
        at += w
    return at


def take_rows(packed, at, height, w):
    rows = packed.shape[0]
    return jnp.concatenate(
        [packed[:, at + i * w : at + (i + 1) * w] for i in range(height // rows)], axis=0
    )


def local_kernel(
    top, split, first, left_top, right_top, right_low, right_v, coupling, gram_top, gram_next, _,
    current_out, keep, send,
):
    rank = left_top.shape[1]
    count, size = first.shape
    current = first[...]
    is_left, _ = sides(split, size)
    halves = jnp.concatenate(
        [jnp.where(is_left, current, 0.0), jnp.where(is_left, 0.0, current)], axis=0
    )
    w = dot(halves, right_top[...])
    z = dot(jnp.concatenate([w[:count], w[count:]], axis=1), coupling[top])
    update = dot(jnp.concatenate([z[:, :rank], z[:, rank:]], axis=0), left_top[...], NT)
    current = current - jnp.where(is_left, update[:count], update[count:])
    current_out[...] = current
    half = parity_of(lax.axis_index(AXES), top) == 1
    n = count // 2
    at = 0
    for basis in (right_low, right_v):
        sums = dot(current, basis[...])
        w = basis.shape[1]
        keep[:, at : at + w] = jnp.where(half, sums[n:], sums[:n])
        send[:, at : at + w] = jnp.where(half, sums[:n], sums[n:])
        at += w
    at = put_rows(send, at, gram_top[...])
    put_rows(send, at, gram_next[...])


def beside(own, got, on_right):
    return jnp.concatenate(
        [jnp.where(on_right, got, own), jnp.where(on_right, own, got)], axis=1
    )


def top_kernel(top, keep, got, gram_top, coupling, sums, next_sums, z_mine, z_other, pair):
    rank = gram_top.shape[0]
    w = (top - 1) * rank
    right = lax.axis_index(AXES) & 1
    own_at, got_at = right * rank, (1 - right) * rank
    pair[pl.ds(pl.multiple_of(own_at, rank), rank), :] = gram_top[...]
    pair[pl.ds(pl.multiple_of(got_at, rank), rank), :] = take_rows(got, top * rank, rank, w)
    is_right = right == 1
    z = dot(beside(keep[:, w:], got[:, w : top * rank], is_right), coupling[top - 1])
    value = keep[:, :w] + got[:, :w] - dot(z, pair[...])
    sums[...] = value[:, : w - rank]
    next_sums[...] = value[:, w - rank :]
    z_mine[...] = jnp.where(is_right, z[:, rank:], z[:, :rank])
    z_other[...] = jnp.where(is_right, z[:, :rank], z[:, rank:])


def side_of(coupling, k, right):
    rank = coupling.shape[2] // 2
    return jnp.where(right, coupling[k, :, rank:], coupling[k, :, :rank])


def next_kernel(top, mine, got, sums, gram_next, got_gram, coupling, z_out, sums_out):
    rank, w = gram_next.shape
    right = (lax.axis_index(AXES) >> 1) & 1 == 1
    z = dot(beside(mine[...], got[...], right), side_of(coupling, top - 2, right))
    at = top * rank + rank // got_gram.shape[0] * (w + rank)
    gram = gram_next[...] + take_rows(got_gram, at, rank, w)
    z_out[...] = z
    sums_out[...] = sums[...] - dot(z, gram)


def merge_kernel(last, low, got, _, mine, rest):
    lower = low.shape[1] - rest.shape[1]
    rest[...] = low[:, lower:] + got[:, lower:]
    mine[:, :lower] = low[:, :lower]
    mine[:, lower : 2 * lower] = got[:, :lower]
    if last:
        mine[:, 2 * lower :] = rest[...]


def couple_kernel(top, k, sums, got, coupling, both, z):
    rank = both.shape[1] // 2
    right = (lax.axis_index(AXES) >> (top - 1 - k)) & 1 == 1
    w = k * rank
    both[...] = beside(sums[:, w:], got[:, w:], right)
    z[...] = dot(both[...], coupling[k])


def level_kernel(top, k, sums, got, z, low, got_low, rest, other, out, pair):
    n = low.shape[0]
    rank, w = 2 * n, k * 2 * n
    bit = top - 1 - k
    device_id = lax.axis_index(AXES)
    half = parity_of(device_id, top)
    right = (device_id >> bit) & 1

    def put(child, mine, theirs):
        pair[pl.ds(pl.multiple_of(child * rank + half * n, n), n), :] = mine
        pair[pl.ds(pl.multiple_of(child * rank + (1 - half) * n, n), n), :] = theirs

    put(right, low[:, :w], other[:, :w])
    put(1 - right, got_low[:, :w], other[:, w : 2 * w])
    out[:, :w] = sums[:, :w] + got[:, :w] - dot(z[...], pair[...])
    if k == 2:
        mine, theirs = rest[...], other[:, 2 * w :]
        is_upper = half == 1
        gram = jnp.concatenate(
            [jnp.where(is_upper, theirs, mine), jnp.where(is_upper, mine, theirs)], axis=0
        )
        put_rows(out, w, gram)


def first_kernel(top, packed, got, coupling, out, both, pair):
    rank = out.shape[1]
    right = (lax.axis_index(AXES) >> (top - 2)) & 1
    for child, value in ((right, packed), (1 - right, got)):
        pair[pl.ds(pl.multiple_of(child * rank, rank), rank), :] = take_rows(
            value, 2 * rank, rank, rank
        )
    both[...] = beside(packed[:, rank : 2 * rank], got[:, rank : 2 * rank], right == 1)
    z = dot(both[...], coupling[1])
    out[...] = packed[:, :rank] + got[:, :rank] - dot(z, pair[...])


def joined(mine, other, top):
    half = parity_of(lax.axis_index(AXES), top) == 1
    return jnp.concatenate(
        [jnp.where(half, other, mine), jnp.where(half, mine, other)], axis=0
    )


def early_kernel(top, current, *refs):
    left_low, left_v, coupling, out, factor = refs[-5:]
    rank = left_v.shape[1] // 3
    device_id = lax.axis_index(AXES)
    z = []
    for k in range(1, top):
        pair = joined(refs[2 * k - 2][...], refs[2 * k - 1][...], top)
        right = (device_id >> (top - 1 - k)) & 1 == 1
        z.append(pair if k >= top - 2 else dot(pair, side_of(coupling, k, right)))
    low = dot(jnp.concatenate(z[: top - 3], axis=1), left_low[...], NT)
    high = dot(jnp.concatenate(z[top - 3 :], axis=1), left_v[:, rank:], NT)
    out[...] = current[...] - (low + high)
    right = (device_id >> (top - 1)) & 1 == 1
    factor[...] = dot(side_of(coupling, 0, right), left_v[:, :rank], NT)


def last_kernel(top, current, mine, other, factor, out):
    out[...] = current[...] - dot(joined(mine[...], other[...], top), factor[...])


def call(kernel, outs, in_specs, out_specs, scratch, *args):
    return pl.pallas_call(
        kernel,
        out_shape=outs,
        in_specs=in_specs,
        out_specs=out_specs,
        scratch_shapes=scratch,
        cost_estimate=pl.CostEstimate(flops=1, bytes_accessed=1, transcendentals=0),
        compiler_params=pltpu.CompilerParams(vmem_limit_bytes=LIMIT),
    )(*args)


def shape(*dims, dtype=F32):
    return jax.ShapeDtypeStruct(dims, dtype)


def in_hbm(*arrays):
    return [pltpu.with_memory_space_constraint(x, pltpu.HBM) for x in arrays]


def exchange(value, mask):
    return lax.ppermute(value, AXES, [(i, i ^ mask) for i in range(lax.axis_size(AXES))])


def per_device(right_side, order, leaf_split, leaf_inverse, basis_left, basis_right, coupling):
    count, size = right_side.shape
    levels, _, rank = basis_left.shape
    top = levels - 1
    n = rank // 2
    rows = count // 2
    wide = top * rank
    low_w = rank * (top - 2) * (top - 3) // 2
    next_w = (top - 2) * rank
    device_id = lax.axis_index(AXES)
    split = leaf_split.reshape(1, 1)
    keep, send, left_low, right_low, rhs, leaf, order = call(
        functools.partial(low_kernel, top),
        [
            shape(n, low_w),
            shape(n, low_w),
            shape(size, (top - 3) * rank),
            shape(size, (top - 3) * rank),
            shape(count, size),
            shape(size, size),
            shape(1, size, dtype=jnp.int32),
        ],
        [HBM] * 5,
        [VMEM] * 7,
        [pltpu.SemaphoreType.DMA((3, max(4, top - 3)))],
        *in_hbm(basis_left, basis_right, right_side, leaf_inverse, order.reshape(1, size)),
    )
    got_low = exchange(send, 1)
    current, gram_top, gram_next, left, right, left_top, right_top, coup = call(
        functools.partial(leaf_kernel, top),
        [
            shape(count, size),
            shape(rank, wide - rank),
            shape(rank, next_w),
            shape(size, 3 * rank),
            shape(size, 3 * rank),
            shape(size, rank),
            shape(size, rank),
            shape(levels, 2 * rank, 2 * rank),
        ],
        [VMEM] * 5 + [HBM] * 3,
        [VMEM] * 8,
        [pltpu.SemaphoreType.DMA((9,))],
        order,
        split,
        rhs,
        leaf,
        right_low,
        *in_hbm(basis_left, basis_right, coupling),
    )
    low = keep + got_low
    current, keep, send = call(
        functools.partial(local_kernel, top),
        [
            shape(count, size),
            shape(rows, wide),
            shape(rows, wide + rank // rows * (wide - rank + next_w)),
        ],
        [VMEM] * 9 + [ANY],
        [VMEM] * 3,
        [],
        split,
        current,
        left_top,
        right_top,
        right_low,
        right,
        coup,
        gram_top,
        gram_next,
        low,
    )
    got = exchange(send, 1)
    sums, next_sums, z_mine, z_other = call(
        functools.partial(top_kernel, top),
        [shape(rows, next_w), shape(rows, rank), shape(rows, rank), shape(rows, rank)],
        [VMEM] * 4,
        [VMEM] * 4,
        [pltpu.VMEM((2 * rank, wide - rank), F32)],
        keep,
        got,
        gram_top,
        coup,
    )
    known = {top - 1: (z_mine, z_other)}
    got_low = exchange(low, 3)
    z, sums = call(
        functools.partial(next_kernel, top),
        [shape(rows, rank), shape(rows, next_w)],
        [VMEM] * 6,
        [VMEM] * 2,
        [],
        next_sums,
        exchange(next_sums, 3),
        sums,
        gram_next,
        got,
        coup,
    )
    known[top - 2] = (z, z)
    low = low + got_low
    sums = sums + exchange(sums, 3)
    for k in range(top - 3, 1, -1):
        mask = 1 << (top - 1 - k) | 1
        w = k * rank
        last = k == 2
        got_low = exchange(low, mask)
        got = exchange(sums, mask)
        mine, rest = call(
            functools.partial(merge_kernel, last),
            [shape(n, 2 * w + (rank if last else 0)), shape(n, low.shape[1] - w)],
            [VMEM, VMEM, ANY],
            [VMEM] * 2,
            [],
            low,
            got_low,
            got,
        )
        both, z = call(
            functools.partial(couple_kernel, top, k),
            [shape(rows, 2 * rank), shape(rows, 2 * rank)],
            [VMEM] * 3,
            [VMEM] * 2,
            [],
            sums,
            got,
            coup,
        )
        sums = call(
            functools.partial(level_kernel, top, k),
            shape(rows, w + (rank // rows * rank if last else 0)),
            [VMEM] * 7,
            VMEM,
            [pltpu.VMEM((2 * rank, w), F32)],
            sums,
            got,
            z,
            low,
            got_low,
            rest,
            exchange(mine, 1),
        )
        known[k] = (both, both)
        low = rest
    sums, both = call(
        functools.partial(first_kernel, top),
        [shape(rows, rank), shape(rows, 2 * rank)],
        [VMEM] * 3,
        [VMEM] * 2,
        [pltpu.VMEM((2 * rank, rank), F32)],
        sums,
        exchange(sums, 1 << (top - 2) | 1),
        coup,
    )
    known[1] = (both, both)
    got_sums = exchange(sums, 1 << (top - 1) | 1)
    names = range(1, top)
    others = exchange(jnp.concatenate([known[k][1] for k in names], axis=1), 1)
    args, at = [], 0
    for k in names:
        mine = known[k][0]
        args += [mine, others[:, at : at + mine.shape[1]]]
        at += mine.shape[1]
    current, factor = call(
        functools.partial(early_kernel, top),
        [shape(count, size), shape(2 * rank, size)],
        [VMEM] * (4 + len(args)),
        [VMEM] * 2,
        [],
        current,
        *args,
        left_low,
        left,
        coup,
    )
    both = beside(sums, got_sums, (device_id >> (top - 1)) & 1 == 1)
    return call(
        functools.partial(last_kernel, top),
        shape(count, size),
        [VMEM] * 4,
        VMEM,
        [],
        current,
        both,
        exchange(both, 1),
        factor,
    )


def solution(mesh):
    in_specs = (
        P(None, AXES),
        P(AXES),
        P(AXES),
        P(AXES, None),
        P(None, AXES, None),
        P(None, AXES, None),
        P(AXES, None, None, None),
    )
    return jax.shard_map(
        per_device, mesh=mesh, in_specs=in_specs, out_specs=P(None, AXES), check_vma=False
    )
```

time: 38.2 us -> 37.5 us (0.982)
  starting transfers between devices: 16.2 us -> 15.6 us
  Pallas kernels: 8.15 us -> 8.55 us
  waiting for transfers between devices: 12.8 us -> 12.4 us
    ppermute x14 -> x12, starting transfers between devices: 16.2 us -> 15.6 us  [exchange(): lax.ppermute(value, AXES, [(i, i ^ mask) for i in range(lax.axis_size(AXE...]
    ppermute x14 -> x12, waiting for transfers between devices: 12.8 us -> 12.4 us  [exchange(): lax.ppermute(value, AXES, [(i, i ^ mask) for i in range(lax.axis_size(AXE...]
    pallas_call x13 -> x11, Pallas kernels: 8.15 us -> 8.55 us  [call(): pl.pallas_call(kernel, out_shape=outs, in_specs=in_specs, out_specs=out_s...]
  transfers between devices with their start and end apart: 14 -> 12, of which waited for: 10 -> 8; matrix products, arithmetic and copies ran while one was open for 0% -> 0% of each run, Pallas kernels for 6% -> 11%
where the time goes in v6:
time: 37.5 us; the launch traced here: 37.4 us
  starting transfers between devices  15.6 us (42%)
  waiting for transfers between devices  12.4 us (33%)
  Pallas kernels  8.55 us (23%)
  between operations  0.76 us (2%)
    ppermute x12, starting transfers between devices, exchange(): lax.ppermute(value, AXES, [(i, i ^ mask) for i in range(lax.axis_size(AXE...  15.6 us
    ppermute x12, waiting for transfers between devices, exchange(): lax.ppermute(value, AXES, [(i, i ^ mask) for i in range(lax.axis_size(AXE...  12.4 us
    pallas_call x11, Pallas kernels, call(): pl.pallas_call(kernel, out_shape=outs, in_specs=in_specs, out_specs=out_s...  8.55 us
  transfers between devices with their start and end apart: 12, of which 8 were waited for; matrix products, arithmetic and copies ran while one was open for 0% of the time, Pallas kernels for 11%

profile of v6, /device:TPU:0, one launch (start us, length us, event | category | flops | bytes accessed | tf_op | source)
XLA Modules:
  0.0 37.4 jit_solution(12330256614567720807)
XLA Ops:
  0.0 1.8 %shard_map.73 = (f32[64,384]{1,0:T(8,128)S(1)}, f32[64,384]{1,0:T(8,128)S(1)}, f32[512,256]{1,0:T(8,128)S(1)}, f32[512,256]{1,0:T(8,128)S(1)}, f32[64,512]{1,0:T...) custom-call(f32[6,512,128]{2,1,0:T(8,128)} %left.3, f32[6,512,128]{2,1,0:T(8,128)} %right.3, f32[64,512]{1,0:T(8,128)} %rhs.1, ...), custom_call_target="tpu_custom_call" | custom-call | flops 1 | bytes 1 | tf_op jit(solution)/shard_map/pallas_call | solution.py:291
  1.8 0.5 %collective-permute-start = (f32[64,384]{1,0:T(8,128)S(1)}, f32[64,384]{1,0:T(8,128)S(1)}, u32[]{:S(2)}, u32[]{:S(2)}) collective-permute-start(f32[64,384]{1,0:T(8,128)S(1)} %get-tuple-element.49), channel_id=1, source_target_pairs={{0,1},{1,0},{2,3},{3,2},{4,5},{5,4},{6,7},{7,6},{8,9},{9,8},{10,11... | collective-permute-start | bytes 294920 | tf_op jit(solution)/shard_map/ppermute | solution.py:311
  2.9 2.6 %shard_map.74 = (f32[64,512]{1,0:T(8,128)S(1)}, f32[128,512]{1,0:T(8,128)S(1)}, f32[128,384]{1,0:T(8,128)S(1)}, f32[512,384]{1,0:T(8,128)S(1)}, f32[512,384]{1,0...) custom-call(s32[1,512]{1,0:T(1,128)S(1)} %get-tuple-element.37.order, ...), custom_call_target="tpu_custom_call" | custom-call | flops 1 | bytes 1 | tf_op jit(solution)/shard_map/pallas_call | solution.py:291
  5.5 0.0 collective-permute-done
  5.6 1.1 %shard_map.75 = (f32[64,512]{1,0:T(8,128)S(1)}, f32[32,640]{1,0:T(8,128)S(1)}, f32[32,4224]{1,0:T(8,128)S(1)}) custom-call(s32[1,1]{1,0:T(1,128)} %bitcast.3.split, f32[64,512]{1,0:T(8,128)S(1)} %get-tuple-element.41.first, f32[512,128]{1,0:T(8,128)S(1)} %get-tuple-element.42.left_top, f32[512,128]{1,0:T(8,128)S(1)} %get-tuple-element.43.right_top, ...), custom_call_target="tpu_custom_call" | custom-call | flops 1 | bytes 1 | tf_op jit(solution)/shard_map/pallas_call | solution.py:291
  6.7 0.1 collective-permute-start.1
  6.8 2.7 %collective-permute-start.5 = (f32[64,384]{1,0:T(8,128)S(1)}, f32[64,384]{1,0:T(8,128)S(1)}, u32[]{:S(2)}, u32[]{:S(2)}) collective-permute-start(f32[64,384]{1,0:T(8,128)S(1)} %add.12._), channel_id=1, source_target_pairs={{0,3},{1,2},{2,1},{3,0},{4,7},{5,6},{6,5},{7,4},{8,11},{9,10},{10,... | collective-permute-start | bytes 294920 | tf_op jit(solution)/shard_map/ppermute | solution.py:311
  9.5 0.0 collective-permute-done.1.got.got_gram
  9.5 0.4 %shard_map.76 = (f32[32,384]{1,0:T(8,128)S(1)}, f32[32,128]{1,0:T(8,128)S(1)}, f32[32,128]{1,0:T(8,128)S(1)}, f32[32,128]{1,0:T(8,128)S(1)}) custom-call(f32[32,640]{1,0:T(8,128)S(1)} %get-tuple-element.51.keep, f32[32,4224]{1,0:T(8,128)S(1)} %collective-permute-done.1.got.got_gram, f32[128,512]{1,0:T(8,128)S(1)} %get-tuple-element.46.gram_top, ...), custom_call_target="tpu_custom_call" | custom-call | flops 1 | bytes 1 | tf_op jit(solution)/shard_map/pallas_call | solution.py:291
  9.9 1.9 %collective-permute-start.2 = (f32[32,128]{1,0:T(8,128)S(1)}, f32[32,128]{1,0:T(8,128)S(1)}, u32[]{:S(2)}, u32[]{:S(2)}) collective-permute-start(f32[32,128]{1,0:T(8,128)S(1)} %get-tuple-element.53.mine), channel_id=1, source_target_pairs={{0,3},{1,2},{2,1},{3,0},{4,7},{5,6},{6,5},{7,4},{8,11},{9,10},{10,... | collective-permute-start | bytes 49160 | tf_op jit(solution)/shard_map/ppermute | solution.py:311
  11.8 0.6 %collective-permute-done.5 = f32[64,384]{1,0:T(8,128)S(1)} collective-permute-done((f32[64,384]{1,0:T(8,128)S(1)}, f32[64,384]{1,0:T(8,128)S(1)}, u32[]{:S(2)}, u32[]{:S(2)}) %collective-permute-start.5) | collective-permute-done | bytes 98336 | tf_op jit(solution)/shard_map/ppermute | solution.py:311
  12.5 0.8 %collective-permute-done.2.got = f32[32,128]{1,0:T(8,128)S(1)} collective-permute-done((f32[32,128]{1,0:T(8,128)S(1)}, f32[32,128]{1,0:T(8,128)S(1)}, u32[]{:S(2)}, u32[]{:S(2)}) %collective-permute-start.2) | collective-permute-done | bytes 16416 | tf_op jit(solution)/shard_map/ppermute | solution.py:311
  13.2 0.3 shard_map.77
  13.5 1.7 %collective-permute-start.3 = (f32[32,384]{1,0:T(8,128)S(1)}, f32[32,384]{1,0:T(8,128)S(1)}, u32[]{:S(2)}, u32[]{:S(2)}) collective-permute-start(f32[32,384]{1,0:T(8,128)S(1)} %get-tuple-element.55), channel_id=1, source_target_pairs={{0,3},{1,2},{2,1},{3,0},{4,7},{5,6},{6,5},{7,4},{8,11},{9,10},{10,... | collective-permute-start | bytes 147464 | tf_op jit(solution)/shard_map/ppermute | solution.py:311
  15.3 2.5 %collective-permute-start.6 = (f32[64,384]{1,0:T(8,128)S(1)}, f32[64,384]{1,0:T(8,128)S(1)}, u32[]{:S(2)}, u32[]{:S(2)}) collective-permute-start(f32[64,384]{1,0:T(8,128)S(1)} %add.14.low), channel_id=1, source_target_pairs={{0,5},{1,4},{2,7},{3,6},{4,1},{5,0},{6,3},{7,2},{8,13},{9,12},{10,... | collective-permute-start | bytes 294920 | tf_op jit(solution)/shard_map/ppermute | solution.py:311
  17.7 0.0 collective-permute-done.3
  17.7 2.6 %collective-permute-start.4 = (f32[32,384]{1,0:T(8,128)S(1)}, f32[32,384]{1,0:T(8,128)S(1)}, u32[]{:S(2)}, u32[]{:S(2)}) collective-permute-start(f32[32,384]{1,0:T(8,128)S(1)} %add.13.sums), channel_id=1, source_target_pairs={{0,5},{1,4},{2,7},{3,6},{4,1},{5,0},{6,3},{7,2},{8,13},{9,12},{10,... | collective-permute-start | bytes 147464 | tf_op jit(solution)/shard_map/ppermute | solution.py:311
  20.3 3.8 %collective-permute-done.6.got.got_low = f32[64,384]{1,0:T(8,128)S(1)} collective-permute-done((f32[64,384]{1,0:T(8,128)S(1)}, f32[64,384]{1,0:T(8,128)S(1)}, u32[]{:S(2)}, u32[]{:S(2)}) %collective-permute-start.6) | collective-permute-done | bytes 98336 | tf_op jit(solution)/shard_map/ppermute | solution.py:311
  24.1 1.1 %collective-permute-done.4.got._ = f32[32,384]{1,0:T(8,128)S(1)} collective-permute-done((f32[32,384]{1,0:T(8,128)S(1)}, f32[32,384]{1,0:T(8,128)S(1)}, u32[]{:S(2)}, u32[]{:S(2)}) %collective-permute-start.4) | collective-permute-done | bytes 49184 | tf_op jit(solution)/shard_map/ppermute | solution.py:311
  25.2 0.2 collective-permute-start.7
  25.4 0.2 shard_map.78
  25.5 1.1 %collective-permute-done.7.other = f32[64,640]{1,0:T(8,128)S(1)} collective-permute-done((f32[64,640]{1,0:T(8,128)S(1)}, f32[64,640]{1,0:T(8,128)S(1)}, u32[]{:S(2)}, u32[]{:S(2)}) %collective-permute-start.7) | collective-permute-done | bytes 163872 | tf_op jit(solution)/shard_map/ppermute | solution.py:311
  26.6 0.2 shard_map.80.packed
  26.8 1.3 %collective-permute-start.8 = (f32[32,768]{1,0:T(8,128)S(1)}, f32[32,768]{1,0:T(8,128)S(1)}, u32[]{:S(2)}, u32[]{:S(2)}) collective-permute-start(f32[32,768]{1,0:T(8,128)S(1)} %shard_map.80.packed), channel_id=1, source_target_pairs={{0,9},{1,8},{2,11},{3,10},{4,13},{5,12},{6,15},{7,14},{8,1},{9,0},... | collective-permute-start | bytes 294920 | tf_op jit(solution)/shard_map/ppermute | solution.py:311
  28.1 3.5 %collective-permute-done.8.got = f32[32,768]{1,0:T(8,128)S(1)} collective-permute-done((f32[32,768]{1,0:T(8,128)S(1)}, f32[32,768]{1,0:T(8,128)S(1)}, u32[]{:S(2)}, u32[]{:S(2)}) %collective-permute-start.8) | collective-permute-done | bytes 98336 | tf_op jit(solution)/shard_map/ppermute | solution.py:311
  31.6 0.3 shard_map.81
  32.0 1.4 %collective-permute-start.10 = (f32[32,128]{1,0:T(8,128)S(1)}, f32[32,128]{1,0:T(8,128)S(1)}, u32[]{:S(2)}, u32[]{:S(2)}) collective-permute-start(f32[32,128]{1,0:T(8,128)S(1)} %get-tuple-element.67), channel_id=1, source_target_pairs={{0,17},{1,16},{2,19},{3,18},{4,21},{5,20},{6,23},{7,22},{8,25},{9,... | collective-permute-start | bytes 49160 | tf_op jit(solution)/shard_map/ppermute | solution.py:311
  33.3 0.4 %collective-permute-start.9 = (f32[32,768]{1,0:T(8,128)S(1)}, f32[32,768]{1,0:T(8,128)S(1)}, u32[]{:S(2)}, u32[]{:S(2)}) collective-permute-start(f32[32,768]{1,0:T(8,128)S(1)} %pad_maximum_fusion), channel_id=1, source_target_pairs={{0,1},{1,0},{2,3},{3,2},{4,5},{5,4},{6,7},{7,6},{8,9},{9,8},{10,11... | collective-permute-start | bytes 294920 | tf_op jit(solution)/shard_map/ppermute | solution.py:311
  33.7 1.4 %collective-permute-done.10 = f32[32,128]{1,0:T(8,128)S(1)} collective-permute-done((f32[32,128]{1,0:T(8,128)S(1)}, f32[32,128]{1,0:T(8,128)S(1)}, u32[]{:S(2)}, u32[]{:S(2)}) %collective-permute-start.10) | collective-permute-done | bytes 16416 | tf_op jit(solution)/shard_map/ppermute | solution.py:311
  35.2 0.2 collective-permute-start.11
  35.4 0.0 collective-permute-done.9
  35.5 0.8 %shard_map.82 = (f32[64,512]{1,0:T(8,128)S(1)}, f32[256,512]{1,0:T(8,128)S(1)}) custom-call(f32[64,512]{1,0:T(8,128)S(1)} %get-tuple-element.50.current, f32[32,256]{1,0:T(8,128)S(1)} %get-tuple-element.59.refs_0_, f32[32,256]{1,0:T(8,128)S(1)} %get-tuple-element.72.refs_1_, f32[32,256]{1,0:T(8,128)S(1)} %get-tuple-element.60.refs_2_, ...), custom_call_target="tpu_custom_call" | custom-call | flops 1 | bytes 1 | tf_op jit(solution)/shard_map/pallas_call | solution.py:291
  36.3 0.2 collective-permute-done.11.other
  36.5 0.9 %shard_map.83 = f32[64,512]{1,0:T(8,128)} custom-call(f32[64,512]{1,0:T(8,128)S(1)} %get-tuple-element.66.current, f32[32,256]{1,0:T(8,128)S(1)} %pad_maximum_fusion.1.mine, f32[32,256]{1,0:T(8,128)S(1)} %collective-permute-done.11.other, f32[256,512]{1,0:T(8,128)S(1)} %get-tuple-element.68.factor), custom_call_target="tpu_custom_call" | custom-call | flops 1 | bytes 1 | tf_op jit(solution)/shard_map/pallas_call | solution.py:291
  (9 shorter events, 0.1 us)
Async XLA Ops:
  1.8 3.8 %collective-permute-start = (f32[64,384]{1,0:T(8,128)S(1)}, f32[64,384]{1,0:T(8,128)S(1)}, u32[]{:S(2)}, u32[]{:S(2)}) collective-permute-start(f32[64,384]{1,0:T(8,128)S(1)} %get-tuple-element.49), channel_id=1, source_target_pairs={{0,1},{1,0},{2,3},{3,2},{4,5},{5,4},{6,7},{7,6},{8,9},{9,8},{10,11... | collective-permute-start | bytes 294920 | tf_op jit(solution)/shard_map/ppermute | solution.py:311
  6.7 2.8 %collective-permute-start.1 = (f32[32,4224]{1,0:T(8,128)S(1)}, f32[32,4224]{1,0:T(8,128)S(1)}, u32[]{:S(2)}, u32[]{:S(2)}) collective-permute-start(f32[32,4224]{1,0:T(8,128)S(1)} %get-tuple-element.52), channel_id=1, source_target_pairs={{0,1},{1,0},{2,3},{3,2},{4,5},{5,4},{6,7},{7,6},{8,9},{9,8},{10,11... | collective-permute-start | bytes 1622024 | tf_op jit(solution)/shard_map/ppermute | solution.py:311
  6.8 5.6 %collective-permute-start.5 = (f32[64,384]{1,0:T(8,128)S(1)}, f32[64,384]{1,0:T(8,128)S(1)}, u32[]{:S(2)}, u32[]{:S(2)}) collective-permute-start(f32[64,384]{1,0:T(8,128)S(1)} %add.12._), channel_id=1, source_target_pairs={{0,3},{1,2},{2,1},{3,0},{4,7},{5,6},{6,5},{7,4},{8,11},{9,10},{10,... | collective-permute-start | bytes 294920 | tf_op jit(solution)/shard_map/ppermute | solution.py:311
  9.9 3.3 %collective-permute-start.2 = (f32[32,128]{1,0:T(8,128)S(1)}, f32[32,128]{1,0:T(8,128)S(1)}, u32[]{:S(2)}, u32[]{:S(2)}) collective-permute-start(f32[32,128]{1,0:T(8,128)S(1)} %get-tuple-element.53.mine), channel_id=1, source_target_pairs={{0,3},{1,2},{2,1},{3,0},{4,7},{5,6},{6,5},{7,4},{8,11},{9,10},{10,... | collective-permute-start | bytes 49160 | tf_op jit(solution)/shard_map/ppermute | solution.py:311
  13.5 4.2 %collective-permute-start.3 = (f32[32,384]{1,0:T(8,128)S(1)}, f32[32,384]{1,0:T(8,128)S(1)}, u32[]{:S(2)}, u32[]{:S(2)}) collective-permute-start(f32[32,384]{1,0:T(8,128)S(1)} %get-tuple-element.55), channel_id=1, source_target_pairs={{0,3},{1,2},{2,1},{3,0},{4,7},{5,6},{6,5},{7,4},{8,11},{9,10},{10,... | collective-permute-start | bytes 147464 | tf_op jit(solution)/shard_map/ppermute | solution.py:311
  15.3 8.8 %collective-permute-start.6 = (f32[64,384]{1,0:T(8,128)S(1)}, f32[64,384]{1,0:T(8,128)S(1)}, u32[]{:S(2)}, u32[]{:S(2)}) collective-permute-start(f32[64,384]{1,0:T(8,128)S(1)} %add.14.low), channel_id=1, source_target_pairs={{0,5},{1,4},{2,7},{3,6},{4,1},{5,0},{6,3},{7,2},{8,13},{9,12},{10,... | collective-permute-start | bytes 294920 | tf_op jit(solution)/shard_map/ppermute | solution.py:311
  17.7 7.4 %collective-permute-start.4 = (f32[32,384]{1,0:T(8,128)S(1)}, f32[32,384]{1,0:T(8,128)S(1)}, u32[]{:S(2)}, u32[]{:S(2)}) collective-permute-start(f32[32,384]{1,0:T(8,128)S(1)} %add.13.sums), channel_id=1, source_target_pairs={{0,5},{1,4},{2,7},{3,6},{4,1},{5,0},{6,3},{7,2},{8,13},{9,12},{10,... | collective-permute-start | bytes 147464 | tf_op jit(solution)/shard_map/ppermute | solution.py:311
  25.2 1.5 %collective-permute-start.7 = (f32[64,640]{1,0:T(8,128)S(1)}, f32[64,640]{1,0:T(8,128)S(1)}, u32[]{:S(2)}, u32[]{:S(2)}) collective-permute-start(f32[64,640]{1,0:T(8,128)S(1)} %get-tuple-element.58), channel_id=1, source_target_pairs={{0,1},{1,0},{2,3},{3,2},{4,5},{5,4},{6,7},{7,6},{8,9},{9,8},{10,11... | collective-permute-start | bytes 491528 | tf_op jit(solution)/shard_map/ppermute | solution.py:311
  26.8 4.8 %collective-permute-start.8 = (f32[32,768]{1,0:T(8,128)S(1)}, f32[32,768]{1,0:T(8,128)S(1)}, u32[]{:S(2)}, u32[]{:S(2)}) collective-permute-start(f32[32,768]{1,0:T(8,128)S(1)} %shard_map.80.packed), channel_id=1, source_target_pairs={{0,9},{1,8},{2,11},{3,10},{4,13},{5,12},{6,15},{7,14},{8,1},{9,0},... | collective-permute-start | bytes 294920 | tf_op jit(solution)/shard_map/ppermute | solution.py:311
  32.0 3.2 %collective-permute-start.10 = (f32[32,128]{1,0:T(8,128)S(1)}, f32[32,128]{1,0:T(8,128)S(1)}, u32[]{:S(2)}, u32[]{:S(2)}) collective-permute-start(f32[32,128]{1,0:T(8,128)S(1)} %get-tuple-element.67), channel_id=1, source_target_pairs={{0,17},{1,16},{2,19},{3,18},{4,21},{5,20},{6,23},{7,22},{8,25},{9,... | collective-permute-start | bytes 49160 | tf_op jit(solution)/shard_map/ppermute | solution.py:311
  33.3 2.1 %collective-permute-start.9 = (f32[32,768]{1,0:T(8,128)S(1)}, f32[32,768]{1,0:T(8,128)S(1)}, u32[]{:S(2)}, u32[]{:S(2)}) collective-permute-start(f32[32,768]{1,0:T(8,128)S(1)} %pad_maximum_fusion), channel_id=1, source_target_pairs={{0,1},{1,0},{2,3},{3,2},{4,5},{5,4},{6,7},{7,6},{8,9},{9,8},{10,11... | collective-permute-start | bytes 294920 | tf_op jit(solution)/shard_map/ppermute | solution.py:311
  35.2 1.3 %collective-permute-start.11 = (f32[32,256]{1,0:T(8,128)S(1)}, f32[32,256]{1,0:T(8,128)S(1)}, u32[]{:S(2)}, u32[]{:S(2)}) collective-permute-start(f32[32,256]{1,0:T(8,128)S(1)} %pad_maximum_fusion.1.mine), channel_id=1, source_target_pairs={{0,1},{1,0},{2,3},{3,2},{4,5},{5,4},{6,7},{7,6},{8,9},{9,8},{10,11... | collective-permute-start | bytes 98312 | tf_op jit(solution)/shard_map/ppermute | solution.py:311

commit v7 on v6

--- a/solution.py
+++ b/solution.py
@@ -45,7 +45,8 @@
 
 
 def low_kernel(
-    top, left, right, rhs, leaf, order, keep, send, left_v, right_v, rhs_v, leaf_v, order_v, sems,
+    top, left, right, rhs, leaf, order, keep, send, left_v, right_v, rhs_v, leaf_v, order_v,
+    left_mid, right_mid, sems,
 ):
     rank = left.shape[2]
     n = rank // 2
@@ -59,6 +60,10 @@
         pltpu.make_async_copy(order, order_v, sems.at[2, 1]),
         pltpu.make_async_copy(rhs, rhs_v, sems.at[2, 2]),
         pltpu.make_async_copy(leaf, leaf_v, sems.at[2, 3]),
+        pltpu.make_async_copy(left.at[top - 2], left_mid.at[:, :rank], sems.at[3, 0]),
+        pltpu.make_async_copy(left.at[top - 1], left_mid.at[:, rank:], sems.at[3, 1]),
+        pltpu.make_async_copy(right.at[top - 3], right_mid.at[:, :rank], sems.at[3, 2]),
+        pltpu.make_async_copy(right.at[top - 2], right_mid.at[:, rank:], sems.at[3, 3]),
     ]
     for copy in bases + rest:
         copy.start()
@@ -86,21 +91,17 @@
 
 
 def leaf_kernel(
-    top, order, split, rhs, leaf, right_low, left, right, coupling, current, gram_top, gram_next,
-    left_v, right_v, left_top, right_top, coupling_v, sems,
+    top, order, split, rhs, leaf, right_low, left_mid, right_mid, left, right, coupling, current,
+    gram_top, gram_next, left_first, right_last, left_top, right_top, coupling_v, sems,
 ):
     rank = left_top.shape[1]
     count, size = rhs.shape
     copies = [
-        pltpu.make_async_copy(left.at[top - 2], left_v.at[:, rank : 2 * rank], sems.at[0]),
-        pltpu.make_async_copy(left.at[top - 1], left_v.at[:, 2 * rank :], sems.at[1]),
-        pltpu.make_async_copy(right.at[top - 3], right_v.at[:, :rank], sems.at[2]),
-        pltpu.make_async_copy(right.at[top - 2], right_v.at[:, rank : 2 * rank], sems.at[3]),
-        pltpu.make_async_copy(right.at[top], right_top, sems.at[4]),
-        pltpu.make_async_copy(coupling.at[0], coupling_v, sems.at[5]),
-        pltpu.make_async_copy(left.at[top], left_top, sems.at[6]),
-        pltpu.make_async_copy(right.at[top - 1], right_v.at[:, 2 * rank :], sems.at[7]),
-        pltpu.make_async_copy(left.at[0], left_v.at[:, :rank], sems.at[8]),
+        pltpu.make_async_copy(right.at[top], right_top, sems.at[0]),
+        pltpu.make_async_copy(coupling.at[0], coupling_v, sems.at[1]),
+        pltpu.make_async_copy(left.at[top], left_top, sems.at[2]),
+        pltpu.make_async_copy(right.at[top - 1], right_last, sems.at[3]),
+        pltpu.make_async_copy(left.at[0], left_first, sems.at[4]),
     ]
     for copy in copies:
         copy.start()
@@ -112,17 +113,15 @@
     lh, ll = parts(jnp.where(rows == columns, leaf[...], 0.0))
     both = product(moved, lh, NN)
     current[...] = both[:count] + (both[count:] + product(moved[:count], ll, NN))
-    for copy in copies[:4]:
-        copy.wait()
     low_w = right_low.shape[1]
-    upper = left_v[:, rank:]
+    upper = left_mid[...]
     value = dot(upper, right_low[...], TN)
     gram_next[:, :low_w] = value[:rank]
     gram_top[:, :low_w] = value[rank:]
-    value = dot(upper, right_v[:, : 2 * rank], TN)
+    value = dot(upper, right_mid[...], TN)
     gram_next[:, low_w:] = value[:rank, :rank]
     gram_top[:, low_w:] = value[rank:]
-    for copy in copies[4:]:
+    for copy in copies:
         copy.wait()
 
 
@@ -142,8 +141,8 @@
 
 
 def local_kernel(
-    top, split, first, left_top, right_top, right_low, right_v, coupling, gram_top, gram_next, _,
-    current_out, keep, send,
+    top, split, first, left_top, right_top, right_low, right_mid, right_last, coupling, gram_top,
+    gram_next, _, current_out, keep, send,
 ):
     rank = left_top.shape[1]
     count, size = first.shape
@@ -160,7 +159,7 @@
     half = parity_of(lax.axis_index(AXES), top) == 1
     n = count // 2
     at = 0
-    for basis in (right_low, right_v):
+    for basis in (right_low, right_mid, right_last):
         sums = dot(current, basis[...])
         w = basis.shape[1]
         keep[:, at : at + w] = jnp.where(half, sums[n:], sums[:n])
@@ -207,13 +206,23 @@
     sums_out[...] = sums[...] - dot(z, gram)
 
 
-def merge_kernel(last, low, got, _, mine, rest):
-    lower = low.shape[1] - rest.shape[1]
-    rest[...] = low[:, lower:] + got[:, lower:]
-    mine[:, :lower] = low[:, :lower]
-    mine[:, lower : 2 * lower] = got[:, :lower]
-    if last:
-        mine[:, 2 * lower :] = rest[...]
+def joined(mine, other, top):
+    half = parity_of(lax.axis_index(AXES), top) == 1
+    return jnp.concatenate(
+        [jnp.where(half, other, mine), jnp.where(half, mine, other)], axis=0
+    )
+
+
+def add_kernel(low, got, _, out):
+    out[...] = low[...] + got[...]
+
+
+def cut_kernel(low, got, _, *out):
+    rank = out[0].shape[1]
+    w = (len(out) - 1) * rank
+    for j, piece in enumerate(out[:-1]):
+        piece[...] = got[:, j * rank : (j + 1) * rank]
+    out[-1][...] = low[:, w:] + got[:, w:]
 
 
 def couple_kernel(top, k, sums, got, coupling, both, z):
@@ -224,7 +233,8 @@
     z[...] = dot(both[...], coupling[k])
 
 
-def level_kernel(top, k, sums, got, z, low, got_low, rest, other, out, pair):
+def level_kernel(top, k, sums, got, z, low, got_low, other, *refs):
+    got_others, rests, (out, pair) = refs[:k], refs[k:-2], refs[-2:]
     n = low.shape[0]
     rank, w = 2 * n, k * 2 * n
     bit = top - 1 - k
@@ -232,20 +242,17 @@
     half = parity_of(device_id, top)
     right = (device_id >> bit) & 1
 
-    def put(child, mine, theirs):
-        pair[pl.ds(pl.multiple_of(child * rank + half * n, n), n), :] = mine
-        pair[pl.ds(pl.multiple_of(child * rank + (1 - half) * n, n), n), :] = theirs
-
-    put(right, low[:, :w], other[:, :w])
-    put(1 - right, got_low[:, :w], other[:, w : 2 * w])
+    def put(child, mine, theirs, cols):
+        pair[pl.ds(pl.multiple_of(child * rank + half * n, n), n), cols] = mine
+        pair[pl.ds(pl.multiple_of(child * rank + (1 - half) * n, n), n), cols] = theirs
+
+    for j in range(k):
+        cols = slice(j * rank, (j + 1) * rank)
+        put(right, low[:, cols], other[:, cols], cols)
+        put(1 - right, got_low[:, cols], got_others[j][...], cols)
     out[:, :w] = sums[:, :w] + got[:, :w] - dot(z[...], pair[...])
-    if k == 2:
-        mine, theirs = rest[...], other[:, 2 * w :]
-        is_upper = half == 1
-        gram = jnp.concatenate(
-            [jnp.where(is_upper, theirs, mine), jnp.where(is_upper, mine, theirs)], axis=0
-        )
-        put_rows(out, w, gram)
+    if rests:
+        put_rows(out, w, joined(rests[0][...], rests[1][...], top))
 
 
 def first_kernel(top, packed, got, coupling, out, both, pair):
@@ -260,16 +267,9 @@
     out[...] = packed[:, :rank] + got[:, :rank] - dot(z, pair[...])
 
 
-def joined(mine, other, top):
-    half = parity_of(lax.axis_index(AXES), top) == 1
-    return jnp.concatenate(
-        [jnp.where(half, other, mine), jnp.where(half, mine, other)], axis=0
-    )
-
-
 def early_kernel(top, current, *refs):
-    left_low, left_v, coupling, out, factor = refs[-5:]
-    rank = left_v.shape[1] // 3
+    left_first, left_low, left_mid, coupling, out, factor = refs[-6:]
+    rank = left_first.shape[1]
     device_id = lax.axis_index(AXES)
     z = []
     for k in range(1, top):
@@ -277,10 +277,10 @@
         right = (device_id >> (top - 1 - k)) & 1 == 1
         z.append(pair if k >= top - 2 else dot(pair, side_of(coupling, k, right)))
     low = dot(jnp.concatenate(z[: top - 3], axis=1), left_low[...], NT)
-    high = dot(jnp.concatenate(z[top - 3 :], axis=1), left_v[:, rank:], NT)
+    high = dot(jnp.concatenate(z[top - 3 :], axis=1), left_mid[...], NT)
     out[...] = current[...] - (low + high)
     right = (device_id >> (top - 1)) & 1 == 1
-    factor[...] = dot(side_of(coupling, 0, right), left_v[:, :rank], NT)
+    factor[...] = dot(side_of(coupling, 0, right), left_first[...], NT)
 
 
 def last_kernel(top, current, mine, other, factor, out):
@@ -322,7 +322,7 @@
     next_w = (top - 2) * rank
     device_id = lax.axis_index(AXES)
     split = leaf_split.reshape(1, 1)
-    keep, send, left_low, right_low, rhs, leaf, order = call(
+    keep, send, left_low, right_low, rhs, leaf, order, left_mid, right_mid = call(
         functools.partial(low_kernel, top),
         [
             shape(n, low_w),
@@ -332,33 +332,37 @@
             shape(count, size),
             shape(size, size),
             shape(1, size, dtype=jnp.int32),
+            shape(size, 2 * rank),
+            shape(size, 2 * rank),
         ],
         [HBM] * 5,
-        [VMEM] * 7,
-        [pltpu.SemaphoreType.DMA((3, max(4, top - 3)))],
+        [VMEM] * 9,
+        [pltpu.SemaphoreType.DMA((4, max(4, top - 3)))],
         *in_hbm(basis_left, basis_right, right_side, leaf_inverse, order.reshape(1, size)),
     )
     got_low = exchange(send, 1)
-    current, gram_top, gram_next, left, right, left_top, right_top, coup = call(
+    current, gram_top, gram_next, left_first, right_last, left_top, right_top, coup = call(
         functools.partial(leaf_kernel, top),
         [
             shape(count, size),
             shape(rank, wide - rank),
             shape(rank, next_w),
-            shape(size, 3 * rank),
-            shape(size, 3 * rank),
+            shape(size, rank),
+            shape(size, rank),
             shape(size, rank),
             shape(size, rank),
             shape(levels, 2 * rank, 2 * rank),
         ],
-        [VMEM] * 5 + [HBM] * 3,
+        [VMEM] * 7 + [HBM] * 3,
         [VMEM] * 8,
-        [pltpu.SemaphoreType.DMA((9,))],
+        [pltpu.SemaphoreType.DMA((5,))],
         order,
         split,
         rhs,
         leaf,
         right_low,
+        left_mid,
+        right_mid,
         *in_hbm(basis_left, basis_right, coupling),
     )
     low = keep + got_low
@@ -369,7 +373,7 @@
             shape(rows, wide),
             shape(rows, wide + rank // rows * (wide - rank + next_w)),
         ],
-        [VMEM] * 9 + [ANY],
+        [VMEM] * 10 + [ANY],
         [VMEM] * 3,
         [],
         split,
@@ -377,7 +381,8 @@
         left_top,
         right_top,
         right_low,
-        right,
+        right_mid,
+        right_last,
         coup,
         gram_top,
         gram_next,
@@ -397,6 +402,7 @@
     )
     known = {top - 1: (z_mine, z_other)}
     got_low = exchange(low, 3)
+    got_next = exchange(next_sums, 3)
     z, sums = call(
         functools.partial(next_kernel, top),
         [shape(rows, rank), shape(rows, next_w)],
@@ -404,14 +410,14 @@
         [VMEM] * 2,
         [],
         next_sums,
-        exchange(next_sums, 3),
+        got_next,
         sums,
         gram_next,
         got,
         coup,
     )
     known[top - 2] = (z, z)
-    low = low + got_low
+    low = call(add_kernel, shape(*low.shape), [VMEM, VMEM, ANY], VMEM, [], low, got_low, got_next)
     sums = sums + exchange(sums, 3)
     for k in range(top - 3, 1, -1):
         mask = 1 << (top - 1 - k) | 1
@@ -419,16 +425,19 @@
         last = k == 2
         got_low = exchange(low, mask)
         got = exchange(sums, mask)
-        mine, rest = call(
-            functools.partial(merge_kernel, last),
-            [shape(n, 2 * w + (rank if last else 0)), shape(n, low.shape[1] - w)],
+        others = exchange(low[:, :w], 1)
+        *pieces, rest = call(
+            cut_kernel,
+            [shape(n, rank)] * k + [shape(n, low.shape[1] - w)],
             [VMEM, VMEM, ANY],
-            [VMEM] * 2,
+            [VMEM] * (k + 1),
             [],
             low,
             got_low,
-            got,
+            sums,
         )
+        pieces = [exchange(piece, 1) for piece in pieces]
+        rests = [rest, exchange(rest, 1)] if last else []
         both, z = call(
             functools.partial(couple_kernel, top, k),
             [shape(rows, 2 * rank), shape(rows, 2 * rank)],
@@ -442,7 +451,7 @@
         sums = call(
             functools.partial(level_kernel, top, k),
             shape(rows, w + (rank // rows * rank if last else 0)),
-            [VMEM] * 7,
+            [VMEM] * (6 + k + len(rests)),
             VMEM,
             [pltpu.VMEM((2 * rank, w), F32)],
             sums,
@@ -450,8 +459,9 @@
             z,
             low,
             got_low,
-            rest,
-            exchange(mine, 1),
+            others,
+            *pieces,
+            *rests,
         )
         known[k] = (both, both)
         low = rest
@@ -477,13 +487,14 @@
     current, factor = call(
         functools.partial(early_kernel, top),
         [shape(count, size), shape(2 * rank, size)],
-        [VMEM] * (4 + len(args)),
+        [VMEM] * (5 + len(args)),
         [VMEM] * 2,
         [],
         current,
         *args,
+        left_first,
         left_low,
-        left,
+        left_mid,
         coup,
     )
     both = beside(sums, got_sums, (device_id >> (top - 1)) & 1 == 1)

time: 37.5 us -> 34.9 us (0.931)
  waiting for transfers between devices: 12.4 us -> 9.7 us
  Pallas kernels: 8.55 us -> 7.9 us
  starting transfers between devices: 15.6 us -> 16.2 us
    ppermute x12 -> x15, waiting for transfers between devices: 12.4 us -> 9.7 us  [exchange(): lax.ppermute(value, AXES, [(i, i ^ mask) for i in range(lax.axis_size(AXE...]
    ppermute x12 -> x15, starting transfers between devices: 15.6 us -> 16.2 us  [exchange(): lax.ppermute(value, AXES, [(i, i ^ mask) for i in range(lax.axis_size(AXE...]
    pallas_call x11 -> x12, Pallas kernels: 8.55 us -> 7.9 us  [call(): pl.pallas_call(kernel, out_shape=outs, in_specs=in_specs, out_specs=out_s...]
  transfers between devices with their start and end apart: 12 -> 15, of which waited for: 8 -> 6; matrix products, arithmetic and copies ran while one was open for 0% -> 0% of each run, Pallas kernels for 11% -> 10%
where the time goes in v7:
time: 34.9 us; the launch traced here: 34.7 us
  starting transfers between devices  16.2 us (46%)
  waiting for transfers between devices  9.7 us (28%)
  Pallas kernels  7.9 us (23%)
  between operations  0.8 us (2%)
    ppermute x15, starting transfers between devices, exchange(): lax.ppermute(value, AXES, [(i, i ^ mask) for i in range(lax.axis_size(AXE...  16.2 us
    ppermute x15, waiting for transfers between devices, exchange(): lax.ppermute(value, AXES, [(i, i ^ mask) for i in range(lax.axis_size(AXE...  9.7 us
    pallas_call x12, Pallas kernels, call(): pl.pallas_call(kernel, out_shape=outs, in_specs=in_specs, out_specs=out_s...  7.9 us
  transfers between devices with their start and end apart: 15, of which 6 were waited for; matrix products, arithmetic and copies ran while one was open for 0% of the time, Pallas kernels for 10%

profile of v7, /device:TPU:0, one launch (start us, length us, event | category | flops | bytes accessed | tf_op | source)
XLA Modules:
  0.0 34.7 jit_solution(13007010744053951915)
XLA Ops:
  0.0 2.0 %shard_map.73 = (f32[64,384]{1,0:T(8,128)S(1)}, f32[64,384]{1,0:T(8,128)S(1)}, f32[512,256]{1,0:T(8,128)S(1)}, f32[512,256]{1,0:T(8,128)S(1)}, f32[64,512]{1,0:T...) custom-call(f32[6,512,128]{2,1,0:T(8,128)} %left.3, ...), custom_call_target="tpu_custom_call" | custom-call | flops 1 | bytes 1 | tf_op jit(solution)/shard_map/pallas_call | solution.py:291
  2.0 0.5 %collective-permute-start = (f32[64,384]{1,0:T(8,128)S(1)}, f32[64,384]{1,0:T(8,128)S(1)}, u32[]{:S(2)}, u32[]{:S(2)}) collective-permute-start(f32[64,384]{1,0:T(8,128)S(1)} %get-tuple-element.54), channel_id=1, source_target_pairs={{0,1},{1,0},{2,3},{3,2},{4,5},{5,4},{6,7},{7,6},{8,9},{9,8},{10,11... | collective-permute-start | bytes 294920 | tf_op jit(solution)/shard_map/ppermute | solution.py:311
  3.2 1.7 %shard_map.74 = (f32[64,512]{1,0:T(8,128)S(1)}, f32[128,512]{1,0:T(8,128)S(1)}, f32[128,384]{1,0:T(8,128)S(1)}, f32[512,128]{1,0:T(8,128)S(1)}, f32[512,128]{1,0...) custom-call(s32[1,512]{1,0:T(1,128)S(1)} %get-tuple-element.40.order, ...), custom_call_target="tpu_custom_call" | custom-call | flops 1 | bytes 1 | tf_op jit(solution)/shard_map/pallas_call | solution.py:291
  4.9 0.0 collective-permute-done
  5.0 1.1 %shard_map.75 = (f32[64,512]{1,0:T(8,128)S(1)}, f32[32,640]{1,0:T(8,128)S(1)}, f32[32,4224]{1,0:T(8,128)S(1)}) custom-call(s32[1,1]{1,0:T(1,128)} %bitcast.3.split, f32[64,512]{1,0:T(8,128)S(1)} %get-tuple-element.46.first, f32[512,128]{1,0:T(8,128)S(1)} %get-tuple-element.47.left_top, f32[512,128]{1,0:T(8,128)S(1)} %get-tuple-element.48.right_top, ...), custom_call_target="tpu_custom_call" | custom-call | flops 1 | bytes 1 | tf_op jit(solution)/shard_map/pallas_call | solution.py:291
  6.0 0.1 collective-permute-start.1
  6.1 2.7 %collective-permute-start.5 = (f32[64,384]{1,0:T(8,128)S(1)}, f32[64,384]{1,0:T(8,128)S(1)}, u32[]{:S(2)}, u32[]{:S(2)}) collective-permute-start(f32[64,384]{1,0:T(8,128)S(1)} %add.9._.low), channel_id=1, source_target_pairs={{0,3},{1,2},{2,1},{3,0},{4,7},{5,6},{6,5},{7,4},{8,11},{9,10},{10,... | collective-permute-start | bytes 294920 | tf_op jit(solution)/shard_map/ppermute | solution.py:311
  8.8 0.0 collective-permute-done.1.got.got_gram
  8.8 0.4 %shard_map.76 = (f32[32,384]{1,0:T(8,128)S(1)}, f32[32,128]{1,0:T(8,128)S(1)}, f32[32,128]{1,0:T(8,128)S(1)}, f32[32,128]{1,0:T(8,128)S(1)}) custom-call(f32[32,640]{1,0:T(8,128)S(1)} %get-tuple-element.56.keep, f32[32,4224]{1,0:T(8,128)S(1)} %collective-permute-done.1.got.got_gram, f32[128,512]{1,0:T(8,128)S(1)} %get-tuple-element.51.gram_top, ...), custom_call_target="tpu_custom_call" | custom-call | flops 1 | bytes 1 | tf_op jit(solution)/shard_map/pallas_call | solution.py:291
  9.2 1.9 %collective-permute-start.2 = (f32[32,128]{1,0:T(8,128)S(1)}, f32[32,128]{1,0:T(8,128)S(1)}, u32[]{:S(2)}, u32[]{:S(2)}) collective-permute-start(f32[32,128]{1,0:T(8,128)S(1)} %get-tuple-element.58.mine), channel_id=1, source_target_pairs={{0,3},{1,2},{2,1},{3,0},{4,7},{5,6},{6,5},{7,4},{8,11},{9,10},{10,... | collective-permute-start | bytes 49160 | tf_op jit(solution)/shard_map/ppermute | solution.py:311
  11.1 0.6 %collective-permute-done.5.got = f32[64,384]{1,0:T(8,128)S(1)} collective-permute-done((f32[64,384]{1,0:T(8,128)S(1)}, f32[64,384]{1,0:T(8,128)S(1)}, u32[]{:S(2)}, u32[]{:S(2)}) %collective-permute-start.5) | collective-permute-done | bytes 98336 | tf_op jit(solution)/shard_map/ppermute | solution.py:311
  11.8 0.8 %collective-permute-done.2.got._ = f32[32,128]{1,0:T(8,128)S(1)} collective-permute-done((f32[32,128]{1,0:T(8,128)S(1)}, f32[32,128]{1,0:T(8,128)S(1)}, u32[]{:S(2)}, u32[]{:S(2)}) %collective-permute-start.2) | collective-permute-done | bytes 16416 | tf_op jit(solution)/shard_map/ppermute | solution.py:311
  12.6 2.8 %collective-permute-start.6 = (f32[64,384]{1,0:T(8,128)S(1)}, f32[64,384]{1,0:T(8,128)S(1)}, u32[]{:S(2)}, u32[]{:S(2)}) collective-permute-start(f32[64,384]{1,0:T(8,128)S(1)} %shard_map.79.low), channel_id=1, source_target_pairs={{0,5},{1,4},{2,7},{3,6},{4,1},{5,0},{6,3},{7,2},{8,13},{9,12},{10,... | collective-permute-start | bytes 294920 | tf_op jit(solution)/shard_map/ppermute | solution.py:311
  15.4 0.3 shard_map.77
  15.7 1.5 %collective-permute-start.3 = (f32[32,384]{1,0:T(8,128)S(1)}, f32[32,384]{1,0:T(8,128)S(1)}, u32[]{:S(2)}, u32[]{:S(2)}) collective-permute-start(f32[32,384]{1,0:T(8,128)S(1)} %get-tuple-element.60), channel_id=1, source_target_pairs={{0,3},{1,2},{2,1},{3,0},{4,7},{5,6},{6,5},{7,4},{8,11},{9,10},{10,... | collective-permute-start | bytes 147464 | tf_op jit(solution)/shard_map/ppermute | solution.py:311
  17.1 0.3 collective-permute-start.7
  17.4 2.0 %collective-permute-done.3 = f32[32,384]{1,0:T(8,128)S(1)} collective-permute-done((f32[32,384]{1,0:T(8,128)S(1)}, f32[32,384]{1,0:T(8,128)S(1)}, u32[]{:S(2)}, u32[]{:S(2)}) %collective-permute-start.3) | collective-permute-done | bytes 49184 | tf_op jit(solution)/shard_map/ppermute | solution.py:311
  19.4 1.7 %collective-permute-start.4 = (f32[32,384]{1,0:T(8,128)S(1)}, f32[32,384]{1,0:T(8,128)S(1)}, u32[]{:S(2)}, u32[]{:S(2)}) collective-permute-start(f32[32,384]{1,0:T(8,128)S(1)} %add.10.sums._), channel_id=1, source_target_pairs={{0,5},{1,4},{2,7},{3,6},{4,1},{5,0},{6,3},{7,2},{8,13},{9,12},{10,... | collective-permute-start | bytes 147464 | tf_op jit(solution)/shard_map/ppermute | solution.py:311
  21.1 0.0 collective-permute-done.6.got.got_low
  21.1 0.4 %collective-permute-start.10 = (f32[64,128]{1,0:T(8,128)S(1)}, f32[64,128]{1,0:T(8,128)S(1)}, u32[]{:S(2)}, u32[]{:S(2)}) collective-permute-start(f32[64,128]{1,0:T(8,128)S(1)} %get-tuple-element.64.refs_2_), channel_id=1, source_target_pairs={{0,1},{1,0},{2,3},{3,2},{4,5},{5,4},{6,7},{7,6},{8,9},{9,8},{10,11... | collective-permute-start | bytes 98312 | tf_op jit(solution)/shard_map/ppermute | solution.py:311
  21.5 0.2 collective-permute-start.8
  21.7 0.3 collective-permute-start.9
  22.0 1.8 %collective-permute-done.4.got = f32[32,384]{1,0:T(8,128)S(1)} collective-permute-done((f32[32,384]{1,0:T(8,128)S(1)}, f32[32,384]{1,0:T(8,128)S(1)}, u32[]{:S(2)}, u32[]{:S(2)}) %collective-permute-start.4) | collective-permute-done | bytes 49184 | tf_op jit(solution)/shard_map/ppermute | solution.py:311
  23.9 0.2 shard_map.78
  24.0 0.0 collective-permute-done.7.other
  24.0 0.0 collective-permute-done.10.refs_3_
  24.1 0.0 collective-permute-done.8.refs_0_
  24.1 0.0 collective-permute-done.9.refs_1_
  24.1 0.2 shard_map.81.packed
  24.3 1.6 %collective-permute-start.11 = (f32[32,768]{1,0:T(8,128)S(1)}, f32[32,768]{1,0:T(8,128)S(1)}, u32[]{:S(2)}, u32[]{:S(2)}) collective-permute-start(f32[32,768]{1,0:T(8,128)S(1)} %shard_map.81.packed), channel_id=1, source_target_pairs={{0,9},{1,8},{2,11},{3,10},{4,13},{5,12},{6,15},{7,14},{8,1},{9,0},... | collective-permute-start | bytes 294920 | tf_op jit(solution)/shard_map/ppermute | solution.py:311
  25.9 2.9 %collective-permute-done.11.got = f32[32,768]{1,0:T(8,128)S(1)} collective-permute-done((f32[32,768]{1,0:T(8,128)S(1)}, f32[32,768]{1,0:T(8,128)S(1)}, u32[]{:S(2)}, u32[]{:S(2)}) %collective-permute-start.11) | collective-permute-done | bytes 98336 | tf_op jit(solution)/shard_map/ppermute | solution.py:311
  28.8 0.3 shard_map.82
  29.2 1.6 %collective-permute-start.13 = (f32[32,128]{1,0:T(8,128)S(1)}, f32[32,128]{1,0:T(8,128)S(1)}, u32[]{:S(2)}, u32[]{:S(2)}) collective-permute-start(f32[32,128]{1,0:T(8,128)S(1)} %get-tuple-element.73), channel_id=1, source_target_pairs={{0,17},{1,16},{2,19},{3,18},{4,21},{5,20},{6,23},{7,22},{8,25},{9,... | collective-permute-start | bytes 49160 | tf_op jit(solution)/shard_map/ppermute | solution.py:311
  30.8 0.1 collective-permute-start.12
  31.0 1.5 %collective-permute-done.13 = f32[32,128]{1,0:T(8,128)S(1)} collective-permute-done((f32[32,128]{1,0:T(8,128)S(1)}, f32[32,128]{1,0:T(8,128)S(1)}, u32[]{:S(2)}, u32[]{:S(2)}) %collective-permute-start.13) | collective-permute-done | bytes 16416 | tf_op jit(solution)/shard_map/ppermute | solution.py:311
  32.4 0.5 %collective-permute-start.14 = (f32[32,256]{1,0:T(8,128)S(1)}, f32[32,256]{1,0:T(8,128)S(1)}, u32[]{:S(2)}, u32[]{:S(2)}) collective-permute-start(f32[32,256]{1,0:T(8,128)S(1)} %pad_maximum_fusion.1.mine), channel_id=1, source_target_pairs={{0,1},{1,0},{2,3},{3,2},{4,5},{5,4},{6,7},{7,6},{8,9},{9,8},{10,11... | collective-permute-start | bytes 98312 | tf_op jit(solution)/shard_map/ppermute | solution.py:311
  32.9 0.0 collective-permute-done.12
  32.9 0.8 %shard_map.83 = (f32[64,512]{1,0:T(8,128)S(1)}, f32[256,512]{1,0:T(8,128)S(1)}) custom-call(f32[64,512]{1,0:T(8,128)S(1)} %get-tuple-element.55.current, f32[32,256]{1,0:T(8,128)S(1)} %get-tuple-element.65.refs_0_, f32[32,256]{1,0:T(8,128)S(1)} %get-tuple-element.78.refs_1_, f32[32,256]{1,0:T(8,128)S(1)} %get-tuple-element.66.refs_2_, ...), custom_call_target="tpu_custom_call" | custom-call | flops 1 | bytes 1 | tf_op jit(solution)/shard_map/pallas_call | solution.py:291
  33.8 0.0 collective-permute-done.14.other
  33.8 0.9 %shard_map.84 = f32[64,512]{1,0:T(8,128)} custom-call(f32[64,512]{1,0:T(8,128)S(1)} %get-tuple-element.72.current, f32[32,256]{1,0:T(8,128)S(1)} %pad_maximum_fusion.1.mine, f32[32,256]{1,0:T(8,128)S(1)} %collective-permute-done.14.other, f32[256,512]{1,0:T(8,128)S(1)} %get-tuple-element.74.factor), custom_call_target="tpu_custom_call" | custom-call | flops 1 | bytes 1 | tf_op jit(solution)/shard_map/pallas_call | solution.py:291
  (10 shorter events, 0.1 us)
Async XLA Ops:
  2.0 2.9 %collective-permute-start = (f32[64,384]{1,0:T(8,128)S(1)}, f32[64,384]{1,0:T(8,128)S(1)}, u32[]{:S(2)}, u32[]{:S(2)}) collective-permute-start(f32[64,384]{1,0:T(8,128)S(1)} %get-tuple-element.54), channel_id=1, source_target_pairs={{0,1},{1,0},{2,3},{3,2},{4,5},{5,4},{6,7},{7,6},{8,9},{9,8},{10,11... | collective-permute-start | bytes 294920 | tf_op jit(solution)/shard_map/ppermute | solution.py:311
  6.0 2.8 %collective-permute-start.1 = (f32[32,4224]{1,0:T(8,128)S(1)}, f32[32,4224]{1,0:T(8,128)S(1)}, u32[]{:S(2)}, u32[]{:S(2)}) collective-permute-start(f32[32,4224]{1,0:T(8,128)S(1)} %get-tuple-element.57), channel_id=1, source_target_pairs={{0,1},{1,0},{2,3},{3,2},{4,5},{5,4},{6,7},{7,6},{8,9},{9,8},{10,11... | collective-permute-start | bytes 1622024 | tf_op jit(solution)/shard_map/ppermute | solution.py:311
  6.1 5.6 %collective-permute-start.5 = (f32[64,384]{1,0:T(8,128)S(1)}, f32[64,384]{1,0:T(8,128)S(1)}, u32[]{:S(2)}, u32[]{:S(2)}) collective-permute-start(f32[64,384]{1,0:T(8,128)S(1)} %add.9._.low), channel_id=1, source_target_pairs={{0,3},{1,2},{2,1},{3,0},{4,7},{5,6},{6,5},{7,4},{8,11},{9,10},{10,... | collective-permute-start | bytes 294920 | tf_op jit(solution)/shard_map/ppermute | solution.py:311
  9.2 3.3 %collective-permute-start.2 = (f32[32,128]{1,0:T(8,128)S(1)}, f32[32,128]{1,0:T(8,128)S(1)}, u32[]{:S(2)}, u32[]{:S(2)}) collective-permute-start(f32[32,128]{1,0:T(8,128)S(1)} %get-tuple-element.58.mine), channel_id=1, source_target_pairs={{0,3},{1,2},{2,1},{3,0},{4,7},{5,6},{6,5},{7,4},{8,11},{9,10},{10,... | collective-permute-start | bytes 49160 | tf_op jit(solution)/shard_map/ppermute | solution.py:311
  12.6 8.5 %collective-permute-start.6 = (f32[64,384]{1,0:T(8,128)S(1)}, f32[64,384]{1,0:T(8,128)S(1)}, u32[]{:S(2)}, u32[]{:S(2)}) collective-permute-start(f32[64,384]{1,0:T(8,128)S(1)} %shard_map.79.low), channel_id=1, source_target_pairs={{0,5},{1,4},{2,7},{3,6},{4,1},{5,0},{6,3},{7,2},{8,13},{9,12},{10,... | collective-permute-start | bytes 294920 | tf_op jit(solution)/shard_map/ppermute | solution.py:311
  15.7 3.7 %collective-permute-start.3 = (f32[32,384]{1,0:T(8,128)S(1)}, f32[32,384]{1,0:T(8,128)S(1)}, u32[]{:S(2)}, u32[]{:S(2)}) collective-permute-start(f32[32,384]{1,0:T(8,128)S(1)} %get-tuple-element.60), channel_id=1, source_target_pairs={{0,3},{1,2},{2,1},{3,0},{4,7},{5,6},{6,5},{7,4},{8,11},{9,10},{10,... | collective-permute-start | bytes 147464 | tf_op jit(solution)/shard_map/ppermute | solution.py:311
  17.1 6.9 %collective-permute-start.7 = (f32[64,256]{1,0:T(8,128)S(1)}, f32[64,256]{1,0:T(8,128)S(1)}, u32[]{:S(2)}, u32[]{:S(2)}) collective-permute-start(f32[64,256]{1,0:T(8,128)S(1)} %slice.20), channel_id=1, source_target_pairs={{0,1},{1,0},{2,3},{3,2},{4,5},{5,4},{6,7},{7,6},{8,9},{9,8},{10,11... | collective-permute-start | bytes 196616 | tf_op jit(solution)/shard_map/ppermute | solution.py:311
  19.4 4.5 %collective-permute-start.4 = (f32[32,384]{1,0:T(8,128)S(1)}, f32[32,384]{1,0:T(8,128)S(1)}, u32[]{:S(2)}, u32[]{:S(2)}) collective-permute-start(f32[32,384]{1,0:T(8,128)S(1)} %add.10.sums._), channel_id=1, source_target_pairs={{0,5},{1,4},{2,7},{3,6},{4,1},{5,0},{6,3},{7,2},{8,13},{9,12},{10,... | collective-permute-start | bytes 147464 | tf_op jit(solution)/shard_map/ppermute | solution.py:311
  21.1 2.9 %collective-permute-start.10 = (f32[64,128]{1,0:T(8,128)S(1)}, f32[64,128]{1,0:T(8,128)S(1)}, u32[]{:S(2)}, u32[]{:S(2)}) collective-permute-start(f32[64,128]{1,0:T(8,128)S(1)} %get-tuple-element.64.refs_2_), channel_id=1, source_target_pairs={{0,1},{1,0},{2,3},{3,2},{4,5},{5,4},{6,7},{7,6},{8,9},{9,8},{10,11... | collective-permute-start | bytes 98312 | tf_op jit(solution)/shard_map/ppermute | solution.py:311
  21.5 2.5 %collective-permute-start.8 = (f32[64,128]{1,0:T(8,128)S(1)}, f32[64,128]{1,0:T(8,128)S(1)}, u32[]{:S(2)}, u32[]{:S(2)}) collective-permute-start(f32[64,128]{1,0:T(8,128)S(1)} %get-tuple-element.62), channel_id=1, source_target_pairs={{0,1},{1,0},{2,3},{3,2},{4,5},{5,4},{6,7},{7,6},{8,9},{9,8},{10,11... | collective-permute-start | bytes 98312 | tf_op jit(solution)/shard_map/ppermute | solution.py:311
  21.7 2.4 %collective-permute-start.9 = (f32[64,128]{1,0:T(8,128)S(1)}, f32[64,128]{1,0:T(8,128)S(1)}, u32[]{:S(2)}, u32[]{:S(2)}) collective-permute-start(f32[64,128]{1,0:T(8,128)S(1)} %get-tuple-element.63), channel_id=1, source_target_pairs={{0,1},{1,0},{2,3},{3,2},{4,5},{5,4},{6,7},{7,6},{8,9},{9,8},{10,11... | collective-permute-start | bytes 98312 | tf_op jit(solution)/shard_map/ppermute | solution.py:311
  24.3 4.6 %collective-permute-start.11 = (f32[32,768]{1,0:T(8,128)S(1)}, f32[32,768]{1,0:T(8,128)S(1)}, u32[]{:S(2)}, u32[]{:S(2)}) collective-permute-start(f32[32,768]{1,0:T(8,128)S(1)} %shard_map.81.packed), channel_id=1, source_target_pairs={{0,9},{1,8},{2,11},{3,10},{4,13},{5,12},{6,15},{7,14},{8,1},{9,0},... | collective-permute-start | bytes 294920 | tf_op jit(solution)/shard_map/ppermute | solution.py:311
  29.2 3.2 %collective-permute-start.13 = (f32[32,128]{1,0:T(8,128)S(1)}, f32[32,128]{1,0:T(8,128)S(1)}, u32[]{:S(2)}, u32[]{:S(2)}) collective-permute-start(f32[32,128]{1,0:T(8,128)S(1)} %get-tuple-element.73), channel_id=1, source_target_pairs={{0,17},{1,16},{2,19},{3,18},{4,21},{5,20},{6,23},{7,22},{8,25},{9,... | collective-permute-start | bytes 49160 | tf_op jit(solution)/shard_map/ppermute | solution.py:311
  30.8 2.1 %collective-permute-start.12 = (f32[32,768]{1,0:T(8,128)S(1)}, f32[32,768]{1,0:T(8,128)S(1)}, u32[]{:S(2)}, u32[]{:S(2)}) collective-permute-start(f32[32,768]{1,0:T(8,128)S(1)} %pad_maximum_fusion), channel_id=1, source_target_pairs={{0,1},{1,0},{2,3},{3,2},{4,5},{5,4},{6,7},{7,6},{8,9},{9,8},{10,11... | collective-permute-start | bytes 294920 | tf_op jit(solution)/shard_map/ppermute | solution.py:311
  32.4 1.4 %collective-permute-start.14 = (f32[32,256]{1,0:T(8,128)S(1)}, f32[32,256]{1,0:T(8,128)S(1)}, u32[]{:S(2)}, u32[]{:S(2)}) collective-permute-start(f32[32,256]{1,0:T(8,128)S(1)} %pad_maximum_fusion.1.mine), channel_id=1, source_target_pairs={{0,1},{1,0},{2,3},{3,2},{4,5},{5,4},{6,7},{7,6},{8,9},{9,8},{10,11... | collective-permute-start | bytes 98312 | tf_op jit(solution)/shard_map/ppermute | solution.py:311

commit v8 on v7

--- a/solution.py
+++ b/solution.py
@@ -92,16 +92,15 @@
 
 def leaf_kernel(
     top, order, split, rhs, leaf, right_low, left_mid, right_mid, left, right, coupling, current,
-    gram_top, gram_next, left_first, right_last, left_top, right_top, coupling_v, sems,
+    gram_top, gram_next, right_last, left_top, right_top, coupling_v, sems,
 ):
     rank = left_top.shape[1]
     count, size = rhs.shape
     copies = [
         pltpu.make_async_copy(right.at[top], right_top, sems.at[0]),
-        pltpu.make_async_copy(coupling.at[0], coupling_v, sems.at[1]),
+        pltpu.make_async_copy(coupling.at[0, pl.ds(top - 2, 3)], coupling_v, sems.at[1]),
         pltpu.make_async_copy(left.at[top], left_top, sems.at[2]),
         pltpu.make_async_copy(right.at[top - 1], right_last, sems.at[3]),
-        pltpu.make_async_copy(left.at[0], left_first, sems.at[4]),
     ]
     for copy in copies:
         copy.start()
@@ -125,6 +124,17 @@
         copy.wait()
 
 
+def fetch_kernel(top, left, coupling, _, left_first, coupling_v, sems):
+    copies = [
+        pltpu.make_async_copy(coupling.at[0, pl.ds(0, top - 2)], coupling_v, sems.at[0]),
+        pltpu.make_async_copy(left.at[0], left_first, sems.at[1]),
+    ]
+    for copy in copies:
+        copy.start()
+    for copy in copies:
+        copy.wait()
+
+
 def put_rows(out, at, value):
     rows, w = out.shape[0], value.shape[1]
     for row in range(0, value.shape[0], rows):
@@ -152,7 +162,7 @@
         [jnp.where(is_left, current, 0.0), jnp.where(is_left, 0.0, current)], axis=0
     )
     w = dot(halves, right_top[...])
-    z = dot(jnp.concatenate([w[:count], w[count:]], axis=1), coupling[top])
+    z = dot(jnp.concatenate([w[:count], w[count:]], axis=1), coupling[2])
     update = dot(jnp.concatenate([z[:, :rank], z[:, rank:]], axis=0), left_top[...], NT)
     current = current - jnp.where(is_left, update[:count], update[count:])
     current_out[...] = current
@@ -183,7 +193,7 @@
     pair[pl.ds(pl.multiple_of(own_at, rank), rank), :] = gram_top[...]
     pair[pl.ds(pl.multiple_of(got_at, rank), rank), :] = take_rows(got, top * rank, rank, w)
     is_right = right == 1
-    z = dot(beside(keep[:, w:], got[:, w : top * rank], is_right), coupling[top - 1])
+    z = dot(beside(keep[:, w:], got[:, w : top * rank], is_right), coupling[1])
     value = keep[:, :w] + got[:, :w] - dot(z, pair[...])
     sums[...] = value[:, : w - rank]
     next_sums[...] = value[:, w - rank :]
@@ -199,7 +209,7 @@
 def next_kernel(top, mine, got, sums, gram_next, got_gram, coupling, z_out, sums_out):
     rank, w = gram_next.shape
     right = (lax.axis_index(AXES) >> 1) & 1 == 1
-    z = dot(beside(mine[...], got[...], right), side_of(coupling, top - 2, right))
+    z = dot(beside(mine[...], got[...], right), side_of(coupling, 0, right))
     at = top * rank + rank // got_gram.shape[0] * (w + rank)
     gram = gram_next[...] + take_rows(got_gram, at, rank, w)
     z_out[...] = z
@@ -341,7 +351,7 @@
         *in_hbm(basis_left, basis_right, right_side, leaf_inverse, order.reshape(1, size)),
     )
     got_low = exchange(send, 1)
-    current, gram_top, gram_next, left_first, right_last, left_top, right_top, coup = call(
+    current, gram_top, gram_next, right_last, left_top, right_top, near = call(
         functools.partial(leaf_kernel, top),
         [
             shape(count, size),
@@ -350,11 +360,10 @@
             shape(size, rank),
             shape(size, rank),
             shape(size, rank),
-            shape(size, rank),
-            shape(levels, 2 * rank, 2 * rank),
+            shape(3, 2 * rank, 2 * rank),
         ],
         [VMEM] * 7 + [HBM] * 3,
-        [VMEM] * 8,
+        [VMEM] * 7,
         [pltpu.SemaphoreType.DMA((5,))],
         order,
         split,
@@ -383,7 +392,7 @@
         right_low,
         right_mid,
         right_last,
-        coup,
+        near,
         gram_top,
         gram_next,
         low,
@@ -398,7 +407,7 @@
         keep,
         got,
         gram_top,
-        coup,
+        near,
     )
     known = {top - 1: (z_mine, z_other)}
     got_low = exchange(low, 3)
@@ -414,11 +423,20 @@
         sums,
         gram_next,
         got,
-        coup,
+        near,
     )
     known[top - 2] = (z, z)
     low = call(add_kernel, shape(*low.shape), [VMEM, VMEM, ANY], VMEM, [], low, got_low, got_next)
     sums = sums + exchange(sums, 3)
+    left_first, coup = call(
+        functools.partial(fetch_kernel, top),
+        [shape(size, rank), shape(top - 2, 2 * rank, 2 * rank)],
+        [HBM] * 2 + [ANY],
+        [VMEM] * 2,
+        [pltpu.SemaphoreType.DMA((2,))],
+        *in_hbm(basis_left, coupling),
+        sums,
+    )
     for k in range(top - 3, 1, -1):
         mask = 1 << (top - 1 - k) | 1
         w = k * rank
@@ -434,7 +452,7 @@
             [],
             low,
             got_low,
-            sums,
+            coup,
         )
         pieces = [exchange(piece, 1) for piece in pieces]
         rests = [rest, exchange(rest, 1)] if last else []

time: 34.9 us -> 34.6 us (level)
  waiting for transfers between devices: 9.7 us -> 8.61 us
  Pallas kernels: 7.9 us -> 8.83 us
    ppermute x15, waiting for transfers between devices: 9.7 us -> 8.61 us  [exchange(): lax.ppermute(value, AXES, [(i, i ^ mask) for i in range(lax.axis_size(AXE...]
    pallas_call x12 -> x13, Pallas kernels: 7.9 us -> 8.83 us  [call(): pl.pallas_call(kernel, out_shape=outs, in_specs=in_specs, out_specs=out_s...]
  transfers between devices with their start and end apart: 15 -> 15, of which waited for: 6 -> 7; matrix products, arithmetic and copies ran while one was open for 0% -> 0% of each run, Pallas kernels for 10% -> 12%
where the time goes in v8:
time: 34.6 us; the launch traced here: 34.5 us
  starting transfers between devices  16.2 us (47%)
  Pallas kernels  8.83 us (26%)
  waiting for transfers between devices  8.61 us (25%)
  between operations  0.81 us (2%)
    ppermute x15, starting transfers between devices, exchange(): lax.ppermute(value, AXES, [(i, i ^ mask) for i in range(lax.axis_size(AXE...  16.2 us
    pallas_call x13, Pallas kernels, call(): pl.pallas_call(kernel, out_shape=outs, in_specs=in_specs, out_specs=out_s...  8.83 us
    ppermute x15, waiting for transfers between devices, exchange(): lax.ppermute(value, AXES, [(i, i ^ mask) for i in range(lax.axis_size(AXE...  8.61 us
  transfers between devices with their start and end apart: 15, of which 7 were waited for; matrix products, arithmetic and copies ran while one was open for 0% of the time, Pallas kernels for 12%

profile of v8, /device:TPU:0, one launch (start us, length us, event | category | flops | bytes accessed | tf_op | source)
XLA Modules:
  0.0 34.5 jit_solution(13461529757174960135)
XLA Ops:
  0.0 2.0 %shard_map.73 = (f32[64,384]{1,0:T(8,128)S(1)}, f32[64,384]{1,0:T(8,128)S(1)}, f32[512,256]{1,0:T(8,128)S(1)}, f32[512,256]{1,0:T(8,128)S(1)}, f32[64,512]{1,0:T...) custom-call(f32[6,512,128]{2,1,0:T(8,128)} %left.5, ...), custom_call_target="tpu_custom_call" | custom-call | flops 1 | bytes 1 | tf_op jit(solution)/shard_map/pallas_call | solution.py:301
  2.0 0.5 %collective-permute-start = (f32[64,384]{1,0:T(8,128)S(1)}, f32[64,384]{1,0:T(8,128)S(1)}, u32[]{:S(2)}, u32[]{:S(2)}) collective-permute-start(f32[64,384]{1,0:T(8,128)S(1)} %get-tuple-element.55), channel_id=1, source_target_pairs={{0,1},{1,0},{2,3},{3,2},{4,5},{5,4},{6,7},{7,6},{8,9},{9,8},{10,11... | collective-permute-start | bytes 294920 | tf_op jit(solution)/shard_map/ppermute | solution.py:321
  3.2 1.4 %shard_map.74 = (f32[64,512]{1,0:T(8,128)S(1)}, f32[128,512]{1,0:T(8,128)S(1)}, f32[128,384]{1,0:T(8,128)S(1)}, f32[512,128]{1,0:T(8,128)S(1)}, f32[512,128]{1,0...) custom-call(s32[1,512]{1,0:T(1,128)S(1)} %get-tuple-element.41.order, s32[1,1]{1,0:T(1,128)} %bitcast.2.split, ...), custom_call_target="tpu_custom_call" | custom-call | flops 1 | bytes 1 | tf_op jit(solution)/shard_map/pallas_call | solution.py:301
  4.6 0.0 collective-permute-done
  4.6 1.1 %shard_map.75 = (f32[64,512]{1,0:T(8,128)S(1)}, f32[32,640]{1,0:T(8,128)S(1)}, f32[32,4224]{1,0:T(8,128)S(1)}) custom-call(s32[1,1]{1,0:T(1,128)} %bitcast.3.split, f32[64,512]{1,0:T(8,128)S(1)} %get-tuple-element.47.first, f32[512,128]{1,0:T(8,128)S(1)} %get-tuple-element.48.left_top, f32[512,128]{1,0:T(8,128)S(1)} %get-tuple-element.49.right_top, ...), custom_call_target="tpu_custom_call" | custom-call | flops 1 | bytes 1 | tf_op jit(solution)/shard_map/pallas_call | solution.py:301
  5.8 0.1 collective-permute-start.1
  5.9 2.7 %collective-permute-start.5 = (f32[64,384]{1,0:T(8,128)S(1)}, f32[64,384]{1,0:T(8,128)S(1)}, u32[]{:S(2)}, u32[]{:S(2)}) collective-permute-start(f32[64,384]{1,0:T(8,128)S(1)} %add.9._.low), channel_id=1, source_target_pairs={{0,3},{1,2},{2,1},{3,0},{4,7},{5,6},{6,5},{7,4},{8,11},{9,10},{10,... | collective-permute-start | bytes 294920 | tf_op jit(solution)/shard_map/ppermute | solution.py:321
  8.6 0.0 collective-permute-done.1.got.got_gram
  8.6 0.4 %shard_map.76 = (f32[32,384]{1,0:T(8,128)S(1)}, f32[32,128]{1,0:T(8,128)S(1)}, f32[32,128]{1,0:T(8,128)S(1)}, f32[32,128]{1,0:T(8,128)S(1)}) custom-call(f32[32,640]{1,0:T(8,128)S(1)} %get-tuple-element.57.keep, f32[32,4224]{1,0:T(8,128)S(1)} %collective-permute-done.1.got.got_gram, f32[128,512]{1,0:T(8,128)S(1)} %get-tuple-element.52.gram_top, ...), custom_call_target="tpu_custom_call" | custom-call | flops 1 | bytes 1 | tf_op jit(solution)/shard_map/pallas_call | solution.py:301
  9.0 1.9 %collective-permute-start.2 = (f32[32,128]{1,0:T(8,128)S(1)}, f32[32,128]{1,0:T(8,128)S(1)}, u32[]{:S(2)}, u32[]{:S(2)}) collective-permute-start(f32[32,128]{1,0:T(8,128)S(1)} %get-tuple-element.59.mine), channel_id=1, source_target_pairs={{0,3},{1,2},{2,1},{3,0},{4,7},{5,6},{6,5},{7,4},{8,11},{9,10},{10,... | collective-permute-start | bytes 49160 | tf_op jit(solution)/shard_map/ppermute | solution.py:321
  10.9 0.6 %collective-permute-done.5.got = f32[64,384]{1,0:T(8,128)S(1)} collective-permute-done((f32[64,384]{1,0:T(8,128)S(1)}, f32[64,384]{1,0:T(8,128)S(1)}, u32[]{:S(2)}, u32[]{:S(2)}) %collective-permute-start.5) | collective-permute-done | bytes 98336 | tf_op jit(solution)/shard_map/ppermute | solution.py:321
  11.5 0.8 %collective-permute-done.2.got._ = f32[32,128]{1,0:T(8,128)S(1)} collective-permute-done((f32[32,128]{1,0:T(8,128)S(1)}, f32[32,128]{1,0:T(8,128)S(1)}, u32[]{:S(2)}, u32[]{:S(2)}) %collective-permute-start.2) | collective-permute-done | bytes 16416 | tf_op jit(solution)/shard_map/ppermute | solution.py:321
  12.3 2.8 %collective-permute-start.6 = (f32[64,384]{1,0:T(8,128)S(1)}, f32[64,384]{1,0:T(8,128)S(1)}, u32[]{:S(2)}, u32[]{:S(2)}) collective-permute-start(f32[64,384]{1,0:T(8,128)S(1)} %shard_map.80.low), channel_id=1, source_target_pairs={{0,5},{1,4},{2,7},{3,6},{4,1},{5,0},{6,3},{7,2},{8,13},{9,12},{10,... | collective-permute-start | bytes 294920 | tf_op jit(solution)/shard_map/ppermute | solution.py:321
  15.1 0.3 shard_map.77
  15.4 1.5 %collective-permute-start.3 = (f32[32,384]{1,0:T(8,128)S(1)}, f32[32,384]{1,0:T(8,128)S(1)}, u32[]{:S(2)}, u32[]{:S(2)}) collective-permute-start(f32[32,384]{1,0:T(8,128)S(1)} %get-tuple-element.61), channel_id=1, source_target_pairs={{0,3},{1,2},{2,1},{3,0},{4,7},{5,6},{6,5},{7,4},{8,11},{9,10},{10,... | collective-permute-start | bytes 147464 | tf_op jit(solution)/shard_map/ppermute | solution.py:321
  16.9 0.3 collective-permute-start.7
  17.1 2.0 %collective-permute-done.3 = f32[32,384]{1,0:T(8,128)S(1)} collective-permute-done((f32[32,384]{1,0:T(8,128)S(1)}, f32[32,384]{1,0:T(8,128)S(1)}, u32[]{:S(2)}, u32[]{:S(2)}) %collective-permute-start.3) | collective-permute-done | bytes 49184 | tf_op jit(solution)/shard_map/ppermute | solution.py:321
  19.1 1.7 %collective-permute-start.4 = (f32[32,384]{1,0:T(8,128)S(1)}, f32[32,384]{1,0:T(8,128)S(1)}, u32[]{:S(2)}, u32[]{:S(2)}) collective-permute-start(f32[32,384]{1,0:T(8,128)S(1)} %add.10._.sums), channel_id=1, source_target_pairs={{0,5},{1,4},{2,7},{3,6},{4,1},{5,0},{6,3},{7,2},{8,13},{9,12},{10,... | collective-permute-start | bytes 147464 | tf_op jit(solution)/shard_map/ppermute | solution.py:321
  20.8 1.2 %shard_map.78 = (f32[512,128]{1,0:T(8,128)S(1)}, f32[3,256,256]{2,1,0:T(8,128)S(1)}) custom-call(f32[6,512,128]{2,1,0:T(8,128)} %left.5, f32[1,6,256,256]{3,2,1,0:T(8,128)} %coupling.3, f32[32,384]{1,0:T(8,128)S(1)} %add.10._.sums), custom_call_target="tpu_custom_call" | custom-call | flops 1 | bytes 1 | tf_op jit(solution)/shard_map/pallas_call | solution.py:301
  22.1 0.0 collective-permute-done.6.got.got_low
  22.1 0.4 %collective-permute-start.10 = (f32[64,128]{1,0:T(8,128)S(1)}, f32[64,128]{1,0:T(8,128)S(1)}, u32[]{:S(2)}, u32[]{:S(2)}) collective-permute-start(f32[64,128]{1,0:T(8,128)S(1)} %get-tuple-element.66.refs_2_), channel_id=1, source_target_pairs={{0,1},{1,0},{2,3},{3,2},{4,5},{5,4},{6,7},{7,6},{8,9},{9,8},{10,11... | collective-permute-start | bytes 98312 | tf_op jit(solution)/shard_map/ppermute | solution.py:321
  22.5 0.2 collective-permute-start.8
  22.7 0.3 collective-permute-start.9
  23.0 0.6 %collective-permute-done.4.got = f32[32,384]{1,0:T(8,128)S(1)} collective-permute-done((f32[32,384]{1,0:T(8,128)S(1)}, f32[32,384]{1,0:T(8,128)S(1)}, u32[]{:S(2)}, u32[]{:S(2)}) %collective-permute-start.4) | collective-permute-done | bytes 49184 | tf_op jit(solution)/shard_map/ppermute | solution.py:321
  23.6 0.2 shard_map.79
  23.8 0.0 collective-permute-done.7.other
  23.8 0.0 collective-permute-done.10.refs_3_
  23.8 0.0 collective-permute-done.8.refs_0_
  23.8 0.1 collective-permute-done.9.refs_1_
  23.9 0.2 shard_map.82.packed
  24.1 1.6 %collective-permute-start.11 = (f32[32,768]{1,0:T(8,128)S(1)}, f32[32,768]{1,0:T(8,128)S(1)}, u32[]{:S(2)}, u32[]{:S(2)}) collective-permute-start(f32[32,768]{1,0:T(8,128)S(1)} %shard_map.82.packed), channel_id=1, source_target_pairs={{0,9},{1,8},{2,11},{3,10},{4,13},{5,12},{6,15},{7,14},{8,1},{9,0},... | collective-permute-start | bytes 294920 | tf_op jit(solution)/shard_map/ppermute | solution.py:321
  25.7 3.0 %collective-permute-done.11.got = f32[32,768]{1,0:T(8,128)S(1)} collective-permute-done((f32[32,768]{1,0:T(8,128)S(1)}, f32[32,768]{1,0:T(8,128)S(1)}, u32[]{:S(2)}, u32[]{:S(2)}) %collective-permute-start.11) | collective-permute-done | bytes 98336 | tf_op jit(solution)/shard_map/ppermute | solution.py:321
  28.7 0.3 shard_map.83
  29.0 1.6 %collective-permute-start.13 = (f32[32,128]{1,0:T(8,128)S(1)}, f32[32,128]{1,0:T(8,128)S(1)}, u32[]{:S(2)}, u32[]{:S(2)}) collective-permute-start(f32[32,128]{1,0:T(8,128)S(1)} %get-tuple-element.75), channel_id=1, source_target_pairs={{0,17},{1,16},{2,19},{3,18},{4,21},{5,20},{6,23},{7,22},{8,25},{9,... | collective-permute-start | bytes 49160 | tf_op jit(solution)/shard_map/ppermute | solution.py:321
  30.6 0.2 collective-permute-start.12
  30.8 1.5 %collective-permute-done.13 = f32[32,128]{1,0:T(8,128)S(1)} collective-permute-done((f32[32,128]{1,0:T(8,128)S(1)}, f32[32,128]{1,0:T(8,128)S(1)}, u32[]{:S(2)}, u32[]{:S(2)}) %collective-permute-start.13) | collective-permute-done | bytes 16416 | tf_op jit(solution)/shard_map/ppermute | solution.py:321
  32.3 0.4 %collective-permute-start.14 = (f32[32,256]{1,0:T(8,128)S(1)}, f32[32,256]{1,0:T(8,128)S(1)}, u32[]{:S(2)}, u32[]{:S(2)}) collective-permute-start(f32[32,256]{1,0:T(8,128)S(1)} %pad_maximum_fusion.1.mine), channel_id=1, source_target_pairs={{0,1},{1,0},{2,3},{3,2},{4,5},{5,4},{6,7},{7,6},{8,9},{9,8},{10,11... | collective-permute-start | bytes 98312 | tf_op jit(solution)/shard_map/ppermute | solution.py:321
  32.7 0.0 collective-permute-done.12
  32.7 0.8 %shard_map.84 = (f32[64,512]{1,0:T(8,128)S(1)}, f32[256,512]{1,0:T(8,128)S(1)}) custom-call(f32[64,512]{1,0:T(8,128)S(1)} %get-tuple-element.56.current, f32[32,256]{1,0:T(8,128)S(1)} %get-tuple-element.67.refs_0_, f32[32,256]{1,0:T(8,128)S(1)} %get-tuple-element.80.refs_1_, f32[32,256]{1,0:T(8,128)S(1)} %get-tuple-element.68.refs_2_, ...), custom_call_target="tpu_custom_call" | custom-call | flops 1 | bytes 1 | tf_op jit(solution)/shard_map/pallas_call | solution.py:301
  33.6 0.0 collective-permute-done.14.other
  33.6 0.9 %shard_map.85 = f32[64,512]{1,0:T(8,128)} custom-call(f32[64,512]{1,0:T(8,128)S(1)} %get-tuple-element.74.current, f32[32,256]{1,0:T(8,128)S(1)} %pad_maximum_fusion.1.mine, f32[32,256]{1,0:T(8,128)S(1)} %collective-permute-done.14.other, f32[256,512]{1,0:T(8,128)S(1)} %get-tuple-element.76.factor), custom_call_target="tpu_custom_call" | custom-call | flops 1 | bytes 1 | tf_op jit(solution)/shard_map/pallas_call | solution.py:301
  (10 shorter events, 0.1 us)
Async XLA Ops:
  2.0 2.6 %collective-permute-start = (f32[64,384]{1,0:T(8,128)S(1)}, f32[64,384]{1,0:T(8,128)S(1)}, u32[]{:S(2)}, u32[]{:S(2)}) collective-permute-start(f32[64,384]{1,0:T(8,128)S(1)} %get-tuple-element.55), channel_id=1, source_target_pairs={{0,1},{1,0},{2,3},{3,2},{4,5},{5,4},{6,7},{7,6},{8,9},{9,8},{10,11... | collective-permute-start | bytes 294920 | tf_op jit(solution)/shard_map/ppermute | solution.py:321
  5.8 2.8 %collective-permute-start.1 = (f32[32,4224]{1,0:T(8,128)S(1)}, f32[32,4224]{1,0:T(8,128)S(1)}, u32[]{:S(2)}, u32[]{:S(2)}) collective-permute-start(f32[32,4224]{1,0:T(8,128)S(1)} %get-tuple-element.58), channel_id=1, source_target_pairs={{0,1},{1,0},{2,3},{3,2},{4,5},{5,4},{6,7},{7,6},{8,9},{9,8},{10,11... | collective-permute-start | bytes 1622024 | tf_op jit(solution)/shard_map/ppermute | solution.py:321
  5.9 5.6 %collective-permute-start.5 = (f32[64,384]{1,0:T(8,128)S(1)}, f32[64,384]{1,0:T(8,128)S(1)}, u32[]{:S(2)}, u32[]{:S(2)}) collective-permute-start(f32[64,384]{1,0:T(8,128)S(1)} %add.9._.low), channel_id=1, source_target_pairs={{0,3},{1,2},{2,1},{3,0},{4,7},{5,6},{6,5},{7,4},{8,11},{9,10},{10,... | collective-permute-start | bytes 294920 | tf_op jit(solution)/shard_map/ppermute | solution.py:321
  9.0 3.3 %collective-permute-start.2 = (f32[32,128]{1,0:T(8,128)S(1)}, f32[32,128]{1,0:T(8,128)S(1)}, u32[]{:S(2)}, u32[]{:S(2)}) collective-permute-start(f32[32,128]{1,0:T(8,128)S(1)} %get-tuple-element.59.mine), channel_id=1, source_target_pairs={{0,3},{1,2},{2,1},{3,0},{4,7},{5,6},{6,5},{7,4},{8,11},{9,10},{10,... | collective-permute-start | bytes 49160 | tf_op jit(solution)/shard_map/ppermute | solution.py:321
  12.3 9.7 %collective-permute-start.6 = (f32[64,384]{1,0:T(8,128)S(1)}, f32[64,384]{1,0:T(8,128)S(1)}, u32[]{:S(2)}, u32[]{:S(2)}) collective-permute-start(f32[64,384]{1,0:T(8,128)S(1)} %shard_map.80.low), channel_id=1, source_target_pairs={{0,5},{1,4},{2,7},{3,6},{4,1},{5,0},{6,3},{7,2},{8,13},{9,12},{10,... | collective-permute-start | bytes 294920 | tf_op jit(solution)/shard_map/ppermute | solution.py:321
  15.4 3.7 %collective-permute-start.3 = (f32[32,384]{1,0:T(8,128)S(1)}, f32[32,384]{1,0:T(8,128)S(1)}, u32[]{:S(2)}, u32[]{:S(2)}) collective-permute-start(f32[32,384]{1,0:T(8,128)S(1)} %get-tuple-element.61), channel_id=1, source_target_pairs={{0,3},{1,2},{2,1},{3,0},{4,7},{5,6},{6,5},{7,4},{8,11},{9,10},{10,... | collective-permute-start | bytes 147464 | tf_op jit(solution)/shard_map/ppermute | solution.py:321
  16.9 6.9 %collective-permute-start.7 = (f32[64,256]{1,0:T(8,128)S(1)}, f32[64,256]{1,0:T(8,128)S(1)}, u32[]{:S(2)}, u32[]{:S(2)}) collective-permute-start(f32[64,256]{1,0:T(8,128)S(1)} %slice.20), channel_id=1, source_target_pairs={{0,1},{1,0},{2,3},{3,2},{4,5},{5,4},{6,7},{7,6},{8,9},{9,8},{10,11... | collective-permute-start | bytes 196616 | tf_op jit(solution)/shard_map/ppermute | solution.py:321
  19.1 4.5 %collective-permute-start.4 = (f32[32,384]{1,0:T(8,128)S(1)}, f32[32,384]{1,0:T(8,128)S(1)}, u32[]{:S(2)}, u32[]{:S(2)}) collective-permute-start(f32[32,384]{1,0:T(8,128)S(1)} %add.10._.sums), channel_id=1, source_target_pairs={{0,5},{1,4},{2,7},{3,6},{4,1},{5,0},{6,3},{7,2},{8,13},{9,12},{10,... | collective-permute-start | bytes 147464 | tf_op jit(solution)/shard_map/ppermute | solution.py:321
  22.1 1.7 %collective-permute-start.10 = (f32[64,128]{1,0:T(8,128)S(1)}, f32[64,128]{1,0:T(8,128)S(1)}, u32[]{:S(2)}, u32[]{:S(2)}) collective-permute-start(f32[64,128]{1,0:T(8,128)S(1)} %get-tuple-element.66.refs_2_), channel_id=1, source_target_pairs={{0,1},{1,0},{2,3},{3,2},{4,5},{5,4},{6,7},{7,6},{8,9},{9,8},{10,11... | collective-permute-start | bytes 98312 | tf_op jit(solution)/shard_map/ppermute | solution.py:321
  22.5 1.3 %collective-permute-start.8 = (f32[64,128]{1,0:T(8,128)S(1)}, f32[64,128]{1,0:T(8,128)S(1)}, u32[]{:S(2)}, u32[]{:S(2)}) collective-permute-start(f32[64,128]{1,0:T(8,128)S(1)} %get-tuple-element.64), channel_id=1, source_target_pairs={{0,1},{1,0},{2,3},{3,2},{4,5},{5,4},{6,7},{7,6},{8,9},{9,8},{10,11... | collective-permute-start | bytes 98312 | tf_op jit(solution)/shard_map/ppermute | solution.py:321
  22.7 1.2 %collective-permute-start.9 = (f32[64,128]{1,0:T(8,128)S(1)}, f32[64,128]{1,0:T(8,128)S(1)}, u32[]{:S(2)}, u32[]{:S(2)}) collective-permute-start(f32[64,128]{1,0:T(8,128)S(1)} %get-tuple-element.65), channel_id=1, source_target_pairs={{0,1},{1,0},{2,3},{3,2},{4,5},{5,4},{6,7},{7,6},{8,9},{9,8},{10,11... | collective-permute-start | bytes 98312 | tf_op jit(solution)/shard_map/ppermute | solution.py:321
  24.1 4.6 %collective-permute-start.11 = (f32[32,768]{1,0:T(8,128)S(1)}, f32[32,768]{1,0:T(8,128)S(1)}, u32[]{:S(2)}, u32[]{:S(2)}) collective-permute-start(f32[32,768]{1,0:T(8,128)S(1)} %shard_map.82.packed), channel_id=1, source_target_pairs={{0,9},{1,8},{2,11},{3,10},{4,13},{5,12},{6,15},{7,14},{8,1},{9,0},... | collective-permute-start | bytes 294920 | tf_op jit(solution)/shard_map/ppermute | solution.py:321
  29.0 3.2 %collective-permute-start.13 = (f32[32,128]{1,0:T(8,128)S(1)}, f32[32,128]{1,0:T(8,128)S(1)}, u32[]{:S(2)}, u32[]{:S(2)}) collective-permute-start(f32[32,128]{1,0:T(8,128)S(1)} %get-tuple-element.75), channel_id=1, source_target_pairs={{0,17},{1,16},{2,19},{3,18},{4,21},{5,20},{6,23},{7,22},{8,25},{9,... | collective-permute-start | bytes 49160 | tf_op jit(solution)/shard_map/ppermute | solution.py:321
  30.6 2.1 %collective-permute-start.12 = (f32[32,768]{1,0:T(8,128)S(1)}, f32[32,768]{1,0:T(8,128)S(1)}, u32[]{:S(2)}, u32[]{:S(2)}) collective-permute-start(f32[32,768]{1,0:T(8,128)S(1)} %pad_maximum_fusion), channel_id=1, source_target_pairs={{0,1},{1,0},{2,3},{3,2},{4,5},{5,4},{6,7},{7,6},{8,9},{9,8},{10,11... | collective-permute-start | bytes 294920 | tf_op jit(solution)/shard_map/ppermute | solution.py:321
  32.3 1.3 %collective-permute-start.14 = (f32[32,256]{1,0:T(8,128)S(1)}, f32[32,256]{1,0:T(8,128)S(1)}, u32[]{:S(2)}, u32[]{:S(2)}) collective-permute-start(f32[32,256]{1,0:T(8,128)S(1)} %pad_maximum_fusion.1.mine), channel_id=1, source_target_pairs={{0,1},{1,0},{2,3},{3,2},{4,5},{5,4},{6,7},{7,6},{8,9},{9,8},{10,11... | collective-permute-start | bytes 98312 | tf_op jit(solution)/shard_map/ppermute | solution.py:321

commit v9 on v8

--- a/solution.py
+++ b/solution.py
@@ -452,7 +452,7 @@
             [],
             low,
             got_low,
-            coup,
+            sums,
         )
         pieces = [exchange(piece, 1) for piece in pieces]
         rests = [rest, exchange(rest, 1)] if last else []

time: 34.6 us -> 34.6 us (level)
  transfers between devices with their start and end apart: 15 -> 15, of which waited for: 7 -> 6; matrix products, arithmetic and copies ran while one was open for 0% -> 0% of each run, Pallas kernels for 12% -> 12%
where the time goes in v9:
time: 34.6 us; the launch traced here: 34.4 us
  starting transfers between devices  16.3 us (47%)
  Pallas kernels  8.84 us (26%)
  waiting for transfers between devices  8.45 us (24%)
  between operations  0.81 us (2%)
    ppermute x15, starting transfers between devices, exchange(): lax.ppermute(value, AXES, [(i, i ^ mask) for i in range(lax.axis_size(AXE...  16.3 us
    pallas_call x13, Pallas kernels, call(): pl.pallas_call(kernel, out_shape=outs, in_specs=in_specs, out_specs=out_s...  8.84 us
    ppermute x15, waiting for transfers between devices, exchange(): lax.ppermute(value, AXES, [(i, i ^ mask) for i in range(lax.axis_size(AXE...  8.45 us
  transfers between devices with their start and end apart: 15, of which 6 were waited for; matrix products, arithmetic and copies ran while one was open for 0% of the time, Pallas kernels for 12%

profile of v9, /device:TPU:0, one launch (start us, length us, event | category | flops | bytes accessed | tf_op | source)
XLA Modules:
  0.0 34.4 jit_solution(1251012804734822321)
XLA Ops:
  0.0 2.0 %shard_map.73 = (f32[64,384]{1,0:T(8,128)S(1)}, f32[64,384]{1,0:T(8,128)S(1)}, f32[512,256]{1,0:T(8,128)S(1)}, f32[512,256]{1,0:T(8,128)S(1)}, f32[64,512]{1,0:T...) custom-call(f32[6,512,128]{2,1,0:T(8,128)} %left.5, ...), custom_call_target="tpu_custom_call" | custom-call | flops 1 | bytes 1 | tf_op jit(solution)/shard_map/pallas_call | solution.py:301
  2.0 0.5 %collective-permute-start = (f32[64,384]{1,0:T(8,128)S(1)}, f32[64,384]{1,0:T(8,128)S(1)}, u32[]{:S(2)}, u32[]{:S(2)}) collective-permute-start(f32[64,384]{1,0:T(8,128)S(1)} %get-tuple-element.55), channel_id=1, source_target_pairs={{0,1},{1,0},{2,3},{3,2},{4,5},{5,4},{6,7},{7,6},{8,9},{9,8},{10,11... | collective-permute-start | bytes 294920 | tf_op jit(solution)/shard_map/ppermute | solution.py:321
  3.2 1.4 %shard_map.74 = (f32[64,512]{1,0:T(8,128)S(1)}, f32[128,512]{1,0:T(8,128)S(1)}, f32[128,384]{1,0:T(8,128)S(1)}, f32[512,128]{1,0:T(8,128)S(1)}, f32[512,128]{1,0...) custom-call(s32[1,512]{1,0:T(1,128)S(1)} %get-tuple-element.41.order, s32[1,1]{1,0:T(1,128)} %bitcast.2.split, ...), custom_call_target="tpu_custom_call" | custom-call | flops 1 | bytes 1 | tf_op jit(solution)/shard_map/pallas_call | solution.py:301
  4.6 0.0 collective-permute-done
  4.6 1.1 %shard_map.75 = (f32[64,512]{1,0:T(8,128)S(1)}, f32[32,640]{1,0:T(8,128)S(1)}, f32[32,4224]{1,0:T(8,128)S(1)}) custom-call(s32[1,1]{1,0:T(1,128)} %bitcast.3.split, f32[64,512]{1,0:T(8,128)S(1)} %get-tuple-element.47.first, f32[512,128]{1,0:T(8,128)S(1)} %get-tuple-element.48.left_top, f32[512,128]{1,0:T(8,128)S(1)} %get-tuple-element.49.right_top, ...), custom_call_target="tpu_custom_call" | custom-call | flops 1 | bytes 1 | tf_op jit(solution)/shard_map/pallas_call | solution.py:301
  5.8 0.1 collective-permute-start.1
  5.9 2.7 %collective-permute-start.5 = (f32[64,384]{1,0:T(8,128)S(1)}, f32[64,384]{1,0:T(8,128)S(1)}, u32[]{:S(2)}, u32[]{:S(2)}) collective-permute-start(f32[64,384]{1,0:T(8,128)S(1)} %add.9._.low), channel_id=1, source_target_pairs={{0,3},{1,2},{2,1},{3,0},{4,7},{5,6},{6,5},{7,4},{8,11},{9,10},{10,... | collective-permute-start | bytes 294920 | tf_op jit(solution)/shard_map/ppermute | solution.py:321
  8.6 0.0 collective-permute-done.1.got.got_gram
  8.6 0.4 %shard_map.76 = (f32[32,384]{1,0:T(8,128)S(1)}, f32[32,128]{1,0:T(8,128)S(1)}, f32[32,128]{1,0:T(8,128)S(1)}, f32[32,128]{1,0:T(8,128)S(1)}) custom-call(f32[32,640]{1,0:T(8,128)S(1)} %get-tuple-element.57.keep, f32[32,4224]{1,0:T(8,128)S(1)} %collective-permute-done.1.got.got_gram, f32[128,512]{1,0:T(8,128)S(1)} %get-tuple-element.52.gram_top, ...), custom_call_target="tpu_custom_call" | custom-call | flops 1 | bytes 1 | tf_op jit(solution)/shard_map/pallas_call | solution.py:301
  9.0 1.9 %collective-permute-start.2 = (f32[32,128]{1,0:T(8,128)S(1)}, f32[32,128]{1,0:T(8,128)S(1)}, u32[]{:S(2)}, u32[]{:S(2)}) collective-permute-start(f32[32,128]{1,0:T(8,128)S(1)} %get-tuple-element.59.mine), channel_id=1, source_target_pairs={{0,3},{1,2},{2,1},{3,0},{4,7},{5,6},{6,5},{7,4},{8,11},{9,10},{10,... | collective-permute-start | bytes 49160 | tf_op jit(solution)/shard_map/ppermute | solution.py:321
  10.9 0.6 %collective-permute-done.5.got = f32[64,384]{1,0:T(8,128)S(1)} collective-permute-done((f32[64,384]{1,0:T(8,128)S(1)}, f32[64,384]{1,0:T(8,128)S(1)}, u32[]{:S(2)}, u32[]{:S(2)}) %collective-permute-start.5) | collective-permute-done | bytes 98336 | tf_op jit(solution)/shard_map/ppermute | solution.py:321
  11.5 0.8 %collective-permute-done.2.got._ = f32[32,128]{1,0:T(8,128)S(1)} collective-permute-done((f32[32,128]{1,0:T(8,128)S(1)}, f32[32,128]{1,0:T(8,128)S(1)}, u32[]{:S(2)}, u32[]{:S(2)}) %collective-permute-start.2) | collective-permute-done | bytes 16416 | tf_op jit(solution)/shard_map/ppermute | solution.py:321
  12.3 2.8 %collective-permute-start.6 = (f32[64,384]{1,0:T(8,128)S(1)}, f32[64,384]{1,0:T(8,128)S(1)}, u32[]{:S(2)}, u32[]{:S(2)}) collective-permute-start(f32[64,384]{1,0:T(8,128)S(1)} %shard_map.80.low), channel_id=1, source_target_pairs={{0,5},{1,4},{2,7},{3,6},{4,1},{5,0},{6,3},{7,2},{8,13},{9,12},{10,... | collective-permute-start | bytes 294920 | tf_op jit(solution)/shard_map/ppermute | solution.py:321
  15.1 0.3 shard_map.77
  15.4 1.5 %collective-permute-start.3 = (f32[32,384]{1,0:T(8,128)S(1)}, f32[32,384]{1,0:T(8,128)S(1)}, u32[]{:S(2)}, u32[]{:S(2)}) collective-permute-start(f32[32,384]{1,0:T(8,128)S(1)} %get-tuple-element.61), channel_id=1, source_target_pairs={{0,3},{1,2},{2,1},{3,0},{4,7},{5,6},{6,5},{7,4},{8,11},{9,10},{10,... | collective-permute-start | bytes 147464 | tf_op jit(solution)/shard_map/ppermute | solution.py:321
  16.9 0.3 collective-permute-start.7
  17.1 2.0 %collective-permute-done.3 = f32[32,384]{1,0:T(8,128)S(1)} collective-permute-done((f32[32,384]{1,0:T(8,128)S(1)}, f32[32,384]{1,0:T(8,128)S(1)}, u32[]{:S(2)}, u32[]{:S(2)}) %collective-permute-start.3) | collective-permute-done | bytes 49184 | tf_op jit(solution)/shard_map/ppermute | solution.py:321
  19.1 1.7 %collective-permute-start.4 = (f32[32,384]{1,0:T(8,128)S(1)}, f32[32,384]{1,0:T(8,128)S(1)}, u32[]{:S(2)}, u32[]{:S(2)}) collective-permute-start(f32[32,384]{1,0:T(8,128)S(1)} %add.10._.sums), channel_id=1, source_target_pairs={{0,5},{1,4},{2,7},{3,6},{4,1},{5,0},{6,3},{7,2},{8,13},{9,12},{10,... | collective-permute-start | bytes 147464 | tf_op jit(solution)/shard_map/ppermute | solution.py:321
  20.8 0.0 collective-permute-done.6.got.got_low
  20.9 0.4 %collective-permute-start.10 = (f32[64,128]{1,0:T(8,128)S(1)}, f32[64,128]{1,0:T(8,128)S(1)}, u32[]{:S(2)}, u32[]{:S(2)}) collective-permute-start(f32[64,128]{1,0:T(8,128)S(1)} %get-tuple-element.66.refs_2_), channel_id=1, source_target_pairs={{0,1},{1,0},{2,3},{3,2},{4,5},{5,4},{6,7},{7,6},{8,9},{9,8},{10,11... | collective-permute-start | bytes 98312 | tf_op jit(solution)/shard_map/ppermute | solution.py:321
  21.3 0.2 collective-permute-start.8
  21.4 0.3 collective-permute-start.9
  21.8 1.2 %shard_map.78 = (f32[512,128]{1,0:T(8,128)S(1)}, f32[3,256,256]{2,1,0:T(8,128)S(1)}) custom-call(f32[6,512,128]{2,1,0:T(8,128)} %left.5, f32[1,6,256,256]{3,2,1,0:T(8,128)} %coupling.3, f32[32,384]{1,0:T(8,128)S(1)} %add.10._.sums), custom_call_target="tpu_custom_call" | custom-call | flops 1 | bytes 1 | tf_op jit(solution)/shard_map/pallas_call | solution.py:301
  23.0 0.6 %collective-permute-done.4.got = f32[32,384]{1,0:T(8,128)S(1)} collective-permute-done((f32[32,384]{1,0:T(8,128)S(1)}, f32[32,384]{1,0:T(8,128)S(1)}, u32[]{:S(2)}, u32[]{:S(2)}) %collective-permute-start.4) | collective-permute-done | bytes 49184 | tf_op jit(solution)/shard_map/ppermute | solution.py:321
  23.6 0.2 shard_map.79
  23.8 0.0 collective-permute-done.7.other
  23.8 0.0 collective-permute-done.10.refs_3_
  23.8 0.0 collective-permute-done.8.refs_0_
  23.8 0.0 collective-permute-done.9.refs_1_
  23.8 0.2 shard_map.82.packed
  24.0 1.6 %collective-permute-start.11 = (f32[32,768]{1,0:T(8,128)S(1)}, f32[32,768]{1,0:T(8,128)S(1)}, u32[]{:S(2)}, u32[]{:S(2)}) collective-permute-start(f32[32,768]{1,0:T(8,128)S(1)} %shard_map.82.packed), channel_id=1, source_target_pairs={{0,9},{1,8},{2,11},{3,10},{4,13},{5,12},{6,15},{7,14},{8,1},{9,0},... | collective-permute-start | bytes 294920 | tf_op jit(solution)/shard_map/ppermute | solution.py:321
  25.6 2.9 %collective-permute-done.11.got = f32[32,768]{1,0:T(8,128)S(1)} collective-permute-done((f32[32,768]{1,0:T(8,128)S(1)}, f32[32,768]{1,0:T(8,128)S(1)}, u32[]{:S(2)}, u32[]{:S(2)}) %collective-permute-start.11) | collective-permute-done | bytes 98336 | tf_op jit(solution)/shard_map/ppermute | solution.py:321
  28.6 0.3 shard_map.83
  28.9 1.6 %collective-permute-start.13 = (f32[32,128]{1,0:T(8,128)S(1)}, f32[32,128]{1,0:T(8,128)S(1)}, u32[]{:S(2)}, u32[]{:S(2)}) collective-permute-start(f32[32,128]{1,0:T(8,128)S(1)} %get-tuple-element.75), channel_id=1, source_target_pairs={{0,17},{1,16},{2,19},{3,18},{4,21},{5,20},{6,23},{7,22},{8,25},{9,... | collective-permute-start | bytes 49160 | tf_op jit(solution)/shard_map/ppermute | solution.py:321
  30.5 0.1 collective-permute-start.12
  30.7 1.5 %collective-permute-done.13 = f32[32,128]{1,0:T(8,128)S(1)} collective-permute-done((f32[32,128]{1,0:T(8,128)S(1)}, f32[32,128]{1,0:T(8,128)S(1)}, u32[]{:S(2)}, u32[]{:S(2)}) %collective-permute-start.13) | collective-permute-done | bytes 16416 | tf_op jit(solution)/shard_map/ppermute | solution.py:321
  32.1 0.5 %collective-permute-start.14 = (f32[32,256]{1,0:T(8,128)S(1)}, f32[32,256]{1,0:T(8,128)S(1)}, u32[]{:S(2)}, u32[]{:S(2)}) collective-permute-start(f32[32,256]{1,0:T(8,128)S(1)} %pad_maximum_fusion.1.mine), channel_id=1, source_target_pairs={{0,1},{1,0},{2,3},{3,2},{4,5},{5,4},{6,7},{7,6},{8,9},{9,8},{10,11... | collective-permute-start | bytes 98312 | tf_op jit(solution)/shard_map/ppermute | solution.py:321
  32.6 0.0 collective-permute-done.12
  32.7 0.8 %shard_map.84 = (f32[64,512]{1,0:T(8,128)S(1)}, f32[256,512]{1,0:T(8,128)S(1)}) custom-call(f32[64,512]{1,0:T(8,128)S(1)} %get-tuple-element.56.current, f32[32,256]{1,0:T(8,128)S(1)} %get-tuple-element.67.refs_0_, f32[32,256]{1,0:T(8,128)S(1)} %get-tuple-element.80.refs_1_, f32[32,256]{1,0:T(8,128)S(1)} %get-tuple-element.68.refs_2_, ...), custom_call_target="tpu_custom_call" | custom-call | flops 1 | bytes 1 | tf_op jit(solution)/shard_map/pallas_call | solution.py:301
  33.5 0.0 collective-permute-done.14.other
  33.5 0.9 %shard_map.85 = f32[64,512]{1,0:T(8,128)} custom-call(f32[64,512]{1,0:T(8,128)S(1)} %get-tuple-element.74.current, f32[32,256]{1,0:T(8,128)S(1)} %pad_maximum_fusion.1.mine, f32[32,256]{1,0:T(8,128)S(1)} %collective-permute-done.14.other, f32[256,512]{1,0:T(8,128)S(1)} %get-tuple-element.76.factor), custom_call_target="tpu_custom_call" | custom-call | flops 1 | bytes 1 | tf_op jit(solution)/shard_map/pallas_call | solution.py:301
  (10 shorter events, 0.1 us)
Async XLA Ops:
  2.0 2.6 %collective-permute-start = (f32[64,384]{1,0:T(8,128)S(1)}, f32[64,384]{1,0:T(8,128)S(1)}, u32[]{:S(2)}, u32[]{:S(2)}) collective-permute-start(f32[64,384]{1,0:T(8,128)S(1)} %get-tuple-element.55), channel_id=1, source_target_pairs={{0,1},{1,0},{2,3},{3,2},{4,5},{5,4},{6,7},{7,6},{8,9},{9,8},{10,11... | collective-permute-start | bytes 294920 | tf_op jit(solution)/shard_map/ppermute | solution.py:321
  5.8 2.8 %collective-permute-start.1 = (f32[32,4224]{1,0:T(8,128)S(1)}, f32[32,4224]{1,0:T(8,128)S(1)}, u32[]{:S(2)}, u32[]{:S(2)}) collective-permute-start(f32[32,4224]{1,0:T(8,128)S(1)} %get-tuple-element.58), channel_id=1, source_target_pairs={{0,1},{1,0},{2,3},{3,2},{4,5},{5,4},{6,7},{7,6},{8,9},{9,8},{10,11... | collective-permute-start | bytes 1622024 | tf_op jit(solution)/shard_map/ppermute | solution.py:321
  5.9 5.6 %collective-permute-start.5 = (f32[64,384]{1,0:T(8,128)S(1)}, f32[64,384]{1,0:T(8,128)S(1)}, u32[]{:S(2)}, u32[]{:S(2)}) collective-permute-start(f32[64,384]{1,0:T(8,128)S(1)} %add.9._.low), channel_id=1, source_target_pairs={{0,3},{1,2},{2,1},{3,0},{4,7},{5,6},{6,5},{7,4},{8,11},{9,10},{10,... | collective-permute-start | bytes 294920 | tf_op jit(solution)/shard_map/ppermute | solution.py:321
  9.0 3.3 %collective-permute-start.2 = (f32[32,128]{1,0:T(8,128)S(1)}, f32[32,128]{1,0:T(8,128)S(1)}, u32[]{:S(2)}, u32[]{:S(2)}) collective-permute-start(f32[32,128]{1,0:T(8,128)S(1)} %get-tuple-element.59.mine), channel_id=1, source_target_pairs={{0,3},{1,2},{2,1},{3,0},{4,7},{5,6},{6,5},{7,4},{8,11},{9,10},{10,... | collective-permute-start | bytes 49160 | tf_op jit(solution)/shard_map/ppermute | solution.py:321
  12.3 8.5 %collective-permute-start.6 = (f32[64,384]{1,0:T(8,128)S(1)}, f32[64,384]{1,0:T(8,128)S(1)}, u32[]{:S(2)}, u32[]{:S(2)}) collective-permute-start(f32[64,384]{1,0:T(8,128)S(1)} %shard_map.80.low), channel_id=1, source_target_pairs={{0,5},{1,4},{2,7},{3,6},{4,1},{5,0},{6,3},{7,2},{8,13},{9,12},{10,... | collective-permute-start | bytes 294920 | tf_op jit(solution)/shard_map/ppermute | solution.py:321
  15.4 3.7 %collective-permute-start.3 = (f32[32,384]{1,0:T(8,128)S(1)}, f32[32,384]{1,0:T(8,128)S(1)}, u32[]{:S(2)}, u32[]{:S(2)}) collective-permute-start(f32[32,384]{1,0:T(8,128)S(1)} %get-tuple-element.61), channel_id=1, source_target_pairs={{0,3},{1,2},{2,1},{3,0},{4,7},{5,6},{6,5},{7,4},{8,11},{9,10},{10,... | collective-permute-start | bytes 147464 | tf_op jit(solution)/shard_map/ppermute | solution.py:321
  16.9 6.9 %collective-permute-start.7 = (f32[64,256]{1,0:T(8,128)S(1)}, f32[64,256]{1,0:T(8,128)S(1)}, u32[]{:S(2)}, u32[]{:S(2)}) collective-permute-start(f32[64,256]{1,0:T(8,128)S(1)} %slice.20), channel_id=1, source_target_pairs={{0,1},{1,0},{2,3},{3,2},{4,5},{5,4},{6,7},{7,6},{8,9},{9,8},{10,11... | collective-permute-start | bytes 196616 | tf_op jit(solution)/shard_map/ppermute | solution.py:321
  19.1 4.5 %collective-permute-start.4 = (f32[32,384]{1,0:T(8,128)S(1)}, f32[32,384]{1,0:T(8,128)S(1)}, u32[]{:S(2)}, u32[]{:S(2)}) collective-permute-start(f32[32,384]{1,0:T(8,128)S(1)} %add.10._.sums), channel_id=1, source_target_pairs={{0,5},{1,4},{2,7},{3,6},{4,1},{5,0},{6,3},{7,2},{8,13},{9,12},{10,... | collective-permute-start | bytes 147464 | tf_op jit(solution)/shard_map/ppermute | solution.py:321
  20.9 2.9 %collective-permute-start.10 = (f32[64,128]{1,0:T(8,128)S(1)}, f32[64,128]{1,0:T(8,128)S(1)}, u32[]{:S(2)}, u32[]{:S(2)}) collective-permute-start(f32[64,128]{1,0:T(8,128)S(1)} %get-tuple-element.66.refs_2_), channel_id=1, source_target_pairs={{0,1},{1,0},{2,3},{3,2},{4,5},{5,4},{6,7},{7,6},{8,9},{9,8},{10,11... | collective-permute-start | bytes 98312 | tf_op jit(solution)/shard_map/ppermute | solution.py:321
  21.3 2.5 %collective-permute-start.8 = (f32[64,128]{1,0:T(8,128)S(1)}, f32[64,128]{1,0:T(8,128)S(1)}, u32[]{:S(2)}, u32[]{:S(2)}) collective-permute-start(f32[64,128]{1,0:T(8,128)S(1)} %get-tuple-element.64), channel_id=1, source_target_pairs={{0,1},{1,0},{2,3},{3,2},{4,5},{5,4},{6,7},{7,6},{8,9},{9,8},{10,11... | collective-permute-start | bytes 98312 | tf_op jit(solution)/shard_map/ppermute | solution.py:321
  21.4 2.4 %collective-permute-start.9 = (f32[64,128]{1,0:T(8,128)S(1)}, f32[64,128]{1,0:T(8,128)S(1)}, u32[]{:S(2)}, u32[]{:S(2)}) collective-permute-start(f32[64,128]{1,0:T(8,128)S(1)} %get-tuple-element.65), channel_id=1, source_target_pairs={{0,1},{1,0},{2,3},{3,2},{4,5},{5,4},{6,7},{7,6},{8,9},{9,8},{10,11... | collective-permute-start | bytes 98312 | tf_op jit(solution)/shard_map/ppermute | solution.py:321
  24.0 4.6 %collective-permute-start.11 = (f32[32,768]{1,0:T(8,128)S(1)}, f32[32,768]{1,0:T(8,128)S(1)}, u32[]{:S(2)}, u32[]{:S(2)}) collective-permute-start(f32[32,768]{1,0:T(8,128)S(1)} %shard_map.82.packed), channel_id=1, source_target_pairs={{0,9},{1,8},{2,11},{3,10},{4,13},{5,12},{6,15},{7,14},{8,1},{9,0},... | collective-permute-start | bytes 294920 | tf_op jit(solution)/shard_map/ppermute | solution.py:321
  28.9 3.2 %collective-permute-start.13 = (f32[32,128]{1,0:T(8,128)S(1)}, f32[32,128]{1,0:T(8,128)S(1)}, u32[]{:S(2)}, u32[]{:S(2)}) collective-permute-start(f32[32,128]{1,0:T(8,128)S(1)} %get-tuple-element.75), channel_id=1, source_target_pairs={{0,17},{1,16},{2,19},{3,18},{4,21},{5,20},{6,23},{7,22},{8,25},{9,... | collective-permute-start | bytes 49160 | tf_op jit(solution)/shard_map/ppermute | solution.py:321
  30.5 2.1 %collective-permute-start.12 = (f32[32,768]{1,0:T(8,128)S(1)}, f32[32,768]{1,0:T(8,128)S(1)}, u32[]{:S(2)}, u32[]{:S(2)}) collective-permute-start(f32[32,768]{1,0:T(8,128)S(1)} %pad_maximum_fusion), channel_id=1, source_target_pairs={{0,1},{1,0},{2,3},{3,2},{4,5},{5,4},{6,7},{7,6},{8,9},{9,8},{10,11... | collective-permute-start | bytes 294920 | tf_op jit(solution)/shard_map/ppermute | solution.py:321
  32.1 1.4 %collective-permute-start.14 = (f32[32,256]{1,0:T(8,128)S(1)}, f32[32,256]{1,0:T(8,128)S(1)}, u32[]{:S(2)}, u32[]{:S(2)}) collective-permute-start(f32[32,256]{1,0:T(8,128)S(1)} %pad_maximum_fusion.1.mine), channel_id=1, source_target_pairs={{0,1},{1,0},{2,3},{3,2},{4,5},{5,4},{6,7},{7,6},{8,9},{9,8},{10,11... | collective-permute-start | bytes 98312 | tf_op jit(solution)/shard_map/ppermute | solution.py:321

commit v10 on v9

--- a/solution.py
+++ b/solution.py
@@ -14,6 +14,7 @@
 TN = (((0,), (0,)), ((), ()))
 ANY = pl.BlockSpec(memory_space=pl.ANY)
 HBM = pl.BlockSpec(memory_space=pltpu.HBM)
+SMEM = pl.BlockSpec(memory_space=pltpu.SMEM)
 VMEM = pl.BlockSpec(memory_space=pltpu.VMEM)
 LIMIT = 24 * 1024 * 1024
 
@@ -44,9 +45,18 @@
     return parity
 
 
-def low_kernel(
-    top, left, right, rhs, leaf, order, keep, send, left_v, right_v, rhs_v, leaf_v, order_v,
-    left_mid, right_mid, sems,
+def sides(split, size):
+    border = split[0:1, 0:1]
+    return (
+        lax.broadcasted_iota(jnp.int32, (1, size), 1) < border,
+        lax.broadcasted_iota(jnp.int32, (size, 1), 0) < border,
+    )
+
+
+def first_reads(
+    top, left, right, coupling, rhs, leaf, order, split, keep, send, current, gram_top, gram_next,
+    left_low, right_low, left_mid, right_mid, left_top, right_top, right_last, near, split_v,
+    rhs_v, leaf_v, order_v, sems,
 ):
     rank = left.shape[2]
     n = rank // 2
@@ -54,23 +64,40 @@
     bases = []
     for j in range(count):
         cols = slice(j * rank, (j + 1) * rank)
-        bases.append(pltpu.make_async_copy(left.at[j + 1], left_v.at[:, cols], sems.at[0, j]))
-        bases.append(pltpu.make_async_copy(right.at[j], right_v.at[:, cols], sems.at[1, j]))
-    rest = [
-        pltpu.make_async_copy(order, order_v, sems.at[2, 1]),
-        pltpu.make_async_copy(rhs, rhs_v, sems.at[2, 2]),
-        pltpu.make_async_copy(leaf, leaf_v, sems.at[2, 3]),
+        bases.append(pltpu.make_async_copy(left.at[j + 1], left_low.at[:, cols], sems.at[0, j]))
+        bases.append(pltpu.make_async_copy(right.at[j], right_low.at[:, cols], sems.at[1, j]))
+    rows = [
+        pltpu.make_async_copy(order, order_v, sems.at[2, 0]),
+        pltpu.make_async_copy(rhs, rhs_v, sems.at[2, 1]),
+    ]
+    leaf_copy = pltpu.make_async_copy(leaf, leaf_v, sems.at[2, 2])
+    mid = [
         pltpu.make_async_copy(left.at[top - 2], left_mid.at[:, :rank], sems.at[3, 0]),
         pltpu.make_async_copy(left.at[top - 1], left_mid.at[:, rank:], sems.at[3, 1]),
         pltpu.make_async_copy(right.at[top - 3], right_mid.at[:, :rank], sems.at[3, 2]),
         pltpu.make_async_copy(right.at[top - 2], right_mid.at[:, rank:], sems.at[3, 3]),
     ]
-    for copy in bases + rest:
+    rest = [
+        pltpu.make_async_copy(right.at[top], right_top, sems.at[4, 0]),
+        pltpu.make_async_copy(coupling.at[0, pl.ds(top - 2, 3)], near, sems.at[4, 1]),
+        pltpu.make_async_copy(left.at[top], left_top, sems.at[4, 2]),
+        pltpu.make_async_copy(right.at[top - 1], right_last, sems.at[4, 3]),
+    ]
+    for copy in rows + bases + [leaf_copy] + mid + rest:
         copy.start()
+    split_v[...] = jnp.full(split_v.shape, split[0], jnp.int32)
+    device_id = lax.axis_index(AXES)
+    half = parity_of(device_id, top) == 1
+    size = rhs_v.shape[1]
+    for copy in rows:
+        copy.wait()
+    local = order_v[...] - device_id * size
+    pick = (lax.broadcasted_iota(jnp.int32, (size, size), 0) == local).astype(F32).astype(BF16)
+    high, low = parts(rhs_v[...])
+    moved = product(jnp.concatenate([high, low], axis=0), pick, NN).astype(BF16)
     for copy in bases:
         copy.wait()
-    half = parity_of(lax.axis_index(AXES), top) == 1
-    grams = dot(left_v[...], right_v[...], TN)
+    grams = dot(left_low[...], right_low[...], TN)
     at = 0
     for k in range(count, 0, -1):
         w = k * rank
@@ -78,40 +105,14 @@
         keep[:, at : at + w] = jnp.where(half, value[n:], value[:n])
         send[:, at : at + w] = jnp.where(half, value[:n], value[n:])
         at += w
-    for copy in rest:
+    leaf_copy.wait()
+    rows_n = rhs_v.shape[0]
+    is_left, left_rows = sides(split_v, size)
+    lh, ll = parts(jnp.where(left_rows == is_left, leaf_v[...], 0.0))
+    both = product(moved, lh, NN)
+    current[...] = both[:rows_n] + (both[rows_n:] + product(moved[:rows_n], ll, NN))
+    for copy in mid:
         copy.wait()
-
-
-def sides(split, size):
-    border = split[...]
-    return (
-        lax.broadcasted_iota(jnp.int32, (1, size), 1) < border,
-        lax.broadcasted_iota(jnp.int32, (size, 1), 0) < border,
-    )
-
-
-def leaf_kernel(
-    top, order, split, rhs, leaf, right_low, left_mid, right_mid, left, right, coupling, current,
-    gram_top, gram_next, right_last, left_top, right_top, coupling_v, sems,
-):
-    rank = left_top.shape[1]
-    count, size = rhs.shape
-    copies = [
-        pltpu.make_async_copy(right.at[top], right_top, sems.at[0]),
-        pltpu.make_async_copy(coupling.at[0, pl.ds(top - 2, 3)], coupling_v, sems.at[1]),
-        pltpu.make_async_copy(left.at[top], left_top, sems.at[2]),
-        pltpu.make_async_copy(right.at[top - 1], right_last, sems.at[3]),
-    ]
-    for copy in copies:
-        copy.start()
-    local = order[...] - lax.axis_index(AXES) * size
-    pick = (lax.broadcasted_iota(jnp.int32, (size, size), 0) == local).astype(F32).astype(BF16)
-    high, low = parts(rhs[...])
-    moved = product(jnp.concatenate([high, low], axis=0), pick, NN).astype(BF16)
-    columns, rows = sides(split, size)
-    lh, ll = parts(jnp.where(rows == columns, leaf[...], 0.0))
-    both = product(moved, lh, NN)
-    current[...] = both[:count] + (both[count:] + product(moved[:count], ll, NN))
     low_w = right_low.shape[1]
     upper = left_mid[...]
     value = dot(upper, right_low[...], TN)
@@ -120,7 +121,8 @@
     value = dot(upper, right_mid[...], TN)
     gram_next[:, low_w:] = value[:rank, :rank]
     gram_top[:, low_w:] = value[rank:]
-    for copy in copies:
+    put_rows(send, at, gram_next[...])
+    for copy in rest:
         copy.wait()
 
 
@@ -152,7 +154,7 @@
 
 def local_kernel(
     top, split, first, left_top, right_top, right_low, right_mid, right_last, coupling, gram_top,
-    gram_next, _, current_out, keep, send,
+    current_out, keep, send,
 ):
     rank = left_top.shape[1]
     count, size = first.shape
@@ -175,8 +177,7 @@
         keep[:, at : at + w] = jnp.where(half, sums[n:], sums[:n])
         send[:, at : at + w] = jnp.where(half, sums[:n], sums[n:])
         at += w
-    at = put_rows(send, at, gram_top[...])
-    put_rows(send, at, gram_next[...])
+    put_rows(send, at, gram_top[...])
 
 
 def beside(own, got, on_right):
@@ -210,7 +211,7 @@
     rank, w = gram_next.shape
     right = (lax.axis_index(AXES) >> 1) & 1 == 1
     z = dot(beside(mine[...], got[...], right), side_of(coupling, 0, right))
-    at = top * rank + rank // got_gram.shape[0] * (w + rank)
+    at = got_gram.shape[1] - rank // got_gram.shape[0] * w
     gram = gram_next[...] + take_rows(got_gram, at, rank, w)
     z_out[...] = z
     sums_out[...] = sums[...] - dot(z, gram)
@@ -331,58 +332,49 @@
     low_w = rank * (top - 2) * (top - 3) // 2
     next_w = (top - 2) * rank
     device_id = lax.axis_index(AXES)
-    split = leaf_split.reshape(1, 1)
-    keep, send, left_low, right_low, rhs, leaf, order, left_mid, right_mid = call(
-        functools.partial(low_kernel, top),
+    f32_shapes = [
+        shape(n, low_w),
+        shape(n, low_w + 2 * next_w),
+        shape(count, size),
+        shape(rank, wide - rank),
+        shape(rank, next_w),
+        shape(size, (top - 3) * rank),
+        shape(size, (top - 3) * rank),
+        shape(size, 2 * rank),
+        shape(size, 2 * rank),
+        shape(size, rank),
+        shape(size, rank),
+        shape(size, rank),
+        shape(3, 2 * rank, 2 * rank),
+    ]
+    (
+        keep, send, current, gram_top, gram_next, left_low, right_low, left_mid, right_mid, left_top,
+        right_top, right_last, near, split,
+    ) = call(
+        functools.partial(first_reads, top),
+        f32_shapes + [shape(8, 128, dtype=jnp.int32)],
+        [HBM] * 6 + [SMEM],
+        [VMEM] * 14,
         [
-            shape(n, low_w),
-            shape(n, low_w),
-            shape(size, (top - 3) * rank),
-            shape(size, (top - 3) * rank),
-            shape(count, size),
-            shape(size, size),
-            shape(1, size, dtype=jnp.int32),
-            shape(size, 2 * rank),
-            shape(size, 2 * rank),
+            pltpu.VMEM((count, size), F32),
+            pltpu.VMEM((size, size), F32),
+            pltpu.VMEM((1, size), jnp.int32),
+            pltpu.SemaphoreType.DMA((5, max(4, top - 3))),
         ],
-        [HBM] * 5,
-        [VMEM] * 9,
-        [pltpu.SemaphoreType.DMA((4, max(4, top - 3)))],
-        *in_hbm(basis_left, basis_right, right_side, leaf_inverse, order.reshape(1, size)),
-    )
-    got_low = exchange(send, 1)
-    current, gram_top, gram_next, right_last, left_top, right_top, near = call(
-        functools.partial(leaf_kernel, top),
-        [
-            shape(count, size),
-            shape(rank, wide - rank),
-            shape(rank, next_w),
-            shape(size, rank),
-            shape(size, rank),
-            shape(size, rank),
-            shape(3, 2 * rank, 2 * rank),
-        ],
-        [VMEM] * 7 + [HBM] * 3,
-        [VMEM] * 7,
-        [pltpu.SemaphoreType.DMA((5,))],
-        order,
-        split,
-        rhs,
-        leaf,
-        right_low,
-        left_mid,
-        right_mid,
-        *in_hbm(basis_left, basis_right, coupling),
-    )
-    low = keep + got_low
+        *in_hbm(basis_left, basis_right, coupling, right_side, leaf_inverse),
+        *in_hbm(order.reshape(1, size)),
+        leaf_split,
+    )
+    got_gram = exchange(send, 1)
+    low = keep + got_gram[:, :low_w]
     current, keep, send = call(
         functools.partial(local_kernel, top),
         [
             shape(count, size),
             shape(rows, wide),
-            shape(rows, wide + rank // rows * (wide - rank + next_w)),
+            shape(rows, wide + rank // rows * (wide - rank)),
         ],
-        [VMEM] * 10 + [ANY],
+        [VMEM] * 9,
         [VMEM] * 3,
         [],
         split,
@@ -394,8 +386,6 @@
         right_last,
         near,
         gram_top,
-        gram_next,
-        low,
     )
     got = exchange(send, 1)
     sums, next_sums, z_mine, z_other = call(
@@ -422,7 +412,7 @@
         got_next,
         sums,
         gram_next,
-        got,
+        got_gram,
         near,
     )
     known[top - 2] = (z, z)

time: 34.6 us -> 34.3 us (level)
    pallas_call x13 -> x12, Pallas kernels: 8.84 us -> 8.8 us  [call(): pl.pallas_call(kernel, out_shape=outs, in_specs=in_specs, out_specs=out_s...]
  transfers between devices with their start and end apart: 15 -> 15, of which waited for: 6 -> 5; matrix products, arithmetic and copies ran while one was open for 0% -> 0% of each run, Pallas kernels for 12% -> 12%
where the time goes in v10:
time: 34.3 us; the launch traced here: 34.2 us
  starting transfers between devices  16.4 us (48%)
  Pallas kernels  8.8 us (26%)
  waiting for transfers between devices  8.15 us (24%)
  between operations  0.79 us (2%)
    ppermute x15, starting transfers between devices, exchange(): lax.ppermute(value, AXES, [(i, i ^ mask) for i in range(lax.axis_size(AXE...  16.4 us
    pallas_call x12, Pallas kernels, call(): pl.pallas_call(kernel, out_shape=outs, in_specs=in_specs, out_specs=out_s...  8.8 us
    ppermute x15, waiting for transfers between devices, exchange(): lax.ppermute(value, AXES, [(i, i ^ mask) for i in range(lax.axis_size(AXE...  8.15 us
  transfers between devices with their start and end apart: 15, of which 5 were waited for; matrix products, arithmetic and copies ran while one was open for 0% of the time, Pallas kernels for 12%

profile of v10, /device:TPU:0, one launch (start us, length us, event | category | flops | bytes accessed | tf_op | source)
XLA Modules:
  0.0 34.2 jit_solution(15054740140665806976)
XLA Ops:
  0.7 3.4 %shard_map.73 = (f32[64,384]{1,0:T(8,128)S(1)}, f32[64,1152]{1,0:T(8,128)S(1)}, f32[64,512]{1,0:T(8,128)S(1)}, f32[128,512]{1,0:T(8,128)S(1)}, f32[128,384]{1,0:...) custom-call(f32[6,512,128]{2,1,0:T(8,128)} %left.3, ...), custom_call_target="tpu_custom_call" | custom-call | flops 1 | bytes 1 | tf_op jit(solution)/shard_map/pallas_call | solution.py:302
  4.1 0.5 %collective-permute-start.2 = (f32[64,1152]{1,0:T(8,128)S(1)}, f32[64,1152]{1,0:T(8,128)S(1)}, u32[]{:S(2)}, u32[]{:S(2)}) collective-permute-start(f32[64,1152]{1,0:T(8,128)S(1)} %get-tuple-element.54), channel_id=1, source_target_pairs={{0,1},{1,0},{2,3},{3,2},{4,5},{5,4},{6,7},{7,6},{8,9},{9,8},{10,11... | collective-permute-start | bytes 884744 | tf_op jit(solution)/shard_map/ppermute | solution.py:322
  4.6 1.1 %shard_map.74 = (f32[64,512]{1,0:T(8,128)S(1)}, f32[32,640]{1,0:T(8,128)S(1)}, f32[32,2688]{1,0:T(8,128)S(1)}) custom-call(s32[8,128]{1,0:T(8,128)S(1)} %get-tuple-element.39.split, f32[64,512]{1,0:T(8,128)S(1)} %get-tuple-element.40.first, f32[512,128]{1,0:T(8,128)S(1)} %get-tuple-element.41.left_top, f32[512,128]{1,0:T(8,128)S(1)} %get-tuple-element.42.right_top, ...), custom_call_target="tpu_custom_call" | custom-call | flops 1 | bytes 1 | tf_op jit(solution)/shard_map/pallas_call | solution.py:302
  5.7 0.1 collective-permute-start
  5.8 0.0 collective-permute-done.2.got_gram
  5.8 2.7 %collective-permute-start.5 = (f32[64,384]{1,0:T(8,128)S(1)}, f32[64,384]{1,0:T(8,128)S(1)}, u32[]{:S(2)}, u32[]{:S(2)}) collective-permute-start(f32[64,384]{1,0:T(8,128)S(1)} %slice_add_fusion.low), channel_id=1, source_target_pairs={{0,3},{1,2},{2,1},{3,0},{4,7},{5,6},{6,5},{7,4},{8,11},{9,10},{10,... | collective-permute-start | bytes 294920 | tf_op jit(solution)/shard_map/ppermute | solution.py:322
  8.6 0.0 collective-permute-done.got
  8.6 0.4 %shard_map.75 = (f32[32,384]{1,0:T(8,128)S(1)}, f32[32,128]{1,0:T(8,128)S(1)}, f32[32,128]{1,0:T(8,128)S(1)}, f32[32,128]{1,0:T(8,128)S(1)}) custom-call(f32[32,640]{1,0:T(8,128)S(1)} %get-tuple-element.49.keep, f32[32,2688]{1,0:T(8,128)S(1)} %collective-permute-done.got, f32[128,512]{1,0:T(8,128)S(1)} %get-tuple-element.47.gram_top, ...), custom_call_target="tpu_custom_call" | custom-call | flops 1 | bytes 1 | tf_op jit(solution)/shard_map/pallas_call | solution.py:302
  9.0 1.5 %collective-permute-start.1 = (f32[32,128]{1,0:T(8,128)S(1)}, f32[32,128]{1,0:T(8,128)S(1)}, u32[]{:S(2)}, u32[]{:S(2)}) collective-permute-start(f32[32,128]{1,0:T(8,128)S(1)} %get-tuple-element.51.mine), channel_id=1, source_target_pairs={{0,3},{1,2},{2,1},{3,0},{4,7},{5,6},{6,5},{7,4},{8,11},{9,10},{10,... | collective-permute-start | bytes 49160 | tf_op jit(solution)/shard_map/ppermute | solution.py:322
  10.5 1.7 %collective-permute-done.1.got._ = f32[32,128]{1,0:T(8,128)S(1)} collective-permute-done((f32[32,128]{1,0:T(8,128)S(1)}, f32[32,128]{1,0:T(8,128)S(1)}, u32[]{:S(2)}, u32[]{:S(2)}) %collective-permute-start.1) | collective-permute-done | bytes 16416 | tf_op jit(solution)/shard_map/ppermute | solution.py:322
  12.2 0.0 collective-permute-done.5.got
  12.2 2.8 %collective-permute-start.6 = (f32[64,384]{1,0:T(8,128)S(1)}, f32[64,384]{1,0:T(8,128)S(1)}, u32[]{:S(2)}, u32[]{:S(2)}) collective-permute-start(f32[64,384]{1,0:T(8,128)S(1)} %shard_map.79.low), channel_id=1, source_target_pairs={{0,5},{1,4},{2,7},{3,6},{4,1},{5,0},{6,3},{7,2},{8,13},{9,12},{10,... | collective-permute-start | bytes 294920 | tf_op jit(solution)/shard_map/ppermute | solution.py:322
  14.9 0.3 shard_map.76
  15.2 1.6 %collective-permute-start.3 = (f32[32,384]{1,0:T(8,128)S(1)}, f32[32,384]{1,0:T(8,128)S(1)}, u32[]{:S(2)}, u32[]{:S(2)}) collective-permute-start(f32[32,384]{1,0:T(8,128)S(1)} %get-tuple-element.55), channel_id=1, source_target_pairs={{0,3},{1,2},{2,1},{3,0},{4,7},{5,6},{6,5},{7,4},{8,11},{9,10},{10,... | collective-permute-start | bytes 147464 | tf_op jit(solution)/shard_map/ppermute | solution.py:322
  16.8 0.1 collective-permute-start.7
  16.9 2.0 %collective-permute-done.3 = f32[32,384]{1,0:T(8,128)S(1)} collective-permute-done((f32[32,384]{1,0:T(8,128)S(1)}, f32[32,384]{1,0:T(8,128)S(1)}, u32[]{:S(2)}, u32[]{:S(2)}) %collective-permute-start.3) | collective-permute-done | bytes 49184 | tf_op jit(solution)/shard_map/ppermute | solution.py:322
  18.9 1.9 %collective-permute-start.4 = (f32[32,384]{1,0:T(8,128)S(1)}, f32[32,384]{1,0:T(8,128)S(1)}, u32[]{:S(2)}, u32[]{:S(2)}) collective-permute-start(f32[32,384]{1,0:T(8,128)S(1)} %add.9._.sums), channel_id=1, source_target_pairs={{0,5},{1,4},{2,7},{3,6},{4,1},{5,0},{6,3},{7,2},{8,13},{9,12},{10,... | collective-permute-start | bytes 147464 | tf_op jit(solution)/shard_map/ppermute | solution.py:322
  20.8 0.0 collective-permute-done.6.got.got_low
  20.8 0.5 %collective-permute-start.10 = (f32[64,128]{1,0:T(8,128)S(1)}, f32[64,128]{1,0:T(8,128)S(1)}, u32[]{:S(2)}, u32[]{:S(2)}) collective-permute-start(f32[64,128]{1,0:T(8,128)S(1)} %get-tuple-element.61.refs_2_), channel_id=1, source_target_pairs={{0,1},{1,0},{2,3},{3,2},{4,5},{5,4},{6,7},{7,6},{8,9},{9,8},{10,11... | collective-permute-start | bytes 98312 | tf_op jit(solution)/shard_map/ppermute | solution.py:322
  21.3 0.1 collective-permute-start.8
  21.4 0.4 %collective-permute-start.9 = (f32[64,128]{1,0:T(8,128)S(1)}, f32[64,128]{1,0:T(8,128)S(1)}, u32[]{:S(2)}, u32[]{:S(2)}) collective-permute-start(f32[64,128]{1,0:T(8,128)S(1)} %get-tuple-element.60), channel_id=1, source_target_pairs={{0,1},{1,0},{2,3},{3,2},{4,5},{5,4},{6,7},{7,6},{8,9},{9,8},{10,11... | collective-permute-start | bytes 98312 | tf_op jit(solution)/shard_map/ppermute | solution.py:322
  21.8 1.2 %shard_map.77 = (f32[512,128]{1,0:T(8,128)S(1)}, f32[3,256,256]{2,1,0:T(8,128)S(1)}) custom-call(f32[6,512,128]{2,1,0:T(8,128)} %left.3, f32[1,6,256,256]{3,2,1,0:T(8,128)} %coupling.3, f32[32,384]{1,0:T(8,128)S(1)} %add.9._.sums), custom_call_target="tpu_custom_call" | custom-call | flops 1 | bytes 1 | tf_op jit(solution)/shard_map/pallas_call | solution.py:302
  23.0 0.4 %collective-permute-done.4.got = f32[32,384]{1,0:T(8,128)S(1)} collective-permute-done((f32[32,384]{1,0:T(8,128)S(1)}, f32[32,384]{1,0:T(8,128)S(1)}, u32[]{:S(2)}, u32[]{:S(2)}) %collective-permute-start.4) | collective-permute-done | bytes 49184 | tf_op jit(solution)/shard_map/ppermute | solution.py:322
  23.4 0.2 shard_map.78
  23.5 0.0 collective-permute-done.7.other
  23.5 0.0 collective-permute-done.10.refs_3_
  23.5 0.0 collective-permute-done.8.refs_0_
  23.5 0.0 collective-permute-done.9.refs_1_
  23.6 0.2 shard_map.81.packed
  23.8 1.8 %collective-permute-start.11 = (f32[32,768]{1,0:T(8,128)S(1)}, f32[32,768]{1,0:T(8,128)S(1)}, u32[]{:S(2)}, u32[]{:S(2)}) collective-permute-start(f32[32,768]{1,0:T(8,128)S(1)} %shard_map.81.packed), channel_id=1, source_target_pairs={{0,9},{1,8},{2,11},{3,10},{4,13},{5,12},{6,15},{7,14},{8,1},{9,0},... | collective-permute-start | bytes 294920 | tf_op jit(solution)/shard_map/ppermute | solution.py:322
  25.5 2.7 %collective-permute-done.11.got = f32[32,768]{1,0:T(8,128)S(1)} collective-permute-done((f32[32,768]{1,0:T(8,128)S(1)}, f32[32,768]{1,0:T(8,128)S(1)}, u32[]{:S(2)}, u32[]{:S(2)}) %collective-permute-start.11) | collective-permute-done | bytes 98336 | tf_op jit(solution)/shard_map/ppermute | solution.py:322
  28.2 0.3 shard_map.82
  28.5 1.7 %collective-permute-start.13 = (f32[32,128]{1,0:T(8,128)S(1)}, f32[32,128]{1,0:T(8,128)S(1)}, u32[]{:S(2)}, u32[]{:S(2)}) collective-permute-start(f32[32,128]{1,0:T(8,128)S(1)} %get-tuple-element.71), channel_id=1, source_target_pairs={{0,17},{1,16},{2,19},{3,18},{4,21},{5,20},{6,23},{7,22},{8,25},{9,... | collective-permute-start | bytes 49160 | tf_op jit(solution)/shard_map/ppermute | solution.py:322
  30.3 0.1 collective-permute-start.12
  30.3 1.4 %collective-permute-done.13 = f32[32,128]{1,0:T(8,128)S(1)} collective-permute-done((f32[32,128]{1,0:T(8,128)S(1)}, f32[32,128]{1,0:T(8,128)S(1)}, u32[]{:S(2)}, u32[]{:S(2)}) %collective-permute-start.13) | collective-permute-done | bytes 16416 | tf_op jit(solution)/shard_map/ppermute | solution.py:322
  31.8 0.6 %collective-permute-start.14 = (f32[32,256]{1,0:T(8,128)S(1)}, f32[32,256]{1,0:T(8,128)S(1)}, u32[]{:S(2)}, u32[]{:S(2)}) collective-permute-start(f32[32,256]{1,0:T(8,128)S(1)} %pad_maximum_fusion.1.mine), channel_id=1, source_target_pairs={{0,1},{1,0},{2,3},{3,2},{4,5},{5,4},{6,7},{7,6},{8,9},{9,8},{10,11... | collective-permute-start | bytes 98312 | tf_op jit(solution)/shard_map/ppermute | solution.py:322
  32.4 0.0 collective-permute-done.12
  32.4 0.8 %shard_map.83 = (f32[64,512]{1,0:T(8,128)S(1)}, f32[256,512]{1,0:T(8,128)S(1)}) custom-call(f32[64,512]{1,0:T(8,128)S(1)} %get-tuple-element.48.current, f32[32,256]{1,0:T(8,128)S(1)} %get-tuple-element.62.refs_0_, f32[32,256]{1,0:T(8,128)S(1)} %get-tuple-element.76.refs_1_, f32[32,256]{1,0:T(8,128)S(1)} %get-tuple-element.63.refs_2_, ...), custom_call_target="tpu_custom_call" | custom-call | flops 1 | bytes 1 | tf_op jit(solution)/shard_map/pallas_call | solution.py:302
  33.3 0.0 collective-permute-done.14.other
  33.3 0.9 %shard_map.84 = f32[64,512]{1,0:T(8,128)} custom-call(f32[64,512]{1,0:T(8,128)S(1)} %get-tuple-element.70.current, f32[32,256]{1,0:T(8,128)S(1)} %pad_maximum_fusion.1.mine, f32[32,256]{1,0:T(8,128)S(1)} %collective-permute-done.14.other, f32[256,512]{1,0:T(8,128)S(1)} %get-tuple-element.72.factor), custom_call_target="tpu_custom_call" | custom-call | flops 1 | bytes 1 | tf_op jit(solution)/shard_map/pallas_call | solution.py:302
  (10 shorter events, 0.1 us)
Async XLA Ops:
  4.1 1.7 %collective-permute-start.2 = (f32[64,1152]{1,0:T(8,128)S(1)}, f32[64,1152]{1,0:T(8,128)S(1)}, u32[]{:S(2)}, u32[]{:S(2)}) collective-permute-start(f32[64,1152]{1,0:T(8,128)S(1)} %get-tuple-element.54), channel_id=1, source_target_pairs={{0,1},{1,0},{2,3},{3,2},{4,5},{5,4},{6,7},{7,6},{8,9},{9,8},{10,11... | collective-permute-start | bytes 884744 | tf_op jit(solution)/shard_map/ppermute | solution.py:322
  5.7 2.9 %collective-permute-start = (f32[32,2688]{1,0:T(8,128)S(1)}, f32[32,2688]{1,0:T(8,128)S(1)}, u32[]{:S(2)}, u32[]{:S(2)}) collective-permute-start(f32[32,2688]{1,0:T(8,128)S(1)} %get-tuple-element.50), channel_id=1, source_target_pairs={{0,1},{1,0},{2,3},{3,2},{4,5},{5,4},{6,7},{7,6},{8,9},{9,8},{10,11... | collective-permute-start | bytes 1032200 | tf_op jit(solution)/shard_map/ppermute | solution.py:322
  5.8 6.3 %collective-permute-start.5 = (f32[64,384]{1,0:T(8,128)S(1)}, f32[64,384]{1,0:T(8,128)S(1)}, u32[]{:S(2)}, u32[]{:S(2)}) collective-permute-start(f32[64,384]{1,0:T(8,128)S(1)} %slice_add_fusion.low), channel_id=1, source_target_pairs={{0,3},{1,2},{2,1},{3,0},{4,7},{5,6},{6,5},{7,4},{8,11},{9,10},{10,... | collective-permute-start | bytes 294920 | tf_op jit(solution)/shard_map/ppermute | solution.py:322
  9.0 3.2 %collective-permute-start.1 = (f32[32,128]{1,0:T(8,128)S(1)}, f32[32,128]{1,0:T(8,128)S(1)}, u32[]{:S(2)}, u32[]{:S(2)}) collective-permute-start(f32[32,128]{1,0:T(8,128)S(1)} %get-tuple-element.51.mine), channel_id=1, source_target_pairs={{0,3},{1,2},{2,1},{3,0},{4,7},{5,6},{6,5},{7,4},{8,11},{9,10},{10,... | collective-permute-start | bytes 49160 | tf_op jit(solution)/shard_map/ppermute | solution.py:322
  12.2 8.6 %collective-permute-start.6 = (f32[64,384]{1,0:T(8,128)S(1)}, f32[64,384]{1,0:T(8,128)S(1)}, u32[]{:S(2)}, u32[]{:S(2)}) collective-permute-start(f32[64,384]{1,0:T(8,128)S(1)} %shard_map.79.low), channel_id=1, source_target_pairs={{0,5},{1,4},{2,7},{3,6},{4,1},{5,0},{6,3},{7,2},{8,13},{9,12},{10,... | collective-permute-start | bytes 294920 | tf_op jit(solution)/shard_map/ppermute | solution.py:322
  15.2 3.7 %collective-permute-start.3 = (f32[32,384]{1,0:T(8,128)S(1)}, f32[32,384]{1,0:T(8,128)S(1)}, u32[]{:S(2)}, u32[]{:S(2)}) collective-permute-start(f32[32,384]{1,0:T(8,128)S(1)} %get-tuple-element.55), channel_id=1, source_target_pairs={{0,3},{1,2},{2,1},{3,0},{4,7},{5,6},{6,5},{7,4},{8,11},{9,10},{10,... | collective-permute-start | bytes 147464 | tf_op jit(solution)/shard_map/ppermute | solution.py:322
  16.8 6.7 %collective-permute-start.7 = (f32[64,256]{1,0:T(8,128)S(1)}, f32[64,256]{1,0:T(8,128)S(1)}, u32[]{:S(2)}, u32[]{:S(2)}) collective-permute-start(f32[64,256]{1,0:T(8,128)S(1)} %slice.25), channel_id=1, source_target_pairs={{0,1},{1,0},{2,3},{3,2},{4,5},{5,4},{6,7},{7,6},{8,9},{9,8},{10,11... | collective-permute-start | bytes 196616 | tf_op jit(solution)/shard_map/ppermute | solution.py:322
  18.9 4.4 %collective-permute-start.4 = (f32[32,384]{1,0:T(8,128)S(1)}, f32[32,384]{1,0:T(8,128)S(1)}, u32[]{:S(2)}, u32[]{:S(2)}) collective-permute-start(f32[32,384]{1,0:T(8,128)S(1)} %add.9._.sums), channel_id=1, source_target_pairs={{0,5},{1,4},{2,7},{3,6},{4,1},{5,0},{6,3},{7,2},{8,13},{9,12},{10,... | collective-permute-start | bytes 147464 | tf_op jit(solution)/shard_map/ppermute | solution.py:322
  20.8 2.7 %collective-permute-start.10 = (f32[64,128]{1,0:T(8,128)S(1)}, f32[64,128]{1,0:T(8,128)S(1)}, u32[]{:S(2)}, u32[]{:S(2)}) collective-permute-start(f32[64,128]{1,0:T(8,128)S(1)} %get-tuple-element.61.refs_2_), channel_id=1, source_target_pairs={{0,1},{1,0},{2,3},{3,2},{4,5},{5,4},{6,7},{7,6},{8,9},{9,8},{10,11... | collective-permute-start | bytes 98312 | tf_op jit(solution)/shard_map/ppermute | solution.py:322
  21.3 2.3 %collective-permute-start.8 = (f32[64,128]{1,0:T(8,128)S(1)}, f32[64,128]{1,0:T(8,128)S(1)}, u32[]{:S(2)}, u32[]{:S(2)}) collective-permute-start(f32[64,128]{1,0:T(8,128)S(1)} %get-tuple-element.59), channel_id=1, source_target_pairs={{0,1},{1,0},{2,3},{3,2},{4,5},{5,4},{6,7},{7,6},{8,9},{9,8},{10,11... | collective-permute-start | bytes 98312 | tf_op jit(solution)/shard_map/ppermute | solution.py:322
  21.4 2.2 %collective-permute-start.9 = (f32[64,128]{1,0:T(8,128)S(1)}, f32[64,128]{1,0:T(8,128)S(1)}, u32[]{:S(2)}, u32[]{:S(2)}) collective-permute-start(f32[64,128]{1,0:T(8,128)S(1)} %get-tuple-element.60), channel_id=1, source_target_pairs={{0,1},{1,0},{2,3},{3,2},{4,5},{5,4},{6,7},{7,6},{8,9},{9,8},{10,11... | collective-permute-start | bytes 98312 | tf_op jit(solution)/shard_map/ppermute | solution.py:322
  23.8 4.4 %collective-permute-start.11 = (f32[32,768]{1,0:T(8,128)S(1)}, f32[32,768]{1,0:T(8,128)S(1)}, u32[]{:S(2)}, u32[]{:S(2)}) collective-permute-start(f32[32,768]{1,0:T(8,128)S(1)} %shard_map.81.packed), channel_id=1, source_target_pairs={{0,9},{1,8},{2,11},{3,10},{4,13},{5,12},{6,15},{7,14},{8,1},{9,0},... | collective-permute-start | bytes 294920 | tf_op jit(solution)/shard_map/ppermute | solution.py:322
  28.5 3.2 %collective-permute-start.13 = (f32[32,128]{1,0:T(8,128)S(1)}, f32[32,128]{1,0:T(8,128)S(1)}, u32[]{:S(2)}, u32[]{:S(2)}) collective-permute-start(f32[32,128]{1,0:T(8,128)S(1)} %get-tuple-element.71), channel_id=1, source_target_pairs={{0,17},{1,16},{2,19},{3,18},{4,21},{5,20},{6,23},{7,22},{8,25},{9,... | collective-permute-start | bytes 49160 | tf_op jit(solution)/shard_map/ppermute | solution.py:322
  30.3 2.1 %collective-permute-start.12 = (f32[32,768]{1,0:T(8,128)S(1)}, f32[32,768]{1,0:T(8,128)S(1)}, u32[]{:S(2)}, u32[]{:S(2)}) collective-permute-start(f32[32,768]{1,0:T(8,128)S(1)} %pad_maximum_fusion), channel_id=1, source_target_pairs={{0,1},{1,0},{2,3},{3,2},{4,5},{5,4},{6,7},{7,6},{8,9},{9,8},{10,11... | collective-permute-start | bytes 294920 | tf_op jit(solution)/shard_map/ppermute | solution.py:322
  31.8 1.5 %collective-permute-start.14 = (f32[32,256]{1,0:T(8,128)S(1)}, f32[32,256]{1,0:T(8,128)S(1)}, u32[]{:S(2)}, u32[]{:S(2)}) collective-permute-start(f32[32,256]{1,0:T(8,128)S(1)} %pad_maximum_fusion.1.mine), channel_id=1, source_target_pairs={{0,1},{1,0},{2,3},{3,2},{4,5},{5,4},{6,7},{7,6},{8,9},{9,8},{10,11... | collective-permute-start | bytes 98312 | tf_op jit(solution)/shard_map/ppermute | solution.py:322

commit v11 on v10

--- a/solution.py
+++ b/solution.py
@@ -236,18 +236,10 @@
     out[-1][...] = low[:, w:] + got[:, w:]
 
 
-def couple_kernel(top, k, sums, got, coupling, both, z):
-    rank = both.shape[1] // 2
-    right = (lax.axis_index(AXES) >> (top - 1 - k)) & 1 == 1
-    w = k * rank
-    both[...] = beside(sums[:, w:], got[:, w:], right)
-    z[...] = dot(both[...], coupling[k])
-
-
-def level_kernel(top, k, sums, got, z, low, got_low, other, *refs):
-    got_others, rests, (out, pair) = refs[:k], refs[k:-2], refs[-2:]
+def factor_kernel(top, k, low, got_low, other, *refs):
+    got_others, (coupling, out, pair) = refs[:k], refs[-3:]
     n = low.shape[0]
-    rank, w = 2 * n, k * 2 * n
+    rank = 2 * n
     bit = top - 1 - k
     device_id = lax.axis_index(AXES)
     half = parity_of(device_id, top)
@@ -261,7 +253,15 @@
         cols = slice(j * rank, (j + 1) * rank)
         put(right, low[:, cols], other[:, cols], cols)
         put(1 - right, got_low[:, cols], got_others[j][...], cols)
-    out[:, :w] = sums[:, :w] + got[:, :w] - dot(z[...], pair[...])
+    out[...] = dot(coupling[k], pair[...])
+
+
+def level_kernel(top, k, sums, got, factor, *refs):
+    rests, (out, both) = refs[:-2], refs[-2:]
+    w = factor.shape[1]
+    right = (lax.axis_index(AXES) >> (top - 1 - k)) & 1 == 1
+    both[...] = beside(sums[:, w:], got[:, w:], right)
+    out[:, :w] = sums[:, :w] + got[:, :w] - dot(both[...], factor[...])
     if rests:
         put_rows(out, w, joined(rests[0][...], rests[1][...], top))
 
@@ -446,29 +446,27 @@
         )
         pieces = [exchange(piece, 1) for piece in pieces]
         rests = [rest, exchange(rest, 1)] if last else []
-        both, z = call(
-            functools.partial(couple_kernel, top, k),
-            [shape(rows, 2 * rank), shape(rows, 2 * rank)],
-            [VMEM] * 3,
+        factor = call(
+            functools.partial(factor_kernel, top, k),
+            shape(2 * rank, w),
+            [VMEM] * (4 + k),
+            VMEM,
+            [pltpu.VMEM((2 * rank, w), F32)],
+            low,
+            got_low,
+            others,
+            *pieces,
+            coup,
+        )
+        sums, both = call(
+            functools.partial(level_kernel, top, k),
+            [shape(rows, w + (rank // rows * rank if last else 0)), shape(rows, 2 * rank)],
+            [VMEM] * (3 + len(rests)),
             [VMEM] * 2,
             [],
             sums,
             got,
-            coup,
-        )
-        sums = call(
-            functools.partial(level_kernel, top, k),
-            shape(rows, w + (rank // rows * rank if last else 0)),
-            [VMEM] * (6 + k + len(rests)),
-            VMEM,
-            [pltpu.VMEM((2 * rank, w), F32)],
-            sums,
-            got,
-            z,
-            low,
-            got_low,
-            others,
-            *pieces,
+            factor,
             *rests,
         )
         known[k] = (both, both)

time: 34.3 us -> 34.1 us (level)
  transfers between devices with their start and end apart: 15 -> 15, of which waited for: 5 -> 4; matrix products, arithmetic and copies ran while one was open for 0% -> 0% of each run, Pallas kernels for 12% -> 12%
where the time goes in v11:
time: 34.1 us; the launch traced here: 33.9 us
  starting transfers between devices  16.4 us (48%)
  Pallas kernels  8.92 us (26%)
  waiting for transfers between devices  7.81 us (23%)
  between operations  0.79 us (2%)
    ppermute x15, starting transfers between devices, exchange(): lax.ppermute(value, AXES, [(i, i ^ mask) for i in range(lax.axis_size(AXE...  16.4 us
    pallas_call x12, Pallas kernels, call(): pl.pallas_call(kernel, out_shape=outs, in_specs=in_specs, out_specs=out_s...  8.92 us
    ppermute x15, waiting for transfers between devices, exchange(): lax.ppermute(value, AXES, [(i, i ^ mask) for i in range(lax.axis_size(AXE...  7.81 us
  transfers between devices with their start and end apart: 15, of which 4 were waited for; matrix products, arithmetic and copies ran while one was open for 0% of the time, Pallas kernels for 12%

profile of v11, /device:TPU:0, one launch (start us, length us, event | category | flops | bytes accessed | tf_op | source)
XLA Modules:
  0.0 33.9 jit_solution(15386454825814692898)
XLA Ops:
  0.7 3.4 %shard_map.73 = (f32[64,384]{1,0:T(8,128)S(1)}, f32[64,1152]{1,0:T(8,128)S(1)}, f32[64,512]{1,0:T(8,128)S(1)}, f32[128,512]{1,0:T(8,128)S(1)}, f32[128,384]{1,0:...) custom-call(f32[6,512,128]{2,1,0:T(8,128)} %left.3, ...), custom_call_target="tpu_custom_call" | custom-call | flops 1 | bytes 1 | tf_op jit(solution)/shard_map/pallas_call | solution.py:302
  4.1 0.5 %collective-permute-start.2 = (f32[64,1152]{1,0:T(8,128)S(1)}, f32[64,1152]{1,0:T(8,128)S(1)}, u32[]{:S(2)}, u32[]{:S(2)}) collective-permute-start(f32[64,1152]{1,0:T(8,128)S(1)} %get-tuple-element.54), channel_id=1, source_target_pairs={{0,1},{1,0},{2,3},{3,2},{4,5},{5,4},{6,7},{7,6},{8,9},{9,8},{10,11... | collective-permute-start | bytes 884744 | tf_op jit(solution)/shard_map/ppermute | solution.py:322
  4.6 1.1 %shard_map.74 = (f32[64,512]{1,0:T(8,128)S(1)}, f32[32,640]{1,0:T(8,128)S(1)}, f32[32,2688]{1,0:T(8,128)S(1)}) custom-call(s32[8,128]{1,0:T(8,128)S(1)} %get-tuple-element.39.split, f32[64,512]{1,0:T(8,128)S(1)} %get-tuple-element.40.first, f32[512,128]{1,0:T(8,128)S(1)} %get-tuple-element.41.left_top, f32[512,128]{1,0:T(8,128)S(1)} %get-tuple-element.42.right_top, ...), custom_call_target="tpu_custom_call" | custom-call | flops 1 | bytes 1 | tf_op jit(solution)/shard_map/pallas_call | solution.py:302
  5.7 0.1 collective-permute-start
  5.8 0.0 collective-permute-done.2.got_gram
  5.8 2.7 %collective-permute-start.5 = (f32[64,384]{1,0:T(8,128)S(1)}, f32[64,384]{1,0:T(8,128)S(1)}, u32[]{:S(2)}, u32[]{:S(2)}) collective-permute-start(f32[64,384]{1,0:T(8,128)S(1)} %slice_add_fusion.low), channel_id=1, source_target_pairs={{0,3},{1,2},{2,1},{3,0},{4,7},{5,6},{6,5},{7,4},{8,11},{9,10},{10,... | collective-permute-start | bytes 294920 | tf_op jit(solution)/shard_map/ppermute | solution.py:322
  8.6 0.0 collective-permute-done.got
  8.6 0.4 %shard_map.75 = (f32[32,384]{1,0:T(8,128)S(1)}, f32[32,128]{1,0:T(8,128)S(1)}, f32[32,128]{1,0:T(8,128)S(1)}, f32[32,128]{1,0:T(8,128)S(1)}) custom-call(f32[32,640]{1,0:T(8,128)S(1)} %get-tuple-element.49.keep, f32[32,2688]{1,0:T(8,128)S(1)} %collective-permute-done.got, f32[128,512]{1,0:T(8,128)S(1)} %get-tuple-element.47.gram_top, ...), custom_call_target="tpu_custom_call" | custom-call | flops 1 | bytes 1 | tf_op jit(solution)/shard_map/pallas_call | solution.py:302
  9.0 1.5 %collective-permute-start.1 = (f32[32,128]{1,0:T(8,128)S(1)}, f32[32,128]{1,0:T(8,128)S(1)}, u32[]{:S(2)}, u32[]{:S(2)}) collective-permute-start(f32[32,128]{1,0:T(8,128)S(1)} %get-tuple-element.51.mine), channel_id=1, source_target_pairs={{0,3},{1,2},{2,1},{3,0},{4,7},{5,6},{6,5},{7,4},{8,11},{9,10},{10,... | collective-permute-start | bytes 49160 | tf_op jit(solution)/shard_map/ppermute | solution.py:322
  10.5 1.7 %collective-permute-done.1.got._ = f32[32,128]{1,0:T(8,128)S(1)} collective-permute-done((f32[32,128]{1,0:T(8,128)S(1)}, f32[32,128]{1,0:T(8,128)S(1)}, u32[]{:S(2)}, u32[]{:S(2)}) %collective-permute-start.1) | collective-permute-done | bytes 16416 | tf_op jit(solution)/shard_map/ppermute | solution.py:322
  12.2 0.0 collective-permute-done.5.got
  12.2 2.8 %collective-permute-start.6 = (f32[64,384]{1,0:T(8,128)S(1)}, f32[64,384]{1,0:T(8,128)S(1)}, u32[]{:S(2)}, u32[]{:S(2)}) collective-permute-start(f32[64,384]{1,0:T(8,128)S(1)} %shard_map.77.low), channel_id=1, source_target_pairs={{0,5},{1,4},{2,7},{3,6},{4,1},{5,0},{6,3},{7,2},{8,13},{9,12},{10,... | collective-permute-start | bytes 294920 | tf_op jit(solution)/shard_map/ppermute | solution.py:322
  14.9 0.3 shard_map.76
  15.2 1.6 %collective-permute-start.3 = (f32[32,384]{1,0:T(8,128)S(1)}, f32[32,384]{1,0:T(8,128)S(1)}, u32[]{:S(2)}, u32[]{:S(2)}) collective-permute-start(f32[32,384]{1,0:T(8,128)S(1)} %get-tuple-element.55), channel_id=1, source_target_pairs={{0,3},{1,2},{2,1},{3,0},{4,7},{5,6},{6,5},{7,4},{8,11},{9,10},{10,... | collective-permute-start | bytes 147464 | tf_op jit(solution)/shard_map/ppermute | solution.py:322
  16.8 0.1 collective-permute-start.7
  16.9 2.0 %collective-permute-done.3 = f32[32,384]{1,0:T(8,128)S(1)} collective-permute-done((f32[32,384]{1,0:T(8,128)S(1)}, f32[32,384]{1,0:T(8,128)S(1)}, u32[]{:S(2)}, u32[]{:S(2)}) %collective-permute-start.3) | collective-permute-done | bytes 49184 | tf_op jit(solution)/shard_map/ppermute | solution.py:322
  18.9 1.9 %collective-permute-start.4 = (f32[32,384]{1,0:T(8,128)S(1)}, f32[32,384]{1,0:T(8,128)S(1)}, u32[]{:S(2)}, u32[]{:S(2)}) collective-permute-start(f32[32,384]{1,0:T(8,128)S(1)} %add.9._.sums), channel_id=1, source_target_pairs={{0,5},{1,4},{2,7},{3,6},{4,1},{5,0},{6,3},{7,2},{8,13},{9,12},{10,... | collective-permute-start | bytes 147464 | tf_op jit(solution)/shard_map/ppermute | solution.py:322
  20.8 0.0 collective-permute-done.6.got.got_low
  20.8 0.5 %collective-permute-start.8 = (f32[64,128]{1,0:T(8,128)S(1)}, f32[64,128]{1,0:T(8,128)S(1)}, u32[]{:S(2)}, u32[]{:S(2)}) collective-permute-start(f32[64,128]{1,0:T(8,128)S(1)} %get-tuple-element.57), channel_id=1, source_target_pairs={{0,1},{1,0},{2,3},{3,2},{4,5},{5,4},{6,7},{7,6},{8,9},{9,8},{10,11... | collective-permute-start | bytes 98312 | tf_op jit(solution)/shard_map/ppermute | solution.py:322
  21.3 0.1 collective-permute-start.9
  21.4 0.4 %collective-permute-start.10 = (f32[64,128]{1,0:T(8,128)S(1)}, f32[64,128]{1,0:T(8,128)S(1)}, u32[]{:S(2)}, u32[]{:S(2)}) collective-permute-start(f32[64,128]{1,0:T(8,128)S(1)} %get-tuple-element.60.refs_0_), channel_id=1, source_target_pairs={{0,1},{1,0},{2,3},{3,2},{4,5},{5,4},{6,7},{7,6},{8,9},{9,8},{10,11... | collective-permute-start | bytes 98312 | tf_op jit(solution)/shard_map/ppermute | solution.py:322
  21.8 1.2 %shard_map.79 = (f32[512,128]{1,0:T(8,128)S(1)}, f32[3,256,256]{2,1,0:T(8,128)S(1)}) custom-call(f32[6,512,128]{2,1,0:T(8,128)} %left.3, f32[1,6,256,256]{3,2,1,0:T(8,128)} %coupling.3, f32[32,384]{1,0:T(8,128)S(1)} %add.9._.sums), custom_call_target="tpu_custom_call" | custom-call | flops 1 | bytes 1 | tf_op jit(solution)/shard_map/pallas_call | solution.py:302
  23.0 0.0 collective-permute-done.7.other
  23.0 0.0 collective-permute-done.8.refs_0_
  23.0 0.0 collective-permute-done.9.refs_1_
  23.0 0.3 shard_map.80.factor
  23.3 0.0 collective-permute-done.4.got
  23.4 0.0 collective-permute-done.10.refs_1_
  23.4 0.2 shard_map.81
  23.5 1.8 %collective-permute-start.11 = (f32[32,768]{1,0:T(8,128)S(1)}, f32[32,768]{1,0:T(8,128)S(1)}, u32[]{:S(2)}, u32[]{:S(2)}) collective-permute-start(f32[32,768]{1,0:T(8,128)S(1)} %get-tuple-element.61.packed), channel_id=1, source_target_pairs={{0,9},{1,8},{2,11},{3,10},{4,13},{5,12},{6,15},{7,14},{8,1},{9,0},... | collective-permute-start | bytes 294920 | tf_op jit(solution)/shard_map/ppermute | solution.py:322
  25.3 2.7 %collective-permute-done.11.got = f32[32,768]{1,0:T(8,128)S(1)} collective-permute-done((f32[32,768]{1,0:T(8,128)S(1)}, f32[32,768]{1,0:T(8,128)S(1)}, u32[]{:S(2)}, u32[]{:S(2)}) %collective-permute-start.11) | collective-permute-done | bytes 98336 | tf_op jit(solution)/shard_map/ppermute | solution.py:322
  28.0 0.3 shard_map.82
  28.3 1.7 %collective-permute-start.13 = (f32[32,128]{1,0:T(8,128)S(1)}, f32[32,128]{1,0:T(8,128)S(1)}, u32[]{:S(2)}, u32[]{:S(2)}) collective-permute-start(f32[32,128]{1,0:T(8,128)S(1)} %get-tuple-element.71), channel_id=1, source_target_pairs={{0,17},{1,16},{2,19},{3,18},{4,21},{5,20},{6,23},{7,22},{8,25},{9,... | collective-permute-start | bytes 49160 | tf_op jit(solution)/shard_map/ppermute | solution.py:322
  30.0 0.1 collective-permute-start.12
  30.1 1.4 %collective-permute-done.13 = f32[32,128]{1,0:T(8,128)S(1)} collective-permute-done((f32[32,128]{1,0:T(8,128)S(1)}, f32[32,128]{1,0:T(8,128)S(1)}, u32[]{:S(2)}, u32[]{:S(2)}) %collective-permute-start.13) | collective-permute-done | bytes 16416 | tf_op jit(solution)/shard_map/ppermute | solution.py:322
  31.6 0.6 %collective-permute-start.14 = (f32[32,256]{1,0:T(8,128)S(1)}, f32[32,256]{1,0:T(8,128)S(1)}, u32[]{:S(2)}, u32[]{:S(2)}) collective-permute-start(f32[32,256]{1,0:T(8,128)S(1)} %pad_maximum_fusion.1.mine), channel_id=1, source_target_pairs={{0,1},{1,0},{2,3},{3,2},{4,5},{5,4},{6,7},{7,6},{8,9},{9,8},{10,11... | collective-permute-start | bytes 98312 | tf_op jit(solution)/shard_map/ppermute | solution.py:322
  32.1 0.0 collective-permute-done.12
  32.2 0.8 %shard_map.83 = (f32[64,512]{1,0:T(8,128)S(1)}, f32[256,512]{1,0:T(8,128)S(1)}) custom-call(f32[64,512]{1,0:T(8,128)S(1)} %get-tuple-element.48.current, f32[32,256]{1,0:T(8,128)S(1)} %get-tuple-element.62.refs_0_, f32[32,256]{1,0:T(8,128)S(1)} %get-tuple-element.76.refs_1_, f32[32,256]{1,0:T(8,128)S(1)} %get-tuple-element.63.refs_2_, ...), custom_call_target="tpu_custom_call" | custom-call | flops 1 | bytes 1 | tf_op jit(solution)/shard_map/pallas_call | solution.py:302
  33.0 0.0 collective-permute-done.14.other
  33.0 0.9 %shard_map.84 = f32[64,512]{1,0:T(8,128)} custom-call(f32[64,512]{1,0:T(8,128)S(1)} %get-tuple-element.70.current, f32[32,256]{1,0:T(8,128)S(1)} %pad_maximum_fusion.1.mine, f32[32,256]{1,0:T(8,128)S(1)} %collective-permute-done.14.other, f32[256,512]{1,0:T(8,128)S(1)} %get-tuple-element.72.factor), custom_call_target="tpu_custom_call" | custom-call | flops 1 | bytes 1 | tf_op jit(solution)/shard_map/pallas_call | solution.py:302
  (10 shorter events, 0.1 us)
Async XLA Ops:
  4.1 1.7 %collective-permute-start.2 = (f32[64,1152]{1,0:T(8,128)S(1)}, f32[64,1152]{1,0:T(8,128)S(1)}, u32[]{:S(2)}, u32[]{:S(2)}) collective-permute-start(f32[64,1152]{1,0:T(8,128)S(1)} %get-tuple-element.54), channel_id=1, source_target_pairs={{0,1},{1,0},{2,3},{3,2},{4,5},{5,4},{6,7},{7,6},{8,9},{9,8},{10,11... | collective-permute-start | bytes 884744 | tf_op jit(solution)/shard_map/ppermute | solution.py:322
  5.7 2.9 %collective-permute-start = (f32[32,2688]{1,0:T(8,128)S(1)}, f32[32,2688]{1,0:T(8,128)S(1)}, u32[]{:S(2)}, u32[]{:S(2)}) collective-permute-start(f32[32,2688]{1,0:T(8,128)S(1)} %get-tuple-element.50), channel_id=1, source_target_pairs={{0,1},{1,0},{2,3},{3,2},{4,5},{5,4},{6,7},{7,6},{8,9},{9,8},{10,11... | collective-permute-start | bytes 1032200 | tf_op jit(solution)/shard_map/ppermute | solution.py:322
  5.8 6.3 %collective-permute-start.5 = (f32[64,384]{1,0:T(8,128)S(1)}, f32[64,384]{1,0:T(8,128)S(1)}, u32[]{:S(2)}, u32[]{:S(2)}) collective-permute-start(f32[64,384]{1,0:T(8,128)S(1)} %slice_add_fusion.low), channel_id=1, source_target_pairs={{0,3},{1,2},{2,1},{3,0},{4,7},{5,6},{6,5},{7,4},{8,11},{9,10},{10,... | collective-permute-start | bytes 294920 | tf_op jit(solution)/shard_map/ppermute | solution.py:322
  9.0 3.2 %collective-permute-start.1 = (f32[32,128]{1,0:T(8,128)S(1)}, f32[32,128]{1,0:T(8,128)S(1)}, u32[]{:S(2)}, u32[]{:S(2)}) collective-permute-start(f32[32,128]{1,0:T(8,128)S(1)} %get-tuple-element.51.mine), channel_id=1, source_target_pairs={{0,3},{1,2},{2,1},{3,0},{4,7},{5,6},{6,5},{7,4},{8,11},{9,10},{10,... | collective-permute-start | bytes 49160 | tf_op jit(solution)/shard_map/ppermute | solution.py:322
  12.2 8.6 %collective-permute-start.6 = (f32[64,384]{1,0:T(8,128)S(1)}, f32[64,384]{1,0:T(8,128)S(1)}, u32[]{:S(2)}, u32[]{:S(2)}) collective-permute-start(f32[64,384]{1,0:T(8,128)S(1)} %shard_map.77.low), channel_id=1, source_target_pairs={{0,5},{1,4},{2,7},{3,6},{4,1},{5,0},{6,3},{7,2},{8,13},{9,12},{10,... | collective-permute-start | bytes 294920 | tf_op jit(solution)/shard_map/ppermute | solution.py:322
  15.2 3.7 %collective-permute-start.3 = (f32[32,384]{1,0:T(8,128)S(1)}, f32[32,384]{1,0:T(8,128)S(1)}, u32[]{:S(2)}, u32[]{:S(2)}) collective-permute-start(f32[32,384]{1,0:T(8,128)S(1)} %get-tuple-element.55), channel_id=1, source_target_pairs={{0,3},{1,2},{2,1},{3,0},{4,7},{5,6},{6,5},{7,4},{8,11},{9,10},{10,... | collective-permute-start | bytes 147464 | tf_op jit(solution)/shard_map/ppermute | solution.py:322
  16.8 6.2 %collective-permute-start.7 = (f32[64,256]{1,0:T(8,128)S(1)}, f32[64,256]{1,0:T(8,128)S(1)}, u32[]{:S(2)}, u32[]{:S(2)}) collective-permute-start(f32[64,256]{1,0:T(8,128)S(1)} %slice.25), channel_id=1, source_target_pairs={{0,1},{1,0},{2,3},{3,2},{4,5},{5,4},{6,7},{7,6},{8,9},{9,8},{10,11... | collective-permute-start | bytes 196616 | tf_op jit(solution)/shard_map/ppermute | solution.py:322
  18.9 4.4 %collective-permute-start.4 = (f32[32,384]{1,0:T(8,128)S(1)}, f32[32,384]{1,0:T(8,128)S(1)}, u32[]{:S(2)}, u32[]{:S(2)}) collective-permute-start(f32[32,384]{1,0:T(8,128)S(1)} %add.9._.sums), channel_id=1, source_target_pairs={{0,5},{1,4},{2,7},{3,6},{4,1},{5,0},{6,3},{7,2},{8,13},{9,12},{10,... | collective-permute-start | bytes 147464 | tf_op jit(solution)/shard_map/ppermute | solution.py:322
  20.8 2.2 %collective-permute-start.8 = (f32[64,128]{1,0:T(8,128)S(1)}, f32[64,128]{1,0:T(8,128)S(1)}, u32[]{:S(2)}, u32[]{:S(2)}) collective-permute-start(f32[64,128]{1,0:T(8,128)S(1)} %get-tuple-element.57), channel_id=1, source_target_pairs={{0,1},{1,0},{2,3},{3,2},{4,5},{5,4},{6,7},{7,6},{8,9},{9,8},{10,11... | collective-permute-start | bytes 98312 | tf_op jit(solution)/shard_map/ppermute | solution.py:322
  21.3 1.7 %collective-permute-start.9 = (f32[64,128]{1,0:T(8,128)S(1)}, f32[64,128]{1,0:T(8,128)S(1)}, u32[]{:S(2)}, u32[]{:S(2)}) collective-permute-start(f32[64,128]{1,0:T(8,128)S(1)} %get-tuple-element.58), channel_id=1, source_target_pairs={{0,1},{1,0},{2,3},{3,2},{4,5},{5,4},{6,7},{7,6},{8,9},{9,8},{10,11... | collective-permute-start | bytes 98312 | tf_op jit(solution)/shard_map/ppermute | solution.py:322
  21.4 2.0 %collective-permute-start.10 = (f32[64,128]{1,0:T(8,128)S(1)}, f32[64,128]{1,0:T(8,128)S(1)}, u32[]{:S(2)}, u32[]{:S(2)}) collective-permute-start(f32[64,128]{1,0:T(8,128)S(1)} %get-tuple-element.60.refs_0_), channel_id=1, source_target_pairs={{0,1},{1,0},{2,3},{3,2},{4,5},{5,4},{6,7},{7,6},{8,9},{9,8},{10,11... | collective-permute-start | bytes 98312 | tf_op jit(solution)/shard_map/ppermute | solution.py:322
  23.5 4.4 %collective-permute-start.11 = (f32[32,768]{1,0:T(8,128)S(1)}, f32[32,768]{1,0:T(8,128)S(1)}, u32[]{:S(2)}, u32[]{:S(2)}) collective-permute-start(f32[32,768]{1,0:T(8,128)S(1)} %get-tuple-element.61.packed), channel_id=1, source_target_pairs={{0,9},{1,8},{2,11},{3,10},{4,13},{5,12},{6,15},{7,14},{8,1},{9,0},... | collective-permute-start | bytes 294920 | tf_op jit(solution)/shard_map/ppermute | solution.py:322
  28.3 3.2 %collective-permute-start.13 = (f32[32,128]{1,0:T(8,128)S(1)}, f32[32,128]{1,0:T(8,128)S(1)}, u32[]{:S(2)}, u32[]{:S(2)}) collective-permute-start(f32[32,128]{1,0:T(8,128)S(1)} %get-tuple-element.71), channel_id=1, source_target_pairs={{0,17},{1,16},{2,19},{3,18},{4,21},{5,20},{6,23},{7,22},{8,25},{9,... | collective-permute-start | bytes 49160 | tf_op jit(solution)/shard_map/ppermute | solution.py:322
  30.0 2.1 %collective-permute-start.12 = (f32[32,768]{1,0:T(8,128)S(1)}, f32[32,768]{1,0:T(8,128)S(1)}, u32[]{:S(2)}, u32[]{:S(2)}) collective-permute-start(f32[32,768]{1,0:T(8,128)S(1)} %pad_maximum_fusion), channel_id=1, source_target_pairs={{0,1},{1,0},{2,3},{3,2},{4,5},{5,4},{6,7},{7,6},{8,9},{9,8},{10,11... | collective-permute-start | bytes 294920 | tf_op jit(solution)/shard_map/ppermute | solution.py:322
  31.6 1.5 %collective-permute-start.14 = (f32[32,256]{1,0:T(8,128)S(1)}, f32[32,256]{1,0:T(8,128)S(1)}, u32[]{:S(2)}, u32[]{:S(2)}) collective-permute-start(f32[32,256]{1,0:T(8,128)S(1)} %pad_maximum_fusion.1.mine), channel_id=1, source_target_pairs={{0,1},{1,0},{2,3},{3,2},{4,5},{5,4},{6,7},{7,6},{8,9},{9,8},{10,11... | collective-permute-start | bytes 98312 | tf_op jit(solution)/shard_map/ppermute | solution.py:322

commit v12 on v11

--- a/solution.py
+++ b/solution.py
@@ -107,10 +107,17 @@
         at += w
     leaf_copy.wait()
     rows_n = rhs_v.shape[0]
-    is_left, left_rows = sides(split_v, size)
-    lh, ll = parts(jnp.where(left_rows == is_left, leaf_v[...], 0.0))
-    both = product(moved, lh, NN)
-    current[...] = both[:rows_n] + (both[rows_n:] + product(moved[:rows_n], ll, NN))
+    is_left, _ = sides(split_v, size)
+    lh, ll = parts(leaf_v[...])
+    zero = jnp.zeros_like(moved)
+    side_left, side_right = jnp.where(is_left, moved, zero), jnp.where(is_left, zero, moved)
+    both = product(jnp.concatenate([side_left, side_right], axis=0), lh, NN)
+    fine = product(
+        jnp.concatenate([side_left[:rows_n], side_right[:rows_n]], axis=0), ll, NN
+    )
+    of_left = both[:rows_n] + (both[rows_n : 2 * rows_n] + fine[:rows_n])
+    of_right = both[2 * rows_n : 3 * rows_n] + (both[3 * rows_n :] + fine[rows_n:])
+    current[...] = jnp.where(is_left, of_left, of_right)
     for copy in mid:
         copy.wait()
     low_w = right_low.shape[1]
@@ -266,7 +273,7 @@
         put_rows(out, w, joined(rests[0][...], rests[1][...], top))
 
 
-def first_kernel(top, packed, got, coupling, out, both, pair):
+def first_kernel(top, packed, got, coupling, _, out, both, pair):
     rank = out.shape[1]
     right = (lax.axis_index(AXES) >> (top - 2)) & 1
     for child, value in ((right, packed), (1 - right, got)):
@@ -279,8 +286,8 @@
 
 
 def early_kernel(top, current, *refs):
-    left_first, left_low, left_mid, coupling, out, factor = refs[-6:]
-    rank = left_first.shape[1]
+    left_low, left_mid, coupling, out = refs[-4:]
+    rank = left_mid.shape[1] // 2
     device_id = lax.axis_index(AXES)
     z = []
     for k in range(1, top):
@@ -290,8 +297,11 @@
     low = dot(jnp.concatenate(z[: top - 3], axis=1), left_low[...], NT)
     high = dot(jnp.concatenate(z[top - 3 :], axis=1), left_mid[...], NT)
     out[...] = current[...] - (low + high)
-    right = (device_id >> (top - 1)) & 1 == 1
-    factor[...] = dot(side_of(coupling, 0, right), left_first[...], NT)
+
+
+def root_kernel(top, left_first, coupling, out):
+    right = (lax.axis_index(AXES) >> (top - 1)) & 1 == 1
+    out[...] = dot(side_of(coupling, 0, right), left_first[...], NT)
 
 
 def last_kernel(top, current, mine, other, factor, out):
@@ -471,15 +481,25 @@
         )
         known[k] = (both, both)
         low = rest
+    factor = call(
+        functools.partial(root_kernel, top),
+        shape(2 * rank, size),
+        [VMEM] * 2,
+        VMEM,
+        [],
+        left_first,
+        coup,
+    )
     sums, both = call(
         functools.partial(first_kernel, top),
         [shape(rows, rank), shape(rows, 2 * rank)],
-        [VMEM] * 3,
+        [VMEM] * 3 + [ANY],
         [VMEM] * 2,
         [pltpu.VMEM((2 * rank, rank), F32)],
         sums,
         exchange(sums, 1 << (top - 2) | 1),
         coup,
+        factor,
     )
     known[1] = (both, both)
     got_sums = exchange(sums, 1 << (top - 1) | 1)
@@ -490,15 +510,14 @@
         mine = known[k][0]
         args += [mine, others[:, at : at + mine.shape[1]]]
         at += mine.shape[1]
-    current, factor = call(
+    current = call(
         functools.partial(early_kernel, top),
-        [shape(count, size), shape(2 * rank, size)],
-        [VMEM] * (5 + len(args)),
-        [VMEM] * 2,
+        shape(count, size),
+        [VMEM] * (4 + len(args)),
+        VMEM,
         [],
         current,
         *args,
-        left_first,
         left_low,
         left_mid,
         coup,

time: 34.1 us -> 34 us (level)
    pallas_call x12 -> x13, Pallas kernels: 8.92 us -> 8.95 us  [call(): pl.pallas_call(kernel, out_shape=outs, in_specs=in_specs, out_specs=out_s...]
  transfers between devices with their start and end apart: 15 -> 15, of which waited for: 4 -> 5; matrix products, arithmetic and copies ran while one was open for 0% -> 0% of each run, Pallas kernels for 12% -> 13%
where the time goes in v12:
time: 34 us; the launch traced here: 33.8 us
  starting transfers between devices  16.4 us (48%)
  Pallas kernels  8.95 us (26%)
  waiting for transfers between devices  7.67 us (23%)
  between operations  0.8 us (2%)
    ppermute x15, starting transfers between devices, exchange(): lax.ppermute(value, AXES, [(i, i ^ mask) for i in range(lax.axis_size(AXE...  16.4 us
    pallas_call x13, Pallas kernels, call(): pl.pallas_call(kernel, out_shape=outs, in_specs=in_specs, out_specs=out_s...  8.95 us
    ppermute x15, waiting for transfers between devices, exchange(): lax.ppermute(value, AXES, [(i, i ^ mask) for i in range(lax.axis_size(AXE...  7.67 us
  transfers between devices with their start and end apart: 15, of which 5 were waited for; matrix products, arithmetic and copies ran while one was open for 0% of the time, Pallas kernels for 13%

profile of v12, /device:TPU:0, one launch (start us, length us, event | category | flops | bytes accessed | tf_op | source)
XLA Modules:
  0.0 33.8 jit_solution(8682992263764721103)
XLA Ops:
  0.7 3.3 %shard_map.73 = (f32[64,384]{1,0:T(8,128)S(1)}, f32[64,1152]{1,0:T(8,128)S(1)}, f32[64,512]{1,0:T(8,128)S(1)}, f32[128,512]{1,0:T(8,128)S(1)}, f32[128,384]{1,0:...) custom-call(f32[6,512,128]{2,1,0:T(8,128)} %left.3, ...), custom_call_target="tpu_custom_call" | custom-call | flops 1 | bytes 1 | tf_op jit(solution)/shard_map/pallas_call | solution.py:312
  4.0 0.5 %collective-permute-start.2 = (f32[64,1152]{1,0:T(8,128)S(1)}, f32[64,1152]{1,0:T(8,128)S(1)}, u32[]{:S(2)}, u32[]{:S(2)}) collective-permute-start(f32[64,1152]{1,0:T(8,128)S(1)} %get-tuple-element.52), channel_id=1, source_target_pairs={{0,1},{1,0},{2,3},{3,2},{4,5},{5,4},{6,7},{7,6},{8,9},{9,8},{10,11... | collective-permute-start | bytes 884744 | tf_op jit(solution)/shard_map/ppermute | solution.py:332
  4.5 1.1 %shard_map.74 = (f32[64,512]{1,0:T(8,128)S(1)}, f32[32,640]{1,0:T(8,128)S(1)}, f32[32,2688]{1,0:T(8,128)S(1)}) custom-call(s32[8,128]{1,0:T(8,128)S(1)} %get-tuple-element.37.split, f32[64,512]{1,0:T(8,128)S(1)} %get-tuple-element.38.first, f32[512,128]{1,0:T(8,128)S(1)} %get-tuple-element.39.left_top, f32[512,128]{1,0:T(8,128)S(1)} %get-tuple-element.40.right_top, ...), custom_call_target="tpu_custom_call" | custom-call | flops 1 | bytes 1 | tf_op jit(solution)/shard_map/pallas_call | solution.py:312
  5.6 0.1 collective-permute-start
  5.7 0.0 collective-permute-done.2.got_gram
  5.7 2.8 %collective-permute-start.5 = (f32[64,384]{1,0:T(8,128)S(1)}, f32[64,384]{1,0:T(8,128)S(1)}, u32[]{:S(2)}, u32[]{:S(2)}) collective-permute-start(f32[64,384]{1,0:T(8,128)S(1)} %slice_add_fusion.low), channel_id=1, source_target_pairs={{0,3},{1,2},{2,1},{3,0},{4,7},{5,6},{6,5},{7,4},{8,11},{9,10},{10,... | collective-permute-start | bytes 294920 | tf_op jit(solution)/shard_map/ppermute | solution.py:332
  8.5 0.0 collective-permute-done.got
  8.5 0.4 %shard_map.75 = (f32[32,384]{1,0:T(8,128)S(1)}, f32[32,128]{1,0:T(8,128)S(1)}, f32[32,128]{1,0:T(8,128)S(1)}, f32[32,128]{1,0:T(8,128)S(1)}) custom-call(f32[32,640]{1,0:T(8,128)S(1)} %get-tuple-element.47.keep, f32[32,2688]{1,0:T(8,128)S(1)} %collective-permute-done.got, f32[128,512]{1,0:T(8,128)S(1)} %get-tuple-element.45.gram_top, ...), custom_call_target="tpu_custom_call" | custom-call | flops 1 | bytes 1 | tf_op jit(solution)/shard_map/pallas_call | solution.py:312
  8.9 1.5 %collective-permute-start.1 = (f32[32,128]{1,0:T(8,128)S(1)}, f32[32,128]{1,0:T(8,128)S(1)}, u32[]{:S(2)}, u32[]{:S(2)}) collective-permute-start(f32[32,128]{1,0:T(8,128)S(1)} %get-tuple-element.49.mine), channel_id=1, source_target_pairs={{0,3},{1,2},{2,1},{3,0},{4,7},{5,6},{6,5},{7,4},{8,11},{9,10},{10,... | collective-permute-start | bytes 49160 | tf_op jit(solution)/shard_map/ppermute | solution.py:332
  10.4 1.6 %collective-permute-done.1.got._ = f32[32,128]{1,0:T(8,128)S(1)} collective-permute-done((f32[32,128]{1,0:T(8,128)S(1)}, f32[32,128]{1,0:T(8,128)S(1)}, u32[]{:S(2)}, u32[]{:S(2)}) %collective-permute-start.1) | collective-permute-done | bytes 16416 | tf_op jit(solution)/shard_map/ppermute | solution.py:332
  12.1 0.0 collective-permute-done.5.got
  12.1 2.7 %collective-permute-start.6 = (f32[64,384]{1,0:T(8,128)S(1)}, f32[64,384]{1,0:T(8,128)S(1)}, u32[]{:S(2)}, u32[]{:S(2)}) collective-permute-start(f32[64,384]{1,0:T(8,128)S(1)} %shard_map.77.low), channel_id=1, source_target_pairs={{0,5},{1,4},{2,7},{3,6},{4,1},{5,0},{6,3},{7,2},{8,13},{9,12},{10,... | collective-permute-start | bytes 294920 | tf_op jit(solution)/shard_map/ppermute | solution.py:332
  14.9 0.3 shard_map.76
  15.1 1.6 %collective-permute-start.3 = (f32[32,384]{1,0:T(8,128)S(1)}, f32[32,384]{1,0:T(8,128)S(1)}, u32[]{:S(2)}, u32[]{:S(2)}) collective-permute-start(f32[32,384]{1,0:T(8,128)S(1)} %get-tuple-element.53), channel_id=1, source_target_pairs={{0,3},{1,2},{2,1},{3,0},{4,7},{5,6},{6,5},{7,4},{8,11},{9,10},{10,... | collective-permute-start | bytes 147464 | tf_op jit(solution)/shard_map/ppermute | solution.py:332
  16.7 0.1 collective-permute-start.7
  16.9 1.9 %collective-permute-done.3 = f32[32,384]{1,0:T(8,128)S(1)} collective-permute-done((f32[32,384]{1,0:T(8,128)S(1)}, f32[32,384]{1,0:T(8,128)S(1)}, u32[]{:S(2)}, u32[]{:S(2)}) %collective-permute-start.3) | collective-permute-done | bytes 49184 | tf_op jit(solution)/shard_map/ppermute | solution.py:332
  18.8 1.9 %collective-permute-start.4 = (f32[32,384]{1,0:T(8,128)S(1)}, f32[32,384]{1,0:T(8,128)S(1)}, u32[]{:S(2)}, u32[]{:S(2)}) collective-permute-start(f32[32,384]{1,0:T(8,128)S(1)} %add.9._.sums), channel_id=1, source_target_pairs={{0,5},{1,4},{2,7},{3,6},{4,1},{5,0},{6,3},{7,2},{8,13},{9,12},{10,... | collective-permute-start | bytes 147464 | tf_op jit(solution)/shard_map/ppermute | solution.py:332
  20.7 0.0 collective-permute-done.6.got.got_low
  20.8 0.5 %collective-permute-start.8 = (f32[64,128]{1,0:T(8,128)S(1)}, f32[64,128]{1,0:T(8,128)S(1)}, u32[]{:S(2)}, u32[]{:S(2)}) collective-permute-start(f32[64,128]{1,0:T(8,128)S(1)} %get-tuple-element.55), channel_id=1, source_target_pairs={{0,1},{1,0},{2,3},{3,2},{4,5},{5,4},{6,7},{7,6},{8,9},{9,8},{10,11... | collective-permute-start | bytes 98312 | tf_op jit(solution)/shard_map/ppermute | solution.py:332
  21.2 0.1 collective-permute-start.9
  21.3 0.4 %collective-permute-start.10 = (f32[64,128]{1,0:T(8,128)S(1)}, f32[64,128]{1,0:T(8,128)S(1)}, u32[]{:S(2)}, u32[]{:S(2)}) collective-permute-start(f32[64,128]{1,0:T(8,128)S(1)} %get-tuple-element.58.refs_0_), channel_id=1, source_target_pairs={{0,1},{1,0},{2,3},{3,2},{4,5},{5,4},{6,7},{7,6},{8,9},{9,8},{10,11... | collective-permute-start | bytes 98312 | tf_op jit(solution)/shard_map/ppermute | solution.py:332
  21.7 1.2 %shard_map.79 = (f32[512,128]{1,0:T(8,128)S(1)}, f32[3,256,256]{2,1,0:T(8,128)S(1)}) custom-call(f32[6,512,128]{2,1,0:T(8,128)} %left.3, f32[1,6,256,256]{3,2,1,0:T(8,128)} %coupling.3, f32[32,384]{1,0:T(8,128)S(1)} %add.9._.sums), custom_call_target="tpu_custom_call" | custom-call | flops 1 | bytes 1 | tf_op jit(solution)/shard_map/pallas_call | solution.py:312
  22.9 0.0 collective-permute-done.7.other
  22.9 0.0 collective-permute-done.8.refs_0_
  23.0 0.0 collective-permute-done.9.refs_1_
  23.0 0.3 shard_map.80.factor
  23.3 0.0 collective-permute-done.4.got
  23.3 0.0 collective-permute-done.10.refs_1_
  23.3 0.2 shard_map.81
  23.5 1.7 %collective-permute-start.11 = (f32[32,768]{1,0:T(8,128)S(1)}, f32[32,768]{1,0:T(8,128)S(1)}, u32[]{:S(2)}, u32[]{:S(2)}) collective-permute-start(f32[32,768]{1,0:T(8,128)S(1)} %get-tuple-element.59.packed), channel_id=1, source_target_pairs={{0,9},{1,8},{2,11},{3,10},{4,13},{5,12},{6,15},{7,14},{8,1},{9,0},... | collective-permute-start | bytes 294920 | tf_op jit(solution)/shard_map/ppermute | solution.py:332
  25.2 0.4 %shard_map.82._.factor = f32[256,512]{1,0:T(8,128)S(1)} custom-call(f32[512,128]{1,0:T(8,128)S(1)} %get-tuple-element.60.left_first, f32[3,256,256]{2,1,0:T(8,128)S(1)} %get-tuple-element.57.refs_2_.coupling.refs_10_), custom_call_target="tpu_custom_call" | custom-call | flops 1 | bytes 1 | tf_op jit(solution)/shard_map/pallas_call | solution.py:312
  25.6 2.4 %collective-permute-done.11.got = f32[32,768]{1,0:T(8,128)S(1)} collective-permute-done((f32[32,768]{1,0:T(8,128)S(1)}, f32[32,768]{1,0:T(8,128)S(1)}, u32[]{:S(2)}, u32[]{:S(2)}) %collective-permute-start.11) | collective-permute-done | bytes 98336 | tf_op jit(solution)/shard_map/ppermute | solution.py:332
  27.9 0.3 shard_map.83
  28.3 1.7 %collective-permute-start.13 = (f32[32,128]{1,0:T(8,128)S(1)}, f32[32,128]{1,0:T(8,128)S(1)}, u32[]{:S(2)}, u32[]{:S(2)}) collective-permute-start(f32[32,128]{1,0:T(8,128)S(1)} %get-tuple-element.68), channel_id=1, source_target_pairs={{0,17},{1,16},{2,19},{3,18},{4,21},{5,20},{6,23},{7,22},{8,25},{9,... | collective-permute-start | bytes 49160 | tf_op jit(solution)/shard_map/ppermute | solution.py:332
  30.0 0.1 collective-permute-start.12
  30.0 1.4 %collective-permute-done.13 = f32[32,128]{1,0:T(8,128)S(1)} collective-permute-done((f32[32,128]{1,0:T(8,128)S(1)}, f32[32,128]{1,0:T(8,128)S(1)}, u32[]{:S(2)}, u32[]{:S(2)}) %collective-permute-start.13) | collective-permute-done | bytes 16416 | tf_op jit(solution)/shard_map/ppermute | solution.py:332
  31.5 0.6 %collective-permute-start.14 = (f32[32,256]{1,0:T(8,128)S(1)}, f32[32,256]{1,0:T(8,128)S(1)}, u32[]{:S(2)}, u32[]{:S(2)}) collective-permute-start(f32[32,256]{1,0:T(8,128)S(1)} %pad_maximum_fusion.1.mine), channel_id=1, source_target_pairs={{0,1},{1,0},{2,3},{3,2},{4,5},{5,4},{6,7},{7,6},{8,9},{9,8},{10,11... | collective-permute-start | bytes 98312 | tf_op jit(solution)/shard_map/ppermute | solution.py:332
  32.1 0.0 collective-permute-done.12
  32.1 0.6 %shard_map.84.current = f32[64,512]{1,0:T(8,128)S(1)} custom-call(f32[64,512]{1,0:T(8,128)S(1)} %get-tuple-element.46.current, f32[32,256]{1,0:T(8,128)S(1)} %get-tuple-element.61.refs_0_, f32[32,256]{1,0:T(8,128)S(1)} %get-tuple-element.72.refs_1_, f32[32,256]{1,0:T(8,128)S(1)} %get-tuple-element.62.refs_2_, f32[32,256]{1,0:T(8,128)S(1)} %get-tuple-element.71.refs_3_, ...), custom_call_target="tpu_custom_call" | custom-call | flops 1 | bytes 1 | tf_op jit(solution)/shard_map/pallas_call | solution.py:312
  32.7 0.2 collective-permute-done.14.other
  33.0 0.9 %shard_map.85 = f32[64,512]{1,0:T(8,128)} custom-call(f32[64,512]{1,0:T(8,128)S(1)} %shard_map.84.current, f32[32,256]{1,0:T(8,128)S(1)} %pad_maximum_fusion.1.mine, f32[32,256]{1,0:T(8,128)S(1)} %collective-permute-done.14.other, f32[256,512]{1,0:T(8,128)S(1)} %shard_map.82._.factor), custom_call_target="tpu_custom_call" | custom-call | flops 1 | bytes 1 | tf_op jit(solution)/shard_map/pallas_call | solution.py:312
  (10 shorter events, 0.1 us)
Async XLA Ops:
  4.0 1.7 %collective-permute-start.2 = (f32[64,1152]{1,0:T(8,128)S(1)}, f32[64,1152]{1,0:T(8,128)S(1)}, u32[]{:S(2)}, u32[]{:S(2)}) collective-permute-start(f32[64,1152]{1,0:T(8,128)S(1)} %get-tuple-element.52), channel_id=1, source_target_pairs={{0,1},{1,0},{2,3},{3,2},{4,5},{5,4},{6,7},{7,6},{8,9},{9,8},{10,11... | collective-permute-start | bytes 884744 | tf_op jit(solution)/shard_map/ppermute | solution.py:332
  5.6 2.9 %collective-permute-start = (f32[32,2688]{1,0:T(8,128)S(1)}, f32[32,2688]{1,0:T(8,128)S(1)}, u32[]{:S(2)}, u32[]{:S(2)}) collective-permute-start(f32[32,2688]{1,0:T(8,128)S(1)} %get-tuple-element.48), channel_id=1, source_target_pairs={{0,1},{1,0},{2,3},{3,2},{4,5},{5,4},{6,7},{7,6},{8,9},{9,8},{10,11... | collective-permute-start | bytes 1032200 | tf_op jit(solution)/shard_map/ppermute | solution.py:332
  5.7 6.4 %collective-permute-start.5 = (f32[64,384]{1,0:T(8,128)S(1)}, f32[64,384]{1,0:T(8,128)S(1)}, u32[]{:S(2)}, u32[]{:S(2)}) collective-permute-start(f32[64,384]{1,0:T(8,128)S(1)} %slice_add_fusion.low), channel_id=1, source_target_pairs={{0,3},{1,2},{2,1},{3,0},{4,7},{5,6},{6,5},{7,4},{8,11},{9,10},{10,... | collective-permute-start | bytes 294920 | tf_op jit(solution)/shard_map/ppermute | solution.py:332
  8.9 3.2 %collective-permute-start.1 = (f32[32,128]{1,0:T(8,128)S(1)}, f32[32,128]{1,0:T(8,128)S(1)}, u32[]{:S(2)}, u32[]{:S(2)}) collective-permute-start(f32[32,128]{1,0:T(8,128)S(1)} %get-tuple-element.49.mine), channel_id=1, source_target_pairs={{0,3},{1,2},{2,1},{3,0},{4,7},{5,6},{6,5},{7,4},{8,11},{9,10},{10,... | collective-permute-start | bytes 49160 | tf_op jit(solution)/shard_map/ppermute | solution.py:332
  12.1 8.6 %collective-permute-start.6 = (f32[64,384]{1,0:T(8,128)S(1)}, f32[64,384]{1,0:T(8,128)S(1)}, u32[]{:S(2)}, u32[]{:S(2)}) collective-permute-start(f32[64,384]{1,0:T(8,128)S(1)} %shard_map.77.low), channel_id=1, source_target_pairs={{0,5},{1,4},{2,7},{3,6},{4,1},{5,0},{6,3},{7,2},{8,13},{9,12},{10,... | collective-permute-start | bytes 294920 | tf_op jit(solution)/shard_map/ppermute | solution.py:332
  15.1 3.7 %collective-permute-start.3 = (f32[32,384]{1,0:T(8,128)S(1)}, f32[32,384]{1,0:T(8,128)S(1)}, u32[]{:S(2)}, u32[]{:S(2)}) collective-permute-start(f32[32,384]{1,0:T(8,128)S(1)} %get-tuple-element.53), channel_id=1, source_target_pairs={{0,3},{1,2},{2,1},{3,0},{4,7},{5,6},{6,5},{7,4},{8,11},{9,10},{10,... | collective-permute-start | bytes 147464 | tf_op jit(solution)/shard_map/ppermute | solution.py:332
  16.7 6.2 %collective-permute-start.7 = (f32[64,256]{1,0:T(8,128)S(1)}, f32[64,256]{1,0:T(8,128)S(1)}, u32[]{:S(2)}, u32[]{:S(2)}) collective-permute-start(f32[64,256]{1,0:T(8,128)S(1)} %slice.25), channel_id=1, source_target_pairs={{0,1},{1,0},{2,3},{3,2},{4,5},{5,4},{6,7},{7,6},{8,9},{9,8},{10,11... | collective-permute-start | bytes 196616 | tf_op jit(solution)/shard_map/ppermute | solution.py:332
  18.8 4.5 %collective-permute-start.4 = (f32[32,384]{1,0:T(8,128)S(1)}, f32[32,384]{1,0:T(8,128)S(1)}, u32[]{:S(2)}, u32[]{:S(2)}) collective-permute-start(f32[32,384]{1,0:T(8,128)S(1)} %add.9._.sums), channel_id=1, source_target_pairs={{0,5},{1,4},{2,7},{3,6},{4,1},{5,0},{6,3},{7,2},{8,13},{9,12},{10,... | collective-permute-start | bytes 147464 | tf_op jit(solution)/shard_map/ppermute | solution.py:332
  20.8 2.2 %collective-permute-start.8 = (f32[64,128]{1,0:T(8,128)S(1)}, f32[64,128]{1,0:T(8,128)S(1)}, u32[]{:S(2)}, u32[]{:S(2)}) collective-permute-start(f32[64,128]{1,0:T(8,128)S(1)} %get-tuple-element.55), channel_id=1, source_target_pairs={{0,1},{1,0},{2,3},{3,2},{4,5},{5,4},{6,7},{7,6},{8,9},{9,8},{10,11... | collective-permute-start | bytes 98312 | tf_op jit(solution)/shard_map/ppermute | solution.py:332
  21.2 1.7 %collective-permute-start.9 = (f32[64,128]{1,0:T(8,128)S(1)}, f32[64,128]{1,0:T(8,128)S(1)}, u32[]{:S(2)}, u32[]{:S(2)}) collective-permute-start(f32[64,128]{1,0:T(8,128)S(1)} %get-tuple-element.56), channel_id=1, source_target_pairs={{0,1},{1,0},{2,3},{3,2},{4,5},{5,4},{6,7},{7,6},{8,9},{9,8},{10,11... | collective-permute-start | bytes 98312 | tf_op jit(solution)/shard_map/ppermute | solution.py:332
  21.3 2.0 %collective-permute-start.10 = (f32[64,128]{1,0:T(8,128)S(1)}, f32[64,128]{1,0:T(8,128)S(1)}, u32[]{:S(2)}, u32[]{:S(2)}) collective-permute-start(f32[64,128]{1,0:T(8,128)S(1)} %get-tuple-element.58.refs_0_), channel_id=1, source_target_pairs={{0,1},{1,0},{2,3},{3,2},{4,5},{5,4},{6,7},{7,6},{8,9},{9,8},{10,11... | collective-permute-start | bytes 98312 | tf_op jit(solution)/shard_map/ppermute | solution.py:332
  23.5 4.5 %collective-permute-start.11 = (f32[32,768]{1,0:T(8,128)S(1)}, f32[32,768]{1,0:T(8,128)S(1)}, u32[]{:S(2)}, u32[]{:S(2)}) collective-permute-start(f32[32,768]{1,0:T(8,128)S(1)} %get-tuple-element.59.packed), channel_id=1, source_target_pairs={{0,9},{1,8},{2,11},{3,10},{4,13},{5,12},{6,15},{7,14},{8,1},{9,0},... | collective-permute-start | bytes 294920 | tf_op jit(solution)/shard_map/ppermute | solution.py:332
  28.3 3.2 %collective-permute-start.13 = (f32[32,128]{1,0:T(8,128)S(1)}, f32[32,128]{1,0:T(8,128)S(1)}, u32[]{:S(2)}, u32[]{:S(2)}) collective-permute-start(f32[32,128]{1,0:T(8,128)S(1)} %get-tuple-element.68), channel_id=1, source_target_pairs={{0,17},{1,16},{2,19},{3,18},{4,21},{5,20},{6,23},{7,22},{8,25},{9,... | collective-permute-start | bytes 49160 | tf_op jit(solution)/shard_map/ppermute | solution.py:332
  30.0 2.1 %collective-permute-start.12 = (f32[32,768]{1,0:T(8,128)S(1)}, f32[32,768]{1,0:T(8,128)S(1)}, u32[]{:S(2)}, u32[]{:S(2)}) collective-permute-start(f32[32,768]{1,0:T(8,128)S(1)} %pad_maximum_fusion), channel_id=1, source_target_pairs={{0,1},{1,0},{2,3},{3,2},{4,5},{5,4},{6,7},{7,6},{8,9},{9,8},{10,11... | collective-permute-start | bytes 294920 | tf_op jit(solution)/shard_map/ppermute | solution.py:332
  31.5 1.4 %collective-permute-start.14 = (f32[32,256]{1,0:T(8,128)S(1)}, f32[32,256]{1,0:T(8,128)S(1)}, u32[]{:S(2)}, u32[]{:S(2)}) collective-permute-start(f32[32,256]{1,0:T(8,128)S(1)} %pad_maximum_fusion.1.mine), channel_id=1, source_target_pairs={{0,1},{1,0},{2,3},{3,2},{4,5},{5,4},{6,7},{7,6},{8,9},{9,8},{10,11... | collective-permute-start | bytes 98312 | tf_op jit(solution)/shard_map/ppermute | solution.py:332

commit v13 on v12

--- a/solution.py
+++ b/solution.py
@@ -133,15 +133,10 @@
         copy.wait()
 
 
-def fetch_kernel(top, left, coupling, _, left_first, coupling_v, sems):
-    copies = [
-        pltpu.make_async_copy(coupling.at[0, pl.ds(0, top - 2)], coupling_v, sems.at[0]),
-        pltpu.make_async_copy(left.at[0], left_first, sems.at[1]),
-    ]
-    for copy in copies:
-        copy.start()
-    for copy in copies:
-        copy.wait()
+def fetch_kernel(top, coupling, _, coupling_v, sem):
+    copy = pltpu.make_async_copy(coupling.at[0, pl.ds(2, top - 4)], coupling_v, sem)
+    copy.start()
+    copy.wait()
 
 
 def put_rows(out, at, value):
@@ -260,7 +255,7 @@
         cols = slice(j * rank, (j + 1) * rank)
         put(right, low[:, cols], other[:, cols], cols)
         put(1 - right, got_low[:, cols], got_others[j][...], cols)
-    out[...] = dot(coupling[k], pair[...])
+    out[...] = dot(coupling[k - 2], pair[...])
 
 
 def level_kernel(top, k, sums, got, factor, *refs):
@@ -286,22 +281,35 @@
 
 
 def early_kernel(top, current, *refs):
-    left_low, left_mid, coupling, out = refs[-4:]
+    left_low, left_mid, root_coupling, coupling, out = refs[-5:]
     rank = left_mid.shape[1] // 2
     device_id = lax.axis_index(AXES)
     z = []
     for k in range(1, top):
         pair = joined(refs[2 * k - 2][...], refs[2 * k - 1][...], top)
         right = (device_id >> (top - 1 - k)) & 1 == 1
-        z.append(pair if k >= top - 2 else dot(pair, side_of(coupling, k, right)))
+        if k >= top - 2:
+            z.append(pair)
+        elif k == 1:
+            z.append(dot(pair, side_of(root_coupling, 1, right)))
+        else:
+            z.append(dot(pair, side_of(coupling, k - 2, right)))
     low = dot(jnp.concatenate(z[: top - 3], axis=1), left_low[...], NT)
     high = dot(jnp.concatenate(z[top - 3 :], axis=1), left_mid[...], NT)
     out[...] = current[...] - (low + high)
 
 
-def root_kernel(top, left_first, coupling, out):
+def root_kernel(top, left, coupling, _, out, coupling_v, left_v, sems):
+    copies = [
+        pltpu.make_async_copy(coupling.at[0, pl.ds(0, 2)], coupling_v, sems.at[0]),
+        pltpu.make_async_copy(left.at[0], left_v, sems.at[1]),
+    ]
+    for copy in copies:
+        copy.start()
+    for copy in copies:
+        copy.wait()
     right = (lax.axis_index(AXES) >> (top - 1)) & 1 == 1
-    out[...] = dot(side_of(coupling, 0, right), left_first[...], NT)
+    out[...] = dot(side_of(coupling_v, 0, right), left_v[...], NT)
 
 
 def last_kernel(top, current, mine, other, factor, out):
@@ -428,13 +436,13 @@
     known[top - 2] = (z, z)
     low = call(add_kernel, shape(*low.shape), [VMEM, VMEM, ANY], VMEM, [], low, got_low, got_next)
     sums = sums + exchange(sums, 3)
-    left_first, coup = call(
+    coup = call(
         functools.partial(fetch_kernel, top),
-        [shape(size, rank), shape(top - 2, 2 * rank, 2 * rank)],
-        [HBM] * 2 + [ANY],
-        [VMEM] * 2,
-        [pltpu.SemaphoreType.DMA((2,))],
-        *in_hbm(basis_left, coupling),
+        shape(top - 4, 2 * rank, 2 * rank),
+        [HBM, ANY],
+        VMEM,
+        [pltpu.SemaphoreType.DMA],
+        *in_hbm(coupling),
         sums,
     )
     for k in range(top - 3, 1, -1):
@@ -481,14 +489,14 @@
         )
         known[k] = (both, both)
         low = rest
-    factor = call(
+    factor, root_coup = call(
         functools.partial(root_kernel, top),
-        shape(2 * rank, size),
+        [shape(2 * rank, size), shape(2, 2 * rank, 2 * rank)],
+        [HBM] * 2 + [ANY],
         [VMEM] * 2,
-        VMEM,
-        [],
-        left_first,
-        coup,
+        [pltpu.VMEM((size, rank), F32), pltpu.SemaphoreType.DMA((2,))],
+        *in_hbm(basis_left, coupling),
+        sums,
     )
     sums, both = call(
         functools.partial(first_kernel, top),
@@ -498,7 +506,7 @@
         [pltpu.VMEM((2 * rank, rank), F32)],
         sums,
         exchange(sums, 1 << (top - 2) | 1),
-        coup,
+        root_coup,
         factor,
     )
     known[1] = (both, both)
@@ -513,13 +521,14 @@
     current = call(
         functools.partial(early_kernel, top),
         shape(count, size),
-        [VMEM] * (4 + len(args)),
+        [VMEM] * (5 + len(args)),
         VMEM,
         [],
         current,
         *args,
         left_low,
         left_mid,
+        root_coup,
         coup,
     )
     both = beside(sums, got_sums, (device_id >> (top - 1)) & 1 == 1)

time: 34 us -> 34 us (level)
  waiting for transfers between devices: 7.67 us -> 6.68 us
  Pallas kernels: 8.95 us -> 9.83 us
    ppermute x15, waiting for transfers between devices: 7.67 us -> 6.68 us  [exchange(): lax.ppermute(value, AXES, [(i, i ^ mask) for i in range(lax.axis_size(AXE...]
    pallas_call x13, Pallas kernels: 8.95 us -> 9.83 us  [call(): pl.pallas_call(kernel, out_shape=outs, in_specs=in_specs, out_specs=out_s...]
  transfers between devices with their start and end apart: 15 -> 15, of which waited for: 5 -> 6; matrix products, arithmetic and copies ran while one was open for 0% -> 0% of each run, Pallas kernels for 13% -> 15%
where the time goes in v13:
time: 34 us; the launch traced here: 33.8 us
  starting transfers between devices  16.5 us (49%)
  Pallas kernels  9.83 us (29%)
  waiting for transfers between devices  6.68 us (20%)
  between operations  0.78 us (2%)
    ppermute x15, starting transfers between devices, exchange(): lax.ppermute(value, AXES, [(i, i ^ mask) for i in range(lax.axis_size(AXE...  16.5 us
    pallas_call x13, Pallas kernels, call(): pl.pallas_call(kernel, out_shape=outs, in_specs=in_specs, out_specs=out_s...  9.83 us
    ppermute x15, waiting for transfers between devices, exchange(): lax.ppermute(value, AXES, [(i, i ^ mask) for i in range(lax.axis_size(AXE...  6.68 us
  transfers between devices with their start and end apart: 15, of which 6 were waited for; matrix products, arithmetic and copies ran while one was open for 0% of the time, Pallas kernels for 15%

profile of v13, /device:TPU:0, one launch (start us, length us, event | category | flops | bytes accessed | tf_op | source)
XLA Modules:
  0.0 33.8 jit_solution(14687961196701121109)
XLA Ops:
  0.7 3.3 %shard_map.73 = (f32[64,384]{1,0:T(8,128)S(1)}, f32[64,1152]{1,0:T(8,128)S(1)}, f32[64,512]{1,0:T(8,128)S(1)}, f32[128,512]{1,0:T(8,128)S(1)}, f32[128,384]{1,0:...) custom-call(f32[6,512,128]{2,1,0:T(8,128)} %left.3, ...), custom_call_target="tpu_custom_call" | custom-call | flops 1 | bytes 1 | tf_op jit(solution)/shard_map/pallas_call | solution.py:320
  4.0 0.5 %collective-permute-start.2 = (f32[64,1152]{1,0:T(8,128)S(1)}, f32[64,1152]{1,0:T(8,128)S(1)}, u32[]{:S(2)}, u32[]{:S(2)}) collective-permute-start(f32[64,1152]{1,0:T(8,128)S(1)} %get-tuple-element.52), channel_id=1, source_target_pairs={{0,1},{1,0},{2,3},{3,2},{4,5},{5,4},{6,7},{7,6},{8,9},{9,8},{10,11... | collective-permute-start | bytes 884744 | tf_op jit(solution)/shard_map/ppermute | solution.py:340
  4.5 1.1 %shard_map.74 = (f32[64,512]{1,0:T(8,128)S(1)}, f32[32,640]{1,0:T(8,128)S(1)}, f32[32,2688]{1,0:T(8,128)S(1)}) custom-call(s32[8,128]{1,0:T(8,128)S(1)} %get-tuple-element.37.split, f32[64,512]{1,0:T(8,128)S(1)} %get-tuple-element.38.first, f32[512,128]{1,0:T(8,128)S(1)} %get-tuple-element.39.left_top, f32[512,128]{1,0:T(8,128)S(1)} %get-tuple-element.40.right_top, ...), custom_call_target="tpu_custom_call" | custom-call | flops 1 | bytes 1 | tf_op jit(solution)/shard_map/pallas_call | solution.py:320
  5.6 0.1 collective-permute-start
  5.7 0.0 collective-permute-done.2.got_gram
  5.7 2.8 %collective-permute-start.5 = (f32[64,384]{1,0:T(8,128)S(1)}, f32[64,384]{1,0:T(8,128)S(1)}, u32[]{:S(2)}, u32[]{:S(2)}) collective-permute-start(f32[64,384]{1,0:T(8,128)S(1)} %slice_add_fusion.low), channel_id=1, source_target_pairs={{0,3},{1,2},{2,1},{3,0},{4,7},{5,6},{6,5},{7,4},{8,11},{9,10},{10,... | collective-permute-start | bytes 294920 | tf_op jit(solution)/shard_map/ppermute | solution.py:340
  8.5 0.0 collective-permute-done.got
  8.5 0.4 %shard_map.75 = (f32[32,384]{1,0:T(8,128)S(1)}, f32[32,128]{1,0:T(8,128)S(1)}, f32[32,128]{1,0:T(8,128)S(1)}, f32[32,128]{1,0:T(8,128)S(1)}) custom-call(f32[32,640]{1,0:T(8,128)S(1)} %get-tuple-element.47.keep, f32[32,2688]{1,0:T(8,128)S(1)} %collective-permute-done.got, f32[128,512]{1,0:T(8,128)S(1)} %get-tuple-element.45.gram_top, ...), custom_call_target="tpu_custom_call" | custom-call | flops 1 | bytes 1 | tf_op jit(solution)/shard_map/pallas_call | solution.py:320
  8.9 1.5 %collective-permute-start.1 = (f32[32,128]{1,0:T(8,128)S(1)}, f32[32,128]{1,0:T(8,128)S(1)}, u32[]{:S(2)}, u32[]{:S(2)}) collective-permute-start(f32[32,128]{1,0:T(8,128)S(1)} %get-tuple-element.49.mine), channel_id=1, source_target_pairs={{0,3},{1,2},{2,1},{3,0},{4,7},{5,6},{6,5},{7,4},{8,11},{9,10},{10,... | collective-permute-start | bytes 49160 | tf_op jit(solution)/shard_map/ppermute | solution.py:340
  10.4 1.6 %collective-permute-done.1.got._ = f32[32,128]{1,0:T(8,128)S(1)} collective-permute-done((f32[32,128]{1,0:T(8,128)S(1)}, f32[32,128]{1,0:T(8,128)S(1)}, u32[]{:S(2)}, u32[]{:S(2)}) %collective-permute-start.1) | collective-permute-done | bytes 16416 | tf_op jit(solution)/shard_map/ppermute | solution.py:340
  12.1 0.0 collective-permute-done.5.got
  12.1 2.7 %collective-permute-start.6 = (f32[64,384]{1,0:T(8,128)S(1)}, f32[64,384]{1,0:T(8,128)S(1)}, u32[]{:S(2)}, u32[]{:S(2)}) collective-permute-start(f32[64,384]{1,0:T(8,128)S(1)} %shard_map.77.low), channel_id=1, source_target_pairs={{0,5},{1,4},{2,7},{3,6},{4,1},{5,0},{6,3},{7,2},{8,13},{9,12},{10,... | collective-permute-start | bytes 294920 | tf_op jit(solution)/shard_map/ppermute | solution.py:340
  14.9 0.3 shard_map.76
  15.1 1.6 %collective-permute-start.3 = (f32[32,384]{1,0:T(8,128)S(1)}, f32[32,384]{1,0:T(8,128)S(1)}, u32[]{:S(2)}, u32[]{:S(2)}) collective-permute-start(f32[32,384]{1,0:T(8,128)S(1)} %get-tuple-element.53), channel_id=1, source_target_pairs={{0,3},{1,2},{2,1},{3,0},{4,7},{5,6},{6,5},{7,4},{8,11},{9,10},{10,... | collective-permute-start | bytes 147464 | tf_op jit(solution)/shard_map/ppermute | solution.py:340
  16.7 0.1 collective-permute-start.7
  16.9 1.9 %collective-permute-done.3 = f32[32,384]{1,0:T(8,128)S(1)} collective-permute-done((f32[32,384]{1,0:T(8,128)S(1)}, f32[32,384]{1,0:T(8,128)S(1)}, u32[]{:S(2)}, u32[]{:S(2)}) %collective-permute-start.3) | collective-permute-done | bytes 49184 | tf_op jit(solution)/shard_map/ppermute | solution.py:340
  18.8 1.9 %collective-permute-start.4 = (f32[32,384]{1,0:T(8,128)S(1)}, f32[32,384]{1,0:T(8,128)S(1)}, u32[]{:S(2)}, u32[]{:S(2)}) collective-permute-start(f32[32,384]{1,0:T(8,128)S(1)} %add.9._.sums), channel_id=1, source_target_pairs={{0,5},{1,4},{2,7},{3,6},{4,1},{5,0},{6,3},{7,2},{8,13},{9,12},{10,... | collective-permute-start | bytes 147464 | tf_op jit(solution)/shard_map/ppermute | solution.py:340
  20.7 0.0 collective-permute-done.6.got.got_low
  20.8 0.5 %collective-permute-start.8 = (f32[64,128]{1,0:T(8,128)S(1)}, f32[64,128]{1,0:T(8,128)S(1)}, u32[]{:S(2)}, u32[]{:S(2)}) collective-permute-start(f32[64,128]{1,0:T(8,128)S(1)} %get-tuple-element.55), channel_id=1, source_target_pairs={{0,1},{1,0},{2,3},{3,2},{4,5},{5,4},{6,7},{7,6},{8,9},{9,8},{10,11... | collective-permute-start | bytes 98312 | tf_op jit(solution)/shard_map/ppermute | solution.py:340
  21.2 0.1 collective-permute-start.9
  21.3 0.4 %collective-permute-start.10 = (f32[64,128]{1,0:T(8,128)S(1)}, f32[64,128]{1,0:T(8,128)S(1)}, u32[]{:S(2)}, u32[]{:S(2)}) collective-permute-start(f32[64,128]{1,0:T(8,128)S(1)} %get-tuple-element.57.refs_0_), channel_id=1, source_target_pairs={{0,1},{1,0},{2,3},{3,2},{4,5},{5,4},{6,7},{7,6},{8,9},{9,8},{10,11... | collective-permute-start | bytes 98312 | tf_op jit(solution)/shard_map/ppermute | solution.py:340
  21.7 1.0 %shard_map.79.refs_2_.refs_11_ = f32[1,256,256]{2,1,0:T(8,128)S(1)} custom-call(f32[1,6,256,256]{3,2,1,0:T(8,128)} %coupling.5, f32[32,384]{1,0:T(8,128)S(1)} %add.9._.sums), custom_call_target="tpu_custom_call" | custom-call | flops 1 | bytes 1 | tf_op jit(solution)/shard_map/pallas_call | solution.py:320
  22.7 0.0 collective-permute-done.7.other
  22.7 0.0 collective-permute-done.8.refs_0_
  22.7 0.0 collective-permute-done.9.refs_1_
  22.7 0.3 shard_map.80.factor
  23.0 0.2 collective-permute-done.4.got
  23.3 0.0 collective-permute-done.10.refs_1_
  23.3 0.2 shard_map.81
  23.4 1.7 %collective-permute-start.11 = (f32[32,768]{1,0:T(8,128)S(1)}, f32[32,768]{1,0:T(8,128)S(1)}, u32[]{:S(2)}, u32[]{:S(2)}) collective-permute-start(f32[32,768]{1,0:T(8,128)S(1)} %get-tuple-element.58._.packed), channel_id=1, source_target_pairs={{0,9},{1,8},{2,11},{3,10},{4,13},{5,12},{6,15},{7,14},{8,1},{9,0},... | collective-permute-start | bytes 294920 | tf_op jit(solution)/shard_map/ppermute | solution.py:340
  25.2 1.5 %shard_map.82 = (f32[256,512]{1,0:T(8,128)S(1)}, f32[2,256,256]{2,1,0:T(8,128)S(1)}) custom-call(f32[6,512,128]{2,1,0:T(8,128)} %left.3, f32[1,6,256,256]{3,2,1,0:T(8,128)} %coupling.5, f32[32,768]{1,0:T(8,128)S(1)} %get-tuple-element.58._.packed), custom_call_target="tpu_custom_call" | custom-call | flops 1 | bytes 1 | tf_op jit(solution)/shard_map/pallas_call | solution.py:320
  26.7 1.2 %collective-permute-done.11.got = f32[32,768]{1,0:T(8,128)S(1)} collective-permute-done((f32[32,768]{1,0:T(8,128)S(1)}, f32[32,768]{1,0:T(8,128)S(1)}, u32[]{:S(2)}, u32[]{:S(2)}) %collective-permute-start.11) | collective-permute-done | bytes 98336 | tf_op jit(solution)/shard_map/ppermute | solution.py:340
  27.9 0.3 shard_map.83
  28.2 1.7 %collective-permute-start.13 = (f32[32,128]{1,0:T(8,128)S(1)}, f32[32,128]{1,0:T(8,128)S(1)}, u32[]{:S(2)}, u32[]{:S(2)}) collective-permute-start(f32[32,128]{1,0:T(8,128)S(1)} %get-tuple-element.68), channel_id=1, source_target_pairs={{0,17},{1,16},{2,19},{3,18},{4,21},{5,20},{6,23},{7,22},{8,25},{9,... | collective-permute-start | bytes 49160 | tf_op jit(solution)/shard_map/ppermute | solution.py:340
  30.0 0.1 collective-permute-start.12
  30.0 1.4 %collective-permute-done.13 = f32[32,128]{1,0:T(8,128)S(1)} collective-permute-done((f32[32,128]{1,0:T(8,128)S(1)}, f32[32,128]{1,0:T(8,128)S(1)}, u32[]{:S(2)}, u32[]{:S(2)}) %collective-permute-start.13) | collective-permute-done | bytes 16416 | tf_op jit(solution)/shard_map/ppermute | solution.py:340
  31.5 0.6 %collective-permute-start.14 = (f32[32,256]{1,0:T(8,128)S(1)}, f32[32,256]{1,0:T(8,128)S(1)}, u32[]{:S(2)}, u32[]{:S(2)}) collective-permute-start(f32[32,256]{1,0:T(8,128)S(1)} %pad_maximum_fusion.1.mine), channel_id=1, source_target_pairs={{0,1},{1,0},{2,3},{3,2},{4,5},{5,4},{6,7},{7,6},{8,9},{9,8},{10,11... | collective-permute-start | bytes 98312 | tf_op jit(solution)/shard_map/ppermute | solution.py:340
  32.1 0.0 collective-permute-done.12
  32.1 0.6 %shard_map.84.current = f32[64,512]{1,0:T(8,128)S(1)} custom-call(f32[64,512]{1,0:T(8,128)S(1)} %get-tuple-element.46.current, f32[32,256]{1,0:T(8,128)S(1)} %get-tuple-element.61.refs_0_, f32[32,256]{1,0:T(8,128)S(1)} %get-tuple-element.72.refs_1_, f32[32,256]{1,0:T(8,128)S(1)} %get-tuple-element.62.refs_2_, f32[32,256]{1,0:T(8,128)S(1)} %get-tuple-element.71.refs_3_, ...), custom_call_target="tpu_custom_call" | custom-call | flops 1 | bytes 1 | tf_op jit(solution)/shard_map/pallas_call | solution.py:320
  32.7 0.2 collective-permute-done.14.other
  32.9 0.9 %shard_map.85 = f32[64,512]{1,0:T(8,128)} custom-call(f32[64,512]{1,0:T(8,128)S(1)} %shard_map.84.current, f32[32,256]{1,0:T(8,128)S(1)} %pad_maximum_fusion.1.mine, f32[32,256]{1,0:T(8,128)S(1)} %collective-permute-done.14.other, f32[256,512]{1,0:T(8,128)S(1)} %get-tuple-element.60._.factor), custom_call_target="tpu_custom_call" | custom-call | flops 1 | bytes 1 | tf_op jit(solution)/shard_map/pallas_call | solution.py:320
  (10 shorter events, 0.1 us)
Async XLA Ops:
  4.0 1.7 %collective-permute-start.2 = (f32[64,1152]{1,0:T(8,128)S(1)}, f32[64,1152]{1,0:T(8,128)S(1)}, u32[]{:S(2)}, u32[]{:S(2)}) collective-permute-start(f32[64,1152]{1,0:T(8,128)S(1)} %get-tuple-element.52), channel_id=1, source_target_pairs={{0,1},{1,0},{2,3},{3,2},{4,5},{5,4},{6,7},{7,6},{8,9},{9,8},{10,11... | collective-permute-start | bytes 884744 | tf_op jit(solution)/shard_map/ppermute | solution.py:340
  5.6 2.9 %collective-permute-start = (f32[32,2688]{1,0:T(8,128)S(1)}, f32[32,2688]{1,0:T(8,128)S(1)}, u32[]{:S(2)}, u32[]{:S(2)}) collective-permute-start(f32[32,2688]{1,0:T(8,128)S(1)} %get-tuple-element.48), channel_id=1, source_target_pairs={{0,1},{1,0},{2,3},{3,2},{4,5},{5,4},{6,7},{7,6},{8,9},{9,8},{10,11... | collective-permute-start | bytes 1032200 | tf_op jit(solution)/shard_map/ppermute | solution.py:340
  5.7 6.4 %collective-permute-start.5 = (f32[64,384]{1,0:T(8,128)S(1)}, f32[64,384]{1,0:T(8,128)S(1)}, u32[]{:S(2)}, u32[]{:S(2)}) collective-permute-start(f32[64,384]{1,0:T(8,128)S(1)} %slice_add_fusion.low), channel_id=1, source_target_pairs={{0,3},{1,2},{2,1},{3,0},{4,7},{5,6},{6,5},{7,4},{8,11},{9,10},{10,... | collective-permute-start | bytes 294920 | tf_op jit(solution)/shard_map/ppermute | solution.py:340
  8.9 3.2 %collective-permute-start.1 = (f32[32,128]{1,0:T(8,128)S(1)}, f32[32,128]{1,0:T(8,128)S(1)}, u32[]{:S(2)}, u32[]{:S(2)}) collective-permute-start(f32[32,128]{1,0:T(8,128)S(1)} %get-tuple-element.49.mine), channel_id=1, source_target_pairs={{0,3},{1,2},{2,1},{3,0},{4,7},{5,6},{6,5},{7,4},{8,11},{9,10},{10,... | collective-permute-start | bytes 49160 | tf_op jit(solution)/shard_map/ppermute | solution.py:340
  12.1 8.6 %collective-permute-start.6 = (f32[64,384]{1,0:T(8,128)S(1)}, f32[64,384]{1,0:T(8,128)S(1)}, u32[]{:S(2)}, u32[]{:S(2)}) collective-permute-start(f32[64,384]{1,0:T(8,128)S(1)} %shard_map.77.low), channel_id=1, source_target_pairs={{0,5},{1,4},{2,7},{3,6},{4,1},{5,0},{6,3},{7,2},{8,13},{9,12},{10,... | collective-permute-start | bytes 294920 | tf_op jit(solution)/shard_map/ppermute | solution.py:340
  15.1 3.7 %collective-permute-start.3 = (f32[32,384]{1,0:T(8,128)S(1)}, f32[32,384]{1,0:T(8,128)S(1)}, u32[]{:S(2)}, u32[]{:S(2)}) collective-permute-start(f32[32,384]{1,0:T(8,128)S(1)} %get-tuple-element.53), channel_id=1, source_target_pairs={{0,3},{1,2},{2,1},{3,0},{4,7},{5,6},{6,5},{7,4},{8,11},{9,10},{10,... | collective-permute-start | bytes 147464 | tf_op jit(solution)/shard_map/ppermute | solution.py:340
  16.7 6.0 %collective-permute-start.7 = (f32[64,256]{1,0:T(8,128)S(1)}, f32[64,256]{1,0:T(8,128)S(1)}, u32[]{:S(2)}, u32[]{:S(2)}) collective-permute-start(f32[64,256]{1,0:T(8,128)S(1)} %slice.25), channel_id=1, source_target_pairs={{0,1},{1,0},{2,3},{3,2},{4,5},{5,4},{6,7},{7,6},{8,9},{9,8},{10,11... | collective-permute-start | bytes 196616 | tf_op jit(solution)/shard_map/ppermute | solution.py:340
  18.8 4.4 %collective-permute-start.4 = (f32[32,384]{1,0:T(8,128)S(1)}, f32[32,384]{1,0:T(8,128)S(1)}, u32[]{:S(2)}, u32[]{:S(2)}) collective-permute-start(f32[32,384]{1,0:T(8,128)S(1)} %add.9._.sums), channel_id=1, source_target_pairs={{0,5},{1,4},{2,7},{3,6},{4,1},{5,0},{6,3},{7,2},{8,13},{9,12},{10,... | collective-permute-start | bytes 147464 | tf_op jit(solution)/shard_map/ppermute | solution.py:340
  20.8 1.9 %collective-permute-start.8 = (f32[64,128]{1,0:T(8,128)S(1)}, f32[64,128]{1,0:T(8,128)S(1)}, u32[]{:S(2)}, u32[]{:S(2)}) collective-permute-start(f32[64,128]{1,0:T(8,128)S(1)} %get-tuple-element.55), channel_id=1, source_target_pairs={{0,1},{1,0},{2,3},{3,2},{4,5},{5,4},{6,7},{7,6},{8,9},{9,8},{10,11... | collective-permute-start | bytes 98312 | tf_op jit(solution)/shard_map/ppermute | solution.py:340
  21.2 1.5 %collective-permute-start.9 = (f32[64,128]{1,0:T(8,128)S(1)}, f32[64,128]{1,0:T(8,128)S(1)}, u32[]{:S(2)}, u32[]{:S(2)}) collective-permute-start(f32[64,128]{1,0:T(8,128)S(1)} %get-tuple-element.56), channel_id=1, source_target_pairs={{0,1},{1,0},{2,3},{3,2},{4,5},{5,4},{6,7},{7,6},{8,9},{9,8},{10,11... | collective-permute-start | bytes 98312 | tf_op jit(solution)/shard_map/ppermute | solution.py:340
  21.3 1.9 %collective-permute-start.10 = (f32[64,128]{1,0:T(8,128)S(1)}, f32[64,128]{1,0:T(8,128)S(1)}, u32[]{:S(2)}, u32[]{:S(2)}) collective-permute-start(f32[64,128]{1,0:T(8,128)S(1)} %get-tuple-element.57.refs_0_), channel_id=1, source_target_pairs={{0,1},{1,0},{2,3},{3,2},{4,5},{5,4},{6,7},{7,6},{8,9},{9,8},{10,11... | collective-permute-start | bytes 98312 | tf_op jit(solution)/shard_map/ppermute | solution.py:340
  23.4 4.4 %collective-permute-start.11 = (f32[32,768]{1,0:T(8,128)S(1)}, f32[32,768]{1,0:T(8,128)S(1)}, u32[]{:S(2)}, u32[]{:S(2)}) collective-permute-start(f32[32,768]{1,0:T(8,128)S(1)} %get-tuple-element.58._.packed), channel_id=1, source_target_pairs={{0,9},{1,8},{2,11},{3,10},{4,13},{5,12},{6,15},{7,14},{8,1},{9,0},... | collective-permute-start | bytes 294920 | tf_op jit(solution)/shard_map/ppermute | solution.py:340
  28.2 3.2 %collective-permute-start.13 = (f32[32,128]{1,0:T(8,128)S(1)}, f32[32,128]{1,0:T(8,128)S(1)}, u32[]{:S(2)}, u32[]{:S(2)}) collective-permute-start(f32[32,128]{1,0:T(8,128)S(1)} %get-tuple-element.68), channel_id=1, source_target_pairs={{0,17},{1,16},{2,19},{3,18},{4,21},{5,20},{6,23},{7,22},{8,25},{9,... | collective-permute-start | bytes 49160 | tf_op jit(solution)/shard_map/ppermute | solution.py:340
  30.0 2.1 %collective-permute-start.12 = (f32[32,768]{1,0:T(8,128)S(1)}, f32[32,768]{1,0:T(8,128)S(1)}, u32[]{:S(2)}, u32[]{:S(2)}) collective-permute-start(f32[32,768]{1,0:T(8,128)S(1)} %pad_maximum_fusion), channel_id=1, source_target_pairs={{0,1},{1,0},{2,3},{3,2},{4,5},{5,4},{6,7},{7,6},{8,9},{9,8},{10,11... | collective-permute-start | bytes 294920 | tf_op jit(solution)/shard_map/ppermute | solution.py:340
  31.5 1.5 %collective-permute-start.14 = (f32[32,256]{1,0:T(8,128)S(1)}, f32[32,256]{1,0:T(8,128)S(1)}, u32[]{:S(2)}, u32[]{:S(2)}) collective-permute-start(f32[32,256]{1,0:T(8,128)S(1)} %pad_maximum_fusion.1.mine), channel_id=1, source_target_pairs={{0,1},{1,0},{2,3},{3,2},{4,5},{5,4},{6,7},{7,6},{8,9},{9,8},{10,11... | collective-permute-start | bytes 98312 | tf_op jit(solution)/shard_map/ppermute | solution.py:340

commit v14 on v13

--- a/solution.py
+++ b/solution.py
@@ -29,10 +29,13 @@
 
 
 def dot(a, b, dims=NN):
+    return dot_parts(a, *parts(b), dims)
+
+
+def dot_parts(a, bh, bl, dims=NN):
     if dims == TN:
         a, dims = a.T, NN
     ah, al = parts(a)
-    bh, bl = parts(b)
     rows = a.shape[0]
     both = product(jnp.concatenate([ah, al], axis=0), bh, dims)
     return both[:rows] + (both[rows:] + product(ah, bl, dims))
@@ -97,7 +100,8 @@
     moved = product(jnp.concatenate([high, low], axis=0), pick, NN).astype(BF16)
     for copy in bases:
         copy.wait()
-    grams = dot(left_low[...], right_low[...], TN)
+    low_parts = parts(right_low[...])
+    grams = dot_parts(left_low[...], *low_parts, TN)
     at = 0
     for k in range(count, 0, -1):
         w = k * rank
@@ -122,7 +126,7 @@
         copy.wait()
     low_w = right_low.shape[1]
     upper = left_mid[...]
-    value = dot(upper, right_low[...], TN)
+    value = dot_parts(upper, *low_parts, TN)
     gram_next[:, :low_w] = value[:rank]
     gram_top[:, :low_w] = value[rank:]
     value = dot(upper, right_mid[...], TN)

time: 34 us -> 34 us (level)
  no operation moved by 1% of the time
where the time goes in v14:
time: 34 us; the launch traced here: 33.8 us
  starting transfers between devices  16.5 us (49%)
  Pallas kernels  9.84 us (29%)
  waiting for transfers between devices  6.63 us (20%)
  between operations  0.78 us (2%)
    ppermute x15, starting transfers between devices, exchange(): lax.ppermute(value, AXES, [(i, i ^ mask) for i in range(lax.axis_size(AXE...  16.5 us
    pallas_call x13, Pallas kernels, call(): pl.pallas_call(kernel, out_shape=outs, in_specs=in_specs, out_specs=out_s...  9.84 us
    ppermute x15, waiting for transfers between devices, exchange(): lax.ppermute(value, AXES, [(i, i ^ mask) for i in range(lax.axis_size(AXE...  6.63 us
  transfers between devices with their start and end apart: 15, of which 6 were waited for; matrix products, arithmetic and copies ran while one was open for 0% of the time, Pallas kernels for 15%

profile of v14, /device:TPU:0, one launch (start us, length us, event | category | flops | bytes accessed | tf_op | source)
XLA Modules:
  0.0 33.8 jit_solution(8453146625347924709)
XLA Ops:
  0.7 3.3 %shard_map.73 = (f32[64,384]{1,0:T(8,128)S(1)}, f32[64,1152]{1,0:T(8,128)S(1)}, f32[64,512]{1,0:T(8,128)S(1)}, f32[128,512]{1,0:T(8,128)S(1)}, f32[128,384]{1,0:...) custom-call(f32[6,512,128]{2,1,0:T(8,128)} %left.3, ...), custom_call_target="tpu_custom_call" | custom-call | flops 1 | bytes 1 | tf_op jit(solution)/shard_map/pallas_call | solution.py:324
  4.0 0.5 %collective-permute-start.2 = (f32[64,1152]{1,0:T(8,128)S(1)}, f32[64,1152]{1,0:T(8,128)S(1)}, u32[]{:S(2)}, u32[]{:S(2)}) collective-permute-start(f32[64,1152]{1,0:T(8,128)S(1)} %get-tuple-element.52), channel_id=1, source_target_pairs={{0,1},{1,0},{2,3},{3,2},{4,5},{5,4},{6,7},{7,6},{8,9},{9,8},{10,11... | collective-permute-start | bytes 884744 | tf_op jit(solution)/shard_map/ppermute | solution.py:344
  4.5 1.1 %shard_map.74 = (f32[64,512]{1,0:T(8,128)S(1)}, f32[32,640]{1,0:T(8,128)S(1)}, f32[32,2688]{1,0:T(8,128)S(1)}) custom-call(s32[8,128]{1,0:T(8,128)S(1)} %get-tuple-element.37.split, f32[64,512]{1,0:T(8,128)S(1)} %get-tuple-element.38.first, f32[512,128]{1,0:T(8,128)S(1)} %get-tuple-element.39.left_top, f32[512,128]{1,0:T(8,128)S(1)} %get-tuple-element.40.right_top, ...), custom_call_target="tpu_custom_call" | custom-call | flops 1 | bytes 1 | tf_op jit(solution)/shard_map/pallas_call | solution.py:324
  5.6 0.1 collective-permute-start
  5.7 0.0 collective-permute-done.2.got_gram
  5.7 2.7 %collective-permute-start.5 = (f32[64,384]{1,0:T(8,128)S(1)}, f32[64,384]{1,0:T(8,128)S(1)}, u32[]{:S(2)}, u32[]{:S(2)}) collective-permute-start(f32[64,384]{1,0:T(8,128)S(1)} %slice_add_fusion.low), channel_id=1, source_target_pairs={{0,3},{1,2},{2,1},{3,0},{4,7},{5,6},{6,5},{7,4},{8,11},{9,10},{10,... | collective-permute-start | bytes 294920 | tf_op jit(solution)/shard_map/ppermute | solution.py:344
  8.5 0.0 collective-permute-done.got
  8.5 0.4 %shard_map.75 = (f32[32,384]{1,0:T(8,128)S(1)}, f32[32,128]{1,0:T(8,128)S(1)}, f32[32,128]{1,0:T(8,128)S(1)}, f32[32,128]{1,0:T(8,128)S(1)}) custom-call(f32[32,640]{1,0:T(8,128)S(1)} %get-tuple-element.47.keep, f32[32,2688]{1,0:T(8,128)S(1)} %collective-permute-done.got, f32[128,512]{1,0:T(8,128)S(1)} %get-tuple-element.45.gram_top, ...), custom_call_target="tpu_custom_call" | custom-call | flops 1 | bytes 1 | tf_op jit(solution)/shard_map/pallas_call | solution.py:324
  8.9 1.5 %collective-permute-start.1 = (f32[32,128]{1,0:T(8,128)S(1)}, f32[32,128]{1,0:T(8,128)S(1)}, u32[]{:S(2)}, u32[]{:S(2)}) collective-permute-start(f32[32,128]{1,0:T(8,128)S(1)} %get-tuple-element.49.mine), channel_id=1, source_target_pairs={{0,3},{1,2},{2,1},{3,0},{4,7},{5,6},{6,5},{7,4},{8,11},{9,10},{10,... | collective-permute-start | bytes 49160 | tf_op jit(solution)/shard_map/ppermute | solution.py:344
  10.4 1.7 %collective-permute-done.1.got._ = f32[32,128]{1,0:T(8,128)S(1)} collective-permute-done((f32[32,128]{1,0:T(8,128)S(1)}, f32[32,128]{1,0:T(8,128)S(1)}, u32[]{:S(2)}, u32[]{:S(2)}) %collective-permute-start.1) | collective-permute-done | bytes 16416 | tf_op jit(solution)/shard_map/ppermute | solution.py:344
  12.1 0.0 collective-permute-done.5.got
  12.1 2.7 %collective-permute-start.6 = (f32[64,384]{1,0:T(8,128)S(1)}, f32[64,384]{1,0:T(8,128)S(1)}, u32[]{:S(2)}, u32[]{:S(2)}) collective-permute-start(f32[64,384]{1,0:T(8,128)S(1)} %shard_map.77.low), channel_id=1, source_target_pairs={{0,5},{1,4},{2,7},{3,6},{4,1},{5,0},{6,3},{7,2},{8,13},{9,12},{10,... | collective-permute-start | bytes 294920 | tf_op jit(solution)/shard_map/ppermute | solution.py:344
  14.9 0.3 shard_map.76
  15.1 1.6 %collective-permute-start.3 = (f32[32,384]{1,0:T(8,128)S(1)}, f32[32,384]{1,0:T(8,128)S(1)}, u32[]{:S(2)}, u32[]{:S(2)}) collective-permute-start(f32[32,384]{1,0:T(8,128)S(1)} %get-tuple-element.53), channel_id=1, source_target_pairs={{0,3},{1,2},{2,1},{3,0},{4,7},{5,6},{6,5},{7,4},{8,11},{9,10},{10,... | collective-permute-start | bytes 147464 | tf_op jit(solution)/shard_map/ppermute | solution.py:344
  16.7 0.1 collective-permute-start.7
  16.9 2.0 %collective-permute-done.3 = f32[32,384]{1,0:T(8,128)S(1)} collective-permute-done((f32[32,384]{1,0:T(8,128)S(1)}, f32[32,384]{1,0:T(8,128)S(1)}, u32[]{:S(2)}, u32[]{:S(2)}) %collective-permute-start.3) | collective-permute-done | bytes 49184 | tf_op jit(solution)/shard_map/ppermute | solution.py:344
  18.8 1.9 %collective-permute-start.4 = (f32[32,384]{1,0:T(8,128)S(1)}, f32[32,384]{1,0:T(8,128)S(1)}, u32[]{:S(2)}, u32[]{:S(2)}) collective-permute-start(f32[32,384]{1,0:T(8,128)S(1)} %add.9._.sums), channel_id=1, source_target_pairs={{0,5},{1,4},{2,7},{3,6},{4,1},{5,0},{6,3},{7,2},{8,13},{9,12},{10,... | collective-permute-start | bytes 147464 | tf_op jit(solution)/shard_map/ppermute | solution.py:344
  20.7 0.0 collective-permute-done.6.got.got_low
  20.7 0.5 %collective-permute-start.8 = (f32[64,128]{1,0:T(8,128)S(1)}, f32[64,128]{1,0:T(8,128)S(1)}, u32[]{:S(2)}, u32[]{:S(2)}) collective-permute-start(f32[64,128]{1,0:T(8,128)S(1)} %get-tuple-element.55), channel_id=1, source_target_pairs={{0,1},{1,0},{2,3},{3,2},{4,5},{5,4},{6,7},{7,6},{8,9},{9,8},{10,11... | collective-permute-start | bytes 98312 | tf_op jit(solution)/shard_map/ppermute | solution.py:344
  21.2 0.1 collective-permute-start.9
  21.3 0.4 %collective-permute-start.10 = (f32[64,128]{1,0:T(8,128)S(1)}, f32[64,128]{1,0:T(8,128)S(1)}, u32[]{:S(2)}, u32[]{:S(2)}) collective-permute-start(f32[64,128]{1,0:T(8,128)S(1)} %get-tuple-element.57.refs_0_), channel_id=1, source_target_pairs={{0,1},{1,0},{2,3},{3,2},{4,5},{5,4},{6,7},{7,6},{8,9},{9,8},{10,11... | collective-permute-start | bytes 98312 | tf_op jit(solution)/shard_map/ppermute | solution.py:344
  21.7 1.0 %shard_map.79.refs_2_.refs_11_ = f32[1,256,256]{2,1,0:T(8,128)S(1)} custom-call(f32[1,6,256,256]{3,2,1,0:T(8,128)} %coupling.5, f32[32,384]{1,0:T(8,128)S(1)} %add.9._.sums), custom_call_target="tpu_custom_call" | custom-call | flops 1 | bytes 1 | tf_op jit(solution)/shard_map/pallas_call | solution.py:324
  22.7 0.0 collective-permute-done.7.other
  22.7 0.0 collective-permute-done.8.refs_0_
  22.7 0.0 collective-permute-done.9.refs_1_
  22.7 0.3 shard_map.80.factor
  23.0 0.3 collective-permute-done.4.got
  23.3 0.0 collective-permute-done.10.refs_1_
  23.3 0.2 shard_map.81
  23.4 1.7 %collective-permute-start.11 = (f32[32,768]{1,0:T(8,128)S(1)}, f32[32,768]{1,0:T(8,128)S(1)}, u32[]{:S(2)}, u32[]{:S(2)}) collective-permute-start(f32[32,768]{1,0:T(8,128)S(1)} %get-tuple-element.58._.packed), channel_id=1, source_target_pairs={{0,9},{1,8},{2,11},{3,10},{4,13},{5,12},{6,15},{7,14},{8,1},{9,0},... | collective-permute-start | bytes 294920 | tf_op jit(solution)/shard_map/ppermute | solution.py:344
  25.2 1.5 %shard_map.82 = (f32[256,512]{1,0:T(8,128)S(1)}, f32[2,256,256]{2,1,0:T(8,128)S(1)}) custom-call(f32[6,512,128]{2,1,0:T(8,128)} %left.3, f32[1,6,256,256]{3,2,1,0:T(8,128)} %coupling.5, f32[32,768]{1,0:T(8,128)S(1)} %get-tuple-element.58._.packed), custom_call_target="tpu_custom_call" | custom-call | flops 1 | bytes 1 | tf_op jit(solution)/shard_map/pallas_call | solution.py:324
  26.7 1.2 %collective-permute-done.11.got = f32[32,768]{1,0:T(8,128)S(1)} collective-permute-done((f32[32,768]{1,0:T(8,128)S(1)}, f32[32,768]{1,0:T(8,128)S(1)}, u32[]{:S(2)}, u32[]{:S(2)}) %collective-permute-start.11) | collective-permute-done | bytes 98336 | tf_op jit(solution)/shard_map/ppermute | solution.py:344
  27.8 0.3 shard_map.83
  28.2 1.8 %collective-permute-start.13 = (f32[32,128]{1,0:T(8,128)S(1)}, f32[32,128]{1,0:T(8,128)S(1)}, u32[]{:S(2)}, u32[]{:S(2)}) collective-permute-start(f32[32,128]{1,0:T(8,128)S(1)} %get-tuple-element.68), channel_id=1, source_target_pairs={{0,17},{1,16},{2,19},{3,18},{4,21},{5,20},{6,23},{7,22},{8,25},{9,... | collective-permute-start | bytes 49160 | tf_op jit(solution)/shard_map/ppermute | solution.py:344
  30.0 0.1 collective-permute-start.12
  30.1 1.4 %collective-permute-done.13 = f32[32,128]{1,0:T(8,128)S(1)} collective-permute-done((f32[32,128]{1,0:T(8,128)S(1)}, f32[32,128]{1,0:T(8,128)S(1)}, u32[]{:S(2)}, u32[]{:S(2)}) %collective-permute-start.13) | collective-permute-done | bytes 16416 | tf_op jit(solution)/shard_map/ppermute | solution.py:344
  31.4 0.6 %collective-permute-start.14 = (f32[32,256]{1,0:T(8,128)S(1)}, f32[32,256]{1,0:T(8,128)S(1)}, u32[]{:S(2)}, u32[]{:S(2)}) collective-permute-start(f32[32,256]{1,0:T(8,128)S(1)} %pad_maximum_fusion.1.mine), channel_id=1, source_target_pairs={{0,1},{1,0},{2,3},{3,2},{4,5},{5,4},{6,7},{7,6},{8,9},{9,8},{10,11... | collective-permute-start | bytes 98312 | tf_op jit(solution)/shard_map/ppermute | solution.py:344
  32.1 0.0 collective-permute-done.12
  32.1 0.6 %shard_map.84.current = f32[64,512]{1,0:T(8,128)S(1)} custom-call(f32[64,512]{1,0:T(8,128)S(1)} %get-tuple-element.46.current, f32[32,256]{1,0:T(8,128)S(1)} %get-tuple-element.61.refs_0_, f32[32,256]{1,0:T(8,128)S(1)} %get-tuple-element.72.refs_1_, f32[32,256]{1,0:T(8,128)S(1)} %get-tuple-element.62.refs_2_, f32[32,256]{1,0:T(8,128)S(1)} %get-tuple-element.71.refs_3_, ...), custom_call_target="tpu_custom_call" | custom-call | flops 1 | bytes 1 | tf_op jit(solution)/shard_map/pallas_call | solution.py:324
  32.7 0.2 collective-permute-done.14.other
  32.9 0.9 %shard_map.85 = f32[64,512]{1,0:T(8,128)} custom-call(f32[64,512]{1,0:T(8,128)S(1)} %shard_map.84.current, f32[32,256]{1,0:T(8,128)S(1)} %pad_maximum_fusion.1.mine, f32[32,256]{1,0:T(8,128)S(1)} %collective-permute-done.14.other, f32[256,512]{1,0:T(8,128)S(1)} %get-tuple-element.60._.factor), custom_call_target="tpu_custom_call" | custom-call | flops 1 | bytes 1 | tf_op jit(solution)/shard_map/pallas_call | solution.py:324
  (10 shorter events, 0.1 us)
Async XLA Ops:
  4.0 1.7 %collective-permute-start.2 = (f32[64,1152]{1,0:T(8,128)S(1)}, f32[64,1152]{1,0:T(8,128)S(1)}, u32[]{:S(2)}, u32[]{:S(2)}) collective-permute-start(f32[64,1152]{1,0:T(8,128)S(1)} %get-tuple-element.52), channel_id=1, source_target_pairs={{0,1},{1,0},{2,3},{3,2},{4,5},{5,4},{6,7},{7,6},{8,9},{9,8},{10,11... | collective-permute-start | bytes 884744 | tf_op jit(solution)/shard_map/ppermute | solution.py:344
  5.6 2.9 %collective-permute-start = (f32[32,2688]{1,0:T(8,128)S(1)}, f32[32,2688]{1,0:T(8,128)S(1)}, u32[]{:S(2)}, u32[]{:S(2)}) collective-permute-start(f32[32,2688]{1,0:T(8,128)S(1)} %get-tuple-element.48), channel_id=1, source_target_pairs={{0,1},{1,0},{2,3},{3,2},{4,5},{5,4},{6,7},{7,6},{8,9},{9,8},{10,11... | collective-permute-start | bytes 1032200 | tf_op jit(solution)/shard_map/ppermute | solution.py:344
  5.7 6.3 %collective-permute-start.5 = (f32[64,384]{1,0:T(8,128)S(1)}, f32[64,384]{1,0:T(8,128)S(1)}, u32[]{:S(2)}, u32[]{:S(2)}) collective-permute-start(f32[64,384]{1,0:T(8,128)S(1)} %slice_add_fusion.low), channel_id=1, source_target_pairs={{0,3},{1,2},{2,1},{3,0},{4,7},{5,6},{6,5},{7,4},{8,11},{9,10},{10,... | collective-permute-start | bytes 294920 | tf_op jit(solution)/shard_map/ppermute | solution.py:344
  8.9 3.2 %collective-permute-start.1 = (f32[32,128]{1,0:T(8,128)S(1)}, f32[32,128]{1,0:T(8,128)S(1)}, u32[]{:S(2)}, u32[]{:S(2)}) collective-permute-start(f32[32,128]{1,0:T(8,128)S(1)} %get-tuple-element.49.mine), channel_id=1, source_target_pairs={{0,3},{1,2},{2,1},{3,0},{4,7},{5,6},{6,5},{7,4},{8,11},{9,10},{10,... | collective-permute-start | bytes 49160 | tf_op jit(solution)/shard_map/ppermute | solution.py:344
  12.1 8.6 %collective-permute-start.6 = (f32[64,384]{1,0:T(8,128)S(1)}, f32[64,384]{1,0:T(8,128)S(1)}, u32[]{:S(2)}, u32[]{:S(2)}) collective-permute-start(f32[64,384]{1,0:T(8,128)S(1)} %shard_map.77.low), channel_id=1, source_target_pairs={{0,5},{1,4},{2,7},{3,6},{4,1},{5,0},{6,3},{7,2},{8,13},{9,12},{10,... | collective-permute-start | bytes 294920 | tf_op jit(solution)/shard_map/ppermute | solution.py:344
  15.1 3.7 %collective-permute-start.3 = (f32[32,384]{1,0:T(8,128)S(1)}, f32[32,384]{1,0:T(8,128)S(1)}, u32[]{:S(2)}, u32[]{:S(2)}) collective-permute-start(f32[32,384]{1,0:T(8,128)S(1)} %get-tuple-element.53), channel_id=1, source_target_pairs={{0,3},{1,2},{2,1},{3,0},{4,7},{5,6},{6,5},{7,4},{8,11},{9,10},{10,... | collective-permute-start | bytes 147464 | tf_op jit(solution)/shard_map/ppermute | solution.py:344
  16.7 6.0 %collective-permute-start.7 = (f32[64,256]{1,0:T(8,128)S(1)}, f32[64,256]{1,0:T(8,128)S(1)}, u32[]{:S(2)}, u32[]{:S(2)}) collective-permute-start(f32[64,256]{1,0:T(8,128)S(1)} %slice.25), channel_id=1, source_target_pairs={{0,1},{1,0},{2,3},{3,2},{4,5},{5,4},{6,7},{7,6},{8,9},{9,8},{10,11... | collective-permute-start | bytes 196616 | tf_op jit(solution)/shard_map/ppermute | solution.py:344
  18.8 4.4 %collective-permute-start.4 = (f32[32,384]{1,0:T(8,128)S(1)}, f32[32,384]{1,0:T(8,128)S(1)}, u32[]{:S(2)}, u32[]{:S(2)}) collective-permute-start(f32[32,384]{1,0:T(8,128)S(1)} %add.9._.sums), channel_id=1, source_target_pairs={{0,5},{1,4},{2,7},{3,6},{4,1},{5,0},{6,3},{7,2},{8,13},{9,12},{10,... | collective-permute-start | bytes 147464 | tf_op jit(solution)/shard_map/ppermute | solution.py:344
  20.7 1.9 %collective-permute-start.8 = (f32[64,128]{1,0:T(8,128)S(1)}, f32[64,128]{1,0:T(8,128)S(1)}, u32[]{:S(2)}, u32[]{:S(2)}) collective-permute-start(f32[64,128]{1,0:T(8,128)S(1)} %get-tuple-element.55), channel_id=1, source_target_pairs={{0,1},{1,0},{2,3},{3,2},{4,5},{5,4},{6,7},{7,6},{8,9},{9,8},{10,11... | collective-permute-start | bytes 98312 | tf_op jit(solution)/shard_map/ppermute | solution.py:344
  21.2 1.5 %collective-permute-start.9 = (f32[64,128]{1,0:T(8,128)S(1)}, f32[64,128]{1,0:T(8,128)S(1)}, u32[]{:S(2)}, u32[]{:S(2)}) collective-permute-start(f32[64,128]{1,0:T(8,128)S(1)} %get-tuple-element.56), channel_id=1, source_target_pairs={{0,1},{1,0},{2,3},{3,2},{4,5},{5,4},{6,7},{7,6},{8,9},{9,8},{10,11... | collective-permute-start | bytes 98312 | tf_op jit(solution)/shard_map/ppermute | solution.py:344
  21.3 2.0 %collective-permute-start.10 = (f32[64,128]{1,0:T(8,128)S(1)}, f32[64,128]{1,0:T(8,128)S(1)}, u32[]{:S(2)}, u32[]{:S(2)}) collective-permute-start(f32[64,128]{1,0:T(8,128)S(1)} %get-tuple-element.57.refs_0_), channel_id=1, source_target_pairs={{0,1},{1,0},{2,3},{3,2},{4,5},{5,4},{6,7},{7,6},{8,9},{9,8},{10,11... | collective-permute-start | bytes 98312 | tf_op jit(solution)/shard_map/ppermute | solution.py:344
  23.4 4.4 %collective-permute-start.11 = (f32[32,768]{1,0:T(8,128)S(1)}, f32[32,768]{1,0:T(8,128)S(1)}, u32[]{:S(2)}, u32[]{:S(2)}) collective-permute-start(f32[32,768]{1,0:T(8,128)S(1)} %get-tuple-element.58._.packed), channel_id=1, source_target_pairs={{0,9},{1,8},{2,11},{3,10},{4,13},{5,12},{6,15},{7,14},{8,1},{9,0},... | collective-permute-start | bytes 294920 | tf_op jit(solution)/shard_map/ppermute | solution.py:344
  28.2 3.2 %collective-permute-start.13 = (f32[32,128]{1,0:T(8,128)S(1)}, f32[32,128]{1,0:T(8,128)S(1)}, u32[]{:S(2)}, u32[]{:S(2)}) collective-permute-start(f32[32,128]{1,0:T(8,128)S(1)} %get-tuple-element.68), channel_id=1, source_target_pairs={{0,17},{1,16},{2,19},{3,18},{4,21},{5,20},{6,23},{7,22},{8,25},{9,... | collective-permute-start | bytes 49160 | tf_op jit(solution)/shard_map/ppermute | solution.py:344
  30.0 2.1 %collective-permute-start.12 = (f32[32,768]{1,0:T(8,128)S(1)}, f32[32,768]{1,0:T(8,128)S(1)}, u32[]{:S(2)}, u32[]{:S(2)}) collective-permute-start(f32[32,768]{1,0:T(8,128)S(1)} %pad_maximum_fusion), channel_id=1, source_target_pairs={{0,1},{1,0},{2,3},{3,2},{4,5},{5,4},{6,7},{7,6},{8,9},{9,8},{10,11... | collective-permute-start | bytes 294920 | tf_op jit(solution)/shard_map/ppermute | solution.py:344
  31.4 1.5 %collective-permute-start.14 = (f32[32,256]{1,0:T(8,128)S(1)}, f32[32,256]{1,0:T(8,128)S(1)}, u32[]{:S(2)}, u32[]{:S(2)}) collective-permute-start(f32[32,256]{1,0:T(8,128)S(1)} %pad_maximum_fusion.1.mine), channel_id=1, source_target_pairs={{0,1},{1,0},{2,3},{3,2},{4,5},{5,4},{6,7},{7,6},{8,9},{9,8},{10,11... | collective-permute-start | bytes 98312 | tf_op jit(solution)/shard_map/ppermute | solution.py:344
